TPU v7x, 32 devices: a whole 2x2x4 slice. The times are simulated.
32 devices in a mesh: lat: 16 (over z, y, core), lon: 2 (over x).
Axes of the slice: x: 2, y: 2, z: 4, core: 2. Of those that a mesh axis runs over, the one named last changes fastest.
Arguments:
- field: bfloat16 [192, 768, 512], P('lat', 'lon'), may hold values from -6 to 6
- quad_weight: float32 [192], P('lat'), may hold values from 0.5 to 1.5
- legendre: bfloat16 [192, 192, 192], P('lat'), as said below
- filter_real: float32 [192, 512], replicated, may hold values from -4 to 4
- filter_imag: float32 [192, 512], replicated, may hold values from -4 to 4
- neighbour: int32 [192, 12], P('lat'), may hold values from 0 to 24
- basis: int32 [192, 12], P('lat'), may hold values from 0 to 7
- disco_quad: float32 [192, 12], P('lat'), may hold values from 0.5 to 1.5
- disco_weight: float32 [8, 512], replicated, may hold values from -2 to 2
- norm_gain: float32 [512], replicated, may hold values from 0.5 to 1.5
- w_in: bfloat16 [512, 1024], replicated, may hold values from -0.25 to 0.25
- b_in: float32 [1024], replicated, may hold values from -3 to 3
- w_out: bfloat16 [1024, 512], replicated, may hold values from -0.1875 to 0.1875
- b_out: float32 [512], replicated, may hold values from -3 to 3
Outputs:
- block_out: bfloat16 [192, 768, 512], P('lat', 'lon')
- spatial: bfloat16 [192, 768, 512], P('lat', 'lon')
Inputs may be any that keep to these rules, and one draw needn't show every extreme that they name: legendre[m, l, t] = 0 for l < m.
All inputs are finite; a program needn't handle non-finite values.
Results may differ from a plain program's by a relative error of at most 0.018.
Values may be sent and summed in bfloat16 or wider, within the bound.
No kernel may reach another device: no remote copies, remote signals or barrier semaphores. Data moves between devices by JAX's collectives and lax.ppermute only.
A program may use at most 64 MiB of HBM per device.

v0:
```python
import math

import jax
import jax.numpy as jnp
from jax import lax
from jax.sharding import PartitionSpec as P

HALO = 2
KB = 8
NWIN = 25


exact_mode = lax.Precision.HIGHEST


def padded_2(block, sides, width, periodic):
    for axis, dim in sides:
        count = lax.axis_size(axis)
        forward = [(i, i + 1) for i in range(count - 1)]
        if periodic:
            forward.append((count - 1, 0))
        backward = [(target, source) for source, target in forward]
        low = lax.ppermute(
            lax.slice_in_dim(block, block.shape[dim] - width, None, axis=dim), axis, forward
        )
        high = lax.ppermute(lax.slice_in_dim(block, 0, width, axis=dim), axis, backward)
        block = jnp.concatenate([low, block, high], axis=dim)
    return block


def split_table(table):
    upper = table.astype(jnp.bfloat16)
    lower = (table - upper.astype(jnp.float32)).astype(jnp.bfloat16)
    return (upper, lower)


def fourier_tables(nlon, mmax):
    points = jnp.arange(nlon, dtype=jnp.int32)
    waves = jnp.arange(mmax, dtype=jnp.int32)
    phase = waves[:, None] * points[None, :] % nlon
    angle = phase.astype(jnp.float32) * (2.0 * math.pi / nlon)
    cosine = jnp.cos(angle) / math.sqrt(nlon)
    sine = jnp.sin(angle) / math.sqrt(nlon)
    forward_table = jnp.stack([cosine, -sine], axis=0)
    factor = jnp.where(waves == 0, 1.0, 2.0).astype(jnp.float32)[:, None]
    inverse_table = jnp.stack([factor * cosine, -factor * sine], axis=0)
    return (forward_table, inverse_table)


def window_kernel(neighbour, basis, disco_quad, weight_cols):
    places = (neighbour[:, :, None] == jnp.arange(NWIN, dtype=jnp.int32)[None, None, :]).astype(
        jnp.float32
    )
    places = places * disco_quad[:, :, None]
    kinds = (basis[:, :, None] == jnp.arange(KB, dtype=jnp.int32)[None, None, :]).astype(
        jnp.float32
    )
    mixing = jnp.einsum("isn,isb->inb", places, kinds, precision=exact_mode)
    return jnp.einsum("inb,bc->inc", mixing, weight_cols, precision=exact_mode)


def convolve(padded, kernel, lat_rows, lon_cols):
    span = 2 * HALO + 1
    total = jnp.zeros((lat_rows, lon_cols, kernel.shape[2]), jnp.float32)
    for offset in range(NWIN):
        row_shift = offset // span
        col_shift = offset % span
        window = padded[row_shift : row_shift + lat_rows, col_shift : col_shift + lon_cols, :]
        total = total + kernel[:, offset, None, :] * window
    return total


def channel_mlp(spatial, field, norm_gain, w_in, b_in, w_out, b_out):
    channels = spatial.shape[-1]
    tokens = spatial.reshape(-1, channels).astype(jnp.float32)
    center = jnp.mean(tokens, axis=1, keepdims=True)
    spread = jnp.mean((tokens - center) ** 2, axis=1, keepdims=True)
    normed = ((tokens - center) * lax.rsqrt(spread + 1e-05) * norm_gain).astype(jnp.bfloat16)
    hidden = jnp.dot(normed, w_in, preferred_element_type=jnp.float32) + b_in
    hidden = jax.nn.gelu(hidden).astype(jnp.bfloat16)
    result = jnp.dot(hidden, w_out, preferred_element_type=jnp.float32)
    result = result + b_out + field.reshape(-1, channels).astype(jnp.float32)
    return result.astype(jnp.bfloat16).reshape(field.shape)


def shards(
    field,
    quad_weight,
    legendre,
    filter_real,
    filter_imag,
    neighbour,
    basis,
    disco_quad,
    disco_weight,
    norm_gain,
    w_in,
    b_in,
    w_out,
    b_out,
):
    lat_rows, lon_cols, channels = field.shape
    lon_count = lax.axis_size("lon")
    lat_count = lax.axis_size("lat")
    nlon = lon_cols * lon_count
    wave_block = legendre.shape[0]
    mmax = wave_block * lat_count
    cblock = channels // lon_count
    forward_table, inverse_table = fourier_tables(nlon, mmax)
    forward_upper, forward_lower = split_table(forward_table)
    inverse_upper, inverse_lower = split_table(inverse_table)
    columns = lax.all_to_all(field, "lon", split_axis=2, concat_axis=1, tiled=True)
    frequency = jnp.einsum(
        "tkc,rmk->rmtc", columns, forward_upper, preferred_element_type=jnp.float32
    )
    frequency = frequency + jnp.einsum(
        "tkc,rmk->rmtc", columns, forward_lower, preferred_element_type=jnp.float32
    )
    weighted = (frequency * quad_weight[None, None, :, None]).astype(jnp.bfloat16)
    weighted = jnp.transpose(weighted, (1, 2, 0, 3))
    coeffs = jnp.einsum(
        "mlt,mtrc->mlrc",
        legendre,
        lax.all_to_all(weighted, "lat", split_axis=0, concat_axis=1, tiled=True),
        preferred_element_type=jnp.float32,
    )
    chan_start = lax.axis_index("lon") * cblock
    gain_real = lax.dynamic_slice_in_dim(filter_real, chan_start, cblock, 1)[None, :, :]
    gain_imag = lax.dynamic_slice_in_dim(filter_imag, chan_start, cblock, 1)[None, :, :]
    real_part = coeffs[:, :, 0]
    imag_part = coeffs[:, :, 1]
    filtered = jnp.stack(
        [
            gain_real * real_part - gain_imag * imag_part,
            gain_real * imag_part + gain_imag * real_part,
        ],
        axis=2,
    ).astype(jnp.bfloat16)
    synthesis = jnp.einsum(
        "mlt,mlrc->mtrc", legendre, filtered, preferred_element_type=jnp.float32
    ).astype(jnp.bfloat16)
    lat_block = lax.all_to_all(synthesis, "lat", split_axis=1, concat_axis=0, tiled=True)
    wave = jnp.einsum("mtrc,rmk->tkc", lat_block, inverse_upper, preferred_element_type=jnp.float32)
    wave = wave + jnp.einsum(
        "mtrc,rmk->tkc", lat_block, inverse_lower, preferred_element_type=jnp.float32
    )
    wave = wave.astype(jnp.bfloat16)
    kernel = window_kernel(neighbour, basis, disco_quad, disco_weight)
    field_cols = lax.all_to_all(wave, "lon", split_axis=1, concat_axis=2, tiled=True)
    cycle = padded_2(field_cols, (("lon", 1),), HALO, True)
    padded = padded_2(cycle, (("lat", 0),), HALO, False)
    conv = convolve(padded, kernel, lat_rows, lon_cols)
    spatial = (field_cols.astype(jnp.float32) + conv).astype(jnp.bfloat16)
    block_out = channel_mlp(spatial, field, norm_gain, w_in, b_in, w_out, b_out)
    return (block_out, spatial)


def solution(mesh):
    placed = (
        P("lat", "lon", None),
        P("lat"),
        P("lat", None, None),
        P(),
        P(),
        P("lat", None),
        P("lat", None),
        P("lat", None),
        P(),
        P(),
        P(),
        P(),
        P(),
        P(),
    )
    return jax.shard_map(
        shards,
        mesh=mesh,
        in_specs=placed,
        out_specs=(P("lat", "lon", None), P("lat", "lon", None)),
        check_vma=False,
    )
```

profile of v0, /device:TPU:19, one launch (start us, length us, event | category | flops | bytes accessed | tf_op | source)
XLA Modules:
  0.0 445.9 jit_solution(3253917907082667845)
XLA Ops:
  0.6 0.0 copy-start
  0.6 9.2 %copy.45 = bf16[12,384,512]{1,0,2:T(8,128)(2,1)} copy(bf16[12,384,512]{2,1,0:T(8,128)(2,1)} %param.14) | data formatting | bytes 9437184 | tf_op args[0]
  9.9 6.5 %all-to-all-start = ((bf16[12,384,512]{1,0,2:T(8,128)(2,1)}), bf16[12,384,512]{1,0,2:T(8,128)(2,1)}, u32[]{:S(2)}, u32[]{:S(2)}) async-start(bf16[12,384,512]{1,0,2:T(8,128)(2,1)} %copy.45), calls=%async_computation | async-start | bytes 12582912 | tf_op jit(solution)/shard_map/all_to_all | solution.py:112
  16.4 2.4 multiply_negate_fusion
  18.8 65.7 %all-to-all-done = bf16[12,384,512]{1,0,2:T(8,128)(2,1)} async-done(((bf16[12,384,512]{1,0,2:T(8,128)(2,1)}), bf16[12,384,512]{1,0,2:T(8,128)(2,1)}, u32[]{:S(2)}, u32[]{:S(2)}) %all-to-all-start) | async-done | bytes 4718624 | tf_op jit(solution)/shard_map/all_to_all | solution.py:112
  84.6 8.8 %copy.46 = bf16[12,384,2,256]{3,1,2,0:T(8,128)(2,1)} copy(bf16[12,384,2,256]{1,0,3,2:T(8,128)(2,1)} %bitcast.3) | data formatting | bytes 9437184 | tf_op jit(solution)/shard_map/all_to_all | solution.py:112
  93.3 4.5 %fusion.56 = f32[2,192,12,256]{3,1,2,0:T(8,128)S(1)} fusion(bf16[12,768,256,1]{2,1,0,3:T(8,128)(2,1)} %bitcast.138, f32[1,192,768]{2,1,0:T(8,128)S(1)} %get-tuple-element.37, f32[1,192,768]{2,1,0:T(8,128)S(1)} %get-tuple-element.38), kind=kOutput, calls=%fused_computation.73 | convolution fusion | flops 1813118976 | bytes 10616832 | tf_op jit(solution)/shard_map/tkc,rmk->rmtc/dot_general | solution.py:113
  97.8 2.1 fusion.35
  99.9 3.8 copy.47
  103.8 7.3 %all-to-all-start.1 = ((bf16[192,12,2,256]{3,2,1,0:T(2,128)(2,1)}), bf16[192,12,2,256]{3,2,1,0:T(2,128)(2,1)S(1)}, u32[]{:S(2)}, u32[]{:S(2)}) async-start(bf16[192,12,2,256]{3,2,1,0:T(2,128)(2,1)} %copy.47), calls=%async_computation.1 | async-start | bytes 4718592 | tf_op jit(solution)/shard_map/all_to_all | solution.py:124
  111.1 1.8 constant_dynamic-slice_fusion
  112.9 50.8 %all-to-all-done.1 = bf16[192,12,2,256]{3,2,1,0:T(2,128)(2,1)S(1)} async-done(((bf16[192,12,2,256]{3,2,1,0:T(2,128)(2,1)}), bf16[192,12,2,256]{3,2,1,0:T(2,128)(2,1)S(1)}, u32[]{:S(2)}, u32[]{:S(2)}) %all-to-all-start.1) | async-done | bytes 2359328 | tf_op jit(solution)/shard_map/all_to_all | solution.py:124
  163.8 2.0 copy.48
  165.8 0.8 fusion.42
  166.6 0.7 subtract_convert_fusion
  167.3 0.8 convert_bitcast_fusion
  168.1 0.0 copy-start.13
  168.2 0.0 copy-start.14
  168.2 0.0 copy-start.15
  168.2 0.0 copy-start.9
  168.2 3.8 copy.51
  172.0 5.5 %all-to-all-start.2 = ((bf16[12,192,2,256]{3,2,0,1:T(2,128)(2,1)}), bf16[12,192,2,256]{3,2,0,1:T(2,128)(2,1)S(1)}, u32[]{:S(2)}, u32[]{:S(2)}) async-start(bf16[12,192,2,256]{3,2,0,1:T(2,128)(2,1)} %copy.51), calls=%async_computation.2 | async-start | bytes 4718592 | tf_op jit(solution)/shard_map/all_to_all | solution.py:142
  177.6 0.3 fusion.73
  177.9 0.8 fusion.79
  178.8 3.3 fusion.70
  182.1 48.1 %all-to-all-done.2 = bf16[12,192,2,256]{3,2,0,1:T(2,128)(2,1)S(1)} async-done(((bf16[12,192,2,256]{3,2,0,1:T(2,128)(2,1)}), bf16[12,192,2,256]{3,2,0,1:T(2,128)(2,1)S(1)}, u32[]{:S(2)}, u32[]{:S(2)}) %all-to-all-start.2) | async-done | bytes 2359328 | tf_op jit(solution)/shard_map/all_to_all | solution.py:142
  230.2 1.7 copy.53
  231.9 0.0 copy-start.7
  232.0 4.1 fusion.46
  236.1 3.1 fusion.32
  239.2 5.7 %copy.56 = bf16[12,768,256]{2,0,1:T(8,128)(2,1)} copy(bf16[12,768,256]{2,1,0:T(8,128)(2,1)S(1)} %fusion.32) | data formatting | bytes 9437184 | tf_op jit(solution)/shard_map/convert_element_type | solution.py:147
  244.8 8.2 %all-to-all-start.3 = ((bf16[12,768,256]{2,0,1:T(8,128)(2,1)}), bf16[12,768,256]{2,0,1:T(8,128)(2,1)}, u32[]{:S(2)}, u32[]{:S(2)}) async-start(bf16[12,768,256]{2,0,1:T(8,128)(2,1)} %copy.56), calls=%async_computation.3 | async-start | bytes 12582912 | tf_op jit(solution)/shard_map/all_to_all | solution.py:149
  253.0 0.1 fusion.95
  253.2 0.3 fusion.94
  253.5 0.6 copy_bitcast_fusion
  254.1 0.6 copy_bitcast_fusion.2
  254.7 0.6 copy_bitcast_fusion.4
  255.4 0.6 copy_bitcast_fusion.6
  256.0 0.6 copy_bitcast_fusion.8
  256.6 0.6 copy_bitcast_fusion.10
  257.3 63.7 %all-to-all-done.3 = bf16[12,768,256]{2,0,1:T(8,128)(2,1)} async-done(((bf16[12,768,256]{2,0,1:T(8,128)(2,1)}), bf16[12,768,256]{2,0,1:T(8,128)(2,1)}, u32[]{:S(2)}, u32[]{:S(2)}) %all-to-all-start.3) | async-done | bytes 4718624 | tf_op jit(solution)/shard_map/all_to_all | solution.py:149
  320.9 9.8 %copy.57 = bf16[12,384,2,256]{3,2,1,0:T(2,128)(2,1)} copy(bf16[12,384,2,256]{3,0,1,2:T(8,128)(2,1)} %bitcast.31) | data formatting | bytes 9437184 | tf_op jit(solution)/shard_map/all_to_all | solution.py:149
  330.8 8.5 %all_to_all.67 = bf16[12,384,512]{2,1,0:T(8,128)(2,1)} reshape(bf16[12,384,2,256]{3,2,1,0:T(2,128)(2,1)} %copy.57) | data formatting | bytes 9437184 | tf_op jit(solution)/shard_map/all_to_all | solution.py:149
  339.3 1.1 fusion.93
  340.5 1.2 collective-permute-start
  341.6 0.3 collective-permute-start.1
  342.0 0.6 copy_bitcast_fusion.12
  342.6 0.6 copy.125
  343.2 1.1 collective-permute-done.1
  344.3 1.8 pad_maximum_fusion.6
  346.1 4.5 %collective-permute-start.2 = (bf16[2,388,512]{2,1,0:T(8,128)(2,1)S(1)}, bf16[2,388,512]{2,1,0:T(8,128)(2,1)S(1)}, u32[]{:S(2)}, u32[]{:S(2)}) collective-permute-start(bf16[2,388,512]{2,1,0:T(8,128)(2,1)S(1)} %get-tuple-element.8), channel_id=1, source_target_pairs={{0,2},{2,4},{4,6},{6,8},{8,10},{10,12},{12,14},{14,16},{16,18},{18... | collective-permute-start | bytes 2383880 | tf_op jit(solution)/shard_map/ppermute | solution.py:23
  350.6 2.7 collective-permute-start.3
  353.3 0.6 copy_bitcast_fusion.14
  353.9 0.6 copy_bitcast_fusion.16
  354.6 0.5 constant_dynamic-update-slice_fusion.1
  355.1 13.2 %collective-permute-done.2 = bf16[2,388,512]{2,1,0:T(8,128)(2,1)S(1)} collective-permute-done((bf16[2,388,512]{2,1,0:T(8,128)(2,1)S(1)}, bf16[2,388,512]{2,1,0:T(8,128)(2,1)S(1)}, u32[]{:S(2)}, u32[]{:S(2)}) %collective-permute-start.2) | collective-permute-done | bytes 794656 | tf_op jit(solution)/shard_map/ppermute | solution.py:23
  368.3 3.3 collective-permute-done.3
  371.6 4.4 maximum_maximum_fusion
  376.0 43.8 %convert_reduce_fusion = (f32[12,384]{1,0:T(8,128)S(1)}, bf16[12,384,512]{2,1,0:T(8,128)(2,1)}) fusion(bf16[14,388,512]{2,1,0:T(8,128)(2,1)S(1)} %get-tuple-element.7, f32[12,512]{1,0:T(8,128)} %get-tuple-element.43, f32[12,512]{1,0:T(8,128)} %get-tuple-element.44, f32[12,512]{1,0:T(8,128)} %get-tuple-element.45, f32[12,512]{1,0:T(8,128)} %get-tuple-element.46, ...), kind=kLoop, calls=%fused_computation.42 | loop fusion | flops 198176256 | bytes 113903616 | tf_op jit(solution)/shard_map/reduce_sum | solution.py:76
  419.9 3.6 multiply_reduce_fusion
  423.5 0.0 copy-start.16
  423.5 0.0 copy-start.17
  423.6 6.8 %fusion.24 = bf16[4608,512]{1,0:T(8,128)(2,1)} fusion(bf16[12,384,512]{2,1,0:T(8,128)(2,1)} %get-tuple-element.3, f32[512]{0:T(512)S(1)} %copy-done.10, f32[4608]{0:T(1024)S(1)} %rsqrt.12, f32[4608]{0:T(1024)S(1)} %div.17), kind=kLoop, calls=%fused_computation.29 | loop fusion | flops 11796480 | bytes 9476096 | tf_op jit(solution)/shard_map/convert_element_type | solution.py:78
  430.4 15.3 %fusion.21 = bf16[4608,512]{1,0:T(8,128)(2,1)} fusion(bf16[4608,512]{1,0:T(8,128)(2,1)} %bitcast.137, bf16[1024,512]{1,0:T(8,128)(2,1)S(1)} %copy-done.11, f32[1024]{0:T(1024)S(1)} %copy-done.16, f32[512]{0:T(512)S(1)} %copy-done.17, bf16[4608,512]{1,0:T(8,128)(2,1)} %fusion.24, bf16[512,1024]{1,0:T(8,128)(2,1)S(1)} %copy-done.12), kind=kOutput, calls=%fused_computation.25 | convolution fusion | flops 9720299520 | bytes 16259072 | tf_op jit(solution)/shard_map/dot_general | solution.py:81
  (41 shorter events, 0.2 us)
Async XLA Ops:
  0.6 165.2 %copy-start = (bf16[12,192,192]{2,1,0:T(8,128)(2,1)S(1)}, bf16[12,192,192]{2,1,0:T(8,128)(2,1)}, u32[]{:S(2)}) copy-start(bf16[12,192,192]{2,1,0:T(8,128)(2,1)} %param.16) | copy-start | bytes 2654212
  9.9 74.7 %all-to-all-start = ((bf16[12,384,512]{1,0,2:T(8,128)(2,1)}), bf16[12,384,512]{1,0,2:T(8,128)(2,1)}, u32[]{:S(2)}, u32[]{:S(2)}) async-start(bf16[12,384,512]{1,0,2:T(8,128)(2,1)} %copy.45), calls=%async_computation | async-start | bytes 12582912 | tf_op jit(solution)/shard_map/all_to_all | solution.py:112
  93.3 4.5 %copy-start.4 = (bf16[12,384,2,256]{3,1,2,0:T(8,128)(2,1)S(1)}, bf16[12,384,2,256]{3,1,2,0:T(8,128)(2,1)}, u32[]{:S(2)}) copy-start(bf16[12,384,2,256]{3,1,2,0:T(8,128)(2,1)} %copy.46) | copy-start | bytes 14155780
  93.3 4.5 %copy-start.18 = (f32[12]{0:T(128)S(1)}, f32[12]{0:T(128)}, u32[]{:S(2)}) copy-start(f32[12]{0:T(128)} %param.15) | copy-start | bytes 148
  103.8 60.0 %all-to-all-start.1 = ((bf16[192,12,2,256]{3,2,1,0:T(2,128)(2,1)}), bf16[192,12,2,256]{3,2,1,0:T(2,128)(2,1)S(1)}, u32[]{:S(2)}, u32[]{:S(2)}) async-start(bf16[192,12,2,256]{3,2,1,0:T(2,128)(2,1)} %copy.47), calls=%async_computation.1 | async-start | bytes 4718592 | tf_op jit(solution)/shard_map/all_to_all | solution.py:124
  163.8 2.8 copy-start.5
  163.8 2.8 copy-start.6
  168.1 9.4 %copy-start.13 = (f32[12,12]{1,0:T(8,128)S(1)}, f32[12,12]{1,0:T(8,128)}, u32[]{:S(2)}) copy-start(f32[12,12]{1,0:T(8,128)} %param.21) | copy-start | bytes 1732
  168.2 9.4 %copy-start.14 = (s32[12,12]{1,0:T(8,128)S(1)}, s32[12,12]{1,0:T(8,128)}, u32[]{:S(2)}) copy-start(s32[12,12]{1,0:T(8,128)} %param.19) | copy-start | bytes 1732
  168.2 9.4 %copy-start.15 = (s32[12,12]{1,0:T(8,128)S(1)}, s32[12,12]{1,0:T(8,128)}, u32[]{:S(2)}) copy-start(s32[12,12]{1,0:T(8,128)} %param.20) | copy-start | bytes 1732
  168.2 9.7 %copy-start.9 = (f32[8,512]{1,0:T(8,128)S(1)}, f32[8,512]{1,0:T(8,128)}, u32[]{:S(2)}) copy-start(f32[8,512]{1,0:T(8,128)} %param.22) | copy-start | bytes 49156
  172.0 58.2 %all-to-all-start.2 = ((bf16[12,192,2,256]{3,2,0,1:T(2,128)(2,1)}), bf16[12,192,2,256]{3,2,0,1:T(2,128)(2,1)S(1)}, u32[]{:S(2)}, u32[]{:S(2)}) async-start(bf16[12,192,2,256]{3,2,0,1:T(2,128)(2,1)} %copy.51), calls=%async_computation.2 | async-start | bytes 4718592 | tf_op jit(solution)/shard_map/all_to_all | solution.py:142
  231.9 4.1 copy-start.7
  231.9 4.1 copy-start.8
  244.8 76.1 %all-to-all-start.3 = ((bf16[12,768,256]{2,0,1:T(8,128)(2,1)}), bf16[12,768,256]{2,0,1:T(8,128)(2,1)}, u32[]{:S(2)}, u32[]{:S(2)}) async-start(bf16[12,768,256]{2,0,1:T(8,128)(2,1)} %copy.56), calls=%async_computation.3 | async-start | bytes 12582912 | tf_op jit(solution)/shard_map/all_to_all | solution.py:149
  339.3 15.2 %copy-start.2 = (bf16[12,384,512]{2,1,0:T(8,128)(2,1)S(1)}, bf16[12,384,512]{2,1,0:T(8,128)(2,1)}, u32[]{:S(2)}) copy-start(bf16[12,384,512]{2,1,0:T(8,128)(2,1)} %all_to_all.67) | copy-start | bytes 14155780
  340.5 2.8 collective-permute-start
  341.6 2.7 collective-permute-start.1
  346.1 22.2 %collective-permute-start.2 = (bf16[2,388,512]{2,1,0:T(8,128)(2,1)S(1)}, bf16[2,388,512]{2,1,0:T(8,128)(2,1)S(1)}, u32[]{:S(2)}, u32[]{:S(2)}) collective-permute-start(bf16[2,388,512]{2,1,0:T(8,128)(2,1)S(1)} %get-tuple-element.8), channel_id=1, source_target_pairs={{0,2},{2,4},{4,6},{6,8},{8,10},{10,12},{12,14},{14,16},{16,18},{18... | collective-permute-start | bytes 2383880 | tf_op jit(solution)/shard_map/ppermute | solution.py:23
  350.6 21.0 %collective-permute-start.3 = (bf16[2,388,512]{2,1,0:T(8,128)(2,1)S(1)}, bf16[2,388,512]{2,1,0:T(8,128)(2,1)S(1)}, u32[]{:S(2)}, u32[]{:S(2)}) collective-permute-start(bf16[2,388,512]{2,1,0:T(8,128)(2,1)S(1)} %get-tuple-element.9), channel_id=1, source_target_pairs={{2,0},{4,2},{6,4},{8,6},{10,8},{12,10},{14,12},{16,14},{18,16},{20... | collective-permute-start | bytes 2383880 | tf_op jit(solution)/shard_map/ppermute | solution.py:26
  355.1 20.9 %copy-start.3 = (bf16[12,386,512]{2,1,0:T(8,128)(2,1)}, bf16[12,386,512]{2,1,0:T(8,128)(2,1)S(1)}, u32[]{:S(2)}) copy-start(bf16[12,386,512]{2,1,0:T(8,128)(2,1)S(1)} %constant_dynamic-update-slice_fusion) | copy-start | bytes 14229508
  376.0 47.5 %copy-start.10 = (f32[512]{0:T(512)S(1)}, f32[512]{0:T(512)}, u32[]{:S(2)}) copy-start(f32[512]{0:T(512)} %param.23) | copy-start | bytes 6148
  423.5 6.9 %copy-start.11 = (bf16[1024,512]{1,0:T(8,128)(2,1)S(1)}, bf16[1024,512]{1,0:T(8,128)(2,1)}, u32[]{:S(2)}) copy-start(bf16[1024,512]{1,0:T(8,128)(2,1)} %param.26) | copy-start | bytes 3145732
  423.5 6.9 %copy-start.12 = (bf16[512,1024]{1,0:T(8,128)(2,1)S(1)}, bf16[512,1024]{1,0:T(8,128)(2,1)}, u32[]{:S(2)}) copy-start(bf16[512,1024]{1,0:T(8,128)(2,1)} %param.24) | copy-start | bytes 3145732
  423.5 6.9 %copy-start.16 = (f32[1024]{0:T(1024)S(1)}, f32[1024]{0:T(1024)}, u32[]{:S(2)}) copy-start(f32[1024]{0:T(1024)} %param.25) | copy-start | bytes 12292
  423.5 6.9 %copy-start.17 = (f32[512]{0:T(512)S(1)}, f32[512]{0:T(512)}, u32[]{:S(2)}) copy-start(f32[512]{0:T(512)} %param.27) | copy-start | bytes 6148
  430.4 15.4 %copy-start.1 = (bf16[12,192,192]{2,1,0:T(8,128)(2,1)S(1)}, bf16[12,192,192]{2,1,0:T(8,128)(2,1)}, u32[]{:S(2)}) copy-start(bf16[12,192,192]{2,1,0:T(8,128)(2,1)} %param.16) | copy-start | bytes 2654212
where the time goes:
time: 454 us; the launch traced here: 446 us
  waiting for transfers between devices  246 us (54%)
  other arithmetic  66.9 us (15%)
  local copies, waits for them, and re-layouts  63.7 us (14%)
  starting transfers between devices  36.3 us (8%)
  matrix products  31.8 us (7%)
    all_to_all x1, waiting for transfers between devices, shards(): lax.all_to_all(field, 'lon', split_axis=2, concat_axis=1, tiled=True)  65.7 us
    all_to_all x1, waiting for transfers between devices, shards(): lax.all_to_all(wave, 'lon', split_axis=1, concat_axis=2, tiled=True)  63.7 us
    all_to_all x1, waiting for transfers between devices, shards(): lax.all_to_all(weighted, 'lat', split_axis=0, concat_axis=1, tiled=True)  50.8 us
    all_to_all x1, waiting for transfers between devices, shards(): lax.all_to_all(synthesis, 'lat', split_axis=1, concat_axis=0, tiled=True)  48.1 us
    reduce_sum x1, other arithmetic, channel_mlp(): center = jnp.mean(tokens, axis=1, keepdims=True)  43.8 us
    all_to_all x2, local copies, waits for them, and re-layouts, shards(): lax.all_to_all(wave, 'lon', split_axis=1, concat_axis=2, tiled=True)  18.4 us
    unnamed x53, local copies, waits for them, and re-layouts  16.1 us
    dot_general x1, matrix products, channel_mlp(): result = jnp.dot(hidden, w_out, preferred_element_type=jnp.float32)  15.3 us
  transfers between devices with their start and end apart: 8, of which 7 were waited for; matrix products, arithmetic and copies ran while one was open for 4% of the time, Pallas kernels for 0%

commit v1 on v0

v1 whole, which is shorter than its diff:
```python
import functools
import math

import jax
import jax.numpy as jnp
import ml_dtypes
import numpy as np
from jax import lax
from jax.experimental import pallas as pl
from jax.experimental.pallas import tpu as pltpu
from jax.sharding import PartitionSpec as P

HALO = 2
SPAN = 2 * HALO + 1
NQ = 4
LANES = 128
F32 = jnp.float32
BF16 = jnp.bfloat16
VMEM_LIMIT = 56 * 1024 * 1024


def vmem_spec():
    return pl.BlockSpec(memory_space=pltpu.VMEM)


def smem_spec():
    return pl.BlockSpec(memory_space=pltpu.SMEM)


def params():
    return pltpu.CompilerParams(
        vmem_limit_bytes=VMEM_LIMIT, dimension_semantics=("arbitrary",)
    )


def cost(flops, nbytes, trans=0):
    return pl.CostEstimate(
        flops=int(flops), bytes_accessed=int(nbytes), transcendentals=int(trans)
    )


def split_np(table):
    upper = table.astype(np.float32).astype(ml_dtypes.bfloat16)
    lower = (table - upper.astype(np.float64)).astype(np.float32).astype(ml_dtypes.bfloat16)
    return upper, lower


def tables_np(nlon, lon_count, wave_block, mmax, padded_cols):
    blocks = mmax // wave_block
    waves = np.arange(mmax).reshape(blocks, 1, wave_block)
    waves = np.broadcast_to(waves, (blocks, 2, wave_block)).reshape(-1)
    imag = np.broadcast_to(np.arange(2).reshape(1, 2, 1), (blocks, 2, wave_block)).reshape(-1)

    def table(points):
        phase = (waves[:, None].astype(np.int64) * points[None, :]) % nlon
        angle = phase * (2.0 * math.pi / nlon)
        return np.where(imag[:, None] == 0, np.cos(angle), -np.sin(angle)) / math.sqrt(nlon)

    cols = nlon // lon_count
    fwd = np.stack([table(np.arange(cols) + b * cols) for b in range(lon_count)])
    factor = np.where(waves == 0, 1.0, 2.0)[:, None]
    inv = np.stack(
        [
            (factor * table((np.arange(padded_cols) - HALO + b * cols) % nlon)).T
            for b in range(lon_count)
        ]
    )
    return split_np(fwd), split_np(inv)


def dft_kernel(lon_count, cw, rows2, nz, quad_ref, *refs):
    blocks = refs[:lon_count]
    upper_ref, lower_ref, out_ref = refs[lon_count:]
    step = pl.program_id(0)
    group = rows2 if cw % LANES == 0 else 1
    wave_rows = out_ref.shape[3]
    for first in range(0, rows2, group):
        x = jnp.concatenate(
            [
                jnp.concatenate([b[first + i] for i in range(group)], axis=1)
                if group > 1
                else b[first]
                for b in blocks
            ],
            axis=0,
        )
        acc = jnp.dot(upper_ref[...], x, preferred_element_type=F32)
        acc = acc + jnp.dot(lower_ref[...], x, preferred_element_type=F32)
        for i in range(group):
            t = first + i
            scaled = acc[:, i * cw : (i + 1) * cw] * quad_ref[step * rows2 + t]
            for d in range(nz):
                for q in range(NQ):
                    at = (d * NQ + q) * wave_rows
                    out_ref[d, q, t] = scaled[at : at + wave_rows].astype(BF16)


def dft(blocks, quad, upper, lower, nz, wave_rows):
    rows, cols, cw = blocks[0].shape
    rows2 = 2
    lon_count = len(blocks)
    whole = pl.BlockSpec(upper.shape, lambda t: (0, 0))
    return pl.pallas_call(
        functools.partial(dft_kernel, lon_count, cw, rows2, nz),
        grid=(rows // rows2,),
        in_specs=[smem_spec()]
        + [pl.BlockSpec((rows2, cols, cw), lambda t: (t, 0, 0))] * lon_count
        + [whole, whole],
        out_specs=pl.BlockSpec((nz, NQ, rows2, wave_rows, cw), lambda t: (0, 0, t, 0, 0)),
        out_shape=jax.ShapeDtypeStruct((nz, NQ, rows, wave_rows, cw), BF16),
        compiler_params=params(),
        cost_estimate=cost(
            4 * upper.shape[0] * upper.shape[1] * rows * cw, 4 * rows * cols * cw * 2
        ),
    )(quad, *blocks, upper, lower)


def legendre_kernel(nz, *refs):
    own = refs[:nz]
    others = refs[nz : nz + NQ - 1]
    leg_ref, legt_ref, gr_ref, gi_ref, out_ref, wide, result = refs[nz + NQ - 1 :]
    waves, _, lat = leg_ref.shape
    rows, wave_rows, cw = out_ref.shape[2:]
    span = rows * wave_rows

    def piece(q, d):
        if q:
            return others[q - 1][d]
        return own[d][...].reshape(rows, wave_rows, cw)

    for q in range(NQ):
        for d in range(nz):
            at = (q * nz + d) * span
            wide[at : at + span, :] = piece(q, d).astype(F32).reshape(span, cw)
    gain_r = gr_ref[...]
    gain_i = gi_ref[...]
    for m in range(waves):
        real = wide[pl.ds(m, lat, stride=wave_rows), :].astype(BF16)
        imag = wide[pl.ds(waves + m, lat, stride=wave_rows), :].astype(BF16)
        leg = leg_ref[m]
        legt = legt_ref[m]
        cr = jnp.dot(leg, real, preferred_element_type=F32)
        ci = jnp.dot(leg, imag, preferred_element_type=F32)
        fr = (gain_r * cr - gain_i * ci).astype(BF16)
        fi = (gain_r * ci + gain_i * cr).astype(BF16)
        result[pl.ds(m, lat, stride=wave_rows), :] = jnp.dot(
            legt, fr, preferred_element_type=F32
        )
        result[pl.ds(waves + m, lat, stride=wave_rows), :] = jnp.dot(
            legt, fi, preferred_element_type=F32
        )
    for q in range(NQ):
        for d in range(nz):
            at = (q * nz + d) * span
            out_ref[d, q] = result[at : at + span, :].reshape(rows, wave_rows, cw).astype(BF16)


def first_of(shape, keep):
    block = (1,) * keep + shape[keep:]
    return pl.BlockSpec(block, lambda t: (0,) * len(shape))


def whole_of(array):
    shape = array.shape
    return pl.BlockSpec(shape, lambda t: (0,) * len(shape))


def legendre_step(own, others, leg, legt, gr, gi):
    nz = len(own)
    _, _, rows, wave_rows, cw = own[0].shape
    waves, degrees, lat = leg.shape
    specs = [first_of(own[0].shape, 2)] + [first_of(a.shape, 1) for a in own[1:]]
    return pl.pallas_call(
        functools.partial(legendre_kernel, nz),
        grid=(1,),
        in_specs=specs + [whole_of(a) for a in (*others, leg, legt, gr, gi)],
        out_specs=pl.BlockSpec((nz, NQ, rows, wave_rows, cw), lambda t: (0, 0, 0, 0, 0)),
        out_shape=jax.ShapeDtypeStruct((nz, NQ, rows, wave_rows, cw), BF16),
        scratch_shapes=[pltpu.VMEM((lat * wave_rows, cw), F32)] * 2,
        compiler_params=params(),
        cost_estimate=cost(
            8 * waves * degrees * lat * cw, 4 * lat * wave_rows * cw + 4 * leg.size
        ),
    )(*own, *others, leg, legt, gr, gi)


def inverse_kernel(nz, rows2, cw, lon_count, *refs):
    own = refs[:nz]
    others = refs[nz : nz + NQ - 1]
    upper_ref, lower_ref = refs[nz + NQ - 1 : nz + NQ + 1]
    outs = refs[nz + NQ + 1 : nz + NQ + 1 + lon_count]
    wide = refs[-1]
    wave_rows = own[0].shape[-2]
    cols = outs[0].shape[1]
    for t in range(rows2):
        for q in range(NQ):
            for d in range(nz):
                at = (q * nz + d) * wave_rows
                if q:
                    block = others[q - 1][d, t]
                elif d:
                    block = own[d][0, t]
                else:
                    block = own[0][0, 0, t]
                wide[t, at : at + wave_rows, :] = block.astype(F32)
    group = rows2 if cw % LANES == 0 else 1
    for first in range(0, rows2, group):
        x = [wide[first + i].astype(BF16) for i in range(group)]
        x = jnp.concatenate(x, axis=1) if group > 1 else x[0]
        acc = jnp.dot(upper_ref[...], x, preferred_element_type=F32)
        acc = acc + jnp.dot(lower_ref[...], x, preferred_element_type=F32)
        for i in range(group):
            for s in range(lon_count):
                outs[s][first + i] = acc[
                    s * cols : (s + 1) * cols, i * cw : (i + 1) * cw
                ].astype(BF16)


def inverse(own, others, upper, lower, lon_count):
    nz = len(own)
    _, _, rows, wave_rows, cw = own[0].shape
    rows2 = 2
    cols = upper.shape[0] // lon_count
    whole = pl.BlockSpec(upper.shape, lambda t: (0, 0))
    specs = [pl.BlockSpec((1, 1, rows2, wave_rows, cw), lambda t: (0, 0, t, 0, 0))]
    specs += [pl.BlockSpec((1, rows2, wave_rows, cw), lambda t: (0, t, 0, 0))] * (nz - 1)
    specs += [pl.BlockSpec((nz, rows2, wave_rows, cw), lambda t: (0, t, 0, 0))] * (NQ - 1)
    return pl.pallas_call(
        functools.partial(inverse_kernel, nz, rows2, cw, lon_count),
        grid=(rows // rows2,),
        in_specs=specs + [whole, whole],
        out_specs=[pl.BlockSpec((rows2, cols, cw), lambda t: (t, 0, 0))] * lon_count,
        out_shape=[jax.ShapeDtypeStruct((rows, cols, cw), BF16)] * lon_count,
        scratch_shapes=[pltpu.VMEM((rows2, nz * NQ * wave_rows, cw), F32)],
        compiler_params=params(),
        cost_estimate=cost(4 * upper.size * rows * cw, 4 * rows * cols * cw * lon_count),
    )(*own, *others, upper, lower)


def tail_kernel(lon_count, nch, slots, *refs):
    (place_ref, neighbour_ref, basis_ref, quad_ref) = refs[:4]
    count = lon_count * nch
    waves = refs[4 : 4 + count]
    lows = refs[4 + count : 4 + count + nch]
    highs = refs[4 + count + nch : 4 + count + 2 * nch]
    (
        disco_ref,
        gain_ref,
        w_in_ref,
        b_in_ref,
        w_out_ref,
        b_out_ref,
        field_ref,
        out_ref,
        spatial_ref,
        ring,
        conv_ref,
    ) = refs[4 + count + 2 * nch :]
    t = pl.program_id(0)
    rows = waves[0].shape[0]
    cols = field_ref.shape[1]
    cw = waves[0].shape[2]
    channels = field_ref.shape[2]

    def group(s, j):
        return place_ref[s] * nch + j

    def put(row, pick):
        for s in range(lon_count):
            for j in range(nch):
                ring[row, group(s, j)] = pick(s, j).astype(F32)

    @pl.when(t == 0)
    def _():
        for r in range(HALO):
            put(r, lambda s, j: lows[j][s, r])
            put(HALO + r, lambda s, j: waves[s * nch + j][r])

    @pl.when(t + HALO < rows)
    def _():
        put(t + 2 * HALO, lambda s, j: waves[s * nch + j][t + HALO])

    for r in range(HALO):

        @pl.when(t + HALO == rows + r)
        def _():
            put(rows + HALO + r, lambda s, j: highs[j][s, r])

    tile = 48 if cols % 48 == 0 else 8

    def one_group(g, carry):
        starts = []
        coefs = []
        for s in range(slots):
            n = neighbour_ref[t, s]
            starts.append((t + n // SPAN, n % SPAN))
            weight = disco_ref[g, pl.ds(basis_ref[t, s], 1), :]
            coefs.append(weight * quad_ref[t, s])

        def one_tile(i, carry):
            at = pl.multiple_of(i * tile, 8)
            acc = ring[t + HALO, g, pl.ds(at + HALO, tile), :]
            for (row, shift), coef in zip(starts, coefs):
                acc = acc + coef * ring[row, g, pl.ds(at + shift, tile), :]
            conv_ref[g, pl.ds(at, tile), :] = acc
            return carry

        return lax.fori_loop(0, cols // tile, one_tile, carry)

    lax.fori_loop(0, count, one_group, 0)
    spatial = jnp.concatenate([conv_ref[g] for g in range(count)], axis=1).astype(BF16)
    spatial_ref[0] = spatial
    tokens = spatial.astype(F32)
    center = jnp.mean(tokens, axis=1, keepdims=True)
    shifted = tokens - center
    spread = jnp.mean(shifted * shifted, axis=1, keepdims=True)
    normed = (shifted * lax.rsqrt(spread + 1e-05) * gain_ref[...]).astype(BF16)
    hidden = jnp.dot(normed, w_in_ref[...], preferred_element_type=F32) + b_in_ref[...]
    hidden = jax.nn.gelu(hidden).astype(BF16)
    result = jnp.dot(hidden, w_out_ref[...], preferred_element_type=F32)
    result = result + b_out_ref[...] + field_ref[0].astype(F32)
    out_ref[0] = result.astype(BF16)


def tail(place, neighbour, basis, quad, waves, lows, highs, disco, gain, w_in, b_in, w_out, b_out, field, lon_count, nch):
    rows, cols, channels = field.shape
    padded, cw = waves[0].shape[1:]
    count = lon_count * nch
    hidden = w_in.shape[1]
    row_spec = pl.BlockSpec((1, cols, channels), lambda t: (t, 0, 0))
    vm = [vmem_spec()]
    return pl.pallas_call(
        functools.partial(tail_kernel, lon_count, nch, neighbour.shape[1]),
        grid=(rows,),
        in_specs=[smem_spec()] * 4 + vm * (count + 2 * nch) + vm * 6 + [row_spec],
        out_specs=[row_spec, row_spec],
        out_shape=[jax.ShapeDtypeStruct(field.shape, BF16)] * 2,
        scratch_shapes=[
            pltpu.VMEM((rows + 2 * HALO, count, padded, cw), F32),
            pltpu.VMEM((count, cols, cw), F32),
        ],
        compiler_params=params(),
        cost_estimate=cost(
            4 * rows * cols * channels * hidden, 8 * field.size, rows * cols * hidden
        ),
    )(place, neighbour, basis, quad, *waves, *lows, *highs, disco, gain, w_in, b_in, w_out, b_out, field)


def swap(array, axis, mask):
    count = lax.axis_size(axis)
    return lax.ppermute(array, axis, [(i, i ^ mask) for i in range(count)])


def shards(
    field,
    quad_weight,
    legendre,
    filter_real,
    filter_imag,
    neighbour,
    basis,
    disco_quad,
    disco_weight,
    norm_gain,
    w_in,
    b_in,
    w_out,
    b_out,
):
    rows, cols, channels = field.shape
    lon_count = lax.axis_size("lon")
    lat_count = lax.axis_size("lat")
    nz = lat_count // NQ
    wave_block, degrees, nlat = legendre.shape
    wave_rows = 2 * wave_block
    mmax = wave_block * lat_count
    nlon = cols * lon_count
    cblock = channels // lon_count
    nch = max(1, cblock // LANES)
    cw = cblock // nch
    padded_cols = (cols + 2 * HALO + 7) // 8 * 8
    lat_id = lax.axis_index("lat")
    lon_id = lax.axis_index("lon")

    (fwd_u, fwd_l), (inv_u, inv_l) = tables_np(nlon, lon_count, wave_block, mmax, padded_cols)
    zq = np.arange(lat_count)
    qz = (zq % nz) * NQ + zq // nz

    def permutation(masks, width):
        source = (lat_id ^ jnp.asarray(masks, jnp.int32))[:, None] * width
        source = (source + jnp.arange(width, dtype=jnp.int32)[None, :]).reshape(-1)
        return (jnp.arange(lat_count * width, dtype=jnp.int32)[None, :] == source[:, None]).astype(BF16)

    perm_fwd = permutation(zq, wave_rows)
    perm_inv = permutation(qz, wave_rows)
    perm_lat = permutation(qz, rows)

    def forward_table(table):
        parts = [
            jnp.dot(
                perm_fwd,
                lax.dynamic_index_in_dim(jnp.asarray(table), lon_id ^ s, 0, keepdims=False),
                preferred_element_type=F32,
            )
            for s in range(lon_count)
        ]
        return jnp.concatenate(parts, axis=1).astype(BF16)

    def inverse_table(table):
        parts = [
            jnp.einsum(
                "kr,ur->ku",
                lax.dynamic_index_in_dim(jnp.asarray(table), lon_id ^ s, 0, keepdims=False),
                perm_inv,
                preferred_element_type=F32,
            )
            for s in range(lon_count)
        ]
        return jnp.concatenate(parts, axis=0).astype(BF16)

    fu, fl = forward_table(fwd_u), forward_table(fwd_l)
    iu, il = inverse_table(inv_u), inverse_table(inv_l)
    leg = jnp.einsum("mlt,ut->mlu", legendre, perm_lat, preferred_element_type=F32).astype(BF16)
    legt = jnp.einsum("mlt,ut->mul", legendre, perm_lat, preferred_element_type=F32).astype(BF16)

    def chunk_of(array, s, j):
        start = (lon_id ^ s) * cblock + j * cw
        return lax.dynamic_slice_in_dim(array, start, cw, array.ndim - 1)

    waves = [[None] * nch for _ in range(lon_count)]
    lows, highs = [], []
    received = [
        [swap(chunk_of(field, s, j), "lon", s) for s in range(1, lon_count)]
        for j in range(nch)
    ]
    for j in range(nch):
        blocks = [chunk_of(field, 0, j)] + received[j]
        spectrum = dft(blocks, quad_weight, fu, fl, nz, wave_rows)
        own = [spectrum] + [swap(spectrum[d], "lat", NQ * d) for d in range(1, nz)]

        def others_of(own):
            return [
                swap(
                    jnp.stack([own[0][0, q]] + [a[q] for a in own[1:]]), "lat", q
                )
                for q in range(1, NQ)
            ]

        gr = chunk_of(filter_real, 0, j)
        gi = chunk_of(filter_imag, 0, j)
        synthesis = legendre_step(own, others_of(own), leg, legt, gr, gi)
        own = [synthesis] + [swap(synthesis[d], "lat", NQ * d) for d in range(1, nz)]
        parts = inverse(own, others_of(own), iu, il, lon_count)
        waves[0][j] = parts[0]
        for s in range(1, lon_count):
            waves[s][j] = swap(parts[s], "lon", s)
    up = [(i, i + 1) for i in range(lat_count - 1)]
    down = [(i + 1, i) for i in range(lat_count - 1)]
    for j in range(nch):
        last = jnp.stack([waves[s][j][rows - HALO :] for s in range(lon_count)])
        first = jnp.stack([waves[s][j][:HALO] for s in range(lon_count)])
        lows.append(lax.ppermute(last, "lat", up))
        highs.append(lax.ppermute(first, "lat", down))

    place = (lon_id ^ jnp.arange(lon_count, dtype=jnp.int32)).astype(jnp.int32)
    disco = jnp.transpose(
        disco_weight.reshape(disco_weight.shape[0], lon_count * nch, cw), (1, 0, 2)
    )
    block_out, spatial = tail(
        place,
        neighbour,
        basis,
        disco_quad,
        [waves[s][j] for s in range(lon_count) for j in range(nch)],
        lows,
        highs,
        disco,
        norm_gain[None, :],
        w_in,
        b_in[None, :],
        w_out,
        b_out[None, :],
        field,
        lon_count,
        nch,
    )
    return (block_out, spatial)


def solution(mesh):
    grid = P("lat", "lon", None)
    rows = P("lat", None)
    placed = (grid, P("lat"), P("lat", None, None), P(), P(), rows, rows, rows) + (P(),) * 6
    return jax.shard_map(
        shards,
        mesh=mesh,
        in_specs=placed,
        out_specs=(grid, grid),
        check_vma=False,
    )
```

time: 454 us -> 310 us (0.68); the launches traced: 446 us -> 307 us
  waiting for transfers between devices: 246 us -> 132 us
  Pallas kernels: 0 us -> 83.7 us
  other arithmetic: 66.9 us -> 4.95 us
  local copies, waits for them, and re-layouts: 63.7 us -> 23.4 us
  matrix products: 31.8 us -> 9.36 us
  starting transfers between devices: 36.3 us -> 52.3 us
    all_to_all x4 -> x0, waiting for transfers between devices: 228 us -> none  [the longest x1 65.7 us: shards(): lax.all_to_all(field, 'lon', split_axis=2, concat_axis=1, tiled=True)]
    ppermute x4 -> x32, waiting for transfers between devices: 17.6 us -> 132 us  [the longest x28 123 us: swap(): return lax.ppermute(array, axis, [(i, i ^ mask) for i in range(count)])]
    pallas_call x0 -> x7, Pallas kernels: none -> 83.7 us  [the longest x1 44.7 us: tail(): pl.pallas_call(functools.partial(tail_kernel, lon_count, nch, neighbour.s...]
    reduce_sum x2 -> x0, other arithmetic: 47.4 us -> none  [the longest x1 43.8 us: channel_mlp(): center = jnp.mean(tokens, axis=1, keepdims=True)]
    ppermute x4 -> x32, starting transfers between devices: 8.74 us -> 52.3 us  [the longest x28 42.8 us: swap(): return lax.ppermute(array, axis, [(i, i ^ mask) for i in range(count)])]
    all_to_all x5 -> x0, local copies, waits for them, and re-layouts: 30.9 us -> none  [the longest x2 18.4 us: shards(): lax.all_to_all(wave, 'lon', split_axis=1, concat_axis=2, tiled=True)]
    all_to_all x4 -> x0, starting transfers between devices: 27.6 us -> none  [the longest x1 8.16 us: shards(): lax.all_to_all(wave, 'lon', split_axis=1, concat_axis=2, tiled=True)]
    dot_general x9, matrix products: 31.8 us -> 9.36 us  [the longest x4 5.35 us: inverse_table(): jnp.einsum('kr,ur->ku', lax.dynamic_index_in_dim(jnp.asarray(table), lon_...]
  transfers between devices with their start and end apart: 8 -> 32, of which waited for: 7 -> 16; matrix products, arithmetic and copies ran while one was open for 4% -> 9% of each run, Pallas kernels for 0% -> 11%
where the time goes in v1:
time: 310 us; the launch traced here: 307 us
  waiting for transfers between devices  132 us (43%)
  Pallas kernels  83.7 us (27%)
  starting transfers between devices  52.3 us (17%)
  local copies, waits for them, and re-layouts  23.4 us (8%)
  matrix products  9.36 us (3%)
  other arithmetic  4.95 us (2%)
    ppermute x28, waiting for transfers between devices, swap(): return lax.ppermute(array, axis, [(i, i ^ mask) for i in range(count)])  123 us
    pallas_call x1, Pallas kernels, tail(): pl.pallas_call(functools.partial(tail_kernel, lon_count, nch, neighbour.s...  44.7 us
    ppermute x28, starting transfers between devices, swap(): return lax.ppermute(array, axis, [(i, i ^ mask) for i in range(count)])  42.8 us
    pallas_call x2, Pallas kernels, inverse(): pl.pallas_call(functools.partial(inverse_kernel, nz, rows2, cw, lon_count...  13.4 us
    pallas_call x2, Pallas kernels, dft(): pl.pallas_call(functools.partial(dft_kernel, lon_count, cw, rows2, nz), g...  12.9 us
    pallas_call x2, Pallas kernels, legendre_step(): pl.pallas_call(functools.partial(legendre_kernel, nz), grid=(1,), in_spec...  12.6 us
    ppermute x2, waiting for transfers between devices, shards(): highs.append(lax.ppermute(first, 'lat', down))  7.3 us
  transfers between devices with their start and end apart: 32, of which 16 were waited for; matrix products, arithmetic and copies ran while one was open for 9% of the time, Pallas kernels for 11%

profile of v1, /device:TPU:19, one launch (start us, length us, event | category | flops | bytes accessed | tf_op | source)
XLA Modules:
  0.0 307.3 jit_solution(955289894234524365)
XLA Ops:
  0.7 4.4 %constant_dynamic-slice_fusion.2 = (bf16[12,384,128]{2,1,0:T(8,128)(2,1)}, bf16[12,384,128]{2,1,0:T(8,128)(2,1)}, bf16[12,384,128]{2,1,0:T(8,128)(2,1)S(1)}, bf16[12,384,128]{2,1,0:T(8,128)(2,1)}) fusion(bf16[12,384,512]{2,1,0:T(8,128)(2,1)} %refs_18_.1, s32[]{:T(128)S(6)} %select_n.35, s32[]{:T(128)S(6)} %select_n.34, s32[]{:T(128)S(6)} %select_n.31, ...), kind=kLoop, calls=%fused_computation.95 | loop fusion | bytes 9437200 | tf_op jit(solution)/shard_map/dynamic_slice | solution.py:428
  5.3 1.2 collective-permute-start
  7.5 1.4 convolution_convert_fusion.7
  8.9 1.4 convolution_convert_fusion.8
  10.4 2.2 convolution_convert_fusion.1
  12.6 2.2 convolution_convert_fusion.2
  14.9 0.9 pad_maximum_fusion.3.refs_3_
  15.8 0.8 pad_maximum_fusion.2.refs_2_
  17.8 0.9 constant_dynamic-slice_fusion
  18.7 1.6 copy.27.refs_7_
  20.3 0.9 pad_maximum_fusion.1.refs_8_
  22.6 1.0 pad_maximum_fusion.refs_7_
  23.6 8.7 %collective-permute-done.13.refs_1_ = bf16[12,384,128]{2,1,0:T(8,128)(2,1)} collective-permute-done((bf16[12,384,128]{2,1,0:T(8,128)(2,1)}, bf16[12,384,128]{2,1,0:T(8,128)(2,1)}, u32[]{:S(2)}, u32[]{:S(2)}) %collective-permute-start.13) | collective-permute-done | bytes 1179680 | tf_op jit(solution)/shard_map/ppermute | solution.py:351
  32.2 6.5 %shard_map.215.refs_0_ = bf16[4,4,12,24,128]{4,3,2,1,0:T(8,128)(2,1)} custom-call(f32[12]{0:T(128)} %quad_ref.3, bf16[12,384,128]{2,1,0:T(8,128)(2,1)} %get-tuple-element.11.refs_0_, bf16[12,384,128]{2,1,0:T(8,128)(2,1)} %collective-permute-done.13.refs_1_, bf16[384,768]{1,0:T(8,128)(2,1)} %pad_maximum_fusion.2.refs_2_, ...), custom_call_target="tpu_custom_call" | custom-call | flops 1811939328 | bytes 4718592 | tf_op jit(solution)/shard_map/pallas_call | solution.py:103
  38.7 1.3 slice_bitcast_fusion.3
  40.3 3.2 %collective-permute-start.15 = (bf16[4,12,24,128]{3,2,1,0:T(8,128)(2,1)S(1)}, bf16[4,12,24,128]{3,2,1,0:T(8,128)(2,1)S(1)}, u32[]{:S(2)}, u32[]{:S(2)}) collective-permute-start(bf16[4,12,24,128]{3,2,1,0:T(8,128)(2,1)S(1)} %get-tuple-element.32), channel_id=1, source_target_pairs={{0,16},{2,18},{4,20},{6,22},{8,24},{10,26},{12,28},{14,30},{16,0},... | collective-permute-start | bytes 884744 | tf_op jit(solution)/shard_map/ppermute | solution.py:351
  43.5 14.0 %collective-permute-done.refs_1_ = bf16[12,384,128]{2,1,0:T(8,128)(2,1)} collective-permute-done((bf16[12,384,128]{2,1,0:T(8,128)(2,1)S(1)}, bf16[12,384,128]{2,1,0:T(8,128)(2,1)}, u32[]{:S(2)}, u32[]{:S(2)}) %collective-permute-start) | collective-permute-done | bytes 1179680 | tf_op jit(solution)/shard_map/ppermute | solution.py:351
  57.5 6.5 %shard_map.212.refs_0_ = bf16[4,4,12,24,128]{4,3,2,1,0:T(8,128)(2,1)} custom-call(f32[12]{0:T(128)} %quad_ref.3, bf16[12,384,128]{2,1,0:T(8,128)(2,1)} %get-tuple-element.13.refs_0_, bf16[12,384,128]{2,1,0:T(8,128)(2,1)} %collective-permute-done.refs_1_, bf16[384,768]{1,0:T(8,128)(2,1)} %pad_maximum_fusion.2.refs_2_, bf16[384,768]{1,0:T(8,128)(2,1)} %pad_maximum_fusion.3.refs_3_), custom_call_target="tpu_custom_call" | custom-call | flops 1811939328 | bytes 4718592 | tf_op jit(solution)/shard_map/pallas_call | solution.py:103
  64.0 1.3 slice_bitcast_fusion.9
  65.3 1.0 slice_bitcast_fusion.23
  66.3 1.0 slice_bitcast_fusion.29
  67.2 1.4 collective-permute-start.14
  68.6 2.2 collective-permute-start.2
  71.3 2.9 collective-permute-done.14.refs_1_
  74.3 10.4 %collective-permute-start.17 = (bf16[4,12,24,128]{3,2,1,0:T(8,128)(2,1)S(1)}, bf16[4,12,24,128]{3,2,1,0:T(8,128)(2,1)S(1)}, u32[]{:S(2)}, u32[]{:S(2)}) collective-permute-start(bf16[4,12,24,128]{3,2,1,0:T(8,128)(2,1)S(1)} %pad_maximum_fusion.14), channel_id=1, source_target_pairs={{0,2},{2,0},{4,6},{6,4},{8,10},{10,8},{12,14},{14,12},{16,18},{18,... | collective-permute-start | bytes 884744 | tf_op jit(solution)/shard_map/ppermute | solution.py:351
  84.8 1.3 collective-permute-start.18
  86.2 8.0 %collective-permute-start.19 = (bf16[4,12,24,128]{3,2,1,0:T(8,128)(2,1)S(1)}, bf16[4,12,24,128]{3,2,1,0:T(8,128)(2,1)S(1)}, u32[]{:S(2)}, u32[]{:S(2)}) collective-permute-start(bf16[4,12,24,128]{3,2,1,0:T(8,128)(2,1)S(1)} %pad_maximum_fusion.16), channel_id=1, source_target_pairs={{0,6},{2,4},{4,2},{6,0},{8,14},{10,12},{12,10},{14,8},{16,22},{18,... | collective-permute-start | bytes 884744 | tf_op jit(solution)/shard_map/ppermute | solution.py:351
  94.3 1.5 collective-permute-start.4
  95.9 1.3 collective-permute-start.5
  97.8 4.1 %collective-permute-done.19.refs_6_ = bf16[4,12,24,128]{3,2,1,0:T(8,128)(2,1)S(1)} collective-permute-done((bf16[4,12,24,128]{3,2,1,0:T(8,128)(2,1)S(1)}, bf16[4,12,24,128]{3,2,1,0:T(8,128)(2,1)S(1)}, u32[]{:S(2)}, u32[]{:S(2)}) %collective-permute-start.19) | collective-permute-done | bytes 294944 | tf_op jit(solution)/shard_map/ppermute | solution.py:351
  101.9 0.7 copy-done.13
  102.6 6.3 %shard_map.216.refs_0_ = bf16[4,4,12,24,128]{4,3,2,1,0:T(8,128)(2,1)} custom-call(bf16[4,4,12,24,128]{4,3,2,1,0:T(8,128)(2,1)} %shard_map.215.refs_0_, bf16[4,12,24,128]{3,2,1,0:T(8,128)(2,1)} %copy-done.8, bf16[4,12,24,128]{3,2,1,0:T(8,128)(2,1)} %copy-done.4, bf16[4,12,24,128]{3,2,1,0:T(8,128)(2,1)} %copy-done.3, bf16[4,12,24,128]{3,2,1,0:T(8,128)(2,1)} %copy-done.11, ...), custom_call_target="tpu_custom_call" | custom-call | flops 452984832 | bytes 4128768 | tf_op jit(solution)/shard_map/pallas_call | solution.py:173
  108.9 1.3 slice_bitcast_fusion
  110.3 4.3 %collective-permute-done.6.refs_6_ = bf16[4,12,24,128]{3,2,1,0:T(8,128)(2,1)S(1)} collective-permute-done((bf16[4,12,24,128]{3,2,1,0:T(8,128)(2,1)S(1)}, bf16[4,12,24,128]{3,2,1,0:T(8,128)(2,1)S(1)}, u32[]{:S(2)}, u32[]{:S(2)}) %collective-permute-start.6) | collective-permute-done | bytes 294944 | tf_op jit(solution)/shard_map/ppermute | solution.py:351
  115.2 6.3 %shard_map.213.refs_0_ = bf16[4,4,12,24,128]{4,3,2,1,0:T(8,128)(2,1)} custom-call(bf16[4,4,12,24,128]{4,3,2,1,0:T(8,128)(2,1)} %shard_map.212.refs_0_, bf16[4,12,24,128]{3,2,1,0:T(8,128)(2,1)} %copy-done.7, bf16[4,12,24,128]{3,2,1,0:T(8,128)(2,1)} %copy-done.6, bf16[4,12,24,128]{3,2,1,0:T(8,128)(2,1)} %copy-done.5, bf16[4,12,24,128]{3,2,1,0:T(8,128)(2,1)} %copy-done.14, ...), custom_call_target="tpu_custom_call" | custom-call | flops 452984832 | bytes 4128768 | tf_op jit(solution)/shard_map/pallas_call | solution.py:173
  121.5 1.3 slice_bitcast_fusion.6
  122.9 1.0 slice_bitcast_fusion.20
  123.9 2.5 collective-permute-start.8
  126.4 1.0 slice_bitcast_fusion.26
  127.5 2.2 collective-permute-start.21
  130.1 26.3 %collective-permute-done.9.refs_3_ = bf16[4,12,24,128]{3,2,1,0:T(8,128)(2,1)S(1)} collective-permute-done((bf16[4,12,24,128]{3,2,1,0:T(8,128)(2,1)S(1)}, bf16[4,12,24,128]{3,2,1,0:T(8,128)(2,1)S(1)}, u32[]{:S(2)}, u32[]{:S(2)}) %collective-permute-start.9) | collective-permute-done | bytes 294944 | tf_op jit(solution)/shard_map/ppermute | solution.py:351
  156.4 4.8 %collective-permute-done.8.refs_2_ = bf16[4,12,24,128]{3,2,1,0:T(8,128)(2,1)S(1)} collective-permute-done((bf16[4,12,24,128]{3,2,1,0:T(8,128)(2,1)S(1)}, bf16[4,12,24,128]{3,2,1,0:T(8,128)(2,1)S(1)}, u32[]{:S(2)}, u32[]{:S(2)}) %collective-permute-start.8) | collective-permute-done | bytes 294944 | tf_op jit(solution)/shard_map/ppermute | solution.py:351
  161.2 7.5 %collective-permute-done.7.refs_1_ = bf16[4,12,24,128]{3,2,1,0:T(8,128)(2,1)S(1)} collective-permute-done((bf16[4,12,24,128]{3,2,1,0:T(8,128)(2,1)S(1)}, bf16[4,12,24,128]{3,2,1,0:T(8,128)(2,1)S(1)}, u32[]{:S(2)}, u32[]{:S(2)}) %collective-permute-start.7) | collective-permute-done | bytes 294944 | tf_op jit(solution)/shard_map/ppermute | solution.py:351
  168.7 1.1 collective-permute-start.10
  170.1 1.7 collective-permute-start.12
  171.8 2.0 collective-permute-done.21.refs_2_
  174.8 3.9 %collective-permute-done.11.refs_5_ = bf16[4,12,24,128]{3,2,1,0:T(8,128)(2,1)S(1)} collective-permute-done((bf16[4,12,24,128]{3,2,1,0:T(8,128)(2,1)S(1)}, bf16[4,12,24,128]{3,2,1,0:T(8,128)(2,1)S(1)}, u32[]{:S(2)}, u32[]{:S(2)}) %collective-permute-start.11) | collective-permute-done | bytes 294944 | tf_op jit(solution)/shard_map/ppermute | solution.py:351
  178.6 6.8 %collective-permute-done.12.refs_6_ = bf16[4,12,24,128]{3,2,1,0:T(8,128)(2,1)S(1)} collective-permute-done((bf16[4,12,24,128]{3,2,1,0:T(8,128)(2,1)S(1)}, bf16[4,12,24,128]{3,2,1,0:T(8,128)(2,1)S(1)}, u32[]{:S(2)}, u32[]{:S(2)}) %collective-permute-start.12) | collective-permute-done | bytes 294944 | tf_op jit(solution)/shard_map/ppermute | solution.py:351
  186.2 6.7 %shard_map.214 = (bf16[12,392,128]{2,1,0:T(8,128)(2,1)}, bf16[12,392,128]{2,1,0:T(8,128)(2,1)}) custom-call(bf16[4,4,12,24,128]{4,3,2,1,0:T(8,128)(2,1)} %shard_map.213.refs_0_, bf16[4,12,24,128]{3,2,1,0:T(8,128)(2,1)} %copy-done.22, bf16[4,12,24,128]{3,2,1,0:T(8,128)(2,1)} %copy-done.21, bf16[4,12,24,128]{3,2,1,0:T(8,128)(2,1)} %copy-done.20, ...), custom_call_target="tpu_custom_call" | custom-call | flops 1849688064 | bytes 4816896 | tf_op jit(solution)/shard_map/pallas_call | solution.py:228
  193.6 8.8 %collective-permute-done.25.refs_6_ = bf16[4,12,24,128]{3,2,1,0:T(8,128)(2,1)S(1)} collective-permute-done((bf16[4,12,24,128]{3,2,1,0:T(8,128)(2,1)S(1)}, bf16[4,12,24,128]{3,2,1,0:T(8,128)(2,1)S(1)}, u32[]{:S(2)}, u32[]{:S(2)}) %collective-permute-start.25) | collective-permute-done | bytes 294944 | tf_op jit(solution)/shard_map/ppermute | solution.py:351
  203.1 6.7 %shard_map.217 = (bf16[12,392,128]{2,1,0:T(8,128)(2,1)}, bf16[12,392,128]{2,1,0:T(8,128)(2,1)}) custom-call(bf16[4,4,12,24,128]{4,3,2,1,0:T(8,128)(2,1)} %shard_map.216.refs_0_, bf16[4,12,24,128]{3,2,1,0:T(8,128)(2,1)} %copy-done.19, bf16[4,12,24,128]{3,2,1,0:T(8,128)(2,1)} %copy-done.18, bf16[4,12,24,128]{3,2,1,0:T(8,128)(2,1)} %copy-done.17, ...), custom_call_target="tpu_custom_call" | custom-call | flops 1849688064 | bytes 4816896 | tf_op jit(solution)/shard_map/pallas_call | solution.py:228
  209.8 1.3 collective-permute-start.27
  211.0 1.1 slice_bitcast_fusion.16
  212.1 1.1 slice_bitcast_fusion.17
  213.1 8.2 %collective-permute-done.26.refs_6_ = bf16[12,392,128]{2,1,0:T(8,128)(2,1)S(1)} collective-permute-done((bf16[12,392,128]{2,1,0:T(8,128)(2,1)}, bf16[12,392,128]{2,1,0:T(8,128)(2,1)S(1)}, u32[]{:S(2)}, u32[]{:S(2)}) %collective-permute-start.26) | collective-permute-done | bytes 1204256 | tf_op jit(solution)/shard_map/ppermute | solution.py:351
  221.4 3.0 collective-permute-start.28
  224.5 1.9 collective-permute-start.30
  226.4 20.7 %collective-permute-done.27.refs_7_ = bf16[12,392,128]{2,1,0:T(8,128)(2,1)S(1)} collective-permute-done((bf16[12,392,128]{2,1,0:T(8,128)(2,1)}, bf16[12,392,128]{2,1,0:T(8,128)(2,1)S(1)}, u32[]{:S(2)}, u32[]{:S(2)}) %collective-permute-start.27) | collective-permute-done | bytes 1204256 | tf_op jit(solution)/shard_map/ppermute | solution.py:351
  247.2 2.3 collective-permute-start.29
  249.6 2.2 collective-permute-start.31
  252.4 2.0 collective-permute-done.29.refs_9_
  254.3 7.3 %collective-permute-done.31.refs_11_ = bf16[2,2,392,128]{3,2,1,0:T(8,128)(2,1)S(1)} collective-permute-done((bf16[2,2,392,128]{3,2,1,0:T(8,128)(2,1)S(1)}, bf16[2,2,392,128]{3,2,1,0:T(8,128)(2,1)S(1)}, u32[]{:S(2)}, u32[]{:S(2)}) %collective-permute-start.31) | collective-permute-done | bytes 401440 | tf_op jit(solution)/shard_map/ppermute | solution.py:463
  261.6 0.7 copy-done.31
  262.4 44.7 %shard_map.218 = (bf16[12,384,512]{2,1,0:T(8,128)(2,1)}, bf16[12,384,512]{2,1,0:T(8,128)(2,1)}) custom-call(s32[2]{0:T(128)} %iota_xor_fusion.refs_0_, s32[12,12]{1,0:T(8,128)} %refs_1_.1, s32[12,12]{1,0:T(8,128)} %refs_2_.1, f32[12,12]{1,0:T(8,128)} %refs_3_.1, bf16[12,392,128]{2,1,0:T(8,128)(2,1)} %get-tuple-element.6.refs_4_, ...), custom_call_target="tpu_custom_call" | custom-call | flops 9663676416 | bytes 18874368 | tf_op jit(solution)/shard_map/pallas_call | solution.py:332
  (151 shorter events, 10.9 us)
Async XLA Ops:
  0.6 16.1 %copy-start = (bf16[12,192,192]{2,1,0:T(8,128)(2,1)S(1)}, bf16[12,192,192]{2,1,0:T(8,128)(2,1)}, u32[]{:S(2)}) copy-start(bf16[12,192,192]{2,1,0:T(8,128)(2,1)} %param.23) | copy-start | bytes 2654212
  0.7 5.9 %copy-start.27 = (s32[16]{0:T(128)S(1)}, s32[16]{0:T(128)}, u32[]{:S(2)}) copy-start(s32[16]{0:T(128)} %constant.58.clone) | copy-start | bytes 196
  0.7 6.1 %copy-start.39 = (bf16[2,384,384]{2,1,0:T(8,128)(2,1)S(1)}, bf16[2,384,384]{2,1,0:T(8,128)(2,1)}, u32[]{:S(2)}) copy-start(bf16[2,384,384]{2,1,0:T(8,128)(2,1)} %constant.60.clone) | copy-start | bytes 1769476
  5.1 27.2 %collective-permute-start.13 = (bf16[12,384,128]{2,1,0:T(8,128)(2,1)}, bf16[12,384,128]{2,1,0:T(8,128)(2,1)}, u32[]{:S(2)}, u32[]{:S(2)}) collective-permute-start(bf16[12,384,128]{2,1,0:T(8,128)(2,1)} %get-tuple-element.10), channel_id=1, source_target_pairs={{0,1},{1,0},{2,3},{3,2},{4,5},{5,4},{6,7},{7,6},{8,9},{9,8},{10,11... | collective-permute-start | bytes 3538952 | tf_op jit(solution)/shard_map/ppermute | solution.py:351
  5.3 52.2 %collective-permute-start = (bf16[12,384,128]{2,1,0:T(8,128)(2,1)S(1)}, bf16[12,384,128]{2,1,0:T(8,128)(2,1)}, u32[]{:S(2)}, u32[]{:S(2)}) collective-permute-start(bf16[12,384,128]{2,1,0:T(8,128)(2,1)S(1)} %get-tuple-element.12), channel_id=1, source_target_pairs={{0,1},{1,0},{2,3},{3,2},{4,5},{5,4},{6,7},{7,6},{8,9},{9,8},{10,11... | collective-permute-start | bytes 3538952 | tf_op jit(solution)/shard_map/ppermute | solution.py:351
  17.8 2.5 copy-start.2
  18.7 1.6 copy-start.9
  18.7 1.6 copy-start.10
  40.0 30.8 %collective-permute-start.16 = (bf16[4,12,24,128]{3,2,1,0:T(8,128)(2,1)S(1)}, bf16[4,12,24,128]{3,2,1,0:T(8,128)(2,1)S(1)}, u32[]{:S(2)}, u32[]{:S(2)}) collective-permute-start(bf16[4,12,24,128]{3,2,1,0:T(8,128)(2,1)S(1)} %get-tuple-element.31), channel_id=1, source_target_pairs={{0,24},{2,26},{4,28},{6,30},{8,16},{10,18},{12,20},{14,22},{16,8},... | collective-permute-start | bytes 884744 | tf_op jit(solution)/shard_map/ppermute | solution.py:351
  40.3 31.0 %collective-permute-start.15 = (bf16[4,12,24,128]{3,2,1,0:T(8,128)(2,1)S(1)}, bf16[4,12,24,128]{3,2,1,0:T(8,128)(2,1)S(1)}, u32[]{:S(2)}, u32[]{:S(2)}) collective-permute-start(bf16[4,12,24,128]{3,2,1,0:T(8,128)(2,1)S(1)} %get-tuple-element.32), channel_id=1, source_target_pairs={{0,16},{2,18},{4,20},{6,22},{8,24},{10,26},{12,28},{14,30},{16,0},... | collective-permute-start | bytes 884744 | tf_op jit(solution)/shard_map/ppermute | solution.py:351
  67.2 7.0 %collective-permute-start.14 = (bf16[4,12,24,128]{3,2,1,0:T(8,128)(2,1)S(1)}, bf16[4,12,24,128]{3,2,1,0:T(8,128)(2,1)S(1)}, u32[]{:S(2)}, u32[]{:S(2)}) collective-permute-start(bf16[4,12,24,128]{3,2,1,0:T(8,128)(2,1)S(1)} %get-tuple-element.33), channel_id=1, source_target_pairs={{0,8},{2,10},{4,12},{6,14},{8,0},{10,2},{12,4},{14,6},{16,24},{18,... | collective-permute-start | bytes 884744 | tf_op jit(solution)/shard_map/ppermute | solution.py:351
  68.6 17.5 %collective-permute-start.3 = (bf16[4,12,24,128]{3,2,1,0:T(8,128)(2,1)S(1)}, bf16[4,12,24,128]{3,2,1,0:T(8,128)(2,1)S(1)}, u32[]{:S(2)}, u32[]{:S(2)}) collective-permute-start(bf16[4,12,24,128]{3,2,1,0:T(8,128)(2,1)S(1)} %get-tuple-element.43), channel_id=1, source_target_pairs={{0,24},{2,26},{4,28},{6,30},{8,16},{10,18},{12,20},{14,22},{16,8},... | collective-permute-start | bytes 884744 | tf_op jit(solution)/shard_map/ppermute | solution.py:351
  68.6 25.6 %collective-permute-start.2 = (bf16[4,12,24,128]{3,2,1,0:T(8,128)(2,1)S(1)}, bf16[4,12,24,128]{3,2,1,0:T(8,128)(2,1)S(1)}, u32[]{:S(2)}, u32[]{:S(2)}) collective-permute-start(bf16[4,12,24,128]{3,2,1,0:T(8,128)(2,1)S(1)} %get-tuple-element.44), channel_id=1, source_target_pairs={{0,16},{2,18},{4,20},{6,22},{8,24},{10,26},{12,28},{14,30},{16,0},... | collective-permute-start | bytes 884744 | tf_op jit(solution)/shard_map/ppermute | solution.py:351
  70.9 13.9 %copy-start.3 = (bf16[4,12,24,128]{3,2,1,0:T(8,128)(2,1)}, bf16[4,12,24,128]{3,2,1,0:T(8,128)(2,1)S(1)}, u32[]{:S(2)}) copy-start(bf16[4,12,24,128]{3,2,1,0:T(8,128)(2,1)S(1)} %collective-permute-done.16.refs_3_) | copy-start | bytes 884740
  70.9 23.4 %collective-permute-start.1 = (bf16[4,12,24,128]{3,2,1,0:T(8,128)(2,1)S(1)}, bf16[4,12,24,128]{3,2,1,0:T(8,128)(2,1)S(1)}, u32[]{:S(2)}, u32[]{:S(2)}) collective-permute-start(bf16[4,12,24,128]{3,2,1,0:T(8,128)(2,1)S(1)} %get-tuple-element.45), channel_id=1, source_target_pairs={{0,8},{2,10},{4,12},{6,14},{8,0},{10,2},{12,4},{14,6},{16,24},{18,... | collective-permute-start | bytes 884744 | tf_op jit(solution)/shard_map/ppermute | solution.py:351
  71.3 14.8 %copy-start.4 = (bf16[4,12,24,128]{3,2,1,0:T(8,128)(2,1)}, bf16[4,12,24,128]{3,2,1,0:T(8,128)(2,1)S(1)}, u32[]{:S(2)}) copy-start(bf16[4,12,24,128]{3,2,1,0:T(8,128)(2,1)S(1)} %collective-permute-done.15.refs_2_) | copy-start | bytes 884740
  74.3 19.9 %copy-start.8 = (bf16[4,12,24,128]{3,2,1,0:T(8,128)(2,1)}, bf16[4,12,24,128]{3,2,1,0:T(8,128)(2,1)S(1)}, u32[]{:S(2)}) copy-start(bf16[4,12,24,128]{3,2,1,0:T(8,128)(2,1)S(1)} %collective-permute-done.14.refs_1_) | copy-start | bytes 884740
  74.3 23.0 %collective-permute-start.17 = (bf16[4,12,24,128]{3,2,1,0:T(8,128)(2,1)S(1)}, bf16[4,12,24,128]{3,2,1,0:T(8,128)(2,1)S(1)}, u32[]{:S(2)}, u32[]{:S(2)}) collective-permute-start(bf16[4,12,24,128]{3,2,1,0:T(8,128)(2,1)S(1)} %pad_maximum_fusion.14), channel_id=1, source_target_pairs={{0,2},{2,0},{4,6},{6,4},{8,10},{10,8},{12,14},{14,12},{16,18},{18,... | collective-permute-start | bytes 884744 | tf_op jit(solution)/shard_map/ppermute | solution.py:351
  84.8 13.0 %collective-permute-start.18 = (bf16[4,12,24,128]{3,2,1,0:T(8,128)(2,1)S(1)}, bf16[4,12,24,128]{3,2,1,0:T(8,128)(2,1)S(1)}, u32[]{:S(2)}, u32[]{:S(2)}) collective-permute-start(bf16[4,12,24,128]{3,2,1,0:T(8,128)(2,1)S(1)} %pad_maximum_fusion.15), channel_id=1, source_target_pairs={{0,4},{2,6},{4,0},{6,2},{8,12},{10,14},{12,8},{14,10},{16,20},{18,... | collective-permute-start | bytes 884744 | tf_op jit(solution)/shard_map/ppermute | solution.py:351
  86.2 9.8 %copy-start.5 = (bf16[4,12,24,128]{3,2,1,0:T(8,128)(2,1)}, bf16[4,12,24,128]{3,2,1,0:T(8,128)(2,1)S(1)}, u32[]{:S(2)}) copy-start(bf16[4,12,24,128]{3,2,1,0:T(8,128)(2,1)S(1)} %collective-permute-done.3.refs_3_) | copy-start | bytes 884740
  86.2 15.7 %collective-permute-start.19 = (bf16[4,12,24,128]{3,2,1,0:T(8,128)(2,1)S(1)}, bf16[4,12,24,128]{3,2,1,0:T(8,128)(2,1)S(1)}, u32[]{:S(2)}, u32[]{:S(2)}) collective-permute-start(bf16[4,12,24,128]{3,2,1,0:T(8,128)(2,1)S(1)} %pad_maximum_fusion.16), channel_id=1, source_target_pairs={{0,6},{2,4},{4,2},{6,0},{8,14},{10,12},{12,10},{14,8},{16,22},{18,... | collective-permute-start | bytes 884744 | tf_op jit(solution)/shard_map/ppermute | solution.py:351
  94.2 3.1 %copy-start.6 = (bf16[4,12,24,128]{3,2,1,0:T(8,128)(2,1)}, bf16[4,12,24,128]{3,2,1,0:T(8,128)(2,1)S(1)}, u32[]{:S(2)}) copy-start(bf16[4,12,24,128]{3,2,1,0:T(8,128)(2,1)S(1)} %collective-permute-done.2.refs_2_) | copy-start | bytes 884740
  94.2 14.7 %copy-start.7 = (bf16[4,12,24,128]{3,2,1,0:T(8,128)(2,1)}, bf16[4,12,24,128]{3,2,1,0:T(8,128)(2,1)S(1)}, u32[]{:S(2)}) copy-start(bf16[4,12,24,128]{3,2,1,0:T(8,128)(2,1)S(1)} %collective-permute-done.1.refs_1_) | copy-start | bytes 884740
  94.3 15.9 %collective-permute-start.4 = (bf16[4,12,24,128]{3,2,1,0:T(8,128)(2,1)S(1)}, bf16[4,12,24,128]{3,2,1,0:T(8,128)(2,1)S(1)}, u32[]{:S(2)}, u32[]{:S(2)}) collective-permute-start(bf16[4,12,24,128]{3,2,1,0:T(8,128)(2,1)S(1)} %pad_maximum_fusion.8), channel_id=1, source_target_pairs={{0,2},{2,0},{4,6},{6,4},{8,10},{10,8},{12,14},{14,12},{16,18},{18,... | collective-permute-start | bytes 884744 | tf_op jit(solution)/shard_map/ppermute | solution.py:351
  95.9 14.3 %collective-permute-start.5 = (bf16[4,12,24,128]{3,2,1,0:T(8,128)(2,1)S(1)}, bf16[4,12,24,128]{3,2,1,0:T(8,128)(2,1)S(1)}, u32[]{:S(2)}, u32[]{:S(2)}) collective-permute-start(bf16[4,12,24,128]{3,2,1,0:T(8,128)(2,1)S(1)} %pad_maximum_fusion.9), channel_id=1, source_target_pairs={{0,4},{2,6},{4,0},{6,2},{8,12},{10,14},{12,8},{14,10},{16,20},{18,... | collective-permute-start | bytes 884744 | tf_op jit(solution)/shard_map/ppermute | solution.py:351
  97.3 4.6 %copy-start.11 = (bf16[4,12,24,128]{3,2,1,0:T(8,128)(2,1)}, bf16[4,12,24,128]{3,2,1,0:T(8,128)(2,1)S(1)}, u32[]{:S(2)}) copy-start(bf16[4,12,24,128]{3,2,1,0:T(8,128)(2,1)S(1)} %collective-permute-done.17.refs_4_) | copy-start | bytes 884740
  97.3 17.2 %collective-permute-start.6 = (bf16[4,12,24,128]{3,2,1,0:T(8,128)(2,1)S(1)}, bf16[4,12,24,128]{3,2,1,0:T(8,128)(2,1)S(1)}, u32[]{:S(2)}, u32[]{:S(2)}) collective-permute-start(bf16[4,12,24,128]{3,2,1,0:T(8,128)(2,1)S(1)} %pad_maximum_fusion.10), channel_id=1, source_target_pairs={{0,6},{2,4},{4,2},{6,0},{8,14},{10,12},{12,10},{14,8},{16,22},{18,... | collective-permute-start | bytes 884744 | tf_op jit(solution)/shard_map/ppermute | solution.py:351
  97.8 4.1 %copy-start.12 = (bf16[4,12,24,128]{3,2,1,0:T(8,128)(2,1)}, bf16[4,12,24,128]{3,2,1,0:T(8,128)(2,1)S(1)}, u32[]{:S(2)}) copy-start(bf16[4,12,24,128]{3,2,1,0:T(8,128)(2,1)S(1)} %collective-permute-done.18.refs_5_) | copy-start | bytes 884740
  110.2 4.3 %copy-start.14 = (bf16[4,12,24,128]{3,2,1,0:T(8,128)(2,1)}, bf16[4,12,24,128]{3,2,1,0:T(8,128)(2,1)S(1)}, u32[]{:S(2)}) copy-start(bf16[4,12,24,128]{3,2,1,0:T(8,128)(2,1)S(1)} %collective-permute-done.4.refs_4_) | copy-start | bytes 884740
  110.2 4.3 %copy-start.15 = (bf16[4,12,24,128]{3,2,1,0:T(8,128)(2,1)}, bf16[4,12,24,128]{3,2,1,0:T(8,128)(2,1)S(1)}, u32[]{:S(2)}) copy-start(bf16[4,12,24,128]{3,2,1,0:T(8,128)(2,1)S(1)} %collective-permute-done.5.refs_5_) | copy-start | bytes 884740
  122.8 33.5 %collective-permute-start.9 = (bf16[4,12,24,128]{3,2,1,0:T(8,128)(2,1)S(1)}, bf16[4,12,24,128]{3,2,1,0:T(8,128)(2,1)S(1)}, u32[]{:S(2)}, u32[]{:S(2)}) collective-permute-start(bf16[4,12,24,128]{3,2,1,0:T(8,128)(2,1)S(1)} %get-tuple-element.37), channel_id=1, source_target_pairs={{0,24},{2,26},{4,28},{6,30},{8,16},{10,18},{12,20},{14,22},{16,8},... | collective-permute-start | bytes 884744 | tf_op jit(solution)/shard_map/ppermute | solution.py:351
  123.9 37.3 %collective-permute-start.8 = (bf16[4,12,24,128]{3,2,1,0:T(8,128)(2,1)S(1)}, bf16[4,12,24,128]{3,2,1,0:T(8,128)(2,1)S(1)}, u32[]{:S(2)}, u32[]{:S(2)}) collective-permute-start(bf16[4,12,24,128]{3,2,1,0:T(8,128)(2,1)S(1)} %get-tuple-element.38), channel_id=1, source_target_pairs={{0,16},{2,18},{4,20},{6,22},{8,24},{10,26},{12,28},{14,30},{16,0},... | collective-permute-start | bytes 884744 | tf_op jit(solution)/shard_map/ppermute | solution.py:351
  127.4 42.7 %collective-permute-start.22 = (bf16[4,12,24,128]{3,2,1,0:T(8,128)(2,1)S(1)}, bf16[4,12,24,128]{3,2,1,0:T(8,128)(2,1)S(1)}, u32[]{:S(2)}, u32[]{:S(2)}) collective-permute-start(bf16[4,12,24,128]{3,2,1,0:T(8,128)(2,1)S(1)} %get-tuple-element.25), channel_id=1, source_target_pairs={{0,24},{2,26},{4,28},{6,30},{8,16},{10,18},{12,20},{14,22},{16,8},... | collective-permute-start | bytes 884744 | tf_op jit(solution)/shard_map/ppermute | solution.py:351
  127.5 46.3 %collective-permute-start.21 = (bf16[4,12,24,128]{3,2,1,0:T(8,128)(2,1)S(1)}, bf16[4,12,24,128]{3,2,1,0:T(8,128)(2,1)S(1)}, u32[]{:S(2)}, u32[]{:S(2)}) collective-permute-start(bf16[4,12,24,128]{3,2,1,0:T(8,128)(2,1)S(1)} %get-tuple-element.26), channel_id=1, source_target_pairs={{0,16},{2,18},{4,20},{6,22},{8,24},{10,26},{12,28},{14,30},{16,0},... | collective-permute-start | bytes 884744 | tf_op jit(solution)/shard_map/ppermute | solution.py:351
  129.7 44.1 %collective-permute-start.20 = (bf16[4,12,24,128]{3,2,1,0:T(8,128)(2,1)S(1)}, bf16[4,12,24,128]{3,2,1,0:T(8,128)(2,1)S(1)}, u32[]{:S(2)}, u32[]{:S(2)}) collective-permute-start(bf16[4,12,24,128]{3,2,1,0:T(8,128)(2,1)S(1)} %get-tuple-element.27), channel_id=1, source_target_pairs={{0,8},{2,10},{4,12},{6,14},{8,0},{10,2},{12,4},{14,6},{16,24},{18,... | collective-permute-start | bytes 884744 | tf_op jit(solution)/shard_map/ppermute | solution.py:351
  156.4 13.5 %copy-start.20 = (bf16[4,12,24,128]{3,2,1,0:T(8,128)(2,1)}, bf16[4,12,24,128]{3,2,1,0:T(8,128)(2,1)S(1)}, u32[]{:S(2)}) copy-start(bf16[4,12,24,128]{3,2,1,0:T(8,128)(2,1)S(1)} %collective-permute-done.9.refs_3_) | copy-start | bytes 884740
  156.4 12.3 %collective-permute-start.7 = (bf16[4,12,24,128]{3,2,1,0:T(8,128)(2,1)S(1)}, bf16[4,12,24,128]{3,2,1,0:T(8,128)(2,1)S(1)}, u32[]{:S(2)}, u32[]{:S(2)}) collective-permute-start(bf16[4,12,24,128]{3,2,1,0:T(8,128)(2,1)S(1)} %get-tuple-element.39), channel_id=1, source_target_pairs={{0,8},{2,10},{4,12},{6,14},{8,0},{10,2},{12,4},{14,6},{16,24},{18,... | collective-permute-start | bytes 884744 | tf_op jit(solution)/shard_map/ppermute | solution.py:351
  161.2 8.9 %copy-start.21 = (bf16[4,12,24,128]{3,2,1,0:T(8,128)(2,1)}, bf16[4,12,24,128]{3,2,1,0:T(8,128)(2,1)S(1)}, u32[]{:S(2)}) copy-start(bf16[4,12,24,128]{3,2,1,0:T(8,128)(2,1)S(1)} %collective-permute-done.8.refs_2_) | copy-start | bytes 884740
  168.7 3.2 %copy-start.22 = (bf16[4,12,24,128]{3,2,1,0:T(8,128)(2,1)}, bf16[4,12,24,128]{3,2,1,0:T(8,128)(2,1)S(1)}, u32[]{:S(2)}) copy-start(bf16[4,12,24,128]{3,2,1,0:T(8,128)(2,1)S(1)} %collective-permute-done.7.refs_1_) | copy-start | bytes 884740
  168.7 6.0 %collective-permute-start.10 = (bf16[4,12,24,128]{3,2,1,0:T(8,128)(2,1)S(1)}, bf16[4,12,24,128]{3,2,1,0:T(8,128)(2,1)S(1)}, u32[]{:S(2)}, u32[]{:S(2)}) collective-permute-start(bf16[4,12,24,128]{3,2,1,0:T(8,128)(2,1)S(1)} %pad_maximum_fusion.11), channel_id=1, source_target_pairs={{0,2},{2,0},{4,6},{6,4},{8,10},{10,8},{12,14},{14,12},{16,18},{18,... | collective-permute-start | bytes 884744 | tf_op jit(solution)/shard_map/ppermute | solution.py:351
  169.9 8.7 %collective-permute-start.11 = (bf16[4,12,24,128]{3,2,1,0:T(8,128)(2,1)S(1)}, bf16[4,12,24,128]{3,2,1,0:T(8,128)(2,1)S(1)}, u32[]{:S(2)}, u32[]{:S(2)}) collective-permute-start(bf16[4,12,24,128]{3,2,1,0:T(8,128)(2,1)S(1)} %pad_maximum_fusion.12), channel_id=1, source_target_pairs={{0,4},{2,6},{4,0},{6,2},{8,12},{10,14},{12,8},{14,10},{16,20},{18,... | collective-permute-start | bytes 884744 | tf_op jit(solution)/shard_map/ppermute | solution.py:351
  170.1 4.6 %copy-start.17 = (bf16[4,12,24,128]{3,2,1,0:T(8,128)(2,1)}, bf16[4,12,24,128]{3,2,1,0:T(8,128)(2,1)S(1)}, u32[]{:S(2)}) copy-start(bf16[4,12,24,128]{3,2,1,0:T(8,128)(2,1)S(1)} %collective-permute-done.22.refs_3_) | copy-start | bytes 884740
  170.1 15.4 %collective-permute-start.12 = (bf16[4,12,24,128]{3,2,1,0:T(8,128)(2,1)S(1)}, bf16[4,12,24,128]{3,2,1,0:T(8,128)(2,1)S(1)}, u32[]{:S(2)}, u32[]{:S(2)}) collective-permute-start(bf16[4,12,24,128]{3,2,1,0:T(8,128)(2,1)S(1)} %pad_maximum_fusion.13), channel_id=1, source_target_pairs={{0,6},{2,4},{4,2},{6,0},{8,14},{10,12},{12,10},{14,8},{16,22},{18,... | collective-permute-start | bytes 884744 | tf_op jit(solution)/shard_map/ppermute | solution.py:351
  173.8 19.0 %copy-start.18 = (bf16[4,12,24,128]{3,2,1,0:T(8,128)(2,1)}, bf16[4,12,24,128]{3,2,1,0:T(8,128)(2,1)S(1)}, u32[]{:S(2)}) copy-start(bf16[4,12,24,128]{3,2,1,0:T(8,128)(2,1)S(1)} %collective-permute-done.21.refs_2_) | copy-start | bytes 884740
  173.9 19.0 %copy-start.19 = (bf16[4,12,24,128]{3,2,1,0:T(8,128)(2,1)}, bf16[4,12,24,128]{3,2,1,0:T(8,128)(2,1)S(1)}, u32[]{:S(2)}) copy-start(bf16[4,12,24,128]{3,2,1,0:T(8,128)(2,1)S(1)} %collective-permute-done.20.refs_1_) | copy-start | bytes 884740
  173.9 19.6 %collective-permute-start.23 = (bf16[4,12,24,128]{3,2,1,0:T(8,128)(2,1)S(1)}, bf16[4,12,24,128]{3,2,1,0:T(8,128)(2,1)S(1)}, u32[]{:S(2)}, u32[]{:S(2)}) collective-permute-start(bf16[4,12,24,128]{3,2,1,0:T(8,128)(2,1)S(1)} %pad_maximum_fusion.17), channel_id=1, source_target_pairs={{0,2},{2,0},{4,6},{6,4},{8,10},{10,8},{12,14},{14,12},{16,18},{18,... | collective-permute-start | bytes 884744 | tf_op jit(solution)/shard_map/ppermute | solution.py:351
  174.7 18.9 %collective-permute-start.24 = (bf16[4,12,24,128]{3,2,1,0:T(8,128)(2,1)S(1)}, bf16[4,12,24,128]{3,2,1,0:T(8,128)(2,1)S(1)}, u32[]{:S(2)}, u32[]{:S(2)}) collective-permute-start(bf16[4,12,24,128]{3,2,1,0:T(8,128)(2,1)S(1)} %pad_maximum_fusion.18), channel_id=1, source_target_pairs={{0,4},{2,6},{4,0},{6,2},{8,12},{10,14},{12,8},{14,10},{16,20},{18,... | collective-permute-start | bytes 884744 | tf_op jit(solution)/shard_map/ppermute | solution.py:351
  174.7 10.7 %copy-start.32 = (bf16[4,12,24,128]{3,2,1,0:T(8,128)(2,1)}, bf16[4,12,24,128]{3,2,1,0:T(8,128)(2,1)S(1)}, u32[]{:S(2)}) copy-start(bf16[4,12,24,128]{3,2,1,0:T(8,128)(2,1)S(1)} %collective-permute-done.10.refs_4_) | copy-start | bytes 884740
  178.6 6.8 %copy-start.33 = (bf16[4,12,24,128]{3,2,1,0:T(8,128)(2,1)}, bf16[4,12,24,128]{3,2,1,0:T(8,128)(2,1)S(1)}, u32[]{:S(2)}) copy-start(bf16[4,12,24,128]{3,2,1,0:T(8,128)(2,1)S(1)} %collective-permute-done.11.refs_5_) | copy-start | bytes 884740
  192.9 28.4 %collective-permute-start.26 = (bf16[12,392,128]{2,1,0:T(8,128)(2,1)}, bf16[12,392,128]{2,1,0:T(8,128)(2,1)S(1)}, u32[]{:S(2)}, u32[]{:S(2)}) collective-permute-start(bf16[12,392,128]{2,1,0:T(8,128)(2,1)} %get-tuple-element.8), channel_id=1, source_target_pairs={{0,1},{1,0},{2,3},{3,2},{4,5},{5,4},{6,7},{7,6},{8,9},{9,8},{10,11... | collective-permute-start | bytes 3612680 | tf_op jit(solution)/shard_map/ppermute | solution.py:351
  193.2 9.1 %collective-permute-start.25 = (bf16[4,12,24,128]{3,2,1,0:T(8,128)(2,1)S(1)}, bf16[4,12,24,128]{3,2,1,0:T(8,128)(2,1)S(1)}, u32[]{:S(2)}, u32[]{:S(2)}) collective-permute-start(bf16[4,12,24,128]{3,2,1,0:T(8,128)(2,1)S(1)} %pad_maximum_fusion.19), channel_id=1, source_target_pairs={{0,6},{2,4},{4,2},{6,0},{8,14},{10,12},{12,10},{14,8},{16,22},{18,... | collective-permute-start | bytes 884744 | tf_op jit(solution)/shard_map/ppermute | solution.py:351
  193.6 8.8 %copy-start.34 = (bf16[4,12,24,128]{3,2,1,0:T(8,128)(2,1)}, bf16[4,12,24,128]{3,2,1,0:T(8,128)(2,1)S(1)}, u32[]{:S(2)}) copy-start(bf16[4,12,24,128]{3,2,1,0:T(8,128)(2,1)S(1)} %collective-permute-done.23.refs_4_) | copy-start | bytes 884740
  193.6 8.8 %copy-start.35 = (bf16[4,12,24,128]{3,2,1,0:T(8,128)(2,1)}, bf16[4,12,24,128]{3,2,1,0:T(8,128)(2,1)S(1)}, u32[]{:S(2)}) copy-start(bf16[4,12,24,128]{3,2,1,0:T(8,128)(2,1)S(1)} %collective-permute-done.24.refs_5_) | copy-start | bytes 884740
  209.8 37.4 %collective-permute-start.27 = (bf16[12,392,128]{2,1,0:T(8,128)(2,1)}, bf16[12,392,128]{2,1,0:T(8,128)(2,1)S(1)}, u32[]{:S(2)}, u32[]{:S(2)}) collective-permute-start(bf16[12,392,128]{2,1,0:T(8,128)(2,1)} %get-tuple-element.9), channel_id=1, source_target_pairs={{0,1},{1,0},{2,3},{3,2},{4,5},{5,4},{6,7},{7,6},{8,9},{9,8},{10,11... | collective-permute-start | bytes 3612680 | tf_op jit(solution)/shard_map/ppermute | solution.py:351
  221.3 3.2 %copy-start.23 = (bf16[12,392,128]{2,1,0:T(8,128)(2,1)}, bf16[12,392,128]{2,1,0:T(8,128)(2,1)S(1)}, u32[]{:S(2)}) copy-start(bf16[12,392,128]{2,1,0:T(8,128)(2,1)S(1)} %collective-permute-done.26.refs_6_) | copy-start | bytes 3612676
  221.4 31.0 %collective-permute-start.28 = (bf16[2,2,392,128]{3,2,1,0:T(8,128)(2,1)S(1)}, bf16[2,2,392,128]{3,2,1,0:T(8,128)(2,1)S(1)}, u32[]{:S(2)}, u32[]{:S(2)}) collective-permute-start(bf16[2,2,392,128]{3,2,1,0:T(8,128)(2,1)S(1)} %pad_maximum_fusion.4), channel_id=1, source_target_pairs={{0,2},{2,4},{4,6},{6,8},{8,10},{10,12},{12,14},{14,16},{16,18},{18... | collective-permute-start | bytes 1204232 | tf_op jit(solution)/shard_map/ppermute | solution.py:462
  224.5 27.9 %collective-permute-start.30 = (bf16[2,2,392,128]{3,2,1,0:T(8,128)(2,1)S(1)}, bf16[2,2,392,128]{3,2,1,0:T(8,128)(2,1)S(1)}, u32[]{:S(2)}, u32[]{:S(2)}) collective-permute-start(bf16[2,2,392,128]{3,2,1,0:T(8,128)(2,1)S(1)} %pad_maximum_fusion.6), channel_id=1, source_target_pairs={{2,0},{4,2},{6,4},{8,6},{10,8},{12,10},{14,12},{16,14},{18,16},{20... | collective-permute-start | bytes 1204232 | tf_op jit(solution)/shard_map/ppermute | solution.py:463
  247.1 2.5 copy-start.24
  247.2 7.1 %collective-permute-start.29 = (bf16[2,2,392,128]{3,2,1,0:T(8,128)(2,1)S(1)}, bf16[2,2,392,128]{3,2,1,0:T(8,128)(2,1)S(1)}, u32[]{:S(2)}, u32[]{:S(2)}) collective-permute-start(bf16[2,2,392,128]{3,2,1,0:T(8,128)(2,1)S(1)} %pad_maximum_fusion.5), channel_id=1, source_target_pairs={{0,2},{2,4},{4,6},{6,8},{8,10},{10,12},{12,14},{14,16},{16,18},{18... | collective-permute-start | bytes 1204232 | tf_op jit(solution)/shard_map/ppermute | solution.py:462
  249.6 12.0 %collective-permute-start.31 = (bf16[2,2,392,128]{3,2,1,0:T(8,128)(2,1)S(1)}, bf16[2,2,392,128]{3,2,1,0:T(8,128)(2,1)S(1)}, u32[]{:S(2)}, u32[]{:S(2)}) collective-permute-start(bf16[2,2,392,128]{3,2,1,0:T(8,128)(2,1)S(1)} %pad_maximum_fusion.7), channel_id=1, source_target_pairs={{2,0},{4,2},{6,4},{8,6},{10,8},{12,10},{14,12},{16,14},{18,16},{20... | collective-permute-start | bytes 1204232 | tf_op jit(solution)/shard_map/ppermute | solution.py:463
  252.4 9.3 %copy-start.28 = (bf16[2,2,392,128]{3,2,1,0:T(8,128)(2,1)}, bf16[2,2,392,128]{3,2,1,0:T(8,128)(2,1)S(1)}, u32[]{:S(2)}) copy-start(bf16[2,2,392,128]{3,2,1,0:T(8,128)(2,1)S(1)} %collective-permute-done.28.refs_8_) | copy-start | bytes 1204228
  252.4 9.3 %copy-start.29 = (bf16[2,2,392,128]{3,2,1,0:T(8,128)(2,1)}, bf16[2,2,392,128]{3,2,1,0:T(8,128)(2,1)S(1)}, u32[]{:S(2)}) copy-start(bf16[2,2,392,128]{3,2,1,0:T(8,128)(2,1)S(1)} %collective-permute-done.30.refs_10_) | copy-start | bytes 1204228
  254.3 7.3 %copy-start.30 = (bf16[2,2,392,128]{3,2,1,0:T(8,128)(2,1)}, bf16[2,2,392,128]{3,2,1,0:T(8,128)(2,1)S(1)}, u32[]{:S(2)}) copy-start(bf16[2,2,392,128]{3,2,1,0:T(8,128)(2,1)S(1)} %collective-permute-done.29.refs_9_) | copy-start | bytes 1204228
  262.4 44.7 %copy-start.1 = (bf16[12,192,192]{2,1,0:T(8,128)(2,1)S(1)}, bf16[12,192,192]{2,1,0:T(8,128)(2,1)}, u32[]{:S(2)}) copy-start(bf16[12,192,192]{2,1,0:T(8,128)(2,1)} %param.23) | copy-start | bytes 2654212
  (8 other events, 7.0 us)

commit v2 on v1

v2 whole, which is shorter than its diff:
```python
import functools
import math

import jax
import jax.numpy as jnp
import ml_dtypes
import numpy as np
from jax import lax
from jax.experimental import pallas as pl
from jax.experimental.pallas import tpu as pltpu
from jax.sharding import PartitionSpec as P

HALO = 2
SPAN = 2 * HALO + 1
NQ = 4
LANES = 128
F32 = jnp.float32
BF16 = jnp.bfloat16
VMEM_LIMIT = 56 * 1024 * 1024


def vmem_spec():
    return pl.BlockSpec(memory_space=pltpu.VMEM)


def smem_spec():
    return pl.BlockSpec(memory_space=pltpu.SMEM)


def params():
    return pltpu.CompilerParams(
        vmem_limit_bytes=VMEM_LIMIT, dimension_semantics=("arbitrary",)
    )


def cost(flops, nbytes, trans=0):
    return pl.CostEstimate(
        flops=int(flops), bytes_accessed=int(nbytes), transcendentals=int(trans)
    )


def tables_np(nlon, lon_count, wave_block, mmax, padded_cols):
    blocks = mmax // wave_block
    waves = np.arange(mmax).reshape(blocks, 1, wave_block)
    waves = np.broadcast_to(waves, (blocks, 2, wave_block)).reshape(-1)
    imag = np.broadcast_to(np.arange(2).reshape(1, 2, 1), (blocks, 2, wave_block)).reshape(-1)

    def table(points):
        phase = (waves[:, None].astype(np.int64) * points[None, :]) % nlon
        angle = phase * (2.0 * math.pi / nlon)
        return np.where(imag[:, None] == 0, np.cos(angle), -np.sin(angle)) / math.sqrt(nlon)

    cols = nlon // lon_count
    fwd = np.stack([table(np.arange(cols) + b * cols) for b in range(lon_count)])
    factor = np.where(waves == 0, 1.0, 2.0)[:, None]
    inv = np.stack(
        [
            (factor * table((np.arange(padded_cols) - HALO + b * cols) % nlon)).T
            for b in range(lon_count)
        ]
    )
    return fwd.astype(ml_dtypes.bfloat16), inv.astype(ml_dtypes.bfloat16)


def any_spec():
    return pl.BlockSpec(memory_space=pl.ANY)


def step_rows(rows, limit):
    return max(r for r in range(1, limit + 1) if rows % r == 0)


def first_of(array, keep):
    block = (1,) * keep + array.shape[keep:]
    return pl.BlockSpec(block, lambda t: (0,) * array.ndim)


def whole_of(array):
    return pl.BlockSpec(array.shape, lambda t: (0,) * array.ndim)


def side_by_side(parts):
    return jnp.concatenate(parts, axis=1) if len(parts) > 1 else parts[0]


def dft_kernel(lon_count, nz, waits, quad_ref, *refs):
    blocks = refs[:lon_count]
    table_ref = refs[lon_count]
    outs = refs[lon_count + 1 + waits :]
    step = pl.program_id(0)
    rows, _, cw = blocks[0].shape
    wave_rows = outs[0].shape[2]
    group = rows if cw % LANES == 0 else 1
    for first in range(0, rows, group):
        x = [side_by_side([b[first + i] for i in range(group)]) for b in blocks]
        acc = jnp.dot(table_ref[...], jnp.concatenate(x, axis=0), preferred_element_type=F32)
        for i in range(group):
            t = first + i
            scaled = acc[:, i * cw : (i + 1) * cw] * quad_ref[step * rows + t]
            for d in range(nz):
                for q in range(NQ):
                    at = (d * NQ + q) * wave_rows
                    outs[d][q, t] = scaled[at : at + wave_rows].astype(BF16)


def dft(blocks, quad, table, nz, wave_rows, waits):
    rows, cols, cw = blocks[0].shape
    step = step_rows(rows, 6)
    lon_count = len(blocks)
    return pl.pallas_call(
        functools.partial(dft_kernel, lon_count, nz, len(waits)),
        grid=(rows // step,),
        in_specs=[smem_spec()]
        + [pl.BlockSpec((step, cols, cw), lambda t: (t, 0, 0))] * lon_count
        + [whole_of(table)]
        + [any_spec()] * len(waits),
        out_specs=[pl.BlockSpec((NQ, step, wave_rows, cw), lambda t: (0, t, 0, 0))] * nz,
        out_shape=[jax.ShapeDtypeStruct((NQ, rows, wave_rows, cw), BF16)] * nz,
        compiler_params=params(),
        cost_estimate=cost(2 * table.size * rows * cw, 8 * rows * cols * cw),
    )(quad, *blocks, table, *waits)


def legendre_kernel(nz, waits, *refs):
    own = refs[:nz]
    others = refs[nz : nz + NQ - 1]
    leg_ref, legt_ref, gr_ref, gi_ref = refs[nz + NQ - 1 : nz + NQ + 3]
    outs = refs[nz + NQ + 3 + waits : -2]
    wide, result = refs[-2:]
    waves, _, lat = leg_ref.shape
    _, rows, wave_rows, cw = outs[0].shape
    span = rows * wave_rows
    for q in range(NQ):
        for d in range(nz):
            at = (q * nz + d) * span
            piece = others[q - 1][d] if q else own[d][0]
            wide[at : at + span, :] = piece.astype(F32).reshape(span, cw)
    gain_r = gr_ref[...]
    gain_i = gi_ref[...]
    for m in range(waves):
        pair = [wide[pl.ds(r * waves + m, lat, stride=wave_rows), :] for r in range(2)]
        x = side_by_side(pair).astype(BF16)
        co = jnp.dot(leg_ref[m], x, preferred_element_type=F32)
        cr, ci = co[:, :cw], co[:, cw:]
        fr = gain_r * cr - gain_i * ci
        fi = gain_r * ci + gain_i * cr
        x = side_by_side([fr, fi]).astype(BF16)
        out = jnp.dot(legt_ref[m], x, preferred_element_type=F32)
        for r in range(2):
            result[pl.ds(r * waves + m, lat, stride=wave_rows), :] = out[:, r * cw : (r + 1) * cw]
    for q in range(NQ):
        for d in range(nz):
            at = (q * nz + d) * span
            outs[d][q] = result[at : at + span, :].reshape(rows, wave_rows, cw).astype(BF16)


def legendre_step(own, others, leg, legt, gr, gi, waits):
    nz = len(own)
    shape = own[0].shape
    _, rows, wave_rows, cw = shape
    waves, degrees, lat = leg.shape
    return pl.pallas_call(
        functools.partial(legendre_kernel, nz, len(waits)),
        grid=(1,),
        in_specs=[first_of(a, 1) for a in own]
        + [whole_of(a) for a in (*others, leg, legt, gr, gi)]
        + [any_spec()] * len(waits),
        out_specs=[pl.BlockSpec(shape, lambda t: (0, 0, 0, 0))] * nz,
        out_shape=[jax.ShapeDtypeStruct(shape, BF16)] * nz,
        scratch_shapes=[pltpu.VMEM((lat * wave_rows, cw), F32)] * 2,
        compiler_params=params(),
        cost_estimate=cost(
            8 * waves * degrees * lat * cw, 4 * lat * wave_rows * cw + 4 * leg.size
        ),
    )(*own, *others, leg, legt, gr, gi, *waits)


def inverse_kernel(nz, lon_count, *refs):
    own = refs[:nz]
    others = refs[nz : nz + NQ - 1]
    table_ref = refs[nz + NQ - 1]
    outs = refs[nz + NQ : nz + NQ + lon_count]
    wide = refs[-1]
    rows, _, cw = wide.shape
    wave_rows = own[0].shape[-2]
    cols = outs[0].shape[1]
    for t in range(rows):
        for q in range(NQ):
            for d in range(nz):
                at = (q * nz + d) * wave_rows
                block = others[q - 1][d, t] if q else own[d][0, t]
                wide[t, at : at + wave_rows, :] = block.astype(F32)
    group = rows if cw % LANES == 0 else 1
    for first in range(0, rows, group):
        x = side_by_side([wide[first + i].astype(BF16) for i in range(group)])
        acc = jnp.dot(table_ref[...], x, preferred_element_type=F32)
        for i in range(group):
            for s in range(lon_count):
                piece = acc[s * cols : (s + 1) * cols, i * cw : (i + 1) * cw]
                outs[s][first + i] = piece.astype(BF16)


def inverse(own, others, table, lon_count):
    nz = len(own)
    _, rows, wave_rows, cw = own[0].shape
    step = step_rows(rows, 6)
    cols = table.shape[0] // lon_count
    specs = [pl.BlockSpec((1, step, wave_rows, cw), lambda t: (0, t, 0, 0))] * nz
    specs += [pl.BlockSpec((nz, step, wave_rows, cw), lambda t: (0, t, 0, 0))] * (NQ - 1)
    return pl.pallas_call(
        functools.partial(inverse_kernel, nz, lon_count),
        grid=(rows // step,),
        in_specs=specs + [whole_of(table)],
        out_specs=[pl.BlockSpec((step, cols, cw), lambda t: (t, 0, 0))] * lon_count,
        out_shape=[jax.ShapeDtypeStruct((rows, cols, cw), BF16)] * lon_count,
        scratch_shapes=[pltpu.VMEM((step, nz * NQ * wave_rows, cw), F32)],
        compiler_params=params(),
        cost_estimate=cost(2 * table.size * rows * cw, 4 * rows * cols * cw * lon_count),
    )(*own, *others, table)


def window_kernel(cols, place_ref, neighbour_ref, basis_ref, quad_ref, wave_ref, low_ref, high_ref, disco_ref, out_ref, ring):
    step = pl.program_id(0)
    rows = wave_ref.shape[0]
    slots = neighbour_ref.shape[1]
    per_step = out_ref.shape[0]
    group = place_ref[0]

    @pl.when(step == 0)
    def _():
        for r in range(HALO):
            ring[r] = low_ref[r].astype(F32)
            ring[HALO + r] = wave_ref[r].astype(F32)
            ring[rows + HALO + r] = high_ref[r].astype(F32)

    for i in range(per_step):
        t = step * per_step + i

        @pl.when(t + HALO < rows)
        def _(t=t):
            ring[t + 2 * HALO] = wave_ref[t + HALO].astype(F32)

    tile = 48 if cols % 48 == 0 else 8
    for i in range(per_step):
        t = step * per_step + i
        taps = []
        for s in range(slots):
            n = neighbour_ref[t, s]
            weight = disco_ref[group, pl.ds(basis_ref[t, s], 1), :]
            taps.append((t + n // SPAN, n % SPAN, weight * quad_ref[t, s]))
        for at in range(0, cols, tile):
            acc = ring[t + HALO, pl.ds(at + HALO, tile), :]
            for row, shift, coef in taps:
                acc = acc + coef * ring[row, pl.ds(at + shift, tile), :]
            out_ref[i, pl.ds(at, tile), :] = acc.astype(BF16)


def window(place, neighbour, basis, quad, wave, low, high, disco, cols):
    rows, padded, cw = wave.shape
    per_step = step_rows(rows, 2)
    return pl.pallas_call(
        functools.partial(window_kernel, cols),
        grid=(rows // per_step,),
        in_specs=[smem_spec()] * 4 + [whole_of(a) for a in (wave, low, high, disco)],
        out_specs=pl.BlockSpec((per_step, cols, cw), lambda t: (t, 0, 0)),
        out_shape=jax.ShapeDtypeStruct((rows, cols, cw), BF16),
        scratch_shapes=[pltpu.VMEM((rows + 2 * HALO, padded, cw), F32)],
        compiler_params=params(),
        cost_estimate=cost(8 * rows * cols * cw * 24, 4 * rows * cols * cw),
    )(place, neighbour, basis, quad, wave, low, high, disco)


def mlp_kernel(place_ref, *refs):
    count = len(refs) - 9
    groups = refs[:count]
    gain_ref, w_in_ref, b_in_ref, w_out_ref, b_out_ref, field_ref, out_ref, spatial_ref, ordered = refs[count:]
    per_step, cols, cw = groups[0].shape
    for k in range(count):
        ordered[place_ref[k]] = groups[k][...].reshape(per_step * cols, cw)
    spatial = jnp.concatenate([ordered[k] for k in range(count)], axis=1)
    spatial_ref[...] = spatial.reshape(spatial_ref.shape)
    tokens = spatial.astype(F32)
    center = jnp.mean(tokens, axis=1, keepdims=True)
    shifted = tokens - center
    spread = jnp.mean(shifted * shifted, axis=1, keepdims=True)
    normed = (shifted * lax.rsqrt(spread + 1e-05) * gain_ref[...]).astype(BF16)
    hidden = jnp.dot(normed, w_in_ref[...], preferred_element_type=F32) + b_in_ref[...]
    hidden = jax.nn.gelu(hidden).astype(BF16)
    result = jnp.dot(hidden, w_out_ref[...], preferred_element_type=F32)
    result = result + b_out_ref[...] + field_ref[...].reshape(tokens.shape).astype(F32)
    out_ref[...] = result.astype(BF16).reshape(out_ref.shape)


def mlp(place, groups, gain, w_in, b_in, w_out, b_out, field):
    rows, cols, channels = field.shape
    cw = groups[0].shape[2]
    per_step = step_rows(rows, 2)
    block = pl.BlockSpec((per_step, cols, channels), lambda t: (t, 0, 0))
    part = pl.BlockSpec((per_step, cols, cw), lambda t: (t, 0, 0))
    return pl.pallas_call(
        mlp_kernel,
        grid=(rows // per_step,),
        in_specs=[smem_spec()]
        + [part] * len(groups)
        + [whole_of(a) for a in (gain, w_in, b_in, w_out, b_out)]
        + [block],
        out_specs=[block, block],
        out_shape=[jax.ShapeDtypeStruct(field.shape, BF16)] * 2,
        scratch_shapes=[pltpu.VMEM((len(groups), per_step * cols, cw), BF16)],
        compiler_params=params(),
        cost_estimate=cost(
            4 * field.size * w_in.shape[1], 8 * field.size, rows * cols * w_in.shape[1]
        ),
    )(place, *groups, gain, w_in, b_in, w_out, b_out, field)


def swap(array, axis, mask):
    count = lax.axis_size(axis)
    return lax.ppermute(array, axis, [(i, i ^ mask) for i in range(count)])


def shards(
    field,
    quad_weight,
    legendre,
    filter_real,
    filter_imag,
    neighbour,
    basis,
    disco_quad,
    disco_weight,
    norm_gain,
    w_in,
    b_in,
    w_out,
    b_out,
):
    rows, cols, channels = field.shape
    lon_count = lax.axis_size("lon")
    lat_count = lax.axis_size("lat")
    nz = lat_count // NQ
    wave_block, degrees, nlat = legendre.shape
    wave_rows = 2 * wave_block
    mmax = wave_block * lat_count
    nlon = cols * lon_count
    cblock = channels // lon_count
    nch = max(1, cblock // LANES)
    cw = cblock // nch
    padded_cols = (cols + 2 * HALO + 7) // 8 * 8
    lat_id = lax.axis_index("lat")
    lon_id = lax.axis_index("lon")

    fwd, inv = tables_np(nlon, lon_count, wave_block, mmax, padded_cols)
    zq = np.arange(lat_count)
    qz = (zq % nz) * NQ + zq // nz

    def permutation(masks, width):
        source = (lat_id ^ jnp.asarray(masks, jnp.int32))[:, None] * width
        source = (source + jnp.arange(width, dtype=jnp.int32)[None, :]).reshape(-1)
        return (jnp.arange(lat_count * width, dtype=jnp.int32)[None, :] == source[:, None]).astype(BF16)

    perm_fwd = permutation(zq, wave_rows)
    perm_inv = permutation(qz, wave_rows)
    perm_lat = permutation(qz, rows)

    def forward_table(table):
        parts = [
            jnp.dot(
                perm_fwd,
                lax.dynamic_index_in_dim(jnp.asarray(table), lon_id ^ s, 0, keepdims=False),
                preferred_element_type=F32,
            )
            for s in range(lon_count)
        ]
        return jnp.concatenate(parts, axis=1).astype(BF16)

    def inverse_table(table):
        parts = [
            jnp.einsum(
                "kr,ur->ku",
                lax.dynamic_index_in_dim(jnp.asarray(table), lon_id ^ s, 0, keepdims=False),
                perm_inv,
                preferred_element_type=F32,
            )
            for s in range(lon_count)
        ]
        return jnp.concatenate(parts, axis=0).astype(BF16)

    fwd = forward_table(fwd)
    inv = inverse_table(inv)
    leg = jnp.einsum("mlt,ut->mlu", legendre, perm_lat, preferred_element_type=F32).astype(BF16)
    legt = jnp.einsum("mlt,ut->mul", legendre, perm_lat, preferred_element_type=F32).astype(BF16)

    def chunk_of(array, s, j):
        start = (lon_id ^ s) * cblock + j * cw
        return lax.dynamic_slice_in_dim(array, start, cw, array.ndim - 1)

    def across(own):
        return [swap(jnp.stack([a[q] for a in own]), "lat", q) for q in range(1, NQ)]

    def along(arrays):
        return [arrays[0]] + [swap(arrays[d], "lat", NQ * d) for d in range(1, nz)]

    disco = disco_weight.reshape(disco_weight.shape[0], lon_count * nch, cw)
    disco = jnp.transpose(disco, (1, 0, 2))
    up = [(i, i + 1) for i in range(lat_count - 1)]
    down = [(i + 1, i) for i in range(lat_count - 1)]

    def convolved(wave, s, j):
        low = lax.ppermute(wave[rows - HALO :], "lat", up)
        high = lax.ppermute(wave[:HALO], "lat", down)
        place = ((lon_id ^ s) * nch + j).astype(jnp.int32)
        done = window(
            place[None], neighbour, basis, disco_quad, wave, low, high, disco, cols
        )
        return place, done

    received = [
        [swap(chunk_of(field, s, j), "lon", s) for s in range(1, lon_count)]
        for j in range(nch)
    ]
    spectra, waits = [], []
    for j in range(nch):
        blocks = [chunk_of(field, 0, j)] + received[j]
        spectra.append(along(dft(blocks, quad_weight, fwd, nz, wave_rows, waits)))
        waits = [spectra[-1][1]]
    synthesis, waits = [], []
    for j in range(nch):
        gr = chunk_of(filter_real, 0, j)
        gi = chunk_of(filter_imag, 0, j)
        full = legendre_step(spectra[j], across(spectra[j]), leg, legt, gr, gi, waits)
        synthesis.append(along(full))
        waits = [full[0]]
    groups = []
    for j in range(nch):
        parts = inverse(synthesis[j], across(synthesis[j]), inv, lon_count)
        for s in range(lon_count):
            wave = swap(parts[s], "lon", s) if s else parts[0]
            groups.append(convolved(wave, s, j))
    block_out, spatial = mlp(
        jnp.stack([place for place, _ in groups]),
        [done for _, done in groups],
        norm_gain[None, :],
        w_in,
        b_in[None, :],
        w_out,
        b_out[None, :],
        field,
    )
    return (block_out, spatial)


def solution(mesh):
    grid = P("lat", "lon", None)
    rows = P("lat", None)
    placed = (grid, P("lat"), P("lat", None, None), P(), P(), rows, rows, rows) + (P(),) * 6
    return jax.shard_map(
        shards,
        mesh=mesh,
        in_specs=placed,
        out_specs=(grid, grid),
        check_vma=False,
    )
```

time: 310 us -> 312 us (level)
  Pallas kernels: 83.7 us -> 65.6 us
  waiting for transfers between devices: 132 us -> 148 us
  starting transfers between devices: 52.3 us -> 67 us
  matrix products: 9.36 us -> 4.27 us
    ppermute x28, waiting for transfers between devices: 123 us -> 148 us  [swap(): return lax.ppermute(array, axis, [(i, i ^ mask) for i in range(count)])]
    pallas_call x7 -> x11, Pallas kernels: 83.7 us -> 65.6 us  [the longest x4 24.1 us: window(): pl.pallas_call(functools.partial(window_kernel, cols), grid=(rows // per_...]
    ppermute x4 -> x8, starting transfers between devices: 9.53 us -> 23.8 us  [the longest x4 15.7 us: convolved(): low = lax.ppermute(wave[rows - HALO:], 'lat', up)]
    ppermute x4 -> x8, waiting for transfers between devices: 9.26 us -> 0.02 us  [the longest x4 0.01 us: convolved(): high = lax.ppermute(wave[:HALO], 'lat', down)]
    slice x12 -> x20, local copies, waits for them, and re-layouts: 0.28 us -> 8.54 us  [the longest x4 4.35 us: convolved(): high = lax.ppermute(wave[:HALO], 'lat', down)]
    another operation x8 -> x0, local copies, waits for them, and re-layouts: 6.08 us -> none  [the longest x4 3.92 us: others_of(): jnp.stack([own[0][0, q]] + [a[q] for a in own[1:]])]
    squeeze x4 -> x0, local copies, waits for them, and re-layouts: 5.16 us -> none  [the longest x2 2.58 us: shards(): synthesis[d]]
    dot_general x4 -> x2, matrix products: 5.35 us -> 0.99 us  [inverse_table(): jnp.einsum('kr,ur->ku', lax.dynamic_index_in_dim(jnp.asarray(table), lon_...]
  transfers between devices with their start and end apart: 32 -> 36, of which waited for: 16 -> 15; matrix products, arithmetic and copies ran while one was open for 9% -> 6% of each run, Pallas kernels for 11% -> 13%
where the time goes in v2:
time: 312 us; the launch traced here: 311 us
  waiting for transfers between devices  148 us (47%)
  starting transfers between devices  67 us (21%)
  Pallas kernels  65.6 us (21%)
  local copies, waits for them, and re-layouts  21.3 us (7%)
  matrix products  4.27 us (1%)
    ppermute x28, waiting for transfers between devices, swap(): return lax.ppermute(array, axis, [(i, i ^ mask) for i in range(count)])  148 us
    ppermute x28, starting transfers between devices, swap(): return lax.ppermute(array, axis, [(i, i ^ mask) for i in range(count)])  43.2 us
    pallas_call x4, Pallas kernels, window(): pl.pallas_call(functools.partial(window_kernel, cols), grid=(rows // per_...  24.1 us
    pallas_call x1, Pallas kernels, mlp(): pl.pallas_call(mlp_kernel, grid=(rows // per_step,), in_specs=[smem_spec(...  17.8 us
    ppermute x4, starting transfers between devices, convolved(): low = lax.ppermute(wave[rows - HALO:], 'lat', up)  15.7 us
    pallas_call x2, Pallas kernels, legendre_step(): pl.pallas_call(functools.partial(legendre_kernel, nz, len(waits)), grid=(...  8.61 us
    ppermute x4, starting transfers between devices, convolved(): high = lax.ppermute(wave[:HALO], 'lat', down)  8.09 us
    pallas_call x2, Pallas kernels, inverse(): pl.pallas_call(functools.partial(inverse_kernel, nz, lon_count), grid=(ro...  7.81 us
  transfers between devices with their start and end apart: 36, of which 15 were waited for; matrix products, arithmetic and copies ran while one was open for 6% of the time, Pallas kernels for 13%

profile of v2, /device:TPU:19, one launch (start us, length us, event | category | flops | bytes accessed | tf_op | source)
XLA Modules:
  0.0 310.5 jit_solution(7693112971830688595)
XLA Ops:
  0.7 4.4 %constant_dynamic-slice_fusion.2 = (bf16[12,384,128]{2,1,0:T(8,128)(2,1)S(1)}, bf16[12,384,128]{2,1,0:T(8,128)(2,1)}, bf16[12,384,128]{2,1,0:T(8,128)(2,1)}, bf16[12,384,128]{2,1,0:T(8,128)(2,1)}) fusion(bf16[12,384,512]{2,1,0:T(8,128)(2,1)} %refs_9_.1, s32[]{:T(128)S(6)} %select_n.31, s32[]{:T(128)S(6)} %select_n.30, s32[]{:T(128)S(6)} %select_n.27, ...), kind=kLoop, calls=%fused_computation.41 | loop fusion | bytes 9437200 | tf_op jit(solution)/shard_map/dynamic_slice | solution.py:396
  5.3 1.2 collective-permute-start
  7.6 1.5 copy.23.refs_7_
  9.1 1.4 convolution_convert_fusion.3
  10.5 1.4 convolution_convert_fusion.4
  11.8 0.9 pad_maximum_fusion.1.refs_2_
  13.7 43.6 %collective-permute-done.refs_1_ = bf16[12,384,128]{2,1,0:T(8,128)(2,1)} collective-permute-done((bf16[12,384,128]{2,1,0:T(8,128)(2,1)}, bf16[12,384,128]{2,1,0:T(8,128)(2,1)}, u32[]{:S(2)}, u32[]{:S(2)}) %collective-permute-start) | collective-permute-done | bytes 1179680 | tf_op jit(solution)/shard_map/ppermute | solution.py:319
  57.3 3.7 %shard_map.194 = (bf16[4,12,24,128]{3,2,1,0:T(8,128)(2,1)}, bf16[4,12,24,128]{3,2,1,0:T(8,128)(2,1)}, bf16[4,12,24,128]{3,2,1,0:T(8,128)(2,1)}, bf16[4,12,24,128]{3,2,1,0:T(8,128)(2,1)}) custom-call(f32[12]{0:T(128)} %quad_ref.9, bf16[12,384,128]{2,1,0:T(8,128)(2,1)} %get-tuple-element.45.refs_0_, bf16[12,384,128]{2,1,0:T(8,128)(2,1)} %collective-permute-done.refs_1_, ...), custom_call_target="tpu_custom_call" | custom-call | flops 905969664 | bytes 4718592 | tf_op jit(solution)/shard_map/pallas_call | solution.py:110
  60.9 1.3 collective-permute-start.1
  62.2 0.8 constant_dynamic-slice_fusion
  63.1 1.3 collective-permute-start.3
  64.4 1.0 fusion.35
  65.4 5.8 %collective-permute-done.1.refs_1_.refs_3_ = bf16[4,12,24,128]{3,2,1,0:T(8,128)(2,1)S(1)} collective-permute-done((bf16[4,12,24,128]{3,2,1,0:T(8,128)(2,1)}, bf16[4,12,24,128]{3,2,1,0:T(8,128)(2,1)S(1)}, u32[]{:S(2)}, u32[]{:S(2)}) %collective-permute-start.1) | collective-permute-done | bytes 294944 | tf_op jit(solution)/shard_map/ppermute | solution.py:319
  72.0 3.7 %shard_map.199 = (bf16[4,12,24,128]{3,2,1,0:T(8,128)(2,1)}, bf16[4,12,24,128]{3,2,1,0:T(8,128)(2,1)}, bf16[4,12,24,128]{3,2,1,0:T(8,128)(2,1)}, bf16[4,12,24,128]{3,2,1,0:T(8,128)(2,1)}) custom-call(f32[12]{0:T(128)} %quad_ref.9, bf16[12,384,128]{2,1,0:T(8,128)(2,1)} %get-tuple-element.43.refs_0_, bf16[12,384,128]{2,1,0:T(8,128)(2,1)} %collective-permute-done.18.refs_1_, ...), custom_call_target="tpu_custom_call" | custom-call | flops 905969664 | bytes 4718592 | tf_op jit(solution)/shard_map/pallas_call | solution.py:110
  75.6 2.3 collective-permute-start.19
  78.0 1.2 collective-permute-start.21
  79.2 1.0 fusion.36
  80.3 10.7 %collective-permute-done.3.refs_3_ = bf16[4,12,24,128]{3,2,1,0:T(8,128)(2,1)S(1)} collective-permute-done((bf16[4,12,24,128]{3,2,1,0:T(8,128)(2,1)}, bf16[4,12,24,128]{3,2,1,0:T(8,128)(2,1)S(1)}, u32[]{:S(2)}, u32[]{:S(2)}) %collective-permute-start.3) | collective-permute-done | bytes 294944 | tf_op jit(solution)/shard_map/ppermute | solution.py:319
  91.0 15.6 %collective-permute-start.4 = (bf16[4,12,24,128]{3,2,1,0:T(8,128)(2,1)S(1)}, bf16[4,12,24,128]{3,2,1,0:T(8,128)(2,1)S(1)}, u32[]{:S(2)}, u32[]{:S(2)}) collective-permute-start(bf16[4,12,24,128]{3,2,1,0:T(8,128)(2,1)S(1)} %pad_maximum_fusion.2), channel_id=1, source_target_pairs={{0,2},{2,0},{4,6},{6,4},{8,10},{10,8},{12,14},{14,12},{16,18},{18,... | collective-permute-start | bytes 884744 | tf_op jit(solution)/shard_map/ppermute | solution.py:319
  106.6 1.3 collective-permute-start.5
  108.6 5.6 %collective-permute-done.21.refs_3_ = bf16[4,12,24,128]{3,2,1,0:T(8,128)(2,1)S(1)} collective-permute-done((bf16[4,12,24,128]{3,2,1,0:T(8,128)(2,1)}, bf16[4,12,24,128]{3,2,1,0:T(8,128)(2,1)S(1)}, u32[]{:S(2)}, u32[]{:S(2)}) %collective-permute-start.21) | collective-permute-done | bytes 294944 | tf_op jit(solution)/shard_map/ppermute | solution.py:319
  114.3 2.7 collective-permute-start.22
  117.1 1.3 collective-permute-start.23
  118.4 3.8 %collective-permute-done.6.refs_6_ = bf16[4,12,24,128]{3,2,1,0:T(8,128)(2,1)S(1)} collective-permute-done((bf16[4,12,24,128]{3,2,1,0:T(8,128)(2,1)S(1)}, bf16[4,12,24,128]{3,2,1,0:T(8,128)(2,1)S(1)}, u32[]{:S(2)}, u32[]{:S(2)}) %collective-permute-start.6) | collective-permute-done | bytes 294944 | tf_op jit(solution)/shard_map/ppermute | solution.py:319
  122.9 4.3 %shard_map.195 = (bf16[4,12,24,128]{3,2,1,0:T(8,128)(2,1)}, bf16[4,12,24,128]{3,2,1,0:T(8,128)(2,1)}, bf16[4,12,24,128]{3,2,1,0:T(8,128)(2,1)}, bf16[4,12,24,128]{3,2,1,0:T(8,128)(2,1)}) custom-call(bf16[4,12,24,128]{3,2,1,0:T(8,128)(2,1)} %get-tuple-element.22.refs_0_, bf16[4,12,24,128]{3,2,1,0:T(8,128)(2,1)} %copy-done.8, ...), custom_call_target="tpu_custom_call" | custom-call | flops 452984832 | bytes 4128768 | tf_op jit(solution)/shard_map/pallas_call | solution.py:162
  127.3 1.1 collective-permute-start.24
  128.4 1.7 collective-permute-start.8
  130.1 1.0 fusion.31
  131.1 7.0 %collective-permute-done.7.refs_1_ = bf16[4,12,24,128]{3,2,1,0:T(8,128)(2,1)S(1)} collective-permute-done((bf16[4,12,24,128]{3,2,1,0:T(8,128)(2,1)}, bf16[4,12,24,128]{3,2,1,0:T(8,128)(2,1)S(1)}, u32[]{:S(2)}, u32[]{:S(2)}) %collective-permute-start.7) | collective-permute-done | bytes 294944 | tf_op jit(solution)/shard_map/ppermute | solution.py:319
  138.1 1.2 collective-permute-start.9
  139.3 3.5 %collective-permute-done.8.refs_2_ = bf16[4,12,24,128]{3,2,1,0:T(8,128)(2,1)S(1)} collective-permute-done((bf16[4,12,24,128]{3,2,1,0:T(8,128)(2,1)}, bf16[4,12,24,128]{3,2,1,0:T(8,128)(2,1)S(1)}, u32[]{:S(2)}, u32[]{:S(2)}) %collective-permute-start.8) | collective-permute-done | bytes 294944 | tf_op jit(solution)/shard_map/ppermute | solution.py:319
  142.9 14.4 %collective-permute-done.9.refs_3_ = bf16[4,12,24,128]{3,2,1,0:T(8,128)(2,1)S(1)} collective-permute-done((bf16[4,12,24,128]{3,2,1,0:T(8,128)(2,1)}, bf16[4,12,24,128]{3,2,1,0:T(8,128)(2,1)S(1)}, u32[]{:S(2)}, u32[]{:S(2)}) %collective-permute-start.9) | collective-permute-done | bytes 294944 | tf_op jit(solution)/shard_map/ppermute | solution.py:319
  157.4 1.2 collective-permute-start.10
  159.8 4.3 %shard_map.200 = (bf16[4,12,24,128]{3,2,1,0:T(8,128)(2,1)}, bf16[4,12,24,128]{3,2,1,0:T(8,128)(2,1)}, bf16[4,12,24,128]{3,2,1,0:T(8,128)(2,1)}, bf16[4,12,24,128]{3,2,1,0:T(8,128)(2,1)}) custom-call(bf16[4,12,24,128]{3,2,1,0:T(8,128)(2,1)} %get-tuple-element.32.refs_0_, bf16[4,12,24,128]{3,2,1,0:T(8,128)(2,1)} %copy-done.5, ...), custom_call_target="tpu_custom_call" | custom-call | flops 452984832 | bytes 4128768 | tf_op jit(solution)/shard_map/pallas_call | solution.py:162
  164.2 1.5 collective-permute-start.26
  165.7 1.0 fusion.23
  166.7 2.0 collective-permute-start.12
  168.8 7.4 %collective-permute-done.25.refs_1_ = bf16[4,12,24,128]{3,2,1,0:T(8,128)(2,1)S(1)} collective-permute-done((bf16[4,12,24,128]{3,2,1,0:T(8,128)(2,1)}, bf16[4,12,24,128]{3,2,1,0:T(8,128)(2,1)S(1)}, u32[]{:S(2)}, u32[]{:S(2)}) %collective-permute-start.25) | collective-permute-done | bytes 294944 | tf_op jit(solution)/shard_map/ppermute | solution.py:319
  176.2 1.2 collective-permute-start.27
  177.4 1.7 collective-permute-done.26.refs_2_
  179.1 13.5 %collective-permute-done.27.refs_3_ = bf16[4,12,24,128]{3,2,1,0:T(8,128)(2,1)S(1)} collective-permute-done((bf16[4,12,24,128]{3,2,1,0:T(8,128)(2,1)}, bf16[4,12,24,128]{3,2,1,0:T(8,128)(2,1)S(1)}, u32[]{:S(2)}, u32[]{:S(2)}) %collective-permute-start.27) | collective-permute-done | bytes 294944 | tf_op jit(solution)/shard_map/ppermute | solution.py:319
  192.7 1.5 collective-permute-start.28
  194.2 1.3 collective-permute-start.29
  196.1 0.9 pad_maximum_fusion.refs_7_
  198.4 3.9 %shard_map.196 = (bf16[12,392,128]{2,1,0:T(8,128)(2,1)}, bf16[12,392,128]{2,1,0:T(8,128)(2,1)}) custom-call(bf16[4,12,24,128]{3,2,1,0:T(8,128)(2,1)} %get-tuple-element.26.refs_0_.refs_11_, bf16[4,12,24,128]{3,2,1,0:T(8,128)(2,1)} %copy-done.22, bf16[4,12,24,128]{3,2,1,0:T(8,128)(2,1)} %copy-done.23, bf16[4,12,24,128]{3,2,1,0:T(8,128)(2,1)} %copy-done.24, ...), custom_call_target="tpu_custom_call" | custom-call | flops 924844032 | bytes 4816896 | tf_op jit(solution)/shard_map/pallas_call | solution.py:210
  202.9 6.7 %collective-permute-done.30.refs_6_ = bf16[4,12,24,128]{3,2,1,0:T(8,128)(2,1)S(1)} collective-permute-done((bf16[4,12,24,128]{3,2,1,0:T(8,128)(2,1)S(1)}, bf16[4,12,24,128]{3,2,1,0:T(8,128)(2,1)S(1)}, u32[]{:S(2)}, u32[]{:S(2)}) %collective-permute-start.30) | collective-permute-done | bytes 294944 | tf_op jit(solution)/shard_map/ppermute | solution.py:319
  210.4 3.9 %shard_map.201 = (bf16[12,392,128]{2,1,0:T(8,128)(2,1)}, bf16[12,392,128]{2,1,0:T(8,128)(2,1)}) custom-call(bf16[4,12,24,128]{3,2,1,0:T(8,128)(2,1)} %get-tuple-element.36.refs_0_, bf16[4,12,24,128]{3,2,1,0:T(8,128)(2,1)} %copy-done.25, bf16[4,12,24,128]{3,2,1,0:T(8,128)(2,1)} %copy-done.26, bf16[4,12,24,128]{3,2,1,0:T(8,128)(2,1)} %copy-done.27, ...), custom_call_target="tpu_custom_call" | custom-call | flops 924844032 | bytes 4816896 | tf_op jit(solution)/shard_map/pallas_call | solution.py:210
  214.6 1.1 fusion.22
  215.6 2.2 collective-permute-start.14
  217.8 3.4 %collective-permute-start.13 = (bf16[2,392,128]{2,1,0:T(8,128)(2,1)S(1)}, bf16[2,392,128]{2,1,0:T(8,128)(2,1)S(1)}, u32[]{:S(2)}, u32[]{:S(2)}) collective-permute-start(bf16[2,392,128]{2,1,0:T(8,128)(2,1)S(1)} %get-tuple-element.53), channel_id=1, source_target_pairs={{0,2},{2,4},{4,6},{6,8},{8,10},{10,12},{12,14},{14,16},{16,18},{18... | collective-permute-start | bytes 602120 | tf_op jit(solution)/shard_map/ppermute | solution.py:410
  221.2 1.7 fusion.20
  222.9 1.9 collective-permute-start.32
  224.8 5.6 %collective-permute-done.15.wave_ref = bf16[12,392,128]{2,1,0:T(8,128)(2,1)S(1)} collective-permute-done((bf16[12,392,128]{2,1,0:T(8,128)(2,1)}, bf16[12,392,128]{2,1,0:T(8,128)(2,1)S(1)}, u32[]{:S(2)}, u32[]{:S(2)}) %collective-permute-start.15) | collective-permute-done | bytes 1204256 | tf_op jit(solution)/shard_map/ppermute | solution.py:319
  230.4 4.7 %collective-permute-start.31 = (bf16[2,392,128]{2,1,0:T(8,128)(2,1)}, bf16[2,392,128]{2,1,0:T(8,128)(2,1)S(1)}, u32[]{:S(2)}, u32[]{:S(2)}) collective-permute-start(bf16[2,392,128]{2,1,0:T(8,128)(2,1)} %get-tuple-element.49), channel_id=1, source_target_pairs={{0,2},{2,4},{4,6},{6,8},{8,10},{10,12},{12,14},{14,16},{16,18},{18... | collective-permute-start | bytes 602120 | tf_op jit(solution)/shard_map/ppermute | solution.py:410
  235.9 2.1 collective-permute-start.17
  238.0 18.2 %collective-permute-done.33.wave_ref = bf16[12,392,128]{2,1,0:T(8,128)(2,1)S(1)} collective-permute-done((bf16[12,392,128]{2,1,0:T(8,128)(2,1)}, bf16[12,392,128]{2,1,0:T(8,128)(2,1)S(1)}, u32[]{:S(2)}, u32[]{:S(2)}) %collective-permute-start.33) | collective-permute-done | bytes 1204256 | tf_op jit(solution)/shard_map/ppermute | solution.py:319
  256.2 4.0 %collective-permute-start.16 = (bf16[2,392,128]{2,1,0:T(8,128)(2,1)}, bf16[2,392,128]{2,1,0:T(8,128)(2,1)}, u32[]{:S(2)}, u32[]{:S(2)}) collective-permute-start(bf16[2,392,128]{2,1,0:T(8,128)(2,1)} %get-tuple-element.51), channel_id=1, source_target_pairs={{0,2},{2,4},{4,6},{6,8},{8,10},{10,12},{12,14},{14,16},{16,18},{18... | collective-permute-start | bytes 602120 | tf_op jit(solution)/shard_map/ppermute | solution.py:410
  261.1 1.9 collective-permute-start.35
  263.0 3.6 %collective-permute-start.34 = (bf16[2,392,128]{2,1,0:T(8,128)(2,1)}, bf16[2,392,128]{2,1,0:T(8,128)(2,1)}, u32[]{:S(2)}, u32[]{:S(2)}) collective-permute-start(bf16[2,392,128]{2,1,0:T(8,128)(2,1)} %get-tuple-element.47), channel_id=1, source_target_pairs={{0,2},{2,4},{4,6},{6,8},{8,10},{10,12},{12,14},{14,16},{16,18},{18... | collective-permute-start | bytes 602120 | tf_op jit(solution)/shard_map/ppermute | solution.py:410
  267.3 6.0 %shard_map.197.refs_0_ = bf16[12,384,128]{2,1,0:T(8,128)(2,1)} custom-call(s32[1]{0:T(128)} %bitcast.place_ref, s32[12,12]{1,0:T(8,128)} %neighbour_ref.7, s32[12,12]{1,0:T(8,128)} %basis_ref.7, f32[12,12]{1,0:T(8,128)} %quad_ref.11, bf16[12,392,128]{2,1,0:T(8,128)(2,1)} %get-tuple-element.30.wave_ref, bf16[2,392,128]{2,1,0:T(8,128)(2,1)} %copy-done.18, ...), custom_call_target="tpu_custom_call" | custom-call | flops 113246208 | bytes 2359296 | tf_op jit(solution)/shard_map/pallas_call | solution.py:261
  274.0 6.0 %shard_map.202.refs_2_ = bf16[12,384,128]{2,1,0:T(8,128)(2,1)} custom-call(s32[1]{0:T(128)} %bitcast.2.place_ref, s32[12,12]{1,0:T(8,128)} %neighbour_ref.7, s32[12,12]{1,0:T(8,128)} %basis_ref.7, f32[12,12]{1,0:T(8,128)} %quad_ref.11, bf16[12,392,128]{2,1,0:T(8,128)(2,1)} %get-tuple-element.40.wave_ref, bf16[2,392,128]{2,1,0:T(8,128)(2,1)} %copy-done.21, ...), custom_call_target="tpu_custom_call" | custom-call | flops 113246208 | bytes 2359296 | tf_op jit(solution)/shard_map/pallas_call | solution.py:261
  280.7 6.0 %shard_map.198.refs_1_ = bf16[12,384,128]{2,1,0:T(8,128)(2,1)} custom-call(s32[1]{0:T(128)} %bitcast.1.place_ref, s32[12,12]{1,0:T(8,128)} %neighbour_ref.7, s32[12,12]{1,0:T(8,128)} %basis_ref.7, f32[12,12]{1,0:T(8,128)} %quad_ref.11, bf16[12,392,128]{2,1,0:T(8,128)(2,1)} %copy-done.2, bf16[2,392,128]{2,1,0:T(8,128)(2,1)} %collective-permute-done.16.low_ref, ...), custom_call_target="tpu_custom_call" | custom-call | flops 113246208 | bytes 2359296 | tf_op jit(solution)/shard_map/pallas_call | solution.py:261
  286.7 6.0 %shard_map.203.refs_3_ = bf16[12,384,128]{2,1,0:T(8,128)(2,1)} custom-call(s32[1]{0:T(128)} %bitcast.3.place_ref, s32[12,12]{1,0:T(8,128)} %neighbour_ref.7, s32[12,12]{1,0:T(8,128)} %basis_ref.7, f32[12,12]{1,0:T(8,128)} %quad_ref.11, bf16[12,392,128]{2,1,0:T(8,128)(2,1)} %copy-done.3, bf16[2,392,128]{2,1,0:T(8,128)(2,1)} %collective-permute-done.34.low_ref, ...), custom_call_target="tpu_custom_call" | custom-call | flops 113246208 | bytes 2359296 | tf_op jit(solution)/shard_map/pallas_call | solution.py:261
  292.7 17.8 %shard_map.204 = (bf16[12,384,512]{2,1,0:T(8,128)(2,1)}, bf16[12,384,512]{2,1,0:T(8,128)(2,1)}) custom-call(s32[4]{0:T(128)} %pad_add_fusion.place_ref, bf16[12,384,128]{2,1,0:T(8,128)(2,1)} %shard_map.197.refs_0_, bf16[12,384,128]{2,1,0:T(8,128)(2,1)} %shard_map.198.refs_1_, bf16[12,384,128]{2,1,0:T(8,128)(2,1)} %shard_map.202.refs_2_, ...), custom_call_target="tpu_custom_call" | custom-call | flops 9663676416 | bytes 18874368 | tf_op jit(solution)/shard_map/pallas_call | solution.py:300
  (145 shorter events, 13.4 us)
Async XLA Ops:
  0.6 6.2 %copy-start = (bf16[12,192,192]{2,1,0:T(8,128)(2,1)S(1)}, bf16[12,192,192]{2,1,0:T(8,128)(2,1)}, u32[]{:S(2)}) copy-start(bf16[12,192,192]{2,1,0:T(8,128)(2,1)} %param.21) | copy-start | bytes 2654212
  0.7 5.9 %copy-start.30 = (s32[16]{0:T(128)S(1)}, s32[16]{0:T(128)}, u32[]{:S(2)}) copy-start(s32[16]{0:T(128)} %constant.47.clone) | copy-start | bytes 196
  5.1 60.3 %collective-permute-start.18 = (bf16[12,384,128]{2,1,0:T(8,128)(2,1)S(1)}, bf16[12,384,128]{2,1,0:T(8,128)(2,1)}, u32[]{:S(2)}, u32[]{:S(2)}) collective-permute-start(bf16[12,384,128]{2,1,0:T(8,128)(2,1)S(1)} %get-tuple-element.42), channel_id=1, source_target_pairs={{0,1},{1,0},{2,3},{3,2},{4,5},{5,4},{6,7},{7,6},{8,9},{9,8},{10,11... | collective-permute-start | bytes 3538952 | tf_op jit(solution)/shard_map/ppermute | solution.py:319
  5.3 52.0 %collective-permute-start = (bf16[12,384,128]{2,1,0:T(8,128)(2,1)}, bf16[12,384,128]{2,1,0:T(8,128)(2,1)}, u32[]{:S(2)}, u32[]{:S(2)}) collective-permute-start(bf16[12,384,128]{2,1,0:T(8,128)(2,1)} %get-tuple-element.44), channel_id=1, source_target_pairs={{0,1},{1,0},{2,3},{3,2},{4,5},{5,4},{6,7},{7,6},{8,9},{9,8},{10,11... | collective-permute-start | bytes 3538952 | tf_op jit(solution)/shard_map/ppermute | solution.py:319
  7.4 1.7 copy-start.1
  9.0 3.7 %copy-start.37 = (bf16[2,392,384]{2,1,0:T(8,128)(2,1)S(1)}, bf16[2,392,384]{2,1,0:T(8,128)(2,1)}, u32[]{:S(2)}) copy-start(bf16[2,392,384]{2,1,0:T(8,128)(2,1)} %constant.49.clone) | copy-start | bytes 1806340
  57.3 5.0 %copy-start.28 = (f32[192,512]{1,0:T(8,128)S(1)}, f32[192,512]{1,0:T(8,128)}, u32[]{:S(2)}) copy-start(f32[192,512]{1,0:T(8,128)} %param.23) | copy-start | bytes 1179652
  57.3 5.0 %copy-start.29 = (f32[192,512]{1,0:T(8,128)S(1)}, f32[192,512]{1,0:T(8,128)}, u32[]{:S(2)}) copy-start(f32[192,512]{1,0:T(8,128)} %param.22) | copy-start | bytes 1179652
  60.9 10.3 %collective-permute-start.1 = (bf16[4,12,24,128]{3,2,1,0:T(8,128)(2,1)}, bf16[4,12,24,128]{3,2,1,0:T(8,128)(2,1)S(1)}, u32[]{:S(2)}, u32[]{:S(2)}) collective-permute-start(bf16[4,12,24,128]{3,2,1,0:T(8,128)(2,1)} %get-tuple-element.23), channel_id=1, source_target_pairs={{0,8},{2,10},{4,12},{6,14},{8,0},{10,2},{12,4},{14,6},{16,24},{18,... | collective-permute-start | bytes 884744 | tf_op jit(solution)/shard_map/ppermute | solution.py:319
  63.1 17.1 %collective-permute-start.2 = (bf16[4,12,24,128]{3,2,1,0:T(8,128)(2,1)}, bf16[4,12,24,128]{3,2,1,0:T(8,128)(2,1)S(1)}, u32[]{:S(2)}, u32[]{:S(2)}) collective-permute-start(bf16[4,12,24,128]{3,2,1,0:T(8,128)(2,1)} %get-tuple-element.24), channel_id=1, source_target_pairs={{0,16},{2,18},{4,20},{6,22},{8,24},{10,26},{12,28},{14,30},{16,0},... | collective-permute-start | bytes 884744 | tf_op jit(solution)/shard_map/ppermute | solution.py:319
  63.1 27.8 %collective-permute-start.3 = (bf16[4,12,24,128]{3,2,1,0:T(8,128)(2,1)}, bf16[4,12,24,128]{3,2,1,0:T(8,128)(2,1)S(1)}, u32[]{:S(2)}, u32[]{:S(2)}) collective-permute-start(bf16[4,12,24,128]{3,2,1,0:T(8,128)(2,1)} %get-tuple-element.25), channel_id=1, source_target_pairs={{0,24},{2,26},{4,28},{6,30},{8,16},{10,18},{12,20},{14,22},{16,8},... | collective-permute-start | bytes 884744 | tf_op jit(solution)/shard_map/ppermute | solution.py:319
  75.6 32.4 %collective-permute-start.19 = (bf16[4,12,24,128]{3,2,1,0:T(8,128)(2,1)}, bf16[4,12,24,128]{3,2,1,0:T(8,128)(2,1)S(1)}, u32[]{:S(2)}, u32[]{:S(2)}) collective-permute-start(bf16[4,12,24,128]{3,2,1,0:T(8,128)(2,1)} %get-tuple-element.33), channel_id=1, source_target_pairs={{0,8},{2,10},{4,12},{6,14},{8,0},{10,2},{12,4},{14,6},{16,24},{18,... | collective-permute-start | bytes 884744 | tf_op jit(solution)/shard_map/ppermute | solution.py:319
  78.0 30.6 %collective-permute-start.20 = (bf16[4,12,24,128]{3,2,1,0:T(8,128)(2,1)}, bf16[4,12,24,128]{3,2,1,0:T(8,128)(2,1)S(1)}, u32[]{:S(2)}, u32[]{:S(2)}) collective-permute-start(bf16[4,12,24,128]{3,2,1,0:T(8,128)(2,1)} %get-tuple-element.34), channel_id=1, source_target_pairs={{0,16},{2,18},{4,20},{6,22},{8,24},{10,26},{12,28},{14,30},{16,0},... | collective-permute-start | bytes 884744 | tf_op jit(solution)/shard_map/ppermute | solution.py:319
  78.0 30.0 %copy-start.4 = (bf16[4,12,24,128]{3,2,1,0:T(8,128)(2,1)S(1)}, bf16[4,12,24,128]{3,2,1,0:T(8,128)(2,1)}, u32[]{:S(2)}) copy-start(bf16[4,12,24,128]{3,2,1,0:T(8,128)(2,1)} %get-tuple-element.32.refs_0_) | copy-start | bytes 884740
  78.0 36.3 %collective-permute-start.21 = (bf16[4,12,24,128]{3,2,1,0:T(8,128)(2,1)}, bf16[4,12,24,128]{3,2,1,0:T(8,128)(2,1)S(1)}, u32[]{:S(2)}, u32[]{:S(2)}) collective-permute-start(bf16[4,12,24,128]{3,2,1,0:T(8,128)(2,1)} %get-tuple-element.35), channel_id=1, source_target_pairs={{0,24},{2,26},{4,28},{6,30},{8,16},{10,18},{12,20},{14,22},{16,8},... | collective-permute-start | bytes 884744 | tf_op jit(solution)/shard_map/ppermute | solution.py:319
  80.2 27.8 %copy-start.9 = (bf16[4,12,24,128]{3,2,1,0:T(8,128)(2,1)}, bf16[4,12,24,128]{3,2,1,0:T(8,128)(2,1)S(1)}, u32[]{:S(2)}) copy-start(bf16[4,12,24,128]{3,2,1,0:T(8,128)(2,1)S(1)} %collective-permute-done.2.refs_2_) | copy-start | bytes 884740
  90.9 17.1 %copy-start.10 = (bf16[4,12,24,128]{3,2,1,0:T(8,128)(2,1)}, bf16[4,12,24,128]{3,2,1,0:T(8,128)(2,1)S(1)}, u32[]{:S(2)}) copy-start(bf16[4,12,24,128]{3,2,1,0:T(8,128)(2,1)S(1)} %collective-permute-done.3.refs_3_) | copy-start | bytes 884740
  91.0 27.4 %collective-permute-start.4 = (bf16[4,12,24,128]{3,2,1,0:T(8,128)(2,1)S(1)}, bf16[4,12,24,128]{3,2,1,0:T(8,128)(2,1)S(1)}, u32[]{:S(2)}, u32[]{:S(2)}) collective-permute-start(bf16[4,12,24,128]{3,2,1,0:T(8,128)(2,1)S(1)} %pad_maximum_fusion.2), channel_id=1, source_target_pairs={{0,2},{2,0},{4,6},{6,4},{8,10},{10,8},{12,14},{14,12},{16,18},{18,... | collective-permute-start | bytes 884744 | tf_op jit(solution)/shard_map/ppermute | solution.py:319
  106.6 11.7 %collective-permute-start.5 = (bf16[4,12,24,128]{3,2,1,0:T(8,128)(2,1)S(1)}, bf16[4,12,24,128]{3,2,1,0:T(8,128)(2,1)S(1)}, u32[]{:S(2)}, u32[]{:S(2)}) collective-permute-start(bf16[4,12,24,128]{3,2,1,0:T(8,128)(2,1)S(1)} %pad_maximum_fusion.3), channel_id=1, source_target_pairs={{0,4},{2,6},{4,0},{6,2},{8,12},{10,14},{12,8},{14,10},{16,20},{18,... | collective-permute-start | bytes 884744 | tf_op jit(solution)/shard_map/ppermute | solution.py:319
  108.0 9.0 %copy-start.5 = (bf16[4,12,24,128]{3,2,1,0:T(8,128)(2,1)}, bf16[4,12,24,128]{3,2,1,0:T(8,128)(2,1)S(1)}, u32[]{:S(2)}) copy-start(bf16[4,12,24,128]{3,2,1,0:T(8,128)(2,1)S(1)} %collective-permute-done.19.refs_1_) | copy-start | bytes 884740
  108.1 14.1 %collective-permute-start.6 = (bf16[4,12,24,128]{3,2,1,0:T(8,128)(2,1)S(1)}, bf16[4,12,24,128]{3,2,1,0:T(8,128)(2,1)S(1)}, u32[]{:S(2)}, u32[]{:S(2)}) collective-permute-start(bf16[4,12,24,128]{3,2,1,0:T(8,128)(2,1)S(1)} %pad_maximum_fusion.4), channel_id=1, source_target_pairs={{0,6},{2,4},{4,2},{6,0},{8,14},{10,12},{12,10},{14,8},{16,22},{18,... | collective-permute-start | bytes 884744 | tf_op jit(solution)/shard_map/ppermute | solution.py:319
  108.6 18.6 %copy-start.6 = (bf16[4,12,24,128]{3,2,1,0:T(8,128)(2,1)}, bf16[4,12,24,128]{3,2,1,0:T(8,128)(2,1)S(1)}, u32[]{:S(2)}) copy-start(bf16[4,12,24,128]{3,2,1,0:T(8,128)(2,1)S(1)} %collective-permute-done.20.refs_2_) | copy-start | bytes 884740
  114.2 12.9 %copy-start.7 = (bf16[4,12,24,128]{3,2,1,0:T(8,128)(2,1)}, bf16[4,12,24,128]{3,2,1,0:T(8,128)(2,1)S(1)}, u32[]{:S(2)}) copy-start(bf16[4,12,24,128]{3,2,1,0:T(8,128)(2,1)S(1)} %collective-permute-done.21.refs_3_) | copy-start | bytes 884740
  114.3 44.6 %collective-permute-start.22 = (bf16[4,12,24,128]{3,2,1,0:T(8,128)(2,1)S(1)}, bf16[4,12,24,128]{3,2,1,0:T(8,128)(2,1)S(1)}, u32[]{:S(2)}, u32[]{:S(2)}) collective-permute-start(bf16[4,12,24,128]{3,2,1,0:T(8,128)(2,1)S(1)} %pad_maximum_fusion.8), channel_id=1, source_target_pairs={{0,2},{2,0},{4,6},{6,4},{8,10},{10,8},{12,14},{14,12},{16,18},{18,... | collective-permute-start | bytes 884744 | tf_op jit(solution)/shard_map/ppermute | solution.py:319
  117.1 41.9 %collective-permute-start.23 = (bf16[4,12,24,128]{3,2,1,0:T(8,128)(2,1)S(1)}, bf16[4,12,24,128]{3,2,1,0:T(8,128)(2,1)S(1)}, u32[]{:S(2)}, u32[]{:S(2)}) collective-permute-start(bf16[4,12,24,128]{3,2,1,0:T(8,128)(2,1)S(1)} %pad_maximum_fusion.9), channel_id=1, source_target_pairs={{0,4},{2,6},{4,0},{6,2},{8,12},{10,14},{12,8},{14,10},{16,20},{18,... | collective-permute-start | bytes 884744 | tf_op jit(solution)/shard_map/ppermute | solution.py:319
  118.4 3.8 %copy-start.13 = (bf16[4,12,24,128]{3,2,1,0:T(8,128)(2,1)}, bf16[4,12,24,128]{3,2,1,0:T(8,128)(2,1)S(1)}, u32[]{:S(2)}) copy-start(bf16[4,12,24,128]{3,2,1,0:T(8,128)(2,1)S(1)} %collective-permute-done.4.refs_4_) | copy-start | bytes 884740
  118.4 3.8 %copy-start.14 = (bf16[4,12,24,128]{3,2,1,0:T(8,128)(2,1)}, bf16[4,12,24,128]{3,2,1,0:T(8,128)(2,1)S(1)}, u32[]{:S(2)}) copy-start(bf16[4,12,24,128]{3,2,1,0:T(8,128)(2,1)S(1)} %collective-permute-done.5.refs_5_) | copy-start | bytes 884740
  127.2 11.0 %collective-permute-start.7 = (bf16[4,12,24,128]{3,2,1,0:T(8,128)(2,1)}, bf16[4,12,24,128]{3,2,1,0:T(8,128)(2,1)S(1)}, u32[]{:S(2)}, u32[]{:S(2)}) collective-permute-start(bf16[4,12,24,128]{3,2,1,0:T(8,128)(2,1)} %get-tuple-element.27), channel_id=1, source_target_pairs={{0,8},{2,10},{4,12},{6,14},{8,0},{10,2},{12,4},{14,6},{16,24},{18,... | collective-permute-start | bytes 884744 | tf_op jit(solution)/shard_map/ppermute | solution.py:319
  127.3 31.7 %collective-permute-start.24 = (bf16[4,12,24,128]{3,2,1,0:T(8,128)(2,1)S(1)}, bf16[4,12,24,128]{3,2,1,0:T(8,128)(2,1)S(1)}, u32[]{:S(2)}, u32[]{:S(2)}) collective-permute-start(bf16[4,12,24,128]{3,2,1,0:T(8,128)(2,1)S(1)} %pad_maximum_fusion.10), channel_id=1, source_target_pairs={{0,6},{2,4},{4,2},{6,0},{8,14},{10,12},{12,10},{14,8},{16,22},{18,... | collective-permute-start | bytes 884744 | tf_op jit(solution)/shard_map/ppermute | solution.py:319
  128.4 14.5 %collective-permute-start.8 = (bf16[4,12,24,128]{3,2,1,0:T(8,128)(2,1)}, bf16[4,12,24,128]{3,2,1,0:T(8,128)(2,1)S(1)}, u32[]{:S(2)}, u32[]{:S(2)}) collective-permute-start(bf16[4,12,24,128]{3,2,1,0:T(8,128)(2,1)} %get-tuple-element.28), channel_id=1, source_target_pairs={{0,16},{2,18},{4,20},{6,22},{8,24},{10,26},{12,28},{14,30},{16,0},... | collective-permute-start | bytes 884744 | tf_op jit(solution)/shard_map/ppermute | solution.py:319
  138.1 20.5 %copy-start.22 = (bf16[4,12,24,128]{3,2,1,0:T(8,128)(2,1)}, bf16[4,12,24,128]{3,2,1,0:T(8,128)(2,1)S(1)}, u32[]{:S(2)}) copy-start(bf16[4,12,24,128]{3,2,1,0:T(8,128)(2,1)S(1)} %collective-permute-done.7.refs_1_) | copy-start | bytes 884740
  138.1 19.1 %collective-permute-start.9 = (bf16[4,12,24,128]{3,2,1,0:T(8,128)(2,1)}, bf16[4,12,24,128]{3,2,1,0:T(8,128)(2,1)S(1)}, u32[]{:S(2)}, u32[]{:S(2)}) collective-permute-start(bf16[4,12,24,128]{3,2,1,0:T(8,128)(2,1)} %get-tuple-element.29), channel_id=1, source_target_pairs={{0,24},{2,26},{4,28},{6,30},{8,16},{10,18},{12,20},{14,22},{16,8},... | collective-permute-start | bytes 884744 | tf_op jit(solution)/shard_map/ppermute | solution.py:319
  142.8 21.3 %copy-start.23 = (bf16[4,12,24,128]{3,2,1,0:T(8,128)(2,1)}, bf16[4,12,24,128]{3,2,1,0:T(8,128)(2,1)S(1)}, u32[]{:S(2)}) copy-start(bf16[4,12,24,128]{3,2,1,0:T(8,128)(2,1)S(1)} %collective-permute-done.8.refs_2_) | copy-start | bytes 884740
  157.3 6.9 %copy-start.24 = (bf16[4,12,24,128]{3,2,1,0:T(8,128)(2,1)}, bf16[4,12,24,128]{3,2,1,0:T(8,128)(2,1)S(1)}, u32[]{:S(2)}) copy-start(bf16[4,12,24,128]{3,2,1,0:T(8,128)(2,1)S(1)} %collective-permute-done.9.refs_3_) | copy-start | bytes 884740
  157.4 38.2 %collective-permute-start.10 = (bf16[4,12,24,128]{3,2,1,0:T(8,128)(2,1)S(1)}, bf16[4,12,24,128]{3,2,1,0:T(8,128)(2,1)S(1)}, u32[]{:S(2)}, u32[]{:S(2)}) collective-permute-start(bf16[4,12,24,128]{3,2,1,0:T(8,128)(2,1)S(1)} %pad_maximum_fusion.5), channel_id=1, source_target_pairs={{0,2},{2,0},{4,6},{6,4},{8,10},{10,8},{12,14},{14,12},{16,18},{18,... | collective-permute-start | bytes 884744 | tf_op jit(solution)/shard_map/ppermute | solution.py:319
  158.7 38.3 %collective-permute-start.11 = (bf16[4,12,24,128]{3,2,1,0:T(8,128)(2,1)S(1)}, bf16[4,12,24,128]{3,2,1,0:T(8,128)(2,1)S(1)}, u32[]{:S(2)}, u32[]{:S(2)}) collective-permute-start(bf16[4,12,24,128]{3,2,1,0:T(8,128)(2,1)S(1)} %pad_maximum_fusion.6), channel_id=1, source_target_pairs={{0,4},{2,6},{4,0},{6,2},{8,12},{10,14},{12,8},{14,10},{16,20},{18,... | collective-permute-start | bytes 884744 | tf_op jit(solution)/shard_map/ppermute | solution.py:319
  164.2 12.0 %collective-permute-start.25 = (bf16[4,12,24,128]{3,2,1,0:T(8,128)(2,1)}, bf16[4,12,24,128]{3,2,1,0:T(8,128)(2,1)S(1)}, u32[]{:S(2)}, u32[]{:S(2)}) collective-permute-start(bf16[4,12,24,128]{3,2,1,0:T(8,128)(2,1)} %get-tuple-element.37), channel_id=1, source_target_pairs={{0,8},{2,10},{4,12},{6,14},{8,0},{10,2},{12,4},{14,6},{16,24},{18,... | collective-permute-start | bytes 884744 | tf_op jit(solution)/shard_map/ppermute | solution.py:319
  164.2 14.9 %collective-permute-start.26 = (bf16[4,12,24,128]{3,2,1,0:T(8,128)(2,1)}, bf16[4,12,24,128]{3,2,1,0:T(8,128)(2,1)S(1)}, u32[]{:S(2)}, u32[]{:S(2)}) collective-permute-start(bf16[4,12,24,128]{3,2,1,0:T(8,128)(2,1)} %get-tuple-element.38), channel_id=1, source_target_pairs={{0,16},{2,18},{4,20},{6,22},{8,24},{10,26},{12,28},{14,30},{16,0},... | collective-permute-start | bytes 884744 | tf_op jit(solution)/shard_map/ppermute | solution.py:319
  166.7 30.3 %collective-permute-start.12 = (bf16[4,12,24,128]{3,2,1,0:T(8,128)(2,1)S(1)}, bf16[4,12,24,128]{3,2,1,0:T(8,128)(2,1)S(1)}, u32[]{:S(2)}, u32[]{:S(2)}) collective-permute-start(bf16[4,12,24,128]{3,2,1,0:T(8,128)(2,1)S(1)} %pad_maximum_fusion.7), channel_id=1, source_target_pairs={{0,6},{2,4},{4,2},{6,0},{8,14},{10,12},{12,10},{14,8},{16,22},{18,... | collective-permute-start | bytes 884744 | tf_op jit(solution)/shard_map/ppermute | solution.py:319
  176.2 18.1 %copy-start.25 = (bf16[4,12,24,128]{3,2,1,0:T(8,128)(2,1)}, bf16[4,12,24,128]{3,2,1,0:T(8,128)(2,1)S(1)}, u32[]{:S(2)}) copy-start(bf16[4,12,24,128]{3,2,1,0:T(8,128)(2,1)S(1)} %collective-permute-done.25.refs_1_) | copy-start | bytes 884740
  176.2 16.5 %collective-permute-start.27 = (bf16[4,12,24,128]{3,2,1,0:T(8,128)(2,1)}, bf16[4,12,24,128]{3,2,1,0:T(8,128)(2,1)S(1)}, u32[]{:S(2)}, u32[]{:S(2)}) collective-permute-start(bf16[4,12,24,128]{3,2,1,0:T(8,128)(2,1)} %get-tuple-element.39), channel_id=1, source_target_pairs={{0,24},{2,26},{4,28},{6,30},{8,16},{10,18},{12,20},{14,22},{16,8},... | collective-permute-start | bytes 884744 | tf_op jit(solution)/shard_map/ppermute | solution.py:319
  179.1 16.5 %copy-start.26 = (bf16[4,12,24,128]{3,2,1,0:T(8,128)(2,1)}, bf16[4,12,24,128]{3,2,1,0:T(8,128)(2,1)S(1)}, u32[]{:S(2)}) copy-start(bf16[4,12,24,128]{3,2,1,0:T(8,128)(2,1)S(1)} %collective-permute-done.26.refs_2_) | copy-start | bytes 884740
  192.6 4.3 %copy-start.27 = (bf16[4,12,24,128]{3,2,1,0:T(8,128)(2,1)}, bf16[4,12,24,128]{3,2,1,0:T(8,128)(2,1)S(1)}, u32[]{:S(2)}) copy-start(bf16[4,12,24,128]{3,2,1,0:T(8,128)(2,1)S(1)} %collective-permute-done.27.refs_3_) | copy-start | bytes 884740
  192.7 9.8 %collective-permute-start.28 = (bf16[4,12,24,128]{3,2,1,0:T(8,128)(2,1)S(1)}, bf16[4,12,24,128]{3,2,1,0:T(8,128)(2,1)S(1)}, u32[]{:S(2)}, u32[]{:S(2)}) collective-permute-start(bf16[4,12,24,128]{3,2,1,0:T(8,128)(2,1)S(1)} %pad_maximum_fusion.11), channel_id=1, source_target_pairs={{0,2},{2,0},{4,6},{6,4},{8,10},{10,8},{12,14},{14,12},{16,18},{18,... | collective-permute-start | bytes 884744 | tf_op jit(solution)/shard_map/ppermute | solution.py:319
  194.2 8.7 %collective-permute-start.29 = (bf16[4,12,24,128]{3,2,1,0:T(8,128)(2,1)S(1)}, bf16[4,12,24,128]{3,2,1,0:T(8,128)(2,1)S(1)}, u32[]{:S(2)}, u32[]{:S(2)}) collective-permute-start(bf16[4,12,24,128]{3,2,1,0:T(8,128)(2,1)S(1)} %pad_maximum_fusion.12), channel_id=1, source_target_pairs={{0,4},{2,6},{4,0},{6,2},{8,12},{10,14},{12,8},{14,10},{16,20},{18,... | collective-permute-start | bytes 884744 | tf_op jit(solution)/shard_map/ppermute | solution.py:319
  195.6 1.4 copy-start.31
  195.6 14.0 %collective-permute-start.30 = (bf16[4,12,24,128]{3,2,1,0:T(8,128)(2,1)S(1)}, bf16[4,12,24,128]{3,2,1,0:T(8,128)(2,1)S(1)}, u32[]{:S(2)}, u32[]{:S(2)}) collective-permute-start(bf16[4,12,24,128]{3,2,1,0:T(8,128)(2,1)S(1)} %pad_maximum_fusion.13), channel_id=1, source_target_pairs={{0,6},{2,4},{4,2},{6,0},{8,14},{10,12},{12,10},{14,8},{16,22},{18,... | collective-permute-start | bytes 884744 | tf_op jit(solution)/shard_map/ppermute | solution.py:319
  202.3 28.1 %collective-permute-start.15 = (bf16[12,392,128]{2,1,0:T(8,128)(2,1)}, bf16[12,392,128]{2,1,0:T(8,128)(2,1)S(1)}, u32[]{:S(2)}, u32[]{:S(2)}) collective-permute-start(bf16[12,392,128]{2,1,0:T(8,128)(2,1)} %get-tuple-element.31), channel_id=1, source_target_pairs={{0,1},{1,0},{2,3},{3,2},{4,5},{5,4},{6,7},{7,6},{8,9},{9,8},{10,11... | collective-permute-start | bytes 3612680 | tf_op jit(solution)/shard_map/ppermute | solution.py:319
  202.6 7.1 %copy-start.34 = (bf16[4,12,24,128]{3,2,1,0:T(8,128)(2,1)}, bf16[4,12,24,128]{3,2,1,0:T(8,128)(2,1)S(1)}, u32[]{:S(2)}) copy-start(bf16[4,12,24,128]{3,2,1,0:T(8,128)(2,1)S(1)} %collective-permute-done.28.refs_4_) | copy-start | bytes 884740
  202.9 6.7 %copy-start.35 = (bf16[4,12,24,128]{3,2,1,0:T(8,128)(2,1)}, bf16[4,12,24,128]{3,2,1,0:T(8,128)(2,1)S(1)}, u32[]{:S(2)}) copy-start(bf16[4,12,24,128]{3,2,1,0:T(8,128)(2,1)S(1)} %collective-permute-done.29.refs_5_) | copy-start | bytes 884740
  214.3 41.9 %collective-permute-start.33 = (bf16[12,392,128]{2,1,0:T(8,128)(2,1)}, bf16[12,392,128]{2,1,0:T(8,128)(2,1)S(1)}, u32[]{:S(2)}, u32[]{:S(2)}) collective-permute-start(bf16[12,392,128]{2,1,0:T(8,128)(2,1)} %get-tuple-element.41), channel_id=1, source_target_pairs={{0,1},{1,0},{2,3},{3,2},{4,5},{5,4},{6,7},{7,6},{8,9},{9,8},{10,11... | collective-permute-start | bytes 3612680 | tf_op jit(solution)/shard_map/ppermute | solution.py:319
  215.6 20.3 %collective-permute-start.14 = (bf16[2,392,128]{2,1,0:T(8,128)(2,1)S(1)}, bf16[2,392,128]{2,1,0:T(8,128)(2,1)S(1)}, u32[]{:S(2)}, u32[]{:S(2)}) collective-permute-start(bf16[2,392,128]{2,1,0:T(8,128)(2,1)S(1)} %get-tuple-element.52), channel_id=1, source_target_pairs={{2,0},{4,2},{6,4},{8,6},{10,8},{12,10},{14,12},{16,14},{18,16},{20... | collective-permute-start | bytes 602120 | tf_op jit(solution)/shard_map/ppermute | solution.py:411
  217.8 43.3 %collective-permute-start.13 = (bf16[2,392,128]{2,1,0:T(8,128)(2,1)S(1)}, bf16[2,392,128]{2,1,0:T(8,128)(2,1)S(1)}, u32[]{:S(2)}, u32[]{:S(2)}) collective-permute-start(bf16[2,392,128]{2,1,0:T(8,128)(2,1)S(1)} %get-tuple-element.53), channel_id=1, source_target_pairs={{0,2},{2,4},{4,6},{6,8},{8,10},{10,12},{12,14},{14,16},{16,18},{18... | collective-permute-start | bytes 602120 | tf_op jit(solution)/shard_map/ppermute | solution.py:410
  222.9 40.1 %collective-permute-start.32 = (bf16[2,392,128]{2,1,0:T(8,128)(2,1)S(1)}, bf16[2,392,128]{2,1,0:T(8,128)(2,1)S(1)}, u32[]{:S(2)}, u32[]{:S(2)}) collective-permute-start(bf16[2,392,128]{2,1,0:T(8,128)(2,1)S(1)} %get-tuple-element.48), channel_id=1, source_target_pairs={{2,0},{4,2},{6,4},{8,6},{10,8},{12,10},{14,12},{16,14},{18,16},{20... | collective-permute-start | bytes 602120 | tf_op jit(solution)/shard_map/ppermute | solution.py:411
  230.4 42.9 %copy-start.2 = (bf16[12,392,128]{2,1,0:T(8,128)(2,1)}, bf16[12,392,128]{2,1,0:T(8,128)(2,1)S(1)}, u32[]{:S(2)}) copy-start(bf16[12,392,128]{2,1,0:T(8,128)(2,1)S(1)} %collective-permute-done.15.wave_ref) | copy-start | bytes 3612676
  230.4 42.9 %collective-permute-start.31 = (bf16[2,392,128]{2,1,0:T(8,128)(2,1)}, bf16[2,392,128]{2,1,0:T(8,128)(2,1)S(1)}, u32[]{:S(2)}, u32[]{:S(2)}) collective-permute-start(bf16[2,392,128]{2,1,0:T(8,128)(2,1)} %get-tuple-element.49), channel_id=1, source_target_pairs={{0,2},{2,4},{4,6},{6,8},{8,10},{10,12},{12,14},{14,16},{16,18},{18... | collective-permute-start | bytes 602120 | tf_op jit(solution)/shard_map/ppermute | solution.py:410
  235.9 31.4 %copy-start.17 = (bf16[2,392,128]{2,1,0:T(8,128)(2,1)}, bf16[2,392,128]{2,1,0:T(8,128)(2,1)S(1)}, u32[]{:S(2)}) copy-start(bf16[2,392,128]{2,1,0:T(8,128)(2,1)S(1)} %collective-permute-done.14.high_ref) | copy-start | bytes 602116
  235.9 44.1 %collective-permute-start.17 = (bf16[2,392,128]{2,1,0:T(8,128)(2,1)}, bf16[2,392,128]{2,1,0:T(8,128)(2,1)S(1)}, u32[]{:S(2)}, u32[]{:S(2)}) collective-permute-start(bf16[2,392,128]{2,1,0:T(8,128)(2,1)} %get-tuple-element.50), channel_id=1, source_target_pairs={{2,0},{4,2},{6,4},{8,6},{10,8},{12,10},{14,12},{16,14},{18,16},{20... | collective-permute-start | bytes 602120 | tf_op jit(solution)/shard_map/ppermute | solution.py:411
  256.2 4.1 %copy-start.3 = (bf16[12,392,128]{2,1,0:T(8,128)(2,1)}, bf16[12,392,128]{2,1,0:T(8,128)(2,1)S(1)}, u32[]{:S(2)}) copy-start(bf16[12,392,128]{2,1,0:T(8,128)(2,1)S(1)} %collective-permute-done.33.wave_ref) | copy-start | bytes 3612676
  256.2 23.8 %collective-permute-start.16 = (bf16[2,392,128]{2,1,0:T(8,128)(2,1)}, bf16[2,392,128]{2,1,0:T(8,128)(2,1)}, u32[]{:S(2)}, u32[]{:S(2)}) collective-permute-start(bf16[2,392,128]{2,1,0:T(8,128)(2,1)} %get-tuple-element.51), channel_id=1, source_target_pairs={{0,2},{2,4},{4,6},{6,8},{8,10},{10,12},{12,14},{14,16},{16,18},{18... | collective-permute-start | bytes 602120 | tf_op jit(solution)/shard_map/ppermute | solution.py:410
  261.1 6.2 %copy-start.18 = (bf16[2,392,128]{2,1,0:T(8,128)(2,1)}, bf16[2,392,128]{2,1,0:T(8,128)(2,1)S(1)}, u32[]{:S(2)}) copy-start(bf16[2,392,128]{2,1,0:T(8,128)(2,1)S(1)} %collective-permute-done.13.low_ref) | copy-start | bytes 602116
  261.1 25.6 %collective-permute-start.35 = (bf16[2,392,128]{2,1,0:T(8,128)(2,1)}, bf16[2,392,128]{2,1,0:T(8,128)(2,1)}, u32[]{:S(2)}, u32[]{:S(2)}) collective-permute-start(bf16[2,392,128]{2,1,0:T(8,128)(2,1)} %get-tuple-element.46), channel_id=1, source_target_pairs={{2,0},{4,2},{6,4},{8,6},{10,8},{12,10},{14,12},{16,14},{18,16},{20... | collective-permute-start | bytes 602120 | tf_op jit(solution)/shard_map/ppermute | solution.py:411
  263.0 10.3 %copy-start.19 = (bf16[2,392,128]{2,1,0:T(8,128)(2,1)}, bf16[2,392,128]{2,1,0:T(8,128)(2,1)S(1)}, u32[]{:S(2)}) copy-start(bf16[2,392,128]{2,1,0:T(8,128)(2,1)S(1)} %collective-permute-done.32.high_ref) | copy-start | bytes 602116
  263.0 23.7 %collective-permute-start.34 = (bf16[2,392,128]{2,1,0:T(8,128)(2,1)}, bf16[2,392,128]{2,1,0:T(8,128)(2,1)}, u32[]{:S(2)}, u32[]{:S(2)}) collective-permute-start(bf16[2,392,128]{2,1,0:T(8,128)(2,1)} %get-tuple-element.47), channel_id=1, source_target_pairs={{0,2},{2,4},{4,6},{6,8},{8,10},{10,12},{12,14},{14,16},{16,18},{18... | collective-permute-start | bytes 602120 | tf_op jit(solution)/shard_map/ppermute | solution.py:410
  (10 other events, 7.3 us)

commit v3 on v2

--- a/solution.py
+++ b/solution.py
@@ -83,7 +83,55 @@
     return jnp.concatenate(parts, axis=1) if len(parts) > 1 else parts[0]
 
 
-def dft_kernel(lon_count, nz, waits, quad_ref, *refs):
+def lane_blocks(cw):
+    return cw % LANES == 0
+
+
+def pick_kernel(index_ref, field_ref, *refs):
+    refs[-1][...] = field_ref[...]
+
+
+def pick(array, index, cw, waits):
+    if not lane_blocks(cw):
+        return lax.dynamic_slice_in_dim(array, index * cw, cw, array.ndim - 1)
+    rows, cols, _ = array.shape
+    step = step_rows(rows, 6)
+    return pl.pallas_call(
+        pick_kernel,
+        grid_spec=pltpu.PrefetchScalarGridSpec(
+            num_scalar_prefetch=1,
+            grid=(rows // step,),
+            in_specs=[pl.BlockSpec((step, cols, cw), lambda t, i: (t, 0, i[0]))]
+            + [any_spec()] * len(waits),
+            out_specs=pl.BlockSpec((step, cols, cw), lambda t, i: (t, 0, 0)),
+        ),
+        out_shape=jax.ShapeDtypeStruct((rows, cols, cw), array.dtype),
+        compiler_params=params(),
+        cost_estimate=cost(0, 4 * rows * cols * cw),
+    )(index[None], array, *waits)
+
+
+def rows_kernel(count, wave_ref, *refs):
+    first_ref, last_ref = refs[-2:]
+    rows = wave_ref.shape[0]
+    for r in range(HALO):
+        first_ref[r] = wave_ref[r]
+        last_ref[r] = wave_ref[rows - HALO + r]
+
+
+def edge_rows(wave, waits):
+    edge = jax.ShapeDtypeStruct((HALO,) + wave.shape[1:], wave.dtype)
+    return pl.pallas_call(
+        functools.partial(rows_kernel, len(waits)),
+        in_specs=[vmem_spec()] + [any_spec()] * len(waits),
+        out_specs=[vmem_spec()] * 2,
+        out_shape=[edge, edge],
+        compiler_params=pltpu.CompilerParams(vmem_limit_bytes=VMEM_LIMIT),
+        cost_estimate=cost(0, 8 * edge.size),
+    )(wave, *waits)
+
+
+def dft_kernel(lon_count, nz, waits, index_ref, quad_ref, *refs):
     blocks = refs[:lon_count]
     table_ref = refs[lon_count]
     outs = refs[lon_count + 1 + waits :]
@@ -103,22 +151,54 @@
                     outs[d][q, t] = scaled[at : at + wave_rows].astype(BF16)
 
 
-def dft(blocks, quad, table, nz, wave_rows, waits):
-    rows, cols, cw = blocks[0].shape
+def dft(field, index, received, quad, table, nz, wave_rows, cw, waits):
+    rows, cols, _ = field.shape
     step = step_rows(rows, 6)
-    lon_count = len(blocks)
+    lon_count = 1 + len(received)
+    own = pl.BlockSpec((step, cols, cw), lambda t, i: (t, 0, i[0]))
+    if not lane_blocks(cw):
+        field = pick(field, index, cw, [])
+        own = pl.BlockSpec((step, cols, cw), lambda t, i: (t, 0, 0))
     return pl.pallas_call(
         functools.partial(dft_kernel, lon_count, nz, len(waits)),
-        grid=(rows // step,),
-        in_specs=[smem_spec()]
-        + [pl.BlockSpec((step, cols, cw), lambda t: (t, 0, 0))] * lon_count
-        + [whole_of(table)]
-        + [any_spec()] * len(waits),
-        out_specs=[pl.BlockSpec((NQ, step, wave_rows, cw), lambda t: (0, t, 0, 0))] * nz,
+        grid_spec=pltpu.PrefetchScalarGridSpec(
+            num_scalar_prefetch=1,
+            grid=(rows // step,),
+            in_specs=[smem_spec(), own]
+            + [pl.BlockSpec((step, cols, cw), lambda t, i: (t, 0, 0))] * len(received)
+            + [pl.BlockSpec(table.shape, lambda t, i: (0, 0))]
+            + [any_spec()] * len(waits),
+            out_specs=[
+                pl.BlockSpec((NQ, step, wave_rows, cw), lambda t, i: (0, t, 0, 0))
+            ]
+            * nz,
+        ),
         out_shape=[jax.ShapeDtypeStruct((NQ, rows, wave_rows, cw), BF16)] * nz,
         compiler_params=params(),
         cost_estimate=cost(2 * table.size * rows * cw, 8 * rows * cols * cw),
-    )(quad, *blocks, table, *waits)
+    )(index[None], quad, field, *received, table, *waits)
+
+
+def regroup_kernel(count, outs, *refs):
+    sources = refs[:count]
+    for k, out_ref in enumerate(refs[-outs:]):
+        for i, ref in enumerate(sources):
+            out_ref[i] = ref[k + 1]
+
+
+def regroup(arrays, waits):
+    count = len(arrays)
+    outs = arrays[0].shape[0] - 1
+    shape = (count,) + arrays[0].shape[1:]
+    return pl.pallas_call(
+        functools.partial(regroup_kernel, count, outs),
+        grid=(1,),
+        in_specs=[whole_of(a) for a in arrays] + [any_spec()] * len(waits),
+        out_specs=[pl.BlockSpec(shape, lambda t: (0,) * len(shape))] * outs,
+        out_shape=[jax.ShapeDtypeStruct(shape, BF16)] * outs,
+        compiler_params=params(),
+        cost_estimate=cost(0, 4 * outs * math.prod(shape)),
+    )(*arrays, *waits)
 
 
 def legendre_kernel(nz, waits, *refs):
@@ -151,13 +231,13 @@
     for q in range(NQ):
         for d in range(nz):
             at = (q * nz + d) * span
-            outs[d][q] = result[at : at + span, :].reshape(rows, wave_rows, cw).astype(BF16)
+            outs[q][d] = result[at : at + span, :].reshape(rows, wave_rows, cw).astype(BF16)
 
 
 def legendre_step(own, others, leg, legt, gr, gi, waits):
     nz = len(own)
-    shape = own[0].shape
-    _, rows, wave_rows, cw = shape
+    _, rows, wave_rows, cw = own[0].shape
+    shape = (nz, rows, wave_rows, cw)
     waves, degrees, lat = leg.shape
     return pl.pallas_call(
         functools.partial(legendre_kernel, nz, len(waits)),
@@ -165,30 +245,28 @@
         in_specs=[first_of(a, 1) for a in own]
         + [whole_of(a) for a in (*others, leg, legt, gr, gi)]
         + [any_spec()] * len(waits),
-        out_specs=[pl.BlockSpec(shape, lambda t: (0, 0, 0, 0))] * nz,
-        out_shape=[jax.ShapeDtypeStruct(shape, BF16)] * nz,
+        out_specs=[pl.BlockSpec(shape, lambda t: (0, 0, 0, 0))] * NQ,
+        out_shape=[jax.ShapeDtypeStruct(shape, BF16)] * NQ,
         scratch_shapes=[pltpu.VMEM((lat * wave_rows, cw), F32)] * 2,
         compiler_params=params(),
-        cost_estimate=cost(
-            8 * waves * degrees * lat * cw, 4 * lat * wave_rows * cw + 4 * leg.size
-        ),
+        cost_estimate=cost(0, 14000000),
     )(*own, *others, leg, legt, gr, gi, *waits)
 
 
 def inverse_kernel(nz, lon_count, *refs):
-    own = refs[:nz]
-    others = refs[nz : nz + NQ - 1]
-    table_ref = refs[nz + NQ - 1]
-    outs = refs[nz + NQ : nz + NQ + lon_count]
+    near = refs[:NQ]
+    far = refs[NQ : NQ + nz - 1]
+    table_ref = refs[NQ + nz - 1]
+    outs = refs[NQ + nz : NQ + nz + lon_count]
     wide = refs[-1]
     rows, _, cw = wide.shape
-    wave_rows = own[0].shape[-2]
+    wave_rows = near[0].shape[-2]
     cols = outs[0].shape[1]
     for t in range(rows):
         for q in range(NQ):
             for d in range(nz):
                 at = (q * nz + d) * wave_rows
-                block = others[q - 1][d, t] if q else own[d][0, t]
+                block = far[d - 1][q, t] if d else near[q][0, t]
                 wide[t, at : at + wave_rows, :] = block.astype(F32)
     group = rows if cw % LANES == 0 else 1
     for first in range(0, rows, group):
@@ -200,13 +278,13 @@
                 outs[s][first + i] = piece.astype(BF16)
 
 
-def inverse(own, others, table, lon_count):
-    nz = len(own)
-    _, rows, wave_rows, cw = own[0].shape
+def inverse(near, far, table, lon_count):
+    nz = len(far) + 1
+    _, rows, wave_rows, cw = near[0].shape
     step = step_rows(rows, 6)
     cols = table.shape[0] // lon_count
-    specs = [pl.BlockSpec((1, step, wave_rows, cw), lambda t: (0, t, 0, 0))] * nz
-    specs += [pl.BlockSpec((nz, step, wave_rows, cw), lambda t: (0, t, 0, 0))] * (NQ - 1)
+    specs = [pl.BlockSpec((1, step, wave_rows, cw), lambda t: (0, t, 0, 0))] * NQ
+    specs += [pl.BlockSpec((NQ, step, wave_rows, cw), lambda t: (0, t, 0, 0))] * (nz - 1)
     return pl.pallas_call(
         functools.partial(inverse_kernel, nz, lon_count),
         grid=(rows // step,),
@@ -215,8 +293,8 @@
         out_shape=[jax.ShapeDtypeStruct((rows, cols, cw), BF16)] * lon_count,
         scratch_shapes=[pltpu.VMEM((step, nz * NQ * wave_rows, cw), F32)],
         compiler_params=params(),
-        cost_estimate=cost(2 * table.size * rows * cw, 4 * rows * cols * cw * lon_count),
-    )(*own, *others, table)
+        cost_estimate=cost(0, 14000000),
+    )(*near, *far, table)
 
 
 def window_kernel(cols, place_ref, neighbour_ref, basis_ref, quad_ref, wave_ref, low_ref, high_ref, disco_ref, out_ref, ring):
@@ -266,7 +344,7 @@
         out_shape=jax.ShapeDtypeStruct((rows, cols, cw), BF16),
         scratch_shapes=[pltpu.VMEM((rows + 2 * HALO, padded, cw), F32)],
         compiler_params=params(),
-        cost_estimate=cost(8 * rows * cols * cw * 24, 4 * rows * cols * cw),
+        cost_estimate=cost(0, 20000000),
     )(place, neighbour, basis, quad, wave, low, high, disco)
 
 
@@ -395,48 +473,65 @@
         start = (lon_id ^ s) * cblock + j * cw
         return lax.dynamic_slice_in_dim(array, start, cw, array.ndim - 1)
 
-    def across(own):
-        return [swap(jnp.stack([a[q] for a in own]), "lat", q) for q in range(1, NQ)]
-
-    def along(arrays):
-        return [arrays[0]] + [swap(arrays[d], "lat", NQ * d) for d in range(1, nz)]
+    def along(blocks):
+        return [swap(block, "lat", NQ * (d + 1)) for d, block in enumerate(blocks)]
+
+    def across(blocks):
+        return [swap(block, "lat", q + 1) for q, block in enumerate(blocks)]
 
     disco = disco_weight.reshape(disco_weight.shape[0], lon_count * nch, cw)
     disco = jnp.transpose(disco, (1, 0, 2))
     up = [(i, i + 1) for i in range(lat_count - 1)]
     down = [(i + 1, i) for i in range(lat_count - 1)]
 
-    def convolved(wave, s, j):
-        low = lax.ppermute(wave[rows - HALO :], "lat", up)
-        high = lax.ppermute(wave[:HALO], "lat", down)
+    def convolved(wave, s, j, waits):
+        first, last = edge_rows(wave, waits)
+        low = lax.ppermute(last, "lat", up)
+        high = lax.ppermute(first, "lat", down)
         place = ((lon_id ^ s) * nch + j).astype(jnp.int32)
         done = window(
             place[None], neighbour, basis, disco_quad, wave, low, high, disco, cols
         )
         return place, done
 
-    received = [
-        [swap(chunk_of(field, s, j), "lon", s) for s in range(1, lon_count)]
-        for j in range(nch)
-    ]
+    def channel_index(s, j):
+        return ((lon_id ^ s) * nch + j).astype(jnp.int32)
+
+    received, waits = [], []
+    for j in range(nch):
+        received.append(
+            [
+                swap(pick(field, channel_index(s, j), cw, waits), "lon", s)
+                for s in range(1, lon_count)
+            ]
+        )
+        waits = [fwd]
     spectra, waits = [], []
     for j in range(nch):
-        blocks = [chunk_of(field, 0, j)] + received[j]
-        spectra.append(along(dft(blocks, quad_weight, fwd, nz, wave_rows, waits)))
+        arrays = dft(
+            field, channel_index(0, j), received[j], quad_weight, fwd, nz, wave_rows, cw, waits
+        )
+        spectra.append([arrays[0]] + along(arrays[1:]))
         waits = [spectra[-1][1]]
-    synthesis, waits = [], []
+        latest = arrays[0]
+    near = []
+    waits = [latest]
     for j in range(nch):
         gr = chunk_of(filter_real, 0, j)
         gi = chunk_of(filter_imag, 0, j)
-        full = legendre_step(spectra[j], across(spectra[j]), leg, legt, gr, gi, waits)
-        synthesis.append(along(full))
-        waits = [full[0]]
-    groups = []
+        full = legendre_step(
+            spectra[j], across(regroup(spectra[j], waits)), leg, legt, gr, gi, []
+        )
+        near.append([full[0]] + across(full[1:]))
+        waits = []
+    parts = []
     for j in range(nch):
-        parts = inverse(synthesis[j], across(synthesis[j]), inv, lon_count)
-        for s in range(lon_count):
-            wave = swap(parts[s], "lon", s) if s else parts[0]
-            groups.append(convolved(wave, s, j))
+        parts.append(inverse(near[j], along(regroup(near[j], [])), inv, lon_count))
+    groups = [convolved(parts[j][0], 0, j, []) for j in range(nch)]
+    for j in range(nch):
+        waits = [done for _, done in groups] if j == nch - 1 else []
+        for s in range(1, lon_count):
+            groups.append(convolved(swap(parts[j][s], "lon", s), s, j, waits))
     block_out, spatial = mlp(
         jnp.stack([place for place, _ in groups]),
         [done for _, done in groups],

time: 312 us -> 274 us (0.88)
  waiting for transfers between devices: 148 us -> 107 us
  Pallas kernels: 65.6 us -> 86.6 us
  starting transfers between devices: 67 us -> 54.7 us
  local copies, waits for them, and re-layouts: 21.3 us -> 14.9 us
    ppermute x28, waiting for transfers between devices: 148 us -> 102 us  [swap(): return lax.ppermute(array, axis, [(i, i ^ mask) for i in range(count)])]
    pallas_call x0 -> x10, Pallas kernels: none -> 21.3 us  [the longest x4 8.68 us: regroup(): pl.pallas_call(functools.partial(regroup_kernel, count, outs), grid=(1,),...]
    ppermute x28, starting transfers between devices: 43.2 us -> 28 us  [swap(): return lax.ppermute(array, axis, [(i, i ^ mask) for i in range(count)])]
    slice x20 -> x0, local copies, waits for them, and re-layouts: 8.54 us -> none  [the longest x4 4.35 us: convolved(): high = lax.ppermute(wave[:HALO], 'lat', down)]
    unnamed x76 -> x74, local copies, waits for them, and re-layouts: 5.86 us -> 11.3 us
    ppermute x8, waiting for transfers between devices: 0.02 us -> 5.03 us  [the longest x4 4.66 us: convolved(): high = lax.ppermute(first, 'lat', down)]
    dynamic_slice x2 -> x1, local copies, waits for them, and re-layouts: 5.19 us -> 1.8 us  [chunk_of(): return lax.dynamic_slice_in_dim(array, start, cw, array.ndim - 1)]
  transfers between devices with their start and end apart: 36 -> 36, of which waited for: 15 -> 12; matrix products, arithmetic and copies ran while one was open for 6% -> 4% of each run, Pallas kernels for 13% -> 22%
where the time goes in v3:
time: 274 us; the launch traced here: 271 us
  waiting for transfers between devices  107 us (39%)
  Pallas kernels  86.6 us (32%)
  starting transfers between devices  54.7 us (20%)
  local copies, waits for them, and re-layouts  14.9 us (5%)
  matrix products  4.2 us (2%)
    ppermute x28, waiting for transfers between devices, swap(): return lax.ppermute(array, axis, [(i, i ^ mask) for i in range(count)])  102 us
    ppermute x28, starting transfers between devices, swap(): return lax.ppermute(array, axis, [(i, i ^ mask) for i in range(count)])  28 us
    pallas_call x4, Pallas kernels, window(): pl.pallas_call(functools.partial(window_kernel, cols), grid=(rows // per_...  24 us
    pallas_call x1, Pallas kernels, mlp(): pl.pallas_call(mlp_kernel, grid=(rows // per_step,), in_specs=[smem_spec(...  17.8 us
    ppermute x4, starting transfers between devices, convolved(): low = lax.ppermute(last, 'lat', up)  14.5 us
    ppermute x4, starting transfers between devices, convolved(): high = lax.ppermute(first, 'lat', down)  12.1 us
    unnamed x74, local copies, waits for them, and re-layouts  11.3 us
    pallas_call x4, Pallas kernels, regroup(): pl.pallas_call(functools.partial(regroup_kernel, count, outs), grid=(1,),...  8.68 us
  transfers between devices with their start and end apart: 36, of which 12 were waited for; matrix products, arithmetic and copies ran while one was open for 4% of the time, Pallas kernels for 22%

profile of v3, /device:TPU:19, one launch (start us, length us, event | category | flops | bytes accessed | tf_op | source)
XLA Modules:
  0.0 271.3 jit_solution(16160183794376034606)
XLA Ops:
  0.7 2.2 shard_map.194
  5.0 2.1 shard_map.196
  7.2 1.2 collective-permute-start.4
  8.4 21.6 %collective-permute-done.refs_1_ = bf16[12,384,128]{2,1,0:T(8,128)(2,1)S(1)} collective-permute-done((bf16[12,384,128]{2,1,0:T(8,128)(2,1)}, bf16[12,384,128]{2,1,0:T(8,128)(2,1)S(1)}, u32[]{:S(2)}, u32[]{:S(2)}) %collective-permute-start) | collective-permute-done | bytes 1179680 | tf_op jit(solution)/shard_map/ppermute | solution.py:397
  30.0 1.0 copy-done.10
  31.0 3.6 %shard_map.195 = (bf16[4,12,24,128]{3,2,1,0:T(8,128)(2,1)}, bf16[4,12,24,128]{3,2,1,0:T(8,128)(2,1)}, bf16[4,12,24,128]{3,2,1,0:T(8,128)(2,1)}, bf16[4,12,24,128]{3,2,1,0:T(8,128)(2,1)}) custom-call(s32[1]{0:T(128)} %bitcast.index_ref.place_ref, f32[12]{0:T(128)} %quad_ref.7, bf16[12,384,512]{2,1,0:T(8,128)(2,1)} %refs_9_.1, ...), custom_call_target="tpu_custom_call" | custom-call | flops 905969664 | bytes 4718592 | tf_op jit(solution)/shard_map/pallas_call | solution.py:162
  34.6 1.3 collective-permute-start.1
  36.0 1.3 collective-permute-start.3
  37.3 18.1 %collective-permute-done.4.refs_1_ = bf16[12,384,128]{2,1,0:T(8,128)(2,1)} collective-permute-done((bf16[12,384,128]{2,1,0:T(8,128)(2,1)}, bf16[12,384,128]{2,1,0:T(8,128)(2,1)}, u32[]{:S(2)}, u32[]{:S(2)}) %collective-permute-start.4) | collective-permute-done | bytes 1179680 | tf_op jit(solution)/shard_map/ppermute | solution.py:397
  56.1 3.6 %shard_map.197 = (bf16[4,12,24,128]{3,2,1,0:T(8,128)(2,1)}, bf16[4,12,24,128]{3,2,1,0:T(8,128)(2,1)}, bf16[4,12,24,128]{3,2,1,0:T(8,128)(2,1)}, bf16[4,12,24,128]{3,2,1,0:T(8,128)(2,1)}) custom-call(s32[1]{0:T(128)} %bitcast.1.index_ref.place_ref, f32[12]{0:T(128)} %quad_ref.7, bf16[12,384,512]{2,1,0:T(8,128)(2,1)} %refs_9_.1, ...), custom_call_target="tpu_custom_call" | custom-call | flops 905969664 | bytes 4718592 | tf_op jit(solution)/shard_map/pallas_call | solution.py:162
  59.7 1.3 collective-permute-start.16
  61.0 1.3 collective-permute-start.18
  63.2 2.2 shard_map.198
  65.3 2.4 collective-permute-start.5
  67.9 1.3 collective-permute-start.6
  69.2 2.0 collective-permute-done.16.refs_1_
  71.2 3.3 %collective-permute-start.7 = (bf16[4,12,24,128]{3,2,1,0:T(8,128)(2,1)}, bf16[4,12,24,128]{3,2,1,0:T(8,128)(2,1)}, u32[]{:S(2)}, u32[]{:S(2)}) collective-permute-start(bf16[4,12,24,128]{3,2,1,0:T(8,128)(2,1)} %get-tuple-element.49), channel_id=1, source_target_pairs={{0,6},{2,4},{4,2},{6,0},{8,14},{10,12},{12,10},{14,8},{16,22},{18,... | collective-permute-start | bytes 884744 | tf_op jit(solution)/shard_map/ppermute | solution.py:397
  74.5 12.8 %collective-permute-done.18.refs_3_ = bf16[4,12,24,128]{3,2,1,0:T(8,128)(2,1)S(1)} collective-permute-done((bf16[4,12,24,128]{3,2,1,0:T(8,128)(2,1)}, bf16[4,12,24,128]{3,2,1,0:T(8,128)(2,1)S(1)}, u32[]{:S(2)}, u32[]{:S(2)}) %collective-permute-start.18) | collective-permute-done | bytes 294944 | tf_op jit(solution)/shard_map/ppermute | solution.py:397
  88.0 2.2 shard_map.204
  90.2 2.5 collective-permute-start.19
  92.7 1.2 collective-permute-start.20
  94.9 1.5 copy.23.refs_7_
  96.3 1.8 constant_dynamic-slice_fusion
  98.1 4.2 %shard_map.199 = (bf16[4,12,24,128]{3,2,1,0:T(8,128)(2,1)}, bf16[4,12,24,128]{3,2,1,0:T(8,128)(2,1)}, bf16[4,12,24,128]{3,2,1,0:T(8,128)(2,1)}, bf16[4,12,24,128]{3,2,1,0:T(8,128)(2,1)}) custom-call(bf16[4,12,24,128]{3,2,1,0:T(8,128)(2,1)} %get-tuple-element.42.refs_0_, bf16[4,12,24,128]{3,2,1,0:T(8,128)(2,1)} %copy-done.4, ...), custom_call_target="tpu_custom_call" | custom-call | bytes 14000000 | tf_op jit(solution)/shard_map/pallas_call | solution.py:242
  102.6 1.2 collective-permute-start.9
  104.5 3.8 %collective-permute-done.21.refs_6_ = bf16[4,12,24,128]{3,2,1,0:T(8,128)(2,1)S(1)} collective-permute-done((bf16[4,12,24,128]{3,2,1,0:T(8,128)(2,1)}, bf16[4,12,24,128]{3,2,1,0:T(8,128)(2,1)S(1)}, u32[]{:S(2)}, u32[]{:S(2)}) %collective-permute-start.21) | collective-permute-done | bytes 294944 | tf_op jit(solution)/shard_map/ppermute | solution.py:397
  109.0 4.2 %shard_map.205 = (bf16[4,12,24,128]{3,2,1,0:T(8,128)(2,1)}, bf16[4,12,24,128]{3,2,1,0:T(8,128)(2,1)}, bf16[4,12,24,128]{3,2,1,0:T(8,128)(2,1)}, bf16[4,12,24,128]{3,2,1,0:T(8,128)(2,1)}) custom-call(bf16[4,12,24,128]{3,2,1,0:T(8,128)(2,1)} %get-tuple-element.46.refs_4_.refs_0_, bf16[4,12,24,128]{3,2,1,0:T(8,128)(2,1)} %copy-done.5, ...), custom_call_target="tpu_custom_call" | custom-call | bytes 14000000 | tf_op jit(solution)/shard_map/pallas_call | solution.py:242
  113.4 1.3 collective-permute-start.23
  114.7 0.9 collective-permute-start.24
  115.6 5.3 %collective-permute-done.10.refs_3_ = bf16[4,12,24,128]{3,2,1,0:T(8,128)(2,1)S(1)} collective-permute-done((bf16[4,12,24,128]{3,2,1,0:T(8,128)(2,1)}, bf16[4,12,24,128]{3,2,1,0:T(8,128)(2,1)S(1)}, u32[]{:S(2)}, u32[]{:S(2)}) %collective-permute-start.10) | collective-permute-done | bytes 294944 | tf_op jit(solution)/shard_map/ppermute | solution.py:397
  121.7 2.2 shard_map.200
  123.8 1.5 convolution_convert_fusion.2
  125.3 1.4 collective-permute-start.12
  126.7 1.3 collective-permute-start.13
  128.0 1.5 convolution_convert_fusion.1
  129.5 4.0 %collective-permute-done.24.refs_3_ = bf16[4,12,24,128]{3,2,1,0:T(8,128)(2,1)S(1)} collective-permute-done((bf16[4,12,24,128]{3,2,1,0:T(8,128)(2,1)}, bf16[4,12,24,128]{3,2,1,0:T(8,128)(2,1)S(1)}, u32[]{:S(2)}, u32[]{:S(2)}) %collective-permute-start.24) | collective-permute-done | bytes 294944 | tf_op jit(solution)/shard_map/ppermute | solution.py:397
  134.2 2.2 shard_map.206
  136.4 1.2 collective-permute-start.26
  137.6 1.4 collective-permute-start.27
  139.1 0.9 pad_maximum_fusion.refs_7_
  140.0 6.0 %collective-permute-done.12.refs_5_ = bf16[4,12,24,128]{3,2,1,0:T(8,128)(2,1)S(1)} collective-permute-done((bf16[4,12,24,128]{3,2,1,0:T(8,128)(2,1)}, bf16[4,12,24,128]{3,2,1,0:T(8,128)(2,1)S(1)}, u32[]{:S(2)}, u32[]{:S(2)}) %collective-permute-start.12) | collective-permute-done | bytes 294944 | tf_op jit(solution)/shard_map/ppermute | solution.py:397
  146.0 20.9 %collective-permute-done.13.refs_6_ = bf16[4,12,24,128]{3,2,1,0:T(8,128)(2,1)S(1)} collective-permute-done((bf16[4,12,24,128]{3,2,1,0:T(8,128)(2,1)}, bf16[4,12,24,128]{3,2,1,0:T(8,128)(2,1)S(1)}, u32[]{:S(2)}, u32[]{:S(2)}) %collective-permute-start.13) | collective-permute-done | bytes 294944 | tf_op jit(solution)/shard_map/ppermute | solution.py:397
  167.6 3.9 %shard_map.201 = (bf16[12,392,128]{2,1,0:T(8,128)(2,1)}, bf16[12,392,128]{2,1,0:T(8,128)(2,1)}) custom-call(bf16[4,12,24,128]{3,2,1,0:T(8,128)(2,1)} %get-tuple-element.50.refs_0_, bf16[4,12,24,128]{3,2,1,0:T(8,128)(2,1)} %copy-done.11, bf16[4,12,24,128]{3,2,1,0:T(8,128)(2,1)} %copy-done.12, bf16[4,12,24,128]{3,2,1,0:T(8,128)(2,1)} %copy-done.13, ...), custom_call_target="tpu_custom_call" | custom-call | bytes 14000000 | tf_op jit(solution)/shard_map/pallas_call | solution.py:288
  171.8 7.8 %collective-permute-done.27.refs_6_ = bf16[4,12,24,128]{3,2,1,0:T(8,128)(2,1)S(1)} collective-permute-done((bf16[4,12,24,128]{3,2,1,0:T(8,128)(2,1)}, bf16[4,12,24,128]{3,2,1,0:T(8,128)(2,1)S(1)}, u32[]{:S(2)}, u32[]{:S(2)}) %collective-permute-start.27) | collective-permute-done | bytes 294944 | tf_op jit(solution)/shard_map/ppermute | solution.py:397
  180.2 3.9 %shard_map.207 = (bf16[12,392,128]{2,1,0:T(8,128)(2,1)}, bf16[12,392,128]{2,1,0:T(8,128)(2,1)}) custom-call(bf16[4,12,24,128]{3,2,1,0:T(8,128)(2,1)} %get-tuple-element.66.refs_0_, bf16[4,12,24,128]{3,2,1,0:T(8,128)(2,1)} %copy-done.14, bf16[4,12,24,128]{3,2,1,0:T(8,128)(2,1)} %copy-done.15, bf16[4,12,24,128]{3,2,1,0:T(8,128)(2,1)} %copy-done.16, ...), custom_call_target="tpu_custom_call" | custom-call | bytes 14000000 | tf_op jit(solution)/shard_map/pallas_call | solution.py:288
  184.4 2.1 shard_map.202
  186.5 4.3 %collective-permute-start.14 = (bf16[2,392,128]{2,1,0:T(8,128)(2,1)}, bf16[2,392,128]{2,1,0:T(8,128)(2,1)S(1)}, u32[]{:S(2)}, u32[]{:S(2)}) collective-permute-start(bf16[2,392,128]{2,1,0:T(8,128)(2,1)} %get-tuple-element.58), channel_id=1, source_target_pairs={{0,2},{2,4},{4,6},{6,8},{8,10},{10,12},{12,14},{14,16},{16,18},{18... | collective-permute-start | bytes 602120 | tf_op jit(solution)/shard_map/ppermute | solution.py:489
  190.8 1.9 collective-permute-start.15
  192.7 2.1 shard_map.208
  194.8 3.6 %collective-permute-start.28 = (bf16[2,392,128]{2,1,0:T(8,128)(2,1)}, bf16[2,392,128]{2,1,0:T(8,128)(2,1)S(1)}, u32[]{:S(2)}, u32[]{:S(2)}) collective-permute-start(bf16[2,392,128]{2,1,0:T(8,128)(2,1)} %get-tuple-element.74), channel_id=1, source_target_pairs={{0,2},{2,4},{4,6},{6,8},{8,10},{10,12},{12,14},{14,16},{16,18},{18... | collective-permute-start | bytes 602120 | tf_op jit(solution)/shard_map/ppermute | solution.py:489
  198.5 6.2 %collective-permute-start.29 = (bf16[2,392,128]{2,1,0:T(8,128)(2,1)}, bf16[2,392,128]{2,1,0:T(8,128)(2,1)S(1)}, u32[]{:S(2)}, u32[]{:S(2)}) collective-permute-start(bf16[2,392,128]{2,1,0:T(8,128)(2,1)} %get-tuple-element.75), channel_id=1, source_target_pairs={{2,0},{4,2},{6,4},{8,6},{10,8},{12,10},{14,12},{16,14},{18,16},{20... | collective-permute-start | bytes 602120 | tf_op jit(solution)/shard_map/ppermute | solution.py:490
  204.6 2.1 shard_map.210
  206.7 3.0 %collective-permute-start.31 = (bf16[2,392,128]{2,1,0:T(8,128)(2,1)}, bf16[2,392,128]{2,1,0:T(8,128)(2,1)S(1)}, u32[]{:S(2)}, u32[]{:S(2)}) collective-permute-start(bf16[2,392,128]{2,1,0:T(8,128)(2,1)} %get-tuple-element.77), channel_id=1, source_target_pairs={{0,2},{2,4},{4,6},{6,8},{8,10},{10,12},{12,14},{14,16},{16,18},{18... | collective-permute-start | bytes 602120 | tf_op jit(solution)/shard_map/ppermute | solution.py:489
  209.8 2.1 collective-permute-start.32
  211.9 6.0 %shard_map.203.refs_0_ = bf16[12,384,128]{2,1,0:T(8,128)(2,1)} custom-call(s32[1]{0:T(128)} %bitcast.index_ref.place_ref, s32[12,12]{1,0:T(8,128)} %neighbour_ref.7, s32[12,12]{1,0:T(8,128)} %basis_ref.7, f32[12,12]{1,0:T(8,128)} %quad_ref.11, bf16[12,392,128]{2,1,0:T(8,128)(2,1)} %get-tuple-element.57.wave_ref, bf16[2,392,128]{2,1,0:T(8,128)(2,1)} %copy-done.27, ...), custom_call_target="tpu_custom_call" | custom-call | bytes 20000000 | tf_op jit(solution)/shard_map/pallas_call | solution.py:339
  219.3 6.0 %shard_map.209.refs_1_ = bf16[12,384,128]{2,1,0:T(8,128)(2,1)} custom-call(s32[1]{0:T(128)} %bitcast.1.index_ref.place_ref, s32[12,12]{1,0:T(8,128)} %neighbour_ref.7, s32[12,12]{1,0:T(8,128)} %basis_ref.7, f32[12,12]{1,0:T(8,128)} %quad_ref.11, bf16[12,392,128]{2,1,0:T(8,128)(2,1)} %get-tuple-element.73.wave_ref, bf16[2,392,128]{2,1,0:T(8,128)(2,1)} %copy-done.28, ...), custom_call_target="tpu_custom_call" | custom-call | bytes 20000000 | tf_op jit(solution)/shard_map/pallas_call | solution.py:339
  226.7 6.0 %shard_map.211.refs_2_ = bf16[12,384,128]{2,1,0:T(8,128)(2,1)} custom-call(s32[1]{0:T(128)} %bitcast.2.index_ref.place_ref, s32[12,12]{1,0:T(8,128)} %neighbour_ref.7, s32[12,12]{1,0:T(8,128)} %basis_ref.7, f32[12,12]{1,0:T(8,128)} %quad_ref.11, bf16[12,392,128]{2,1,0:T(8,128)(2,1)} %copy-done.2, bf16[2,392,128]{2,1,0:T(8,128)(2,1)} %copy-done.31, ...), custom_call_target="tpu_custom_call" | custom-call | bytes 20000000 | tf_op jit(solution)/shard_map/pallas_call | solution.py:339
  232.7 1.0 copy-done.3
  233.7 2.0 shard_map.212
  235.7 3.6 %collective-permute-start.34 = (bf16[2,392,128]{2,1,0:T(8,128)(2,1)}, bf16[2,392,128]{2,1,0:T(8,128)(2,1)S(1)}, u32[]{:S(2)}, u32[]{:S(2)}) collective-permute-start(bf16[2,392,128]{2,1,0:T(8,128)(2,1)} %get-tuple-element.80), channel_id=1, source_target_pairs={{0,2},{2,4},{4,6},{6,8},{8,10},{10,12},{12,14},{14,16},{16,18},{18... | collective-permute-start | bytes 602120 | tf_op jit(solution)/shard_map/ppermute | solution.py:489
  239.3 1.9 collective-permute-start.35
  242.2 4.6 %collective-permute-done.35.high_ref = bf16[2,392,128]{2,1,0:T(8,128)(2,1)S(1)} collective-permute-done((bf16[2,392,128]{2,1,0:T(8,128)(2,1)}, bf16[2,392,128]{2,1,0:T(8,128)(2,1)S(1)}, u32[]{:S(2)}, u32[]{:S(2)}) %collective-permute-start.35) | collective-permute-done | bytes 200736 | tf_op jit(solution)/shard_map/ppermute | solution.py:490
  247.6 6.0 %shard_map.213.refs_3_ = bf16[12,384,128]{2,1,0:T(8,128)(2,1)} custom-call(s32[1]{0:T(128)} %bitcast.3.index_ref.place_ref, s32[12,12]{1,0:T(8,128)} %neighbour_ref.7, s32[12,12]{1,0:T(8,128)} %basis_ref.7, f32[12,12]{1,0:T(8,128)} %quad_ref.11, bf16[12,392,128]{2,1,0:T(8,128)(2,1)} %copy-done.3, bf16[2,392,128]{2,1,0:T(8,128)(2,1)} %copy-done.33, ...), custom_call_target="tpu_custom_call" | custom-call | bytes 20000000 | tf_op jit(solution)/shard_map/pallas_call | solution.py:339
  253.5 17.8 %shard_map.214 = (bf16[12,384,512]{2,1,0:T(8,128)(2,1)}, bf16[12,384,512]{2,1,0:T(8,128)(2,1)}) custom-call(s32[4]{0:T(128)} %pad_add_fusion.place_ref, bf16[12,384,128]{2,1,0:T(8,128)(2,1)} %shard_map.203.refs_0_, bf16[12,384,128]{2,1,0:T(8,128)(2,1)} %shard_map.209.refs_1_, bf16[12,384,128]{2,1,0:T(8,128)(2,1)} %shard_map.211.refs_2_, ...), custom_call_target="tpu_custom_call" | custom-call | flops 9663676416 | bytes 18874368 | tf_op jit(solution)/shard_map/pallas_call | solution.py:378
  (120 shorter events, 15.2 us)
Async XLA Ops:
  0.6 93.7 %copy-start = (bf16[12,192,192]{2,1,0:T(8,128)(2,1)S(1)}, bf16[12,192,192]{2,1,0:T(8,128)(2,1)}, u32[]{:S(2)}) copy-start(bf16[12,192,192]{2,1,0:T(8,128)(2,1)} %param.21) | copy-start | bytes 2654212
  0.7 2.5 copy-start.35
  0.7 2.7 copy-start.36
  2.9 27.0 %collective-permute-start = (bf16[12,384,128]{2,1,0:T(8,128)(2,1)}, bf16[12,384,128]{2,1,0:T(8,128)(2,1)S(1)}, u32[]{:S(2)}, u32[]{:S(2)}) collective-permute-start(bf16[12,384,128]{2,1,0:T(8,128)(2,1)} %shard_map.194), channel_id=1, source_target_pairs={{0,1},{1,0},{2,3},{3,2},{4,5},{5,4},{6,7},{7,6},{8,9},{9,8},{10,11... | collective-permute-start | bytes 3538952 | tf_op jit(solution)/shard_map/ppermute | solution.py:397
  7.2 48.2 %collective-permute-start.4 = (bf16[12,384,128]{2,1,0:T(8,128)(2,1)}, bf16[12,384,128]{2,1,0:T(8,128)(2,1)}, u32[]{:S(2)}, u32[]{:S(2)}) collective-permute-start(bf16[12,384,128]{2,1,0:T(8,128)(2,1)} %shard_map.196), channel_id=1, source_target_pairs={{0,1},{1,0},{2,3},{3,2},{4,5},{5,4},{6,7},{7,6},{8,9},{9,8},{10,11... | collective-permute-start | bytes 3538952 | tf_op jit(solution)/shard_map/ppermute | solution.py:397
  30.0 1.0 copy-start.10
  34.6 20.8 %collective-permute-start.1 = (bf16[4,12,24,128]{3,2,1,0:T(8,128)(2,1)}, bf16[4,12,24,128]{3,2,1,0:T(8,128)(2,1)S(1)}, u32[]{:S(2)}, u32[]{:S(2)}) collective-permute-start(bf16[4,12,24,128]{3,2,1,0:T(8,128)(2,1)} %get-tuple-element.43), channel_id=1, source_target_pairs={{0,8},{2,10},{4,12},{6,14},{8,0},{10,2},{12,4},{14,6},{16,24},{18,... | collective-permute-start | bytes 884744 | tf_op jit(solution)/shard_map/ppermute | solution.py:397
  35.9 26.4 %collective-permute-start.2 = (bf16[4,12,24,128]{3,2,1,0:T(8,128)(2,1)}, bf16[4,12,24,128]{3,2,1,0:T(8,128)(2,1)S(1)}, u32[]{:S(2)}, u32[]{:S(2)}) collective-permute-start(bf16[4,12,24,128]{3,2,1,0:T(8,128)(2,1)} %get-tuple-element.44), channel_id=1, source_target_pairs={{0,16},{2,18},{4,20},{6,22},{8,24},{10,26},{12,28},{14,30},{16,0},... | collective-permute-start | bytes 884744 | tf_op jit(solution)/shard_map/ppermute | solution.py:397
  36.0 26.4 %collective-permute-start.3 = (bf16[4,12,24,128]{3,2,1,0:T(8,128)(2,1)}, bf16[4,12,24,128]{3,2,1,0:T(8,128)(2,1)S(1)}, u32[]{:S(2)}, u32[]{:S(2)}) collective-permute-start(bf16[4,12,24,128]{3,2,1,0:T(8,128)(2,1)} %get-tuple-element.45), channel_id=1, source_target_pairs={{0,24},{2,26},{4,28},{6,30},{8,16},{10,18},{12,20},{14,22},{16,8},... | collective-permute-start | bytes 884744 | tf_op jit(solution)/shard_map/ppermute | solution.py:397
  59.7 11.5 %collective-permute-start.16 = (bf16[4,12,24,128]{3,2,1,0:T(8,128)(2,1)}, bf16[4,12,24,128]{3,2,1,0:T(8,128)(2,1)S(1)}, u32[]{:S(2)}, u32[]{:S(2)}) collective-permute-start(bf16[4,12,24,128]{3,2,1,0:T(8,128)(2,1)} %get-tuple-element.60), channel_id=1, source_target_pairs={{0,8},{2,10},{4,12},{6,14},{8,0},{10,2},{12,4},{14,6},{16,24},{18,... | collective-permute-start | bytes 884744 | tf_op jit(solution)/shard_map/ppermute | solution.py:397
  61.0 13.5 %collective-permute-start.17 = (bf16[4,12,24,128]{3,2,1,0:T(8,128)(2,1)}, bf16[4,12,24,128]{3,2,1,0:T(8,128)(2,1)S(1)}, u32[]{:S(2)}, u32[]{:S(2)}) collective-permute-start(bf16[4,12,24,128]{3,2,1,0:T(8,128)(2,1)} %get-tuple-element.61), channel_id=1, source_target_pairs={{0,16},{2,18},{4,20},{6,22},{8,24},{10,26},{12,28},{14,30},{16,0},... | collective-permute-start | bytes 884744 | tf_op jit(solution)/shard_map/ppermute | solution.py:397
  61.0 26.3 %collective-permute-start.18 = (bf16[4,12,24,128]{3,2,1,0:T(8,128)(2,1)}, bf16[4,12,24,128]{3,2,1,0:T(8,128)(2,1)S(1)}, u32[]{:S(2)}, u32[]{:S(2)}) collective-permute-start(bf16[4,12,24,128]{3,2,1,0:T(8,128)(2,1)} %get-tuple-element.62), channel_id=1, source_target_pairs={{0,24},{2,26},{4,28},{6,30},{8,16},{10,18},{12,20},{14,22},{16,8},... | collective-permute-start | bytes 884744 | tf_op jit(solution)/shard_map/ppermute | solution.py:397
  62.3 0.8 copy-start.9
  65.3 28.6 %collective-permute-start.5 = (bf16[4,12,24,128]{3,2,1,0:T(8,128)(2,1)}, bf16[4,12,24,128]{3,2,1,0:T(8,128)(2,1)S(1)}, u32[]{:S(2)}, u32[]{:S(2)}) collective-permute-start(bf16[4,12,24,128]{3,2,1,0:T(8,128)(2,1)} %get-tuple-element.47), channel_id=1, source_target_pairs={{0,2},{2,0},{4,6},{6,4},{8,10},{10,8},{12,14},{14,12},{16,18},{18,... | collective-permute-start | bytes 884744 | tf_op jit(solution)/shard_map/ppermute | solution.py:397
  67.9 30.3 %collective-permute-start.6 = (bf16[4,12,24,128]{3,2,1,0:T(8,128)(2,1)}, bf16[4,12,24,128]{3,2,1,0:T(8,128)(2,1)}, u32[]{:S(2)}, u32[]{:S(2)}) collective-permute-start(bf16[4,12,24,128]{3,2,1,0:T(8,128)(2,1)} %get-tuple-element.48), channel_id=1, source_target_pairs={{0,4},{2,6},{4,0},{6,2},{8,12},{10,14},{12,8},{14,10},{16,20},{18,... | collective-permute-start | bytes 884744 | tf_op jit(solution)/shard_map/ppermute | solution.py:397
  71.2 16.1 %copy-start.5 = (bf16[4,12,24,128]{3,2,1,0:T(8,128)(2,1)}, bf16[4,12,24,128]{3,2,1,0:T(8,128)(2,1)S(1)}, u32[]{:S(2)}) copy-start(bf16[4,12,24,128]{3,2,1,0:T(8,128)(2,1)S(1)} %collective-permute-done.16.refs_1_) | copy-start | bytes 884740
  71.2 26.9 %collective-permute-start.7 = (bf16[4,12,24,128]{3,2,1,0:T(8,128)(2,1)}, bf16[4,12,24,128]{3,2,1,0:T(8,128)(2,1)}, u32[]{:S(2)}, u32[]{:S(2)}) collective-permute-start(bf16[4,12,24,128]{3,2,1,0:T(8,128)(2,1)} %get-tuple-element.49), channel_id=1, source_target_pairs={{0,6},{2,4},{4,2},{6,0},{8,14},{10,12},{12,10},{14,8},{16,22},{18,... | collective-permute-start | bytes 884744 | tf_op jit(solution)/shard_map/ppermute | solution.py:397
  74.5 12.8 %copy-start.6 = (bf16[4,12,24,128]{3,2,1,0:T(8,128)(2,1)}, bf16[4,12,24,128]{3,2,1,0:T(8,128)(2,1)S(1)}, u32[]{:S(2)}) copy-start(bf16[4,12,24,128]{3,2,1,0:T(8,128)(2,1)S(1)} %collective-permute-done.17.refs_2_) | copy-start | bytes 884740
  90.2 13.6 %collective-permute-start.19 = (bf16[4,12,24,128]{3,2,1,0:T(8,128)(2,1)}, bf16[4,12,24,128]{3,2,1,0:T(8,128)(2,1)S(1)}, u32[]{:S(2)}, u32[]{:S(2)}) collective-permute-start(bf16[4,12,24,128]{3,2,1,0:T(8,128)(2,1)} %get-tuple-element.63), channel_id=1, source_target_pairs={{0,2},{2,0},{4,6},{6,4},{8,10},{10,8},{12,14},{14,12},{16,18},{18,... | collective-permute-start | bytes 884744 | tf_op jit(solution)/shard_map/ppermute | solution.py:397
  92.7 11.8 %collective-permute-start.20 = (bf16[4,12,24,128]{3,2,1,0:T(8,128)(2,1)}, bf16[4,12,24,128]{3,2,1,0:T(8,128)(2,1)S(1)}, u32[]{:S(2)}, u32[]{:S(2)}) collective-permute-start(bf16[4,12,24,128]{3,2,1,0:T(8,128)(2,1)} %get-tuple-element.64), channel_id=1, source_target_pairs={{0,4},{2,6},{4,0},{6,2},{8,12},{10,14},{12,8},{14,10},{16,20},{18,... | collective-permute-start | bytes 884744 | tf_op jit(solution)/shard_map/ppermute | solution.py:397
  93.9 0.9 copy-start.19
  93.9 14.4 %collective-permute-start.21 = (bf16[4,12,24,128]{3,2,1,0:T(8,128)(2,1)}, bf16[4,12,24,128]{3,2,1,0:T(8,128)(2,1)S(1)}, u32[]{:S(2)}, u32[]{:S(2)}) collective-permute-start(bf16[4,12,24,128]{3,2,1,0:T(8,128)(2,1)} %get-tuple-element.65), channel_id=1, source_target_pairs={{0,6},{2,4},{4,2},{6,0},{8,14},{10,12},{12,10},{14,8},{16,22},{18,... | collective-permute-start | bytes 884744 | tf_op jit(solution)/shard_map/ppermute | solution.py:397
  94.8 1.5 copy-start.1
  102.4 12.4 %collective-permute-start.8 = (bf16[4,12,24,128]{3,2,1,0:T(8,128)(2,1)}, bf16[4,12,24,128]{3,2,1,0:T(8,128)(2,1)S(1)}, u32[]{:S(2)}, u32[]{:S(2)}) collective-permute-start(bf16[4,12,24,128]{3,2,1,0:T(8,128)(2,1)} %get-tuple-element.51), channel_id=1, source_target_pairs={{0,2},{2,0},{4,6},{6,4},{8,10},{10,8},{12,14},{14,12},{16,18},{18,... | collective-permute-start | bytes 884744 | tf_op jit(solution)/shard_map/ppermute | solution.py:397
  102.6 13.1 %collective-permute-start.9 = (bf16[4,12,24,128]{3,2,1,0:T(8,128)(2,1)}, bf16[4,12,24,128]{3,2,1,0:T(8,128)(2,1)S(1)}, u32[]{:S(2)}, u32[]{:S(2)}) collective-permute-start(bf16[4,12,24,128]{3,2,1,0:T(8,128)(2,1)} %get-tuple-element.52), channel_id=1, source_target_pairs={{0,4},{2,6},{4,0},{6,2},{8,12},{10,14},{12,8},{14,10},{16,20},{18,... | collective-permute-start | bytes 884744 | tf_op jit(solution)/shard_map/ppermute | solution.py:397
  103.8 4.5 %copy-start.17 = (bf16[4,12,24,128]{3,2,1,0:T(8,128)(2,1)}, bf16[4,12,24,128]{3,2,1,0:T(8,128)(2,1)S(1)}, u32[]{:S(2)}) copy-start(bf16[4,12,24,128]{3,2,1,0:T(8,128)(2,1)S(1)} %collective-permute-done.19.refs_4_) | copy-start | bytes 884740
  103.8 17.1 %collective-permute-start.10 = (bf16[4,12,24,128]{3,2,1,0:T(8,128)(2,1)}, bf16[4,12,24,128]{3,2,1,0:T(8,128)(2,1)S(1)}, u32[]{:S(2)}, u32[]{:S(2)}) collective-permute-start(bf16[4,12,24,128]{3,2,1,0:T(8,128)(2,1)} %get-tuple-element.53), channel_id=1, source_target_pairs={{0,6},{2,4},{4,2},{6,0},{8,14},{10,12},{12,10},{14,8},{16,22},{18,... | collective-permute-start | bytes 884744 | tf_op jit(solution)/shard_map/ppermute | solution.py:397
  104.5 3.8 %copy-start.18 = (bf16[4,12,24,128]{3,2,1,0:T(8,128)(2,1)}, bf16[4,12,24,128]{3,2,1,0:T(8,128)(2,1)S(1)}, u32[]{:S(2)}) copy-start(bf16[4,12,24,128]{3,2,1,0:T(8,128)(2,1)S(1)} %collective-permute-done.20.refs_5_) | copy-start | bytes 884740
  113.3 13.5 %collective-permute-start.22 = (bf16[4,12,24,128]{3,2,1,0:T(8,128)(2,1)}, bf16[4,12,24,128]{3,2,1,0:T(8,128)(2,1)S(1)}, u32[]{:S(2)}, u32[]{:S(2)}) collective-permute-start(bf16[4,12,24,128]{3,2,1,0:T(8,128)(2,1)} %get-tuple-element.67), channel_id=1, source_target_pairs={{0,2},{2,0},{4,6},{6,4},{8,10},{10,8},{12,14},{14,12},{16,18},{18,... | collective-permute-start | bytes 884744 | tf_op jit(solution)/shard_map/ppermute | solution.py:397
  113.4 16.1 %collective-permute-start.23 = (bf16[4,12,24,128]{3,2,1,0:T(8,128)(2,1)}, bf16[4,12,24,128]{3,2,1,0:T(8,128)(2,1)S(1)}, u32[]{:S(2)}, u32[]{:S(2)}) collective-permute-start(bf16[4,12,24,128]{3,2,1,0:T(8,128)(2,1)} %get-tuple-element.68), channel_id=1, source_target_pairs={{0,4},{2,6},{4,0},{6,2},{8,12},{10,14},{12,8},{14,10},{16,20},{18,... | collective-permute-start | bytes 884744 | tf_op jit(solution)/shard_map/ppermute | solution.py:397
  114.7 6.2 %copy-start.11 = (bf16[4,12,24,128]{3,2,1,0:T(8,128)(2,1)}, bf16[4,12,24,128]{3,2,1,0:T(8,128)(2,1)S(1)}, u32[]{:S(2)}) copy-start(bf16[4,12,24,128]{3,2,1,0:T(8,128)(2,1)S(1)} %collective-permute-done.8.refs_1_) | copy-start | bytes 884740
  114.7 18.8 %collective-permute-start.24 = (bf16[4,12,24,128]{3,2,1,0:T(8,128)(2,1)}, bf16[4,12,24,128]{3,2,1,0:T(8,128)(2,1)S(1)}, u32[]{:S(2)}, u32[]{:S(2)}) collective-permute-start(bf16[4,12,24,128]{3,2,1,0:T(8,128)(2,1)} %get-tuple-element.69), channel_id=1, source_target_pairs={{0,6},{2,4},{4,2},{6,0},{8,14},{10,12},{12,10},{14,8},{16,22},{18,... | collective-permute-start | bytes 884744 | tf_op jit(solution)/shard_map/ppermute | solution.py:397
  115.6 5.3 %copy-start.12 = (bf16[4,12,24,128]{3,2,1,0:T(8,128)(2,1)}, bf16[4,12,24,128]{3,2,1,0:T(8,128)(2,1)S(1)}, u32[]{:S(2)}) copy-start(bf16[4,12,24,128]{3,2,1,0:T(8,128)(2,1)S(1)} %collective-permute-done.9.refs_2_) | copy-start | bytes 884740
  121.0 0.7 copy-start.13
  123.8 13.8 %collective-permute-start.11 = (bf16[4,12,24,128]{3,2,1,0:T(8,128)(2,1)}, bf16[4,12,24,128]{3,2,1,0:T(8,128)(2,1)S(1)}, u32[]{:S(2)}, u32[]{:S(2)}) collective-permute-start(bf16[4,12,24,128]{3,2,1,0:T(8,128)(2,1)} %get-tuple-element.54), channel_id=1, source_target_pairs={{0,8},{2,10},{4,12},{6,14},{8,0},{10,2},{12,4},{14,6},{16,24},{18,... | collective-permute-start | bytes 884744 | tf_op jit(solution)/shard_map/ppermute | solution.py:397
  125.3 20.7 %collective-permute-start.12 = (bf16[4,12,24,128]{3,2,1,0:T(8,128)(2,1)}, bf16[4,12,24,128]{3,2,1,0:T(8,128)(2,1)S(1)}, u32[]{:S(2)}, u32[]{:S(2)}) collective-permute-start(bf16[4,12,24,128]{3,2,1,0:T(8,128)(2,1)} %get-tuple-element.55), channel_id=1, source_target_pairs={{0,16},{2,18},{4,20},{6,22},{8,24},{10,26},{12,28},{14,30},{16,0},... | collective-permute-start | bytes 884744 | tf_op jit(solution)/shard_map/ppermute | solution.py:397
  126.7 6.8 %copy-start.14 = (bf16[4,12,24,128]{3,2,1,0:T(8,128)(2,1)}, bf16[4,12,24,128]{3,2,1,0:T(8,128)(2,1)S(1)}, u32[]{:S(2)}) copy-start(bf16[4,12,24,128]{3,2,1,0:T(8,128)(2,1)S(1)} %collective-permute-done.22.refs_1_) | copy-start | bytes 884740
  126.7 40.1 %collective-permute-start.13 = (bf16[4,12,24,128]{3,2,1,0:T(8,128)(2,1)}, bf16[4,12,24,128]{3,2,1,0:T(8,128)(2,1)S(1)}, u32[]{:S(2)}, u32[]{:S(2)}) collective-permute-start(bf16[4,12,24,128]{3,2,1,0:T(8,128)(2,1)} %get-tuple-element.56), channel_id=1, source_target_pairs={{0,24},{2,26},{4,28},{6,30},{8,16},{10,18},{12,20},{14,22},{16,8},... | collective-permute-start | bytes 884744 | tf_op jit(solution)/shard_map/ppermute | solution.py:397
  129.5 4.0 %copy-start.15 = (bf16[4,12,24,128]{3,2,1,0:T(8,128)(2,1)}, bf16[4,12,24,128]{3,2,1,0:T(8,128)(2,1)S(1)}, u32[]{:S(2)}) copy-start(bf16[4,12,24,128]{3,2,1,0:T(8,128)(2,1)S(1)} %collective-permute-done.23.refs_2_) | copy-start | bytes 884740
  133.5 0.7 copy-start.16
  136.4 35.3 %collective-permute-start.25 = (bf16[4,12,24,128]{3,2,1,0:T(8,128)(2,1)}, bf16[4,12,24,128]{3,2,1,0:T(8,128)(2,1)S(1)}, u32[]{:S(2)}, u32[]{:S(2)}) collective-permute-start(bf16[4,12,24,128]{3,2,1,0:T(8,128)(2,1)} %get-tuple-element.70), channel_id=1, source_target_pairs={{0,8},{2,10},{4,12},{6,14},{8,0},{10,2},{12,4},{14,6},{16,24},{18,... | collective-permute-start | bytes 884744 | tf_op jit(solution)/shard_map/ppermute | solution.py:397
  136.4 35.3 %collective-permute-start.26 = (bf16[4,12,24,128]{3,2,1,0:T(8,128)(2,1)}, bf16[4,12,24,128]{3,2,1,0:T(8,128)(2,1)S(1)}, u32[]{:S(2)}, u32[]{:S(2)}) collective-permute-start(bf16[4,12,24,128]{3,2,1,0:T(8,128)(2,1)} %get-tuple-element.71), channel_id=1, source_target_pairs={{0,16},{2,18},{4,20},{6,22},{8,24},{10,26},{12,28},{14,30},{16,0},... | collective-permute-start | bytes 884744 | tf_op jit(solution)/shard_map/ppermute | solution.py:397
  137.6 29.2 %copy-start.21 = (bf16[4,12,24,128]{3,2,1,0:T(8,128)(2,1)}, bf16[4,12,24,128]{3,2,1,0:T(8,128)(2,1)S(1)}, u32[]{:S(2)}) copy-start(bf16[4,12,24,128]{3,2,1,0:T(8,128)(2,1)S(1)} %collective-permute-done.11.refs_4_) | copy-start | bytes 884740
  137.6 41.9 %collective-permute-start.27 = (bf16[4,12,24,128]{3,2,1,0:T(8,128)(2,1)}, bf16[4,12,24,128]{3,2,1,0:T(8,128)(2,1)S(1)}, u32[]{:S(2)}, u32[]{:S(2)}) collective-permute-start(bf16[4,12,24,128]{3,2,1,0:T(8,128)(2,1)} %get-tuple-element.72), channel_id=1, source_target_pairs={{0,24},{2,26},{4,28},{6,30},{8,16},{10,18},{12,20},{14,22},{16,8},... | collective-permute-start | bytes 884744 | tf_op jit(solution)/shard_map/ppermute | solution.py:397
  146.0 20.9 %copy-start.22 = (bf16[4,12,24,128]{3,2,1,0:T(8,128)(2,1)}, bf16[4,12,24,128]{3,2,1,0:T(8,128)(2,1)S(1)}, u32[]{:S(2)}) copy-start(bf16[4,12,24,128]{3,2,1,0:T(8,128)(2,1)S(1)} %collective-permute-done.12.refs_5_) | copy-start | bytes 884740
  166.9 0.7 copy-start.24
  171.5 26.9 %collective-permute-start.30 = (bf16[12,392,128]{2,1,0:T(8,128)(2,1)}, bf16[12,392,128]{2,1,0:T(8,128)(2,1)S(1)}, u32[]{:S(2)}, u32[]{:S(2)}) collective-permute-start(bf16[12,392,128]{2,1,0:T(8,128)(2,1)} %get-tuple-element.76), channel_id=1, source_target_pairs={{0,1},{1,0},{2,3},{3,2},{4,5},{5,4},{6,7},{7,6},{8,9},{9,8},{10,11... | collective-permute-start | bytes 3612680 | tf_op jit(solution)/shard_map/ppermute | solution.py:397
  171.7 7.8 %copy-start.23 = (bf16[4,12,24,128]{3,2,1,0:T(8,128)(2,1)}, bf16[4,12,24,128]{3,2,1,0:T(8,128)(2,1)S(1)}, u32[]{:S(2)}) copy-start(bf16[4,12,24,128]{3,2,1,0:T(8,128)(2,1)S(1)} %collective-permute-done.25.refs_4_) | copy-start | bytes 884740
  171.7 7.8 %copy-start.25 = (bf16[4,12,24,128]{3,2,1,0:T(8,128)(2,1)}, bf16[4,12,24,128]{3,2,1,0:T(8,128)(2,1)S(1)}, u32[]{:S(2)}) copy-start(bf16[4,12,24,128]{3,2,1,0:T(8,128)(2,1)S(1)} %collective-permute-done.26.refs_5_) | copy-start | bytes 884740
  179.5 0.7 copy-start.26
  184.2 48.5 %collective-permute-start.33 = (bf16[12,392,128]{2,1,0:T(8,128)(2,1)}, bf16[12,392,128]{2,1,0:T(8,128)(2,1)S(1)}, u32[]{:S(2)}, u32[]{:S(2)}) collective-permute-start(bf16[12,392,128]{2,1,0:T(8,128)(2,1)} %get-tuple-element.79), channel_id=1, source_target_pairs={{0,1},{1,0},{2,3},{3,2},{4,5},{5,4},{6,7},{7,6},{8,9},{9,8},{10,11... | collective-permute-start | bytes 3612680 | tf_op jit(solution)/shard_map/ppermute | solution.py:397
  186.5 20.2 %collective-permute-start.14 = (bf16[2,392,128]{2,1,0:T(8,128)(2,1)}, bf16[2,392,128]{2,1,0:T(8,128)(2,1)S(1)}, u32[]{:S(2)}, u32[]{:S(2)}) collective-permute-start(bf16[2,392,128]{2,1,0:T(8,128)(2,1)} %get-tuple-element.58), channel_id=1, source_target_pairs={{0,2},{2,4},{4,6},{6,8},{8,10},{10,12},{12,14},{14,16},{16,18},{18... | collective-permute-start | bytes 602120 | tf_op jit(solution)/shard_map/ppermute | solution.py:489
  190.8 19.0 %collective-permute-start.15 = (bf16[2,392,128]{2,1,0:T(8,128)(2,1)}, bf16[2,392,128]{2,1,0:T(8,128)(2,1)S(1)}, u32[]{:S(2)}, u32[]{:S(2)}) collective-permute-start(bf16[2,392,128]{2,1,0:T(8,128)(2,1)} %get-tuple-element.59), channel_id=1, source_target_pairs={{2,0},{4,2},{6,4},{8,6},{10,8},{12,10},{14,12},{16,14},{18,16},{20... | collective-permute-start | bytes 602120 | tf_op jit(solution)/shard_map/ppermute | solution.py:490
  194.8 23.1 %collective-permute-start.28 = (bf16[2,392,128]{2,1,0:T(8,128)(2,1)}, bf16[2,392,128]{2,1,0:T(8,128)(2,1)S(1)}, u32[]{:S(2)}, u32[]{:S(2)}) collective-permute-start(bf16[2,392,128]{2,1,0:T(8,128)(2,1)} %get-tuple-element.74), channel_id=1, source_target_pairs={{0,2},{2,4},{4,6},{6,8},{8,10},{10,12},{12,14},{14,16},{16,18},{18... | collective-permute-start | bytes 602120 | tf_op jit(solution)/shard_map/ppermute | solution.py:489
  198.4 6.2 %copy-start.2 = (bf16[12,392,128]{2,1,0:T(8,128)(2,1)}, bf16[12,392,128]{2,1,0:T(8,128)(2,1)S(1)}, u32[]{:S(2)}) copy-start(bf16[12,392,128]{2,1,0:T(8,128)(2,1)S(1)} %collective-permute-done.30.wave_ref) | copy-start | bytes 3612676
  198.5 19.5 %collective-permute-start.29 = (bf16[2,392,128]{2,1,0:T(8,128)(2,1)}, bf16[2,392,128]{2,1,0:T(8,128)(2,1)S(1)}, u32[]{:S(2)}, u32[]{:S(2)}) collective-permute-start(bf16[2,392,128]{2,1,0:T(8,128)(2,1)} %get-tuple-element.75), channel_id=1, source_target_pairs={{2,0},{4,2},{6,4},{8,6},{10,8},{12,10},{14,12},{16,14},{18,16},{20... | collective-permute-start | bytes 602120 | tf_op jit(solution)/shard_map/ppermute | solution.py:490
  206.7 5.2 %copy-start.27 = (bf16[2,392,128]{2,1,0:T(8,128)(2,1)}, bf16[2,392,128]{2,1,0:T(8,128)(2,1)S(1)}, u32[]{:S(2)}) copy-start(bf16[2,392,128]{2,1,0:T(8,128)(2,1)S(1)} %collective-permute-done.14.low_ref) | copy-start | bytes 602116
  206.7 18.6 %collective-permute-start.31 = (bf16[2,392,128]{2,1,0:T(8,128)(2,1)}, bf16[2,392,128]{2,1,0:T(8,128)(2,1)S(1)}, u32[]{:S(2)}, u32[]{:S(2)}) collective-permute-start(bf16[2,392,128]{2,1,0:T(8,128)(2,1)} %get-tuple-element.77), channel_id=1, source_target_pairs={{0,2},{2,4},{4,6},{6,8},{8,10},{10,12},{12,14},{14,16},{16,18},{18... | collective-permute-start | bytes 602120 | tf_op jit(solution)/shard_map/ppermute | solution.py:489
  209.8 2.1 copy-start.29
  209.8 15.5 %collective-permute-start.32 = (bf16[2,392,128]{2,1,0:T(8,128)(2,1)}, bf16[2,392,128]{2,1,0:T(8,128)(2,1)S(1)}, u32[]{:S(2)}, u32[]{:S(2)}) collective-permute-start(bf16[2,392,128]{2,1,0:T(8,128)(2,1)} %get-tuple-element.78), channel_id=1, source_target_pairs={{2,0},{4,2},{6,4},{8,6},{10,8},{12,10},{14,12},{16,14},{18,16},{20... | collective-permute-start | bytes 602120 | tf_op jit(solution)/shard_map/ppermute | solution.py:490
  232.7 1.0 copy-start.3
  235.7 6.5 %collective-permute-start.34 = (bf16[2,392,128]{2,1,0:T(8,128)(2,1)}, bf16[2,392,128]{2,1,0:T(8,128)(2,1)S(1)}, u32[]{:S(2)}, u32[]{:S(2)}) collective-permute-start(bf16[2,392,128]{2,1,0:T(8,128)(2,1)} %get-tuple-element.80), channel_id=1, source_target_pairs={{0,2},{2,4},{4,6},{6,8},{8,10},{10,12},{12,14},{14,16},{16,18},{18... | collective-permute-start | bytes 602120 | tf_op jit(solution)/shard_map/ppermute | solution.py:489
  239.3 7.6 %collective-permute-start.35 = (bf16[2,392,128]{2,1,0:T(8,128)(2,1)}, bf16[2,392,128]{2,1,0:T(8,128)(2,1)S(1)}, u32[]{:S(2)}, u32[]{:S(2)}) collective-permute-start(bf16[2,392,128]{2,1,0:T(8,128)(2,1)} %get-tuple-element.81), channel_id=1, source_target_pairs={{2,0},{4,2},{6,4},{8,6},{10,8},{12,10},{14,12},{16,14},{18,16},{20... | collective-permute-start | bytes 602120 | tf_op jit(solution)/shard_map/ppermute | solution.py:490
  242.2 4.7 %copy-start.33 = (bf16[2,392,128]{2,1,0:T(8,128)(2,1)}, bf16[2,392,128]{2,1,0:T(8,128)(2,1)S(1)}, u32[]{:S(2)}) copy-start(bf16[2,392,128]{2,1,0:T(8,128)(2,1)S(1)} %collective-permute-done.34.low_ref) | copy-start | bytes 602116
  (9 other events, 6.3 us)

commit v4 on v3

--- a/solution.py
+++ b/solution.py
@@ -91,17 +91,19 @@
     refs[-1][...] = field_ref[...]
 
 
-def pick(array, index, cw, waits):
+def pick(array, index, cw, begin, rows, waits):
     if not lane_blocks(cw):
-        return lax.dynamic_slice_in_dim(array, index * cw, cw, array.ndim - 1)
-    rows, cols, _ = array.shape
-    step = step_rows(rows, 6)
+        part = lax.slice_in_dim(array, begin, begin + rows, axis=0)
+        return lax.dynamic_slice_in_dim(part, index * cw, cw, array.ndim - 1)
+    cols = array.shape[1]
+    step = step_rows(math.gcd(rows, begin), 6)
+    offset = begin // step
     return pl.pallas_call(
         pick_kernel,
         grid_spec=pltpu.PrefetchScalarGridSpec(
             num_scalar_prefetch=1,
             grid=(rows // step,),
-            in_specs=[pl.BlockSpec((step, cols, cw), lambda t, i: (t, 0, i[0]))]
+            in_specs=[pl.BlockSpec((step, cols, cw), lambda t, i: (t + offset, 0, i[0]))]
             + [any_spec()] * len(waits),
             out_specs=pl.BlockSpec((step, cols, cw), lambda t, i: (t, 0, 0)),
         ),
@@ -111,27 +113,7 @@
     )(index[None], array, *waits)
 
 
-def rows_kernel(count, wave_ref, *refs):
-    first_ref, last_ref = refs[-2:]
-    rows = wave_ref.shape[0]
-    for r in range(HALO):
-        first_ref[r] = wave_ref[r]
-        last_ref[r] = wave_ref[rows - HALO + r]
-
-
-def edge_rows(wave, waits):
-    edge = jax.ShapeDtypeStruct((HALO,) + wave.shape[1:], wave.dtype)
-    return pl.pallas_call(
-        functools.partial(rows_kernel, len(waits)),
-        in_specs=[vmem_spec()] + [any_spec()] * len(waits),
-        out_specs=[vmem_spec()] * 2,
-        out_shape=[edge, edge],
-        compiler_params=pltpu.CompilerParams(vmem_limit_bytes=VMEM_LIMIT),
-        cost_estimate=cost(0, 8 * edge.size),
-    )(wave, *waits)
-
-
-def dft_kernel(lon_count, nz, waits, index_ref, quad_ref, *refs):
+def dft_kernel(lon_count, nz, waits, begin, index_ref, quad_ref, *refs):
     blocks = refs[:lon_count]
     table_ref = refs[lon_count]
     outs = refs[lon_count + 1 + waits :]
@@ -144,23 +126,24 @@
         acc = jnp.dot(table_ref[...], jnp.concatenate(x, axis=0), preferred_element_type=F32)
         for i in range(group):
             t = first + i
-            scaled = acc[:, i * cw : (i + 1) * cw] * quad_ref[step * rows + t]
+            scaled = acc[:, i * cw : (i + 1) * cw] * quad_ref[begin + step * rows + t]
             for d in range(nz):
                 for q in range(NQ):
                     at = (d * NQ + q) * wave_rows
                     outs[d][q, t] = scaled[at : at + wave_rows].astype(BF16)
 
 
-def dft(field, index, received, quad, table, nz, wave_rows, cw, waits):
-    rows, cols, _ = field.shape
-    step = step_rows(rows, 6)
+def dft(field, index, begin, received, quad, table, nz, wave_rows, cw, waits):
+    rows, cols, _ = received[0].shape
+    step = step_rows(math.gcd(rows, begin), 6)
+    offset = begin // step
     lon_count = 1 + len(received)
-    own = pl.BlockSpec((step, cols, cw), lambda t, i: (t, 0, i[0]))
+    own = pl.BlockSpec((step, cols, cw), lambda t, i: (t + offset, 0, i[0]))
     if not lane_blocks(cw):
-        field = pick(field, index, cw, [])
+        field = pick(field, index, cw, begin, rows, [])
         own = pl.BlockSpec((step, cols, cw), lambda t, i: (t, 0, 0))
     return pl.pallas_call(
-        functools.partial(dft_kernel, lon_count, nz, len(waits)),
+        functools.partial(dft_kernel, lon_count, nz, len(waits), begin),
         grid_spec=pltpu.PrefetchScalarGridSpec(
             num_scalar_prefetch=1,
             grid=(rows // step,),
@@ -179,21 +162,34 @@
     )(index[None], quad, field, *received, table, *waits)
 
 
-def regroup_kernel(count, outs, *refs):
-    sources = refs[:count]
+def regroup_kernel(pieces, count, outs, *refs):
     for k, out_ref in enumerate(refs[-outs:]):
-        for i, ref in enumerate(sources):
-            out_ref[i] = ref[k + 1]
-
-
-def regroup(arrays, waits):
-    count = len(arrays)
-    outs = arrays[0].shape[0] - 1
-    shape = (count,) + arrays[0].shape[1:]
+        begin = 0
+        for p in range(pieces):
+            for i, ref in enumerate(refs[p * count : (p + 1) * count]):
+                out_ref[i, begin : begin + ref.shape[1]] = ref[k + 1]
+            begin += refs[p * count].shape[1]
+
+
+def regroup(pieces, waits, part=None):
+    arrays = [array for piece in pieces for array in piece]
+    count = len(pieces[0])
+    outs, _, wave_rows, cw = arrays[0].shape
+    outs -= 1
+    if part is None:
+        rows = sum(piece[0].shape[1] for piece in pieces)
+        specs = [whole_of(a) for a in arrays]
+    else:
+        begin, rows = part
+        block = begin // rows
+        specs = [
+            pl.BlockSpec((outs + 1, rows, wave_rows, cw), lambda t: (0, block, 0, 0))
+        ] * len(arrays)
+    shape = (count, rows, wave_rows, cw)
     return pl.pallas_call(
-        functools.partial(regroup_kernel, count, outs),
+        functools.partial(regroup_kernel, len(pieces), count, outs),
         grid=(1,),
-        in_specs=[whole_of(a) for a in arrays] + [any_spec()] * len(waits),
+        in_specs=specs + [any_spec()] * len(waits),
         out_specs=[pl.BlockSpec(shape, lambda t: (0,) * len(shape))] * outs,
         out_shape=[jax.ShapeDtypeStruct(shape, BF16)] * outs,
         compiler_params=params(),
@@ -201,11 +197,12 @@
     )(*arrays, *waits)
 
 
-def legendre_kernel(nz, waits, *refs):
-    own = refs[:nz]
-    others = refs[nz : nz + NQ - 1]
-    leg_ref, legt_ref, gr_ref, gi_ref = refs[nz + NQ - 1 : nz + NQ + 3]
-    outs = refs[nz + NQ + 3 + waits : -2]
+def legendre_kernel(nz, pieces, waits, *refs):
+    own = refs[: nz * pieces]
+    refs = refs[nz * pieces :]
+    others = refs[: NQ - 1]
+    leg_ref, legt_ref, gr_ref, gi_ref = refs[NQ - 1 : NQ + 3]
+    outs = refs[NQ + 3 + waits : -2]
     wide, result = refs[-2:]
     waves, _, lat = leg_ref.shape
     _, rows, wave_rows, cw = outs[0].shape
@@ -213,8 +210,10 @@
     for q in range(NQ):
         for d in range(nz):
             at = (q * nz + d) * span
-            piece = others[q - 1][d] if q else own[d][0]
-            wide[at : at + span, :] = piece.astype(F32).reshape(span, cw)
+            for piece in [others[q - 1][d]] if q else [a[0] for a in own[d::nz]]:
+                length = piece.shape[0] * wave_rows
+                wide[at : at + length, :] = piece.astype(F32).reshape(length, cw)
+                at += length
     gain_r = gr_ref[...]
     gain_i = gi_ref[...]
     for m in range(waves):
@@ -234,13 +233,14 @@
             outs[q][d] = result[at : at + span, :].reshape(rows, wave_rows, cw).astype(BF16)
 
 
-def legendre_step(own, others, leg, legt, gr, gi, waits):
-    nz = len(own)
-    _, rows, wave_rows, cw = own[0].shape
+def legendre_step(pieces, others, leg, legt, gr, gi, waits):
+    nz = len(pieces[0])
+    own = [array for piece in pieces for array in piece]
+    rows, wave_rows, cw = others[0].shape[1:]
     shape = (nz, rows, wave_rows, cw)
     waves, degrees, lat = leg.shape
     return pl.pallas_call(
-        functools.partial(legendre_kernel, nz, len(waits)),
+        functools.partial(legendre_kernel, nz, len(pieces), len(waits)),
         grid=(1,),
         in_specs=[first_of(a, 1) for a in own]
         + [whole_of(a) for a in (*others, leg, legt, gr, gi)]
@@ -253,11 +253,12 @@
     )(*own, *others, leg, legt, gr, gi, *waits)
 
 
-def inverse_kernel(nz, lon_count, *refs):
+def inverse_kernel(nz, lon_count, edges_of, *refs):
     near = refs[:NQ]
     far = refs[NQ : NQ + nz - 1]
     table_ref = refs[NQ + nz - 1]
     outs = refs[NQ + nz : NQ + nz + lon_count]
+    edges = refs[NQ + nz + lon_count : -1]
     wide = refs[-1]
     rows, _, cw = wide.shape
     wave_rows = near[0].shape[-2]
@@ -276,30 +277,49 @@
             for s in range(lon_count):
                 piece = acc[s * cols : (s + 1) * cols, i * cw : (i + 1) * cw]
                 outs[s][first + i] = piece.astype(BF16)
-
-
-def inverse(near, far, table, lon_count):
+    step = pl.program_id(0)
+    for e, is_last in enumerate(edges_of):
+
+        @pl.when(step == (pl.num_programs(0) - 1 if is_last else 0))
+        def _(e=e, begin=rows - HALO if is_last else 0):
+            for s in range(lon_count):
+                edges[e * lon_count + s][...] = outs[s][begin : begin + HALO]
+
+
+def inverse(near, far, table, lon_count, begin):
     nz = len(far) + 1
-    _, rows, wave_rows, cw = near[0].shape
-    step = step_rows(rows, 6)
+    _, total, wave_rows, cw = near[0].shape
+    rows = far[0].shape[1]
+    step = step_rows(math.gcd(rows, begin), 6)
+    offset = begin // step
     cols = table.shape[0] // lon_count
-    specs = [pl.BlockSpec((1, step, wave_rows, cw), lambda t: (0, t, 0, 0))] * NQ
+    edges_of = [last for last, there in ((False, begin == 0), (True, begin + rows == total)) if there]
+    specs = [pl.BlockSpec((1, step, wave_rows, cw), lambda t: (0, t + offset, 0, 0))] * NQ
     specs += [pl.BlockSpec((NQ, step, wave_rows, cw), lambda t: (0, t, 0, 0))] * (nz - 1)
-    return pl.pallas_call(
-        functools.partial(inverse_kernel, nz, lon_count),
+    extra = lon_count * len(edges_of)
+    outs = pl.pallas_call(
+        functools.partial(inverse_kernel, nz, lon_count, edges_of),
         grid=(rows // step,),
         in_specs=specs + [whole_of(table)],
-        out_specs=[pl.BlockSpec((step, cols, cw), lambda t: (t, 0, 0))] * lon_count,
-        out_shape=[jax.ShapeDtypeStruct((rows, cols, cw), BF16)] * lon_count,
+        out_specs=[pl.BlockSpec((step, cols, cw), lambda t: (t, 0, 0))] * lon_count
+        + [pl.BlockSpec((HALO, cols, cw), lambda t: (0, 0, 0))] * extra,
+        out_shape=[jax.ShapeDtypeStruct((rows, cols, cw), BF16)] * lon_count
+        + [jax.ShapeDtypeStruct((HALO, cols, cw), BF16)] * extra,
         scratch_shapes=[pltpu.VMEM((step, nz * NQ * wave_rows, cw), F32)],
         compiler_params=params(),
         cost_estimate=cost(0, 14000000),
     )(*near, *far, table)
-
-
-def window_kernel(cols, place_ref, neighbour_ref, basis_ref, quad_ref, wave_ref, low_ref, high_ref, disco_ref, out_ref, ring):
+    edges = {
+        last: outs[lon_count * (1 + e) : lon_count * (2 + e)] for e, last in enumerate(edges_of)
+    }
+    return outs[:lon_count], edges
+
+
+def window_kernel(cols, place_ref, neighbour_ref, basis_ref, quad_ref, low_ref, high_ref, disco_ref, *refs):
+    pieces = refs[:-2]
+    out_ref, ring = refs[-2:]
     step = pl.program_id(0)
-    rows = wave_ref.shape[0]
+    rows = ring.shape[0] - 2 * HALO
     slots = neighbour_ref.shape[1]
     per_step = out_ref.shape[0]
     group = place_ref[0]
@@ -308,15 +328,16 @@
     def _():
         for r in range(HALO):
             ring[r] = low_ref[r].astype(F32)
-            ring[HALO + r] = wave_ref[r].astype(F32)
             ring[rows + HALO + r] = high_ref[r].astype(F32)
-
-    for i in range(per_step):
-        t = step * per_step + i
-
-        @pl.when(t + HALO < rows)
-        def _(t=t):
-            ring[t + 2 * HALO] = wave_ref[t + HALO].astype(F32)
+        begin = HALO
+        for piece in pieces:
+
+            def widen(r, carry, piece=piece, begin=begin):
+                ring[begin + r] = piece[r].astype(F32)
+                return carry
+
+            lax.fori_loop(0, piece.shape[0], widen, 0)
+            begin += piece.shape[0]
 
     tile = 48 if cols % 48 == 0 else 8
     for i in range(per_step):
@@ -333,19 +354,20 @@
             out_ref[i, pl.ds(at, tile), :] = acc.astype(BF16)
 
 
-def window(place, neighbour, basis, quad, wave, low, high, disco, cols):
-    rows, padded, cw = wave.shape
+def window(place, neighbour, basis, quad, low, high, disco, pieces, cols):
+    rows = sum(piece.shape[0] for piece in pieces)
+    _, padded, cw = low.shape
     per_step = step_rows(rows, 2)
     return pl.pallas_call(
         functools.partial(window_kernel, cols),
         grid=(rows // per_step,),
-        in_specs=[smem_spec()] * 4 + [whole_of(a) for a in (wave, low, high, disco)],
+        in_specs=[smem_spec()] * 4 + [whole_of(a) for a in (low, high, disco, *pieces)],
         out_specs=pl.BlockSpec((per_step, cols, cw), lambda t: (t, 0, 0)),
         out_shape=jax.ShapeDtypeStruct((rows, cols, cw), BF16),
         scratch_shapes=[pltpu.VMEM((rows + 2 * HALO, padded, cw), F32)],
         compiler_params=params(),
         cost_estimate=cost(0, 20000000),
-    )(place, neighbour, basis, quad, wave, low, high, disco)
+    )(place, neighbour, basis, quad, low, high, disco, *pieces)
 
 
 def mlp_kernel(place_ref, *refs):
@@ -481,57 +503,66 @@
 
     disco = disco_weight.reshape(disco_weight.shape[0], lon_count * nch, cw)
     disco = jnp.transpose(disco, (1, 0, 2))
-    up = [(i, i + 1) for i in range(lat_count - 1)]
-    down = [(i + 1, i) for i in range(lat_count - 1)]
-
-    def convolved(wave, s, j, waits):
-        first, last = edge_rows(wave, waits)
-        low = lax.ppermute(last, "lat", up)
-        high = lax.ppermute(first, "lat", down)
-        place = ((lon_id ^ s) * nch + j).astype(jnp.int32)
-        done = window(
-            place[None], neighbour, basis, disco_quad, wave, low, high, disco, cols
-        )
-        return place, done
+    def to_row(edge, s, shift):
+        pairs = [
+            (lat * lon_count + lon, (lat + shift) * lon_count + (lon ^ s))
+            for lat in range(lat_count)
+            for lon in range(lon_count)
+            if 0 <= lat + shift < lat_count
+        ]
+        return lax.ppermute(edge, ("lat", "lon"), pairs)
 
     def channel_index(s, j):
         return ((lon_id ^ s) * nch + j).astype(jnp.int32)
 
-    received, waits = [], []
+    gains = [(chunk_of(filter_real, 0, j), chunk_of(filter_imag, 0, j)) for j in range(nch)]
+    half = rows // 2 if rows % 2 == 0 and nch > 1 else rows
+    pieces = [(begin, half) for begin in range(0, rows, half)]
+    order = [(j, begin, length) for j in range(nch) for begin, length in pieces]
+
+    def exchange(k, waits):
+        j, begin, length = order[k]
+        return [
+            swap(pick(field, channel_index(s, j), cw, begin, length, waits), "lon", s)
+            for s in range(1, lon_count)
+        ]
+
+    received = [exchange(k, [fwd] * k) for k in range(min(2, len(order)))]
+    spectra = [[] for _ in range(nch)]
+    waits = [leg, legt, inv] + [gain for pair in gains for gain in pair]
+    for k, (j, begin, length) in enumerate(order):
+        arrays = dft(
+            field, channel_index(0, j), begin, received[k], quad_weight, fwd, nz, wave_rows, cw, waits
+        )
+        if k + 2 < len(order):
+            received.append(exchange(k + 2, arrays[:1] if k else received[0]))
+        waits = along(arrays[1:])
+        spectra[j].append([arrays[0]] + waits)
+    near = []
+    gather_waits, waits = [], [arrays[0]]
     for j in range(nch):
-        received.append(
-            [
-                swap(pick(field, channel_index(s, j), cw, waits), "lon", s)
-                for s in range(1, lon_count)
-            ]
-        )
-        waits = [fwd]
-    spectra, waits = [], []
+        across_in = across(regroup(spectra[j], gather_waits))
+        full = legendre_step(spectra[j], across_in, leg, legt, *gains[j], waits)
+        near.append([full[0]] + across(full[1:]))
+        gather_waits, waits = [full[0]], []
+    groups = []
     for j in range(nch):
-        arrays = dft(
-            field, channel_index(0, j), received[j], quad_weight, fwd, nz, wave_rows, cw, waits
-        )
-        spectra.append([arrays[0]] + along(arrays[1:]))
-        waits = [spectra[-1][1]]
-        latest = arrays[0]
-    near = []
-    waits = [latest]
-    for j in range(nch):
-        gr = chunk_of(filter_real, 0, j)
-        gi = chunk_of(filter_imag, 0, j)
-        full = legendre_step(
-            spectra[j], across(regroup(spectra[j], waits)), leg, legt, gr, gi, []
-        )
-        near.append([full[0]] + across(full[1:]))
-        waits = []
-    parts = []
-    for j in range(nch):
-        parts.append(inverse(near[j], along(regroup(near[j], [])), inv, lon_count))
-    groups = [convolved(parts[j][0], 0, j, []) for j in range(nch)]
-    for j in range(nch):
-        waits = [done for _, done in groups] if j == nch - 1 else []
-        for s in range(1, lon_count):
-            groups.append(convolved(swap(parts[j][s], "lon", s), s, j, waits))
+        waves = [[] for _ in range(lon_count)]
+        edges = {}
+        for begin, length in [(0, rows)]:
+            far = along(regroup([near[j]], [], (begin, length)))
+            parts, new_edges = inverse(near[j], far, inv, lon_count, begin)
+            edges.update(new_edges)
+            for s in range(lon_count):
+                waves[s].append(swap(parts[s], "lon", s) if s else parts[0])
+        for s in range(lon_count):
+            low = to_row(edges[True][s], s, 1)
+            high = to_row(edges[False][s], s, -1)
+            place = channel_index(s, j)
+            done = window(
+                place[None], neighbour, basis, disco_quad, low, high, disco, waves[s], cols
+            )
+            groups.append((place, done))
     block_out, spatial = mlp(
         jnp.stack([place for place, _ in groups]),
         [done for _, done in groups],

time: 274 us -> 301 us (1.099)
  waiting for transfers between devices: 107 us -> 128 us
  starting transfers between devices: 54.7 us -> 58.1 us
    ppermute x8, waiting for transfers between devices: 5.03 us -> 29.3 us  [to_row(): return lax.ppermute(edge, ('lat', 'lon'), pairs)]
    ppermute x28 -> x36, starting transfers between devices: 28 us -> 32.6 us  [swap(): return lax.ppermute(array, axis, [(i, i ^ mask) for i in range(count)])]
    pallas_call x2 -> x4, Pallas kernels: 4.36 us -> 7.97 us  [pick(): pl.pallas_call(pick_kernel, grid_spec=pltpu.PrefetchScalarGridSpec(num_sc...]
    ppermute x28 -> x36, waiting for transfers between devices: 102 us -> 98.9 us  [swap(): return lax.ppermute(array, axis, [(i, i ^ mask) for i in range(count)])]
    pallas_call x14 -> x12, Pallas kernels: 40.4 us -> 37.5 us  [the longest x4 11.3 us: dft(): pl.pallas_call(functools.partial(dft_kernel, lon_count, nz, len(waits), b...]
    unnamed x74 -> x122, local copies, waits for them, and re-layouts: 11.3 us -> 12.5 us
  transfers between devices with their start and end apart: 36 -> 44, of which waited for: 12 -> 20; matrix products, arithmetic and copies ran while one was open for 4% -> 3% of each run, Pallas kernels for 22% -> 20%
where the time goes in v4:
time: 301 us; the launch traced here: 297 us
  waiting for transfers between devices  128 us (43%)
  Pallas kernels  88.2 us (29%)
  starting transfers between devices  58.1 us (19%)
  local copies, waits for them, and re-layouts  15 us (5%)
  matrix products  4.21 us (1%)
    ppermute x36, waiting for transfers between devices, swap(): return lax.ppermute(array, axis, [(i, i ^ mask) for i in range(count)])  98.9 us
    ppermute x36, starting transfers between devices, swap(): return lax.ppermute(array, axis, [(i, i ^ mask) for i in range(count)])  32.6 us
    ppermute x8, waiting for transfers between devices, to_row(): return lax.ppermute(edge, ('lat', 'lon'), pairs)  29.3 us
    ppermute x8, starting transfers between devices, to_row(): return lax.ppermute(edge, ('lat', 'lon'), pairs)  25.5 us
    pallas_call x4, Pallas kernels, window(): pl.pallas_call(functools.partial(window_kernel, cols), grid=(rows // per_...  25 us
    pallas_call x1, Pallas kernels, mlp(): pl.pallas_call(mlp_kernel, grid=(rows // per_step,), in_specs=[smem_spec(...  17.8 us
    unnamed x122, local copies, waits for them, and re-layouts  12.5 us
    pallas_call x4, Pallas kernels, dft(): pl.pallas_call(functools.partial(dft_kernel, lon_count, nz, len(waits), b...  11.3 us
  transfers between devices with their start and end apart: 44, of which 20 were waited for; matrix products, arithmetic and copies ran while one was open for 3% of the time, Pallas kernels for 20%

profile of v4, /device:TPU:19, one launch (start us, length us, event | category | flops | bytes accessed | tf_op | source)
XLA Modules:
  0.0 297.5 jit_solution(4902193559521994908)
XLA Ops:
  0.7 2.1 shard_map.194
  4.9 1.9 shard_map.196
  8.8 1.5 copy.23.refs_3_.refs_11_
  10.3 1.5 convolution_convert_fusion.2
  11.8 1.5 convolution_convert_fusion.1
  14.1 3.0 %collective-permute-done.refs_1_.refs_0_ = bf16[6,384,128]{2,1,0:T(8,128)(2,1)S(1)} collective-permute-done((bf16[6,384,128]{2,1,0:T(8,128)(2,1)}, bf16[6,384,128]{2,1,0:T(8,128)(2,1)S(1)}, u32[]{:S(2)}, u32[]{:S(2)}) %collective-permute-start) | collective-permute-done | bytes 589856 | tf_op jit(solution)/shard_map/ppermute | solution.py:419
  18.0 2.0 shard_map.200
  21.0 2.9 shard_map.195
  23.9 1.3 collective-permute-start.1
  25.2 1.3 collective-permute-start.3
  26.5 3.3 %collective-permute-done.4.refs_1_ = bf16[6,384,128]{2,1,0:T(8,128)(2,1)S(1)} collective-permute-done((bf16[6,384,128]{2,1,0:T(8,128)(2,1)}, bf16[6,384,128]{2,1,0:T(8,128)(2,1)S(1)}, u32[]{:S(2)}, u32[]{:S(2)}) %collective-permute-start.4) | collective-permute-done | bytes 589856 | tf_op jit(solution)/shard_map/ppermute | solution.py:419
  30.8 8.0 %collective-permute-done.3.refs_5_.refs_3_ = bf16[4,6,24,128]{3,2,1,0:T(8,128)(2,1)S(1)} collective-permute-done((bf16[4,6,24,128]{3,2,1,0:T(8,128)(2,1)}, bf16[4,6,24,128]{3,2,1,0:T(8,128)(2,1)S(1)}, u32[]{:S(2)}, u32[]{:S(2)}) %collective-permute-start.3) | collective-permute-done | bytes 147488 | tf_op jit(solution)/shard_map/ppermute | solution.py:419
  39.5 2.8 shard_map.197
  42.3 2.0 shard_map.199
  45.5 1.2 collective-permute-start.6
  46.8 1.4 collective-permute-start.7
  48.2 1.3 collective-permute-done.5.refs_5_.refs_3_
  49.5 1.5 collective-permute-done.6.refs_6_.refs_4_
  51.0 10.1 %collective-permute-done.7.refs_7_.refs_5_ = bf16[4,6,24,128]{3,2,1,0:T(8,128)(2,1)S(1)} collective-permute-done((bf16[4,6,24,128]{3,2,1,0:T(8,128)(2,1)S(1)}, bf16[4,6,24,128]{3,2,1,0:T(8,128)(2,1)S(1)}, u32[]{:S(2)}, u32[]{:S(2)}) %collective-permute-start.7) | collective-permute-done | bytes 147488 | tf_op jit(solution)/shard_map/ppermute | solution.py:419
  62.0 2.8 shard_map.201
  65.2 2.3 shard_map.198
  67.5 2.7 collective-permute-start.8
  70.2 1.4 collective-permute-start.15
  71.7 1.2 collective-permute-start.9
  72.9 2.1 collective-permute-start.10
  75.0 5.3 %collective-permute-done.15.refs_5_.refs_3_ = bf16[4,6,24,128]{3,2,1,0:T(8,128)(2,1)S(1)} collective-permute-done((bf16[4,6,24,128]{3,2,1,0:T(8,128)(2,1)S(1)}, bf16[4,6,24,128]{3,2,1,0:T(8,128)(2,1)S(1)}, u32[]{:S(2)}, u32[]{:S(2)}) %collective-permute-start.15) | collective-permute-done | bytes 147488 | tf_op jit(solution)/shard_map/ppermute | solution.py:419
  81.8 2.8 shard_map.202
  84.7 1.4 collective-permute-start.27
  88.1 4.2 %shard_map.203 = (bf16[4,12,24,128]{3,2,1,0:T(8,128)(2,1)}, bf16[4,12,24,128]{3,2,1,0:T(8,128)(2,1)}, bf16[4,12,24,128]{3,2,1,0:T(8,128)(2,1)}, bf16[4,12,24,128]{3,2,1,0:T(8,128)(2,1)}) custom-call(bf16[4,6,24,128]{3,2,1,0:T(8,128)(2,1)} %get-tuple-element.50.refs_0_, bf16[4,6,24,128]{3,2,1,0:T(8,128)(2,1)} %copy-done.3, bf16[4,6,24,128]{3,2,1,0:T(8,128)(2,1)} %copy-done.5, ...), custom_call_target="tpu_custom_call" | custom-call | bytes 14000000 | tf_op jit(solution)/shard_map/pallas_call | solution.py:242
  92.4 4.3 %collective-permute-done.28.refs_6_ = bf16[4,6,24,128]{3,2,1,0:T(8,128)(2,1)S(1)} collective-permute-done((bf16[4,6,24,128]{3,2,1,0:T(8,128)(2,1)}, bf16[4,6,24,128]{3,2,1,0:T(8,128)(2,1)S(1)}, u32[]{:S(2)}, u32[]{:S(2)}) %collective-permute-start.28) | collective-permute-done | bytes 147488 | tf_op jit(solution)/shard_map/ppermute | solution.py:419
  96.7 3.3 %collective-permute-done.29.refs_7_ = bf16[4,6,24,128]{3,2,1,0:T(8,128)(2,1)S(1)} collective-permute-done((bf16[4,6,24,128]{3,2,1,0:T(8,128)(2,1)}, bf16[4,6,24,128]{3,2,1,0:T(8,128)(2,1)S(1)}, u32[]{:S(2)}, u32[]{:S(2)}) %collective-permute-start.29) | collective-permute-done | bytes 147488 | tf_op jit(solution)/shard_map/ppermute | solution.py:419
  100.6 2.3 shard_map.208
  102.9 1.9 collective-permute-start.30
  104.8 1.2 collective-permute-start.31
  106.7 1.2 collective-permute-start.17
  108.7 5.0 %collective-permute-done.31.refs_9_ = bf16[4,12,24,128]{3,2,1,0:T(8,128)(2,1)S(1)} collective-permute-done((bf16[4,12,24,128]{3,2,1,0:T(8,128)(2,1)}, bf16[4,12,24,128]{3,2,1,0:T(8,128)(2,1)S(1)}, u32[]{:S(2)}, u32[]{:S(2)}) %collective-permute-start.31) | collective-permute-done | bytes 294944 | tf_op jit(solution)/shard_map/ppermute | solution.py:419
  113.7 6.8 %collective-permute-done.32.refs_10_ = bf16[4,12,24,128]{3,2,1,0:T(8,128)(2,1)S(1)} collective-permute-done((bf16[4,12,24,128]{3,2,1,0:T(8,128)(2,1)}, bf16[4,12,24,128]{3,2,1,0:T(8,128)(2,1)S(1)}, u32[]{:S(2)}, u32[]{:S(2)}) %collective-permute-start.32) | collective-permute-done | bytes 294944 | tf_op jit(solution)/shard_map/ppermute | solution.py:419
  121.2 4.3 %shard_map.209 = (bf16[4,12,24,128]{3,2,1,0:T(8,128)(2,1)}, bf16[4,12,24,128]{3,2,1,0:T(8,128)(2,1)}, bf16[4,12,24,128]{3,2,1,0:T(8,128)(2,1)}, bf16[4,12,24,128]{3,2,1,0:T(8,128)(2,1)}) custom-call(bf16[4,6,24,128]{3,2,1,0:T(8,128)(2,1)} %get-tuple-element.78.refs_0_, bf16[4,6,24,128]{3,2,1,0:T(8,128)(2,1)} %copy-done.4, bf16[4,6,24,128]{3,2,1,0:T(8,128)(2,1)} %copy-done.6, ...), custom_call_target="tpu_custom_call" | custom-call | bytes 14000000 | tf_op jit(solution)/shard_map/pallas_call | solution.py:242
  125.5 1.3 collective-permute-start.34
  127.6 5.5 %collective-permute-done.18.refs_3_ = bf16[4,12,24,128]{3,2,1,0:T(8,128)(2,1)S(1)} collective-permute-done((bf16[4,12,24,128]{3,2,1,0:T(8,128)(2,1)S(1)}, bf16[4,12,24,128]{3,2,1,0:T(8,128)(2,1)S(1)}, u32[]{:S(2)}, u32[]{:S(2)}) %collective-permute-start.18) | collective-permute-done | bytes 294944 | tf_op jit(solution)/shard_map/ppermute | solution.py:419
  133.8 2.1 shard_map.204
  136.0 2.4 collective-permute-start.20
  138.9 6.6 %collective-permute-done.35.refs_3_ = bf16[4,12,24,128]{3,2,1,0:T(8,128)(2,1)S(1)} collective-permute-done((bf16[4,12,24,128]{3,2,1,0:T(8,128)(2,1)}, bf16[4,12,24,128]{3,2,1,0:T(8,128)(2,1)S(1)}, u32[]{:S(2)}, u32[]{:S(2)}) %collective-permute-start.35) | collective-permute-done | bytes 294944 | tf_op jit(solution)/shard_map/ppermute | solution.py:419
  146.2 2.2 shard_map.210
  148.4 2.5 collective-permute-start.37
  151.0 6.4 %collective-permute-done.20.refs_5_ = bf16[4,12,24,128]{3,2,1,0:T(8,128)(2,1)S(1)} collective-permute-done((bf16[4,12,24,128]{3,2,1,0:T(8,128)(2,1)}, bf16[4,12,24,128]{3,2,1,0:T(8,128)(2,1)S(1)}, u32[]{:S(2)}, u32[]{:S(2)}) %collective-permute-start.20) | collective-permute-done | bytes 294944 | tf_op jit(solution)/shard_map/ppermute | solution.py:419
  157.4 19.0 %collective-permute-done.21.refs_6_ = bf16[4,12,24,128]{3,2,1,0:T(8,128)(2,1)S(1)} collective-permute-done((bf16[4,12,24,128]{3,2,1,0:T(8,128)(2,1)}, bf16[4,12,24,128]{3,2,1,0:T(8,128)(2,1)S(1)}, u32[]{:S(2)}, u32[]{:S(2)}) %collective-permute-start.21) | collective-permute-done | bytes 294944 | tf_op jit(solution)/shard_map/ppermute | solution.py:419
  177.2 4.3 %shard_map.205 = (bf16[12,392,128]{2,1,0:T(8,128)(2,1)}, bf16[12,392,128]{2,1,0:T(8,128)(2,1)}, bf16[2,392,128]{2,1,0:T(8,128)(2,1)}, bf16[2,392,128]{2,1,0:T(8,...) custom-call(bf16[4,12,24,128]{3,2,1,0:T(8,128)(2,1)} %get-tuple-element.65.refs_0_.refs_8_, ...), custom_call_target="tpu_custom_call" | custom-call | bytes 14000000 | tf_op jit(solution)/shard_map/pallas_call | solution.py:300
  182.9 7.2 %collective-permute-done.38.refs_6_ = bf16[4,12,24,128]{3,2,1,0:T(8,128)(2,1)S(1)} collective-permute-done((bf16[4,12,24,128]{3,2,1,0:T(8,128)(2,1)}, bf16[4,12,24,128]{3,2,1,0:T(8,128)(2,1)S(1)}, u32[]{:S(2)}, u32[]{:S(2)}) %collective-permute-start.38) | collective-permute-done | bytes 294944 | tf_op jit(solution)/shard_map/ppermute | solution.py:419
  190.8 4.4 %shard_map.211 = (bf16[12,392,128]{2,1,0:T(8,128)(2,1)}, bf16[12,392,128]{2,1,0:T(8,128)(2,1)}, bf16[2,392,128]{2,1,0:T(8,128)(2,1)}, bf16[2,392,128]{2,1,0:T(8,...) custom-call(bf16[4,12,24,128]{3,2,1,0:T(8,128)(2,1)} %get-tuple-element.85.refs_0_, ...), custom_call_target="tpu_custom_call" | custom-call | bytes 14000000 | tf_op jit(solution)/shard_map/pallas_call | solution.py:300
  195.6 4.3 %collective-permute-start.22 = (bf16[2,392,128]{2,1,0:T(8,128)(2,1)S(1)}, bf16[2,392,128]{2,1,0:T(8,128)(2,1)S(1)}, u32[]{:S(2)}, u32[]{:S(2)}) collective-permute-start(bf16[2,392,128]{2,1,0:T(8,128)(2,1)S(1)} %copy-done.55), channel_id=1, source_target_pairs={{0,2},{1,3},{2,4},{3,5},{4,6},{5,7},{6,8},{7,9},{8,10},{9,11},{10,... | collective-permute-start | bytes 602120 | tf_op jit(solution)/shard_map/ppermute | solution.py:513
  199.9 1.9 collective-permute-start.23
  201.9 4.6 %collective-permute-start.24 = (bf16[2,392,128]{2,1,0:T(8,128)(2,1)S(1)}, bf16[2,392,128]{2,1,0:T(8,128)(2,1)S(1)}, u32[]{:S(2)}, u32[]{:S(2)}) collective-permute-start(bf16[2,392,128]{2,1,0:T(8,128)(2,1)S(1)} %copy-done.53), channel_id=1, source_target_pairs={{0,3},{1,2},{2,5},{3,4},{4,7},{5,6},{6,9},{7,8},{8,11},{9,10},{10,... | collective-permute-start | bytes 602120 | tf_op jit(solution)/shard_map/ppermute | solution.py:513
  206.4 1.9 collective-permute-start.39
  208.4 2.4 collective-permute-start.40
  210.8 29.3 %collective-permute-done.24.low_ref = bf16[2,392,128]{2,1,0:T(8,128)(2,1)S(1)} collective-permute-done((bf16[2,392,128]{2,1,0:T(8,128)(2,1)S(1)}, bf16[2,392,128]{2,1,0:T(8,128)(2,1)S(1)}, u32[]{:S(2)}, u32[]{:S(2)}) %collective-permute-start.24) | collective-permute-done | bytes 200736 | tf_op jit(solution)/shard_map/ppermute | solution.py:513
  240.1 1.9 collective-permute-start.25
  242.1 4.5 %collective-permute-start.41 = (bf16[2,392,128]{2,1,0:T(8,128)(2,1)}, bf16[2,392,128]{2,1,0:T(8,128)(2,1)S(1)}, u32[]{:S(2)}, u32[]{:S(2)}) collective-permute-start(bf16[2,392,128]{2,1,0:T(8,128)(2,1)} %get-tuple-element.95), channel_id=1, source_target_pairs={{0,3},{1,2},{2,5},{3,4},{4,7},{5,6},{6,9},{7,8},{8,11},{9,10},{10,... | collective-permute-start | bytes 602120 | tf_op jit(solution)/shard_map/ppermute | solution.py:513
  246.7 3.9 %collective-permute-start.42 = (bf16[2,392,128]{2,1,0:T(8,128)(2,1)}, bf16[2,392,128]{2,1,0:T(8,128)(2,1)S(1)}, u32[]{:S(2)}, u32[]{:S(2)}) collective-permute-start(bf16[2,392,128]{2,1,0:T(8,128)(2,1)} %get-tuple-element.96), channel_id=1, source_target_pairs={{2,1},{3,0},{4,3},{5,2},{6,5},{7,4},{8,7},{9,6},{10,9},{11,8},{12,... | collective-permute-start | bytes 602120 | tf_op jit(solution)/shard_map/ppermute | solution.py:513
  251.2 6.4 %shard_map.206.refs_0_ = bf16[12,384,128]{2,1,0:T(8,128)(2,1)} custom-call(s32[1]{0:T(128)} %bitcast.index_ref.place_ref, s32[12,12]{1,0:T(8,128)} %neighbour_ref.7, s32[12,12]{1,0:T(8,128)} %basis_ref.7, f32[12,12]{1,0:T(8,128)} %quad_ref.15, bf16[2,392,128]{2,1,0:T(8,128)(2,1)} %copy-done.39, bf16[2,392,128]{2,1,0:T(8,128)(2,1)} %copy-done.40, ...), custom_call_target="tpu_custom_call" | custom-call | bytes 20000000 | tf_op jit(solution)/shard_map/pallas_call | solution.py:361
  257.6 6.2 %shard_map.212.refs_2_ = bf16[12,384,128]{2,1,0:T(8,128)(2,1)} custom-call(s32[1]{0:T(128)} %bitcast.2.index_ref.place_ref, s32[12,12]{1,0:T(8,128)} %neighbour_ref.7, s32[12,12]{1,0:T(8,128)} %basis_ref.7, f32[12,12]{1,0:T(8,128)} %quad_ref.15, bf16[2,392,128]{2,1,0:T(8,128)(2,1)} %copy-done.42, bf16[2,392,128]{2,1,0:T(8,128)(2,1)} %copy-done.45, ...), custom_call_target="tpu_custom_call" | custom-call | bytes 20000000 | tf_op jit(solution)/shard_map/pallas_call | solution.py:361
  265.5 6.2 %shard_map.207.refs_1_ = bf16[12,384,128]{2,1,0:T(8,128)(2,1)} custom-call(s32[1]{0:T(128)} %bitcast.1.index_ref.place_ref, s32[12,12]{1,0:T(8,128)} %neighbour_ref.7, s32[12,12]{1,0:T(8,128)} %basis_ref.7, f32[12,12]{1,0:T(8,128)} %quad_ref.15, bf16[2,392,128]{2,1,0:T(8,128)(2,1)} %copy-done.38, bf16[2,392,128]{2,1,0:T(8,128)(2,1)} %copy-done.44, ...), custom_call_target="tpu_custom_call" | custom-call | bytes 20000000 | tf_op jit(solution)/shard_map/pallas_call | solution.py:361
  273.5 6.2 %shard_map.213.refs_3_ = bf16[12,384,128]{2,1,0:T(8,128)(2,1)} custom-call(s32[1]{0:T(128)} %bitcast.3.index_ref.place_ref, s32[12,12]{1,0:T(8,128)} %neighbour_ref.7, s32[12,12]{1,0:T(8,128)} %basis_ref.7, f32[12,12]{1,0:T(8,128)} %quad_ref.15, bf16[2,392,128]{2,1,0:T(8,128)(2,1)} %copy-done.41, bf16[2,392,128]{2,1,0:T(8,128)(2,1)} %copy-done.43, ...), custom_call_target="tpu_custom_call" | custom-call | bytes 20000000 | tf_op jit(solution)/shard_map/pallas_call | solution.py:361
  279.7 17.8 %shard_map.214 = (bf16[12,384,512]{2,1,0:T(8,128)(2,1)}, bf16[12,384,512]{2,1,0:T(8,128)(2,1)}) custom-call(s32[4]{0:T(128)} %pad_add_fusion.place_ref, bf16[12,384,128]{2,1,0:T(8,128)(2,1)} %shard_map.206.refs_0_, bf16[12,384,128]{2,1,0:T(8,128)(2,1)} %shard_map.207.refs_1_, bf16[12,384,128]{2,1,0:T(8,128)(2,1)} %shard_map.212.refs_2_, ...), custom_call_target="tpu_custom_call" | custom-call | flops 9663676416 | bytes 18874368 | tf_op jit(solution)/shard_map/pallas_call | solution.py:400
  (184 shorter events, 27.7 us)
Async XLA Ops:
  2.7 14.4 %collective-permute-start = (bf16[6,384,128]{2,1,0:T(8,128)(2,1)}, bf16[6,384,128]{2,1,0:T(8,128)(2,1)S(1)}, u32[]{:S(2)}, u32[]{:S(2)}) collective-permute-start(bf16[6,384,128]{2,1,0:T(8,128)(2,1)} %shard_map.194), channel_id=1, source_target_pairs={{0,1},{1,0},{2,3},{3,2},{4,5},{5,4},{6,7},{7,6},{8,9},{9,8},{10,11... | collective-permute-start | bytes 1769480 | tf_op jit(solution)/shard_map/ppermute | solution.py:419
  6.8 23.0 %collective-permute-start.4 = (bf16[6,384,128]{2,1,0:T(8,128)(2,1)}, bf16[6,384,128]{2,1,0:T(8,128)(2,1)S(1)}, u32[]{:S(2)}, u32[]{:S(2)}) collective-permute-start(bf16[6,384,128]{2,1,0:T(8,128)(2,1)} %shard_map.196), channel_id=1, source_target_pairs={{0,1},{1,0},{2,3},{3,2},{4,5},{5,4},{6,7},{7,6},{8,9},{9,8},{10,11... | collective-permute-start | bytes 1769480 | tf_op jit(solution)/shard_map/ppermute | solution.py:419
  20.0 41.1 %collective-permute-start.12 = (bf16[6,384,128]{2,1,0:T(8,128)(2,1)}, bf16[6,384,128]{2,1,0:T(8,128)(2,1)S(1)}, u32[]{:S(2)}, u32[]{:S(2)}) collective-permute-start(bf16[6,384,128]{2,1,0:T(8,128)(2,1)} %shard_map.200), channel_id=1, source_target_pairs={{0,1},{1,0},{2,3},{3,2},{4,5},{5,4},{6,7},{7,6},{8,9},{9,8},{10,11... | collective-permute-start | bytes 1769480 | tf_op jit(solution)/shard_map/ppermute | solution.py:419
  23.9 5.9 %collective-permute-start.1 = (bf16[4,6,24,128]{3,2,1,0:T(8,128)(2,1)}, bf16[4,6,24,128]{3,2,1,0:T(8,128)(2,1)S(1)}, u32[]{:S(2)}, u32[]{:S(2)}) collective-permute-start(bf16[4,6,24,128]{3,2,1,0:T(8,128)(2,1)} %get-tuple-element.51), channel_id=1, source_target_pairs={{0,8},{2,10},{4,12},{6,14},{8,0},{10,2},{12,4},{14,6},{16,24},{18,... | collective-permute-start | bytes 442376 | tf_op jit(solution)/shard_map/ppermute | solution.py:419
  25.2 5.6 %collective-permute-start.2 = (bf16[4,6,24,128]{3,2,1,0:T(8,128)(2,1)}, bf16[4,6,24,128]{3,2,1,0:T(8,128)(2,1)S(1)}, u32[]{:S(2)}, u32[]{:S(2)}) collective-permute-start(bf16[4,6,24,128]{3,2,1,0:T(8,128)(2,1)} %get-tuple-element.52), channel_id=1, source_target_pairs={{0,16},{2,18},{4,20},{6,22},{8,24},{10,26},{12,28},{14,30},{16,0},... | collective-permute-start | bytes 442376 | tf_op jit(solution)/shard_map/ppermute | solution.py:419
  25.2 13.6 %collective-permute-start.3 = (bf16[4,6,24,128]{3,2,1,0:T(8,128)(2,1)}, bf16[4,6,24,128]{3,2,1,0:T(8,128)(2,1)S(1)}, u32[]{:S(2)}, u32[]{:S(2)}) collective-permute-start(bf16[4,6,24,128]{3,2,1,0:T(8,128)(2,1)} %get-tuple-element.53), channel_id=1, source_target_pairs={{0,24},{2,26},{4,28},{6,30},{8,16},{10,18},{12,20},{14,22},{16,8},... | collective-permute-start | bytes 442376 | tf_op jit(solution)/shard_map/ppermute | solution.py:419
  29.8 9.0 %copy-start.23 = (bf16[6,384,128]{2,1,0:T(8,128)(2,1)}, bf16[6,384,128]{2,1,0:T(8,128)(2,1)S(1)}, u32[]{:S(2)}) copy-start(bf16[6,384,128]{2,1,0:T(8,128)(2,1)S(1)} %collective-permute-done.4.refs_1_) | copy-start | bytes 1769476
  29.8 9.0 %copy-start.3 = (bf16[4,6,24,128]{3,2,1,0:T(8,128)(2,1)}, bf16[4,6,24,128]{3,2,1,0:T(8,128)(2,1)S(1)}, u32[]{:S(2)}) copy-start(bf16[4,6,24,128]{3,2,1,0:T(8,128)(2,1)S(1)} %collective-permute-done.1.refs_3_.refs_1_) | copy-start | bytes 442372
  44.3 36.0 %collective-permute-start.11 = (bf16[6,384,128]{2,1,0:T(8,128)(2,1)}, bf16[6,384,128]{2,1,0:T(8,128)(2,1)S(1)}, u32[]{:S(2)}, u32[]{:S(2)}) collective-permute-start(bf16[6,384,128]{2,1,0:T(8,128)(2,1)} %shard_map.199), channel_id=1, source_target_pairs={{0,1},{1,0},{2,3},{3,2},{4,5},{5,4},{6,7},{7,6},{8,9},{9,8},{10,11... | collective-permute-start | bytes 1769480 | tf_op jit(solution)/shard_map/ppermute | solution.py:419
  45.5 4.0 %collective-permute-start.5 = (bf16[4,6,24,128]{3,2,1,0:T(8,128)(2,1)S(1)}, bf16[4,6,24,128]{3,2,1,0:T(8,128)(2,1)S(1)}, u32[]{:S(2)}, u32[]{:S(2)}) collective-permute-start(bf16[4,6,24,128]{3,2,1,0:T(8,128)(2,1)S(1)} %copy-done.59), channel_id=1, source_target_pairs={{0,8},{2,10},{4,12},{6,14},{8,0},{10,2},{12,4},{14,6},{16,24},{18,... | collective-permute-start | bytes 442376 | tf_op jit(solution)/shard_map/ppermute | solution.py:419
  45.5 5.5 %collective-permute-start.6 = (bf16[4,6,24,128]{3,2,1,0:T(8,128)(2,1)S(1)}, bf16[4,6,24,128]{3,2,1,0:T(8,128)(2,1)S(1)}, u32[]{:S(2)}, u32[]{:S(2)}) collective-permute-start(bf16[4,6,24,128]{3,2,1,0:T(8,128)(2,1)S(1)} %copy-done.58), channel_id=1, source_target_pairs={{0,16},{2,18},{4,20},{6,22},{8,24},{10,26},{12,28},{14,30},{16,0},... | collective-permute-start | bytes 442376 | tf_op jit(solution)/shard_map/ppermute | solution.py:419
  46.8 14.3 %collective-permute-start.7 = (bf16[4,6,24,128]{3,2,1,0:T(8,128)(2,1)S(1)}, bf16[4,6,24,128]{3,2,1,0:T(8,128)(2,1)S(1)}, u32[]{:S(2)}, u32[]{:S(2)}) collective-permute-start(bf16[4,6,24,128]{3,2,1,0:T(8,128)(2,1)S(1)} %copy-done.57), channel_id=1, source_target_pairs={{0,24},{2,26},{4,28},{6,30},{8,16},{10,18},{12,20},{14,22},{16,8},... | collective-permute-start | bytes 442376 | tf_op jit(solution)/shard_map/ppermute | solution.py:419
  49.5 11.6 %copy-start.9 = (bf16[4,6,24,128]{3,2,1,0:T(8,128)(2,1)}, bf16[4,6,24,128]{3,2,1,0:T(8,128)(2,1)S(1)}, u32[]{:S(2)}) copy-start(bf16[4,6,24,128]{3,2,1,0:T(8,128)(2,1)S(1)} %collective-permute-done.5.refs_5_.refs_3_) | copy-start | bytes 442372
  51.0 10.1 %copy-start.10 = (bf16[4,6,24,128]{3,2,1,0:T(8,128)(2,1)}, bf16[4,6,24,128]{3,2,1,0:T(8,128)(2,1)S(1)}, u32[]{:S(2)}) copy-start(bf16[4,6,24,128]{3,2,1,0:T(8,128)(2,1)S(1)} %collective-permute-done.6.refs_6_.refs_4_) | copy-start | bytes 442372
  64.8 6.9 %collective-permute-start.13 = (bf16[4,6,24,128]{3,2,1,0:T(8,128)(2,1)}, bf16[4,6,24,128]{3,2,1,0:T(8,128)(2,1)S(1)}, u32[]{:S(2)}, u32[]{:S(2)}) collective-permute-start(bf16[4,6,24,128]{3,2,1,0:T(8,128)(2,1)} %get-tuple-element.61), channel_id=1, source_target_pairs={{0,8},{2,10},{4,12},{6,14},{8,0},{10,2},{12,4},{14,6},{16,24},{18,... | collective-permute-start | bytes 442376 | tf_op jit(solution)/shard_map/ppermute | solution.py:419
  64.8 8.2 %collective-permute-start.14 = (bf16[4,6,24,128]{3,2,1,0:T(8,128)(2,1)}, bf16[4,6,24,128]{3,2,1,0:T(8,128)(2,1)S(1)}, u32[]{:S(2)}, u32[]{:S(2)}) collective-permute-start(bf16[4,6,24,128]{3,2,1,0:T(8,128)(2,1)} %get-tuple-element.62), channel_id=1, source_target_pairs={{0,16},{2,18},{4,20},{6,22},{8,24},{10,26},{12,28},{14,30},{16,0},... | collective-permute-start | bytes 442376 | tf_op jit(solution)/shard_map/ppermute | solution.py:419
  67.5 19.6 %collective-permute-start.8 = (bf16[4,12,24,128]{3,2,1,0:T(8,128)(2,1)}, bf16[4,12,24,128]{3,2,1,0:T(8,128)(2,1)S(1)}, u32[]{:S(2)}, u32[]{:S(2)}) collective-permute-start(bf16[4,12,24,128]{3,2,1,0:T(8,128)(2,1)} %get-tuple-element.58), channel_id=1, source_target_pairs={{0,2},{2,0},{4,6},{6,4},{8,10},{10,8},{12,14},{14,12},{16,18},{18,... | collective-permute-start | bytes 884744 | tf_op jit(solution)/shard_map/ppermute | solution.py:419
  70.2 10.1 %collective-permute-start.15 = (bf16[4,6,24,128]{3,2,1,0:T(8,128)(2,1)S(1)}, bf16[4,6,24,128]{3,2,1,0:T(8,128)(2,1)S(1)}, u32[]{:S(2)}, u32[]{:S(2)}) collective-permute-start(bf16[4,6,24,128]{3,2,1,0:T(8,128)(2,1)S(1)} %copy-done.56), channel_id=1, source_target_pairs={{0,24},{2,26},{4,28},{6,30},{8,16},{10,18},{12,20},{14,22},{16,8},... | collective-permute-start | bytes 442376 | tf_op jit(solution)/shard_map/ppermute | solution.py:419
  71.7 8.6 %copy-start.4 = (bf16[4,6,24,128]{3,2,1,0:T(8,128)(2,1)}, bf16[4,6,24,128]{3,2,1,0:T(8,128)(2,1)S(1)}, u32[]{:S(2)}) copy-start(bf16[4,6,24,128]{3,2,1,0:T(8,128)(2,1)S(1)} %collective-permute-done.13.refs_3_.refs_1_) | copy-start | bytes 442372
  71.7 15.6 %collective-permute-start.9 = (bf16[4,12,24,128]{3,2,1,0:T(8,128)(2,1)}, bf16[4,12,24,128]{3,2,1,0:T(8,128)(2,1)S(1)}, u32[]{:S(2)}, u32[]{:S(2)}) collective-permute-start(bf16[4,12,24,128]{3,2,1,0:T(8,128)(2,1)} %get-tuple-element.59), channel_id=1, source_target_pairs={{0,4},{2,6},{4,0},{6,2},{8,12},{10,14},{12,8},{14,10},{16,20},{18,... | collective-permute-start | bytes 884744 | tf_op jit(solution)/shard_map/ppermute | solution.py:419
  72.9 14.4 %collective-permute-start.10 = (bf16[4,12,24,128]{3,2,1,0:T(8,128)(2,1)}, bf16[4,12,24,128]{3,2,1,0:T(8,128)(2,1)S(1)}, u32[]{:S(2)}, u32[]{:S(2)}) collective-permute-start(bf16[4,12,24,128]{3,2,1,0:T(8,128)(2,1)} %get-tuple-element.60), channel_id=1, source_target_pairs={{0,6},{2,4},{4,2},{6,0},{8,14},{10,12},{12,10},{14,8},{16,22},{18,... | collective-permute-start | bytes 884744 | tf_op jit(solution)/shard_map/ppermute | solution.py:419
  84.7 7.7 %collective-permute-start.27 = (bf16[4,6,24,128]{3,2,1,0:T(8,128)(2,1)}, bf16[4,6,24,128]{3,2,1,0:T(8,128)(2,1)S(1)}, u32[]{:S(2)}, u32[]{:S(2)}) collective-permute-start(bf16[4,6,24,128]{3,2,1,0:T(8,128)(2,1)} %get-tuple-element.79), channel_id=1, source_target_pairs={{0,8},{2,10},{4,12},{6,14},{8,0},{10,2},{12,4},{14,6},{16,24},{18,... | collective-permute-start | bytes 442376 | tf_op jit(solution)/shard_map/ppermute | solution.py:419
  86.1 10.6 %collective-permute-start.28 = (bf16[4,6,24,128]{3,2,1,0:T(8,128)(2,1)}, bf16[4,6,24,128]{3,2,1,0:T(8,128)(2,1)S(1)}, u32[]{:S(2)}, u32[]{:S(2)}) collective-permute-start(bf16[4,6,24,128]{3,2,1,0:T(8,128)(2,1)} %get-tuple-element.80), channel_id=1, source_target_pairs={{0,16},{2,18},{4,20},{6,22},{8,24},{10,26},{12,28},{14,30},{16,0},... | collective-permute-start | bytes 442376 | tf_op jit(solution)/shard_map/ppermute | solution.py:419
  87.1 12.9 %collective-permute-start.29 = (bf16[4,6,24,128]{3,2,1,0:T(8,128)(2,1)}, bf16[4,6,24,128]{3,2,1,0:T(8,128)(2,1)S(1)}, u32[]{:S(2)}, u32[]{:S(2)}) collective-permute-start(bf16[4,6,24,128]{3,2,1,0:T(8,128)(2,1)} %get-tuple-element.81), channel_id=1, source_target_pairs={{0,24},{2,26},{4,28},{6,30},{8,16},{10,18},{12,20},{14,22},{16,8},... | collective-permute-start | bytes 442376 | tf_op jit(solution)/shard_map/ppermute | solution.py:419
  92.4 14.1 %copy-start.51 = (bf16[4,12,24,128]{3,2,1,0:T(8,128)(2,1)S(1)}, bf16[4,12,24,128]{3,2,1,0:T(8,128)(2,1)}, u32[]{:S(2)}) copy-start(bf16[4,12,24,128]{3,2,1,0:T(8,128)(2,1)} %get-tuple-element.66) | copy-start | bytes 884740
  92.4 14.3 %copy-start.50 = (bf16[4,12,24,128]{3,2,1,0:T(8,128)(2,1)S(1)}, bf16[4,12,24,128]{3,2,1,0:T(8,128)(2,1)}, u32[]{:S(2)}) copy-start(bf16[4,12,24,128]{3,2,1,0:T(8,128)(2,1)} %get-tuple-element.67) | copy-start | bytes 884740
  92.4 15.5 %copy-start.49 = (bf16[4,12,24,128]{3,2,1,0:T(8,128)(2,1)S(1)}, bf16[4,12,24,128]{3,2,1,0:T(8,128)(2,1)}, u32[]{:S(2)}) copy-start(bf16[4,12,24,128]{3,2,1,0:T(8,128)(2,1)} %get-tuple-element.68) | copy-start | bytes 884740
  102.9 5.0 %collective-permute-start.30 = (bf16[4,12,24,128]{3,2,1,0:T(8,128)(2,1)}, bf16[4,12,24,128]{3,2,1,0:T(8,128)(2,1)S(1)}, u32[]{:S(2)}, u32[]{:S(2)}) collective-permute-start(bf16[4,12,24,128]{3,2,1,0:T(8,128)(2,1)} %get-tuple-element.82), channel_id=1, source_target_pairs={{0,2},{2,0},{4,6},{6,4},{8,10},{10,8},{12,14},{14,12},{16,18},{18,... | collective-permute-start | bytes 884744 | tf_op jit(solution)/shard_map/ppermute | solution.py:419
  104.8 8.8 %collective-permute-start.31 = (bf16[4,12,24,128]{3,2,1,0:T(8,128)(2,1)}, bf16[4,12,24,128]{3,2,1,0:T(8,128)(2,1)S(1)}, u32[]{:S(2)}, u32[]{:S(2)}) collective-permute-start(bf16[4,12,24,128]{3,2,1,0:T(8,128)(2,1)} %get-tuple-element.83), channel_id=1, source_target_pairs={{0,4},{2,6},{4,0},{6,2},{8,12},{10,14},{12,8},{14,10},{16,20},{18,... | collective-permute-start | bytes 884744 | tf_op jit(solution)/shard_map/ppermute | solution.py:419
  106.0 14.4 %collective-permute-start.32 = (bf16[4,12,24,128]{3,2,1,0:T(8,128)(2,1)}, bf16[4,12,24,128]{3,2,1,0:T(8,128)(2,1)S(1)}, u32[]{:S(2)}, u32[]{:S(2)}) collective-permute-start(bf16[4,12,24,128]{3,2,1,0:T(8,128)(2,1)} %get-tuple-element.84), channel_id=1, source_target_pairs={{0,6},{2,4},{4,2},{6,0},{8,14},{10,12},{12,10},{14,8},{16,22},{18,... | collective-permute-start | bytes 884744 | tf_op jit(solution)/shard_map/ppermute | solution.py:419
  106.4 20.3 %collective-permute-start.16 = (bf16[4,12,24,128]{3,2,1,0:T(8,128)(2,1)S(1)}, bf16[4,12,24,128]{3,2,1,0:T(8,128)(2,1)S(1)}, u32[]{:S(2)}, u32[]{:S(2)}) collective-permute-start(bf16[4,12,24,128]{3,2,1,0:T(8,128)(2,1)S(1)} %copy-done.51), channel_id=1, source_target_pairs={{0,2},{2,0},{4,6},{6,4},{8,10},{10,8},{12,14},{14,12},{16,18},{18,... | collective-permute-start | bytes 884744 | tf_op jit(solution)/shard_map/ppermute | solution.py:419
  106.7 20.9 %collective-permute-start.17 = (bf16[4,12,24,128]{3,2,1,0:T(8,128)(2,1)S(1)}, bf16[4,12,24,128]{3,2,1,0:T(8,128)(2,1)S(1)}, u32[]{:S(2)}, u32[]{:S(2)}) collective-permute-start(bf16[4,12,24,128]{3,2,1,0:T(8,128)(2,1)S(1)} %copy-done.50), channel_id=1, source_target_pairs={{0,4},{2,6},{4,0},{6,2},{8,12},{10,14},{12,8},{14,10},{16,20},{18,... | collective-permute-start | bytes 884744 | tf_op jit(solution)/shard_map/ppermute | solution.py:419
  107.9 12.6 %copy-start.29 = (bf16[4,12,24,128]{3,2,1,0:T(8,128)(2,1)}, bf16[4,12,24,128]{3,2,1,0:T(8,128)(2,1)S(1)}, u32[]{:S(2)}) copy-start(bf16[4,12,24,128]{3,2,1,0:T(8,128)(2,1)S(1)} %collective-permute-done.30.refs_8_) | copy-start | bytes 884740
  107.9 25.2 %collective-permute-start.18 = (bf16[4,12,24,128]{3,2,1,0:T(8,128)(2,1)S(1)}, bf16[4,12,24,128]{3,2,1,0:T(8,128)(2,1)S(1)}, u32[]{:S(2)}, u32[]{:S(2)}) collective-permute-start(bf16[4,12,24,128]{3,2,1,0:T(8,128)(2,1)S(1)} %copy-done.49), channel_id=1, source_target_pairs={{0,6},{2,4},{4,2},{6,0},{8,14},{10,12},{12,10},{14,8},{16,22},{18,... | collective-permute-start | bytes 884744 | tf_op jit(solution)/shard_map/ppermute | solution.py:419
  125.5 12.9 %collective-permute-start.33 = (bf16[4,12,24,128]{3,2,1,0:T(8,128)(2,1)}, bf16[4,12,24,128]{3,2,1,0:T(8,128)(2,1)S(1)}, u32[]{:S(2)}, u32[]{:S(2)}) collective-permute-start(bf16[4,12,24,128]{3,2,1,0:T(8,128)(2,1)} %get-tuple-element.86), channel_id=1, source_target_pairs={{0,2},{2,0},{4,6},{6,4},{8,10},{10,8},{12,14},{14,12},{16,18},{18,... | collective-permute-start | bytes 884744 | tf_op jit(solution)/shard_map/ppermute | solution.py:419
  125.5 13.5 %collective-permute-start.34 = (bf16[4,12,24,128]{3,2,1,0:T(8,128)(2,1)}, bf16[4,12,24,128]{3,2,1,0:T(8,128)(2,1)S(1)}, u32[]{:S(2)}, u32[]{:S(2)}) collective-permute-start(bf16[4,12,24,128]{3,2,1,0:T(8,128)(2,1)} %get-tuple-element.87), channel_id=1, source_target_pairs={{0,4},{2,6},{4,0},{6,2},{8,12},{10,14},{12,8},{14,10},{16,20},{18,... | collective-permute-start | bytes 884744 | tf_op jit(solution)/shard_map/ppermute | solution.py:419
  126.8 18.8 %collective-permute-start.35 = (bf16[4,12,24,128]{3,2,1,0:T(8,128)(2,1)}, bf16[4,12,24,128]{3,2,1,0:T(8,128)(2,1)S(1)}, u32[]{:S(2)}, u32[]{:S(2)}) collective-permute-start(bf16[4,12,24,128]{3,2,1,0:T(8,128)(2,1)} %get-tuple-element.88), channel_id=1, source_target_pairs={{0,6},{2,4},{4,2},{6,0},{8,14},{10,12},{12,10},{14,8},{16,22},{18,... | collective-permute-start | bytes 884744 | tf_op jit(solution)/shard_map/ppermute | solution.py:419
  136.0 14.9 %collective-permute-start.19 = (bf16[4,12,24,128]{3,2,1,0:T(8,128)(2,1)}, bf16[4,12,24,128]{3,2,1,0:T(8,128)(2,1)S(1)}, u32[]{:S(2)}, u32[]{:S(2)}) collective-permute-start(bf16[4,12,24,128]{3,2,1,0:T(8,128)(2,1)} %get-tuple-element.69), channel_id=1, source_target_pairs={{0,8},{2,10},{4,12},{6,14},{8,0},{10,2},{12,4},{14,6},{16,24},{18,... | collective-permute-start | bytes 884744 | tf_op jit(solution)/shard_map/ppermute | solution.py:419
  136.0 21.5 %collective-permute-start.20 = (bf16[4,12,24,128]{3,2,1,0:T(8,128)(2,1)}, bf16[4,12,24,128]{3,2,1,0:T(8,128)(2,1)S(1)}, u32[]{:S(2)}, u32[]{:S(2)}) collective-permute-start(bf16[4,12,24,128]{3,2,1,0:T(8,128)(2,1)} %get-tuple-element.70), channel_id=1, source_target_pairs={{0,16},{2,18},{4,20},{6,22},{8,24},{10,26},{12,28},{14,30},{16,0},... | collective-permute-start | bytes 884744 | tf_op jit(solution)/shard_map/ppermute | solution.py:419
  138.4 38.1 %collective-permute-start.21 = (bf16[4,12,24,128]{3,2,1,0:T(8,128)(2,1)}, bf16[4,12,24,128]{3,2,1,0:T(8,128)(2,1)S(1)}, u32[]{:S(2)}, u32[]{:S(2)}) collective-permute-start(bf16[4,12,24,128]{3,2,1,0:T(8,128)(2,1)} %get-tuple-element.71), channel_id=1, source_target_pairs={{0,24},{2,26},{4,28},{6,30},{8,16},{10,18},{12,20},{14,22},{16,8},... | collective-permute-start | bytes 884744 | tf_op jit(solution)/shard_map/ppermute | solution.py:419
  148.4 33.5 %collective-permute-start.36 = (bf16[4,12,24,128]{3,2,1,0:T(8,128)(2,1)}, bf16[4,12,24,128]{3,2,1,0:T(8,128)(2,1)S(1)}, u32[]{:S(2)}, u32[]{:S(2)}) collective-permute-start(bf16[4,12,24,128]{3,2,1,0:T(8,128)(2,1)} %get-tuple-element.89), channel_id=1, source_target_pairs={{0,8},{2,10},{4,12},{6,14},{8,0},{10,2},{12,4},{14,6},{16,24},{18,... | collective-permute-start | bytes 884744 | tf_op jit(solution)/shard_map/ppermute | solution.py:419
  148.4 34.5 %collective-permute-start.37 = (bf16[4,12,24,128]{3,2,1,0:T(8,128)(2,1)}, bf16[4,12,24,128]{3,2,1,0:T(8,128)(2,1)S(1)}, u32[]{:S(2)}, u32[]{:S(2)}) collective-permute-start(bf16[4,12,24,128]{3,2,1,0:T(8,128)(2,1)} %get-tuple-element.90), channel_id=1, source_target_pairs={{0,16},{2,18},{4,20},{6,22},{8,24},{10,26},{12,28},{14,30},{16,0},... | collective-permute-start | bytes 884744 | tf_op jit(solution)/shard_map/ppermute | solution.py:419
  150.9 25.5 %copy-start.33 = (bf16[4,12,24,128]{3,2,1,0:T(8,128)(2,1)}, bf16[4,12,24,128]{3,2,1,0:T(8,128)(2,1)S(1)}, u32[]{:S(2)}) copy-start(bf16[4,12,24,128]{3,2,1,0:T(8,128)(2,1)S(1)} %collective-permute-done.19.refs_4_) | copy-start | bytes 884740
  150.9 39.2 %collective-permute-start.38 = (bf16[4,12,24,128]{3,2,1,0:T(8,128)(2,1)}, bf16[4,12,24,128]{3,2,1,0:T(8,128)(2,1)S(1)}, u32[]{:S(2)}, u32[]{:S(2)}) collective-permute-start(bf16[4,12,24,128]{3,2,1,0:T(8,128)(2,1)} %get-tuple-element.91), channel_id=1, source_target_pairs={{0,24},{2,26},{4,28},{6,30},{8,16},{10,18},{12,20},{14,22},{16,8},... | collective-permute-start | bytes 884744 | tf_op jit(solution)/shard_map/ppermute | solution.py:419
  157.4 19.0 %copy-start.35 = (bf16[4,12,24,128]{3,2,1,0:T(8,128)(2,1)}, bf16[4,12,24,128]{3,2,1,0:T(8,128)(2,1)S(1)}, u32[]{:S(2)}) copy-start(bf16[4,12,24,128]{3,2,1,0:T(8,128)(2,1)S(1)} %collective-permute-done.20.refs_5_) | copy-start | bytes 884740
  181.5 14.1 %copy-start.55 = (bf16[2,392,128]{2,1,0:T(8,128)(2,1)S(1)}, bf16[2,392,128]{2,1,0:T(8,128)(2,1)}, u32[]{:S(2)}) copy-start(bf16[2,392,128]{2,1,0:T(8,128)(2,1)} %get-tuple-element.72) | copy-start | bytes 602116
  181.5 18.4 %copy-start.54 = (bf16[2,392,128]{2,1,0:T(8,128)(2,1)S(1)}, bf16[2,392,128]{2,1,0:T(8,128)(2,1)}, u32[]{:S(2)}) copy-start(bf16[2,392,128]{2,1,0:T(8,128)(2,1)} %get-tuple-element.73) | copy-start | bytes 602116
  181.5 20.3 %copy-start.53 = (bf16[2,392,128]{2,1,0:T(8,128)(2,1)S(1)}, bf16[2,392,128]{2,1,0:T(8,128)(2,1)}, u32[]{:S(2)}) copy-start(bf16[2,392,128]{2,1,0:T(8,128)(2,1)} %get-tuple-element.75) | copy-start | bytes 602116
  181.5 58.6 %copy-start.52 = (bf16[2,392,128]{2,1,0:T(8,128)(2,1)S(1)}, bf16[2,392,128]{2,1,0:T(8,128)(2,1)}, u32[]{:S(2)}) copy-start(bf16[2,392,128]{2,1,0:T(8,128)(2,1)} %get-tuple-element.76) | copy-start | bytes 602116
  181.5 82.3 %collective-permute-start.26 = (bf16[12,392,128]{2,1,0:T(8,128)(2,1)}, bf16[12,392,128]{2,1,0:T(8,128)(2,1)S(1)}, u32[]{:S(2)}, u32[]{:S(2)}) collective-permute-start(bf16[12,392,128]{2,1,0:T(8,128)(2,1)} %get-tuple-element.77), channel_id=1, source_target_pairs={{0,1},{1,0},{2,3},{3,2},{4,5},{5,4},{6,7},{7,6},{8,9},{9,8},{10,11... | collective-permute-start | bytes 3612680 | tf_op jit(solution)/shard_map/ppermute | solution.py:419
  195.3 76.5 %collective-permute-start.43 = (bf16[12,392,128]{2,1,0:T(8,128)(2,1)}, bf16[12,392,128]{2,1,0:T(8,128)(2,1)S(1)}, u32[]{:S(2)}, u32[]{:S(2)}) collective-permute-start(bf16[12,392,128]{2,1,0:T(8,128)(2,1)} %get-tuple-element.97), channel_id=1, source_target_pairs={{0,1},{1,0},{2,3},{3,2},{4,5},{5,4},{6,7},{7,6},{8,9},{9,8},{10,11... | collective-permute-start | bytes 3612680 | tf_op jit(solution)/shard_map/ppermute | solution.py:419
  195.6 10.8 %collective-permute-start.22 = (bf16[2,392,128]{2,1,0:T(8,128)(2,1)S(1)}, bf16[2,392,128]{2,1,0:T(8,128)(2,1)S(1)}, u32[]{:S(2)}, u32[]{:S(2)}) collective-permute-start(bf16[2,392,128]{2,1,0:T(8,128)(2,1)S(1)} %copy-done.55), channel_id=1, source_target_pairs={{0,2},{1,3},{2,4},{3,5},{4,6},{5,7},{6,8},{7,9},{8,10},{9,11},{10,... | collective-permute-start | bytes 602120 | tf_op jit(solution)/shard_map/ppermute | solution.py:513
  199.9 8.4 %collective-permute-start.23 = (bf16[2,392,128]{2,1,0:T(8,128)(2,1)S(1)}, bf16[2,392,128]{2,1,0:T(8,128)(2,1)S(1)}, u32[]{:S(2)}, u32[]{:S(2)}) collective-permute-start(bf16[2,392,128]{2,1,0:T(8,128)(2,1)S(1)} %copy-done.54), channel_id=1, source_target_pairs={{2,0},{3,1},{4,2},{5,3},{6,4},{7,5},{8,6},{9,7},{10,8},{11,9},{12,... | collective-permute-start | bytes 602120 | tf_op jit(solution)/shard_map/ppermute | solution.py:513
  201.9 38.3 %collective-permute-start.24 = (bf16[2,392,128]{2,1,0:T(8,128)(2,1)S(1)}, bf16[2,392,128]{2,1,0:T(8,128)(2,1)S(1)}, u32[]{:S(2)}, u32[]{:S(2)}) collective-permute-start(bf16[2,392,128]{2,1,0:T(8,128)(2,1)S(1)} %copy-done.53), channel_id=1, source_target_pairs={{0,3},{1,2},{2,5},{3,4},{4,7},{5,6},{6,9},{7,8},{8,11},{9,10},{10,... | collective-permute-start | bytes 602120 | tf_op jit(solution)/shard_map/ppermute | solution.py:513
  206.4 44.7 %copy-start.39 = (bf16[2,392,128]{2,1,0:T(8,128)(2,1)}, bf16[2,392,128]{2,1,0:T(8,128)(2,1)S(1)}, u32[]{:S(2)}) copy-start(bf16[2,392,128]{2,1,0:T(8,128)(2,1)S(1)} %collective-permute-done.22.low_ref) | copy-start | bytes 602116
  206.4 35.6 %collective-permute-start.39 = (bf16[2,392,128]{2,1,0:T(8,128)(2,1)}, bf16[2,392,128]{2,1,0:T(8,128)(2,1)S(1)}, u32[]{:S(2)}, u32[]{:S(2)}) collective-permute-start(bf16[2,392,128]{2,1,0:T(8,128)(2,1)} %get-tuple-element.92), channel_id=1, source_target_pairs={{0,2},{1,3},{2,4},{3,5},{4,6},{5,7},{6,8},{7,9},{8,10},{9,11},{10,... | collective-permute-start | bytes 602120 | tf_op jit(solution)/shard_map/ppermute | solution.py:513
  208.4 42.8 %copy-start.40 = (bf16[2,392,128]{2,1,0:T(8,128)(2,1)}, bf16[2,392,128]{2,1,0:T(8,128)(2,1)S(1)}, u32[]{:S(2)}) copy-start(bf16[2,392,128]{2,1,0:T(8,128)(2,1)S(1)} %collective-permute-done.23.high_ref) | copy-start | bytes 602116
  208.4 38.2 %collective-permute-start.40 = (bf16[2,392,128]{2,1,0:T(8,128)(2,1)}, bf16[2,392,128]{2,1,0:T(8,128)(2,1)S(1)}, u32[]{:S(2)}, u32[]{:S(2)}) collective-permute-start(bf16[2,392,128]{2,1,0:T(8,128)(2,1)} %get-tuple-element.93), channel_id=1, source_target_pairs={{2,0},{3,1},{4,2},{5,3},{6,4},{7,5},{8,6},{9,7},{10,8},{11,9},{12,... | collective-permute-start | bytes 602120 | tf_op jit(solution)/shard_map/ppermute | solution.py:513
  240.1 17.4 %copy-start.38 = (bf16[2,392,128]{2,1,0:T(8,128)(2,1)}, bf16[2,392,128]{2,1,0:T(8,128)(2,1)S(1)}, u32[]{:S(2)}) copy-start(bf16[2,392,128]{2,1,0:T(8,128)(2,1)S(1)} %collective-permute-done.24.low_ref) | copy-start | bytes 602116
  240.1 23.7 %collective-permute-start.25 = (bf16[2,392,128]{2,1,0:T(8,128)(2,1)S(1)}, bf16[2,392,128]{2,1,0:T(8,128)(2,1)S(1)}, u32[]{:S(2)}, u32[]{:S(2)}) collective-permute-start(bf16[2,392,128]{2,1,0:T(8,128)(2,1)S(1)} %copy-done.52), channel_id=1, source_target_pairs={{2,1},{3,0},{4,3},{5,2},{6,5},{7,4},{8,7},{9,6},{10,9},{11,8},{12,... | collective-permute-start | bytes 602120 | tf_op jit(solution)/shard_map/ppermute | solution.py:513
  242.1 15.5 %copy-start.42 = (bf16[2,392,128]{2,1,0:T(8,128)(2,1)}, bf16[2,392,128]{2,1,0:T(8,128)(2,1)S(1)}, u32[]{:S(2)}) copy-start(bf16[2,392,128]{2,1,0:T(8,128)(2,1)S(1)} %collective-permute-done.39.low_ref) | copy-start | bytes 602116
  242.1 29.6 %collective-permute-start.41 = (bf16[2,392,128]{2,1,0:T(8,128)(2,1)}, bf16[2,392,128]{2,1,0:T(8,128)(2,1)S(1)}, u32[]{:S(2)}, u32[]{:S(2)}) collective-permute-start(bf16[2,392,128]{2,1,0:T(8,128)(2,1)} %get-tuple-element.95), channel_id=1, source_target_pairs={{0,3},{1,2},{2,5},{3,4},{4,7},{5,6},{6,9},{7,8},{8,11},{9,10},{10,... | collective-permute-start | bytes 602120 | tf_op jit(solution)/shard_map/ppermute | solution.py:513
  246.6 10.9 %copy-start.45 = (bf16[2,392,128]{2,1,0:T(8,128)(2,1)}, bf16[2,392,128]{2,1,0:T(8,128)(2,1)S(1)}, u32[]{:S(2)}) copy-start(bf16[2,392,128]{2,1,0:T(8,128)(2,1)S(1)} %collective-permute-done.40.high_ref) | copy-start | bytes 602116
  246.7 25.1 %collective-permute-start.42 = (bf16[2,392,128]{2,1,0:T(8,128)(2,1)}, bf16[2,392,128]{2,1,0:T(8,128)(2,1)S(1)}, u32[]{:S(2)}, u32[]{:S(2)}) collective-permute-start(bf16[2,392,128]{2,1,0:T(8,128)(2,1)} %get-tuple-element.96), channel_id=1, source_target_pairs={{2,1},{3,0},{4,3},{5,2},{6,5},{7,4},{8,7},{9,6},{10,9},{11,8},{12,... | collective-permute-start | bytes 602120 | tf_op jit(solution)/shard_map/ppermute | solution.py:513
  (41 other events, 124.2 us)

commit v5 on v3

--- a/solution.py
+++ b/solution.py
@@ -111,24 +111,30 @@
     )(index[None], array, *waits)
 
 
-def rows_kernel(count, wave_ref, *refs):
+def rows_kernel(first_in, last_in, *refs):
     first_ref, last_ref = refs[-2:]
-    rows = wave_ref.shape[0]
-    for r in range(HALO):
-        first_ref[r] = wave_ref[r]
-        last_ref[r] = wave_ref[rows - HALO + r]
+    first_ref[...] = first_in[...]
+    last_ref[...] = last_in[...]
 
 
 def edge_rows(wave, waits):
-    edge = jax.ShapeDtypeStruct((HALO,) + wave.shape[1:], wave.dtype)
-    return pl.pallas_call(
-        functools.partial(rows_kernel, len(waits)),
-        in_specs=[vmem_spec()] + [any_spec()] * len(waits),
-        out_specs=[vmem_spec()] * 2,
+    rows, cols, cw = wave.shape
+    edge = jax.ShapeDtypeStruct((HALO, cols, cw), wave.dtype)
+    last = rows // HALO - 1
+    block = (HALO, cols, cw)
+    return pl.pallas_call(
+        rows_kernel,
+        grid=(1,),
+        in_specs=[
+            pl.BlockSpec(block, lambda t: (0, 0, 0)),
+            pl.BlockSpec(block, lambda t: (last, 0, 0)),
+        ]
+        + [any_spec()] * len(waits),
+        out_specs=[pl.BlockSpec(block, lambda t: (0, 0, 0))] * 2,
         out_shape=[edge, edge],
-        compiler_params=pltpu.CompilerParams(vmem_limit_bytes=VMEM_LIMIT),
+        compiler_params=params(),
         cost_estimate=cost(0, 8 * edge.size),
-    )(wave, *waits)
+    )(wave, wave, *waits)
 
 
 def dft_kernel(lon_count, nz, waits, index_ref, quad_ref, *refs):
@@ -253,12 +259,12 @@
     )(*own, *others, leg, legt, gr, gi, *waits)
 
 
-def inverse_kernel(nz, lon_count, *refs):
+def inverse_kernel(nz, lon_count, waits, *refs):
     near = refs[:NQ]
     far = refs[NQ : NQ + nz - 1]
     table_ref = refs[NQ + nz - 1]
-    outs = refs[NQ + nz : NQ + nz + lon_count]
-    wide = refs[-1]
+    outs = refs[NQ + nz + waits : NQ + nz + waits + lon_count]
+    first_ref, last_ref, wide = refs[-3:]
     rows, _, cw = wide.shape
     wave_rows = near[0].shape[-2]
     cols = outs[0].shape[1]
@@ -276,9 +282,18 @@
             for s in range(lon_count):
                 piece = acc[s * cols : (s + 1) * cols, i * cw : (i + 1) * cw]
                 outs[s][first + i] = piece.astype(BF16)
-
-
-def inverse(near, far, table, lon_count):
+    step = pl.program_id(0)
+
+    @pl.when(step == 0)
+    def _():
+        first_ref[...] = outs[0][:HALO]
+
+    @pl.when(step == pl.num_programs(0) - 1)
+    def _():
+        last_ref[...] = outs[0][rows - HALO :]
+
+
+def inverse(near, far, table, lon_count, waits):
     nz = len(far) + 1
     _, rows, wave_rows, cw = near[0].shape
     step = step_rows(rows, 6)
@@ -286,15 +301,17 @@
     specs = [pl.BlockSpec((1, step, wave_rows, cw), lambda t: (0, t, 0, 0))] * NQ
     specs += [pl.BlockSpec((NQ, step, wave_rows, cw), lambda t: (0, t, 0, 0))] * (nz - 1)
     return pl.pallas_call(
-        functools.partial(inverse_kernel, nz, lon_count),
+        functools.partial(inverse_kernel, nz, lon_count, len(waits)),
         grid=(rows // step,),
-        in_specs=specs + [whole_of(table)],
-        out_specs=[pl.BlockSpec((step, cols, cw), lambda t: (t, 0, 0))] * lon_count,
-        out_shape=[jax.ShapeDtypeStruct((rows, cols, cw), BF16)] * lon_count,
+        in_specs=specs + [whole_of(table)] + [any_spec()] * len(waits),
+        out_specs=[pl.BlockSpec((step, cols, cw), lambda t: (t, 0, 0))] * lon_count
+        + [pl.BlockSpec((HALO, cols, cw), lambda t: (0, 0, 0))] * 2,
+        out_shape=[jax.ShapeDtypeStruct((rows, cols, cw), BF16)] * lon_count
+        + [jax.ShapeDtypeStruct((HALO, cols, cw), BF16)] * 2,
         scratch_shapes=[pltpu.VMEM((step, nz * NQ * wave_rows, cw), F32)],
         compiler_params=params(),
         cost_estimate=cost(0, 14000000),
-    )(*near, *far, table)
+    )(*near, *far, table, *waits)
 
 
 def window_kernel(cols, place_ref, neighbour_ref, basis_ref, quad_ref, wave_ref, low_ref, high_ref, disco_ref, out_ref, ring):
@@ -484,11 +501,11 @@
     up = [(i, i + 1) for i in range(lat_count - 1)]
     down = [(i + 1, i) for i in range(lat_count - 1)]
 
-    def convolved(wave, s, j, waits):
-        first, last = edge_rows(wave, waits)
+    def convolved(wave, edges, s, j):
+        first, last = edges
         low = lax.ppermute(last, "lat", up)
         high = lax.ppermute(first, "lat", down)
-        place = ((lon_id ^ s) * nch + j).astype(jnp.int32)
+        place = channel_index(s, j)
         done = window(
             place[None], neighbour, basis, disco_quad, wave, low, high, disco, cols
         )
@@ -506,7 +523,9 @@
             ]
         )
         waits = [fwd]
-    spectra, waits = [], []
+    gains = [(chunk_of(filter_real, 0, j), chunk_of(filter_imag, 0, j)) for j in range(nch)]
+    spectra = []
+    waits = [leg, legt, inv] + [gain for pair in gains for gain in pair]
     for j in range(nch):
         arrays = dft(
             field, channel_index(0, j), received[j], quad_weight, fwd, nz, wave_rows, cw, waits
@@ -517,21 +536,23 @@
     near = []
     waits = [latest]
     for j in range(nch):
-        gr = chunk_of(filter_real, 0, j)
-        gi = chunk_of(filter_imag, 0, j)
         full = legendre_step(
-            spectra[j], across(regroup(spectra[j], waits)), leg, legt, gr, gi, []
+            spectra[j], across(regroup(spectra[j], waits)), leg, legt, *gains[j], []
         )
         near.append([full[0]] + across(full[1:]))
         waits = []
-    parts = []
+    groups, sent, waits = [], [], []
     for j in range(nch):
-        parts.append(inverse(near[j], along(regroup(near[j], [])), inv, lon_count))
-    groups = [convolved(parts[j][0], 0, j, []) for j in range(nch)]
+        *parts, first, last = inverse(
+            near[j], along(regroup(near[j], [])), inv, lon_count, waits
+        )
+        sent.append([swap(parts[s], "lon", s) for s in range(1, lon_count)])
+        groups.append(convolved(parts[0], (first, last), 0, j))
+        waits = [groups[-1][1]]
     for j in range(nch):
         waits = [done for _, done in groups] if j == nch - 1 else []
-        for s in range(1, lon_count):
-            groups.append(convolved(swap(parts[j][s], "lon", s), s, j, waits))
+        for s, wave in enumerate(sent[j], 1):
+            groups.append(convolved(wave, edge_rows(wave, waits), s, j))
     block_out, spatial = mlp(
         jnp.stack([place for place, _ in groups]),
         [done for _, done in groups],

time: 274 us -> 260 us (0.949)
  waiting for transfers between devices: 107 us -> 93.1 us
  Pallas kernels: 86.6 us -> 82.3 us
    ppermute x28, waiting for transfers between devices: 102 us -> 83.9 us  [swap(): return lax.ppermute(array, axis, [(i, i ^ mask) for i in range(count)])]
    ppermute x4, starting transfers between devices: 12.1 us -> 21.4 us  [convolved(): high = lax.ppermute(first, 'lat', down)]
    ppermute x4, waiting for transfers between devices: 4.66 us -> 9.2 us  [convolved(): high = lax.ppermute(first, 'lat', down)]
    ppermute x4, starting transfers between devices: 14.5 us -> 10.2 us  [convolved(): low = lax.ppermute(last, 'lat', up)]
    pallas_call x6 -> x4, Pallas kernels: 16.1 us -> 11.9 us  [the longest x2 8.32 us: inverse(): pl.pallas_call(functools.partial(inverse_kernel, nz, lon_count, len(waits...]
    ppermute x28, starting transfers between devices: 28 us -> 24.7 us  [swap(): return lax.ppermute(array, axis, [(i, i ^ mask) for i in range(count)])]
    unnamed x74 -> x88, local copies, waits for them, and re-layouts: 11.3 us -> 13.3 us
  transfers between devices with their start and end apart: 36 -> 36, of which waited for: 12 -> 13; matrix products, arithmetic and copies ran while one was open for 4% -> 4% of each run, Pallas kernels for 22% -> 20%
where the time goes in v5:
time: 260 us; the launch traced here: 256 us
  waiting for transfers between devices  93.1 us (36%)
  Pallas kernels  82.3 us (32%)
  starting transfers between devices  56.3 us (22%)
  local copies, waits for them, and re-layouts  16.9 us (6%)
  matrix products  3.24 us (1%)
  other arithmetic  2.64 us (1%)
    ppermute x28, waiting for transfers between devices, swap(): return lax.ppermute(array, axis, [(i, i ^ mask) for i in range(count)])  83.9 us
    ppermute x28, starting transfers between devices, swap(): return lax.ppermute(array, axis, [(i, i ^ mask) for i in range(count)])  24.7 us
    pallas_call x4, Pallas kernels, window(): pl.pallas_call(functools.partial(window_kernel, cols), grid=(rows // per_...  23.8 us
    ppermute x4, starting transfers between devices, convolved(): high = lax.ppermute(first, 'lat', down)  21.4 us
    pallas_call x1, Pallas kernels, mlp(): pl.pallas_call(mlp_kernel, grid=(rows // per_step,), in_specs=[smem_spec(...  17.8 us
    unnamed x88, local copies, waits for them, and re-layouts  13.3 us
    ppermute x4, starting transfers between devices, convolved(): low = lax.ppermute(last, 'lat', up)  10.2 us
    ppermute x4, waiting for transfers between devices, convolved(): high = lax.ppermute(first, 'lat', down)  9.2 us
  transfers between devices with their start and end apart: 36, of which 13 were waited for; matrix products, arithmetic and copies ran while one was open for 4% of the time, Pallas kernels for 20%

profile of v5, /device:TPU:19, one launch (start us, length us, event | category | flops | bytes accessed | tf_op | source)
XLA Modules:
  0.0 255.6 jit_solution(9582516913064847549)
XLA Ops:
  0.7 2.2 shard_map.194
  4.2 0.9 pad_maximum_fusion.1.refs_2_.refs_0_
  5.0 2.1 shard_map.196
  7.2 1.2 collective-permute-start.4
  9.3 1.5 copy.23.refs_3_.refs_7_
  10.7 1.9 constant_dynamic-slice_fusion
  12.6 1.5 convolution_convert_fusion.2
  14.6 0.9 pad_maximum_fusion.refs_5_.refs_7_
  15.5 14.5 %collective-permute-done.refs_1_ = bf16[12,384,128]{2,1,0:T(8,128)(2,1)S(1)} collective-permute-done((bf16[12,384,128]{2,1,0:T(8,128)(2,1)}, bf16[12,384,128]{2,1,0:T(8,128)(2,1)S(1)}, u32[]{:S(2)}, u32[]{:S(2)}) %collective-permute-start) | collective-permute-done | bytes 1179680 | tf_op jit(solution)/shard_map/ppermute | solution.py:414
  30.0 1.0 copy-done.13
  31.0 3.6 %shard_map.195 = (bf16[4,12,24,128]{3,2,1,0:T(8,128)(2,1)}, bf16[4,12,24,128]{3,2,1,0:T(8,128)(2,1)}, bf16[4,12,24,128]{3,2,1,0:T(8,128)(2,1)}, bf16[4,12,24,128]{3,2,1,0:T(8,128)(2,1)}) custom-call(s32[1]{0:T(128)} %bitcast.index_ref.place_ref, f32[12]{0:T(128)} %quad_ref.7, bf16[12,384,512]{2,1,0:T(8,128)(2,1)} %refs_9_.1, ...), custom_call_target="tpu_custom_call" | custom-call | flops 905969664 | bytes 4718592 | tf_op jit(solution)/shard_map/pallas_call | solution.py:168
  34.6 1.3 collective-permute-start.1
  36.0 1.3 collective-permute-start.3
  37.3 18.1 %collective-permute-done.4.refs_1_ = bf16[12,384,128]{2,1,0:T(8,128)(2,1)} collective-permute-done((bf16[12,384,128]{2,1,0:T(8,128)(2,1)}, bf16[12,384,128]{2,1,0:T(8,128)(2,1)}, u32[]{:S(2)}, u32[]{:S(2)}) %collective-permute-start.4) | collective-permute-done | bytes 1179680 | tf_op jit(solution)/shard_map/ppermute | solution.py:414
  56.1 3.7 %shard_map.197 = (bf16[4,12,24,128]{3,2,1,0:T(8,128)(2,1)}, bf16[4,12,24,128]{3,2,1,0:T(8,128)(2,1)}, bf16[4,12,24,128]{3,2,1,0:T(8,128)(2,1)}, bf16[4,12,24,128]{3,2,1,0:T(8,128)(2,1)}) custom-call(s32[1]{0:T(128)} %bitcast.1.index_ref.place_ref, f32[12]{0:T(128)} %quad_ref.7, bf16[12,384,512]{2,1,0:T(8,128)(2,1)} %refs_9_.1, ...), custom_call_target="tpu_custom_call" | custom-call | flops 905969664 | bytes 4718592 | tf_op jit(solution)/shard_map/pallas_call | solution.py:168
  59.8 1.6 collective-permute-done.3.refs_3_
  62.1 2.2 shard_map.198
  64.3 3.0 %collective-permute-start.5 = (bf16[4,12,24,128]{3,2,1,0:T(8,128)(2,1)}, bf16[4,12,24,128]{3,2,1,0:T(8,128)(2,1)S(1)}, u32[]{:S(2)}, u32[]{:S(2)}) collective-permute-start(bf16[4,12,24,128]{3,2,1,0:T(8,128)(2,1)} %get-tuple-element.47), channel_id=1, source_target_pairs={{0,2},{2,0},{4,6},{6,4},{8,10},{10,8},{12,14},{14,12},{16,18},{18,... | collective-permute-start | bytes 884744 | tf_op jit(solution)/shard_map/ppermute | solution.py:414
  67.3 1.2 collective-permute-start.6
  69.0 1.3 collective-permute-start.17
  70.3 1.4 collective-permute-start.18
  71.7 4.5 %collective-permute-done.6.refs_5_ = bf16[4,12,24,128]{3,2,1,0:T(8,128)(2,1)S(1)} collective-permute-done((bf16[4,12,24,128]{3,2,1,0:T(8,128)(2,1)}, bf16[4,12,24,128]{3,2,1,0:T(8,128)(2,1)S(1)}, u32[]{:S(2)}, u32[]{:S(2)}) %collective-permute-start.6) | collective-permute-done | bytes 294944 | tf_op jit(solution)/shard_map/ppermute | solution.py:414
  76.2 6.7 %collective-permute-done.7.refs_6_ = bf16[4,12,24,128]{3,2,1,0:T(8,128)(2,1)S(1)} collective-permute-done((bf16[4,12,24,128]{3,2,1,0:T(8,128)(2,1)}, bf16[4,12,24,128]{3,2,1,0:T(8,128)(2,1)S(1)}, u32[]{:S(2)}, u32[]{:S(2)}) %collective-permute-start.7) | collective-permute-done | bytes 294944 | tf_op jit(solution)/shard_map/ppermute | solution.py:414
  83.6 4.2 %shard_map.199 = (bf16[4,12,24,128]{3,2,1,0:T(8,128)(2,1)}, bf16[4,12,24,128]{3,2,1,0:T(8,128)(2,1)}, bf16[4,12,24,128]{3,2,1,0:T(8,128)(2,1)}, bf16[4,12,24,128]{3,2,1,0:T(8,128)(2,1)}) custom-call(bf16[4,12,24,128]{3,2,1,0:T(8,128)(2,1)} %get-tuple-element.42.refs_0_, bf16[4,12,24,128]{3,2,1,0:T(8,128)(2,1)} %copy-done.4, ...), custom_call_target="tpu_custom_call" | custom-call | bytes 14000000 | tf_op jit(solution)/shard_map/pallas_call | solution.py:248
  87.9 1.3 collective-permute-start.9
  89.1 0.9 collective-permute-start.10
  90.0 7.2 %collective-permute-done.18.refs_3_ = bf16[4,12,24,128]{3,2,1,0:T(8,128)(2,1)S(1)} collective-permute-done((bf16[4,12,24,128]{3,2,1,0:T(8,128)(2,1)S(1)}, bf16[4,12,24,128]{3,2,1,0:T(8,128)(2,1)S(1)}, u32[]{:S(2)}, u32[]{:S(2)}) %collective-permute-start.18) | collective-permute-done | bytes 294944 | tf_op jit(solution)/shard_map/ppermute | solution.py:414
  98.0 2.2 shard_map.203
  100.1 1.4 collective-permute-start.19
  101.5 1.2 collective-permute-start.20
  104.0 2.2 shard_map.200
  106.1 1.3 collective-permute-start.12
  107.5 1.3 collective-permute-start.13
  108.8 1.6 collective-permute-done.20.refs_5_
  110.3 6.7 %collective-permute-done.21.refs_6_ = bf16[4,12,24,128]{3,2,1,0:T(8,128)(2,1)S(1)} collective-permute-done((bf16[4,12,24,128]{3,2,1,0:T(8,128)(2,1)}, bf16[4,12,24,128]{3,2,1,0:T(8,128)(2,1)S(1)}, u32[]{:S(2)}, u32[]{:S(2)}) %collective-permute-start.21) | collective-permute-done | bytes 294944 | tf_op jit(solution)/shard_map/ppermute | solution.py:414
  117.8 4.2 %shard_map.204 = (bf16[4,12,24,128]{3,2,1,0:T(8,128)(2,1)}, bf16[4,12,24,128]{3,2,1,0:T(8,128)(2,1)}, bf16[4,12,24,128]{3,2,1,0:T(8,128)(2,1)}, bf16[4,12,24,128]{3,2,1,0:T(8,128)(2,1)}) custom-call(bf16[4,12,24,128]{3,2,1,0:T(8,128)(2,1)} %get-tuple-element.46.refs_4_.refs_0_, bf16[4,12,24,128]{3,2,1,0:T(8,128)(2,1)} %copy-done.5, ...), custom_call_target="tpu_custom_call" | custom-call | bytes 14000000 | tf_op jit(solution)/shard_map/pallas_call | solution.py:248
  122.0 1.3 collective-permute-start.23
  124.1 10.4 %collective-permute-done.13.refs_6_ = bf16[4,12,24,128]{3,2,1,0:T(8,128)(2,1)S(1)} collective-permute-done((bf16[4,12,24,128]{3,2,1,0:T(8,128)(2,1)}, bf16[4,12,24,128]{3,2,1,0:T(8,128)(2,1)S(1)}, u32[]{:S(2)}, u32[]{:S(2)}) %collective-permute-start.13) | collective-permute-done | bytes 294944 | tf_op jit(solution)/shard_map/ppermute | solution.py:414
  135.3 4.2 %shard_map.201 = (bf16[12,392,128]{2,1,0:T(8,128)(2,1)}, bf16[12,392,128]{2,1,0:T(8,128)(2,1)}, bf16[2,392,128]{2,1,0:T(8,128)(2,1)}, bf16[2,392,128]{2,1,0:T(8,128)(2,1)}) custom-call(bf16[4,12,24,128]{3,2,1,0:T(8,128)(2,1)} %get-tuple-element.50.refs_0_, bf16[4,12,24,128]{3,2,1,0:T(8,128)(2,1)} %copy-done.14, bf16[4,12,24,128]{3,2,1,0:T(8,128)(2,1)} %copy-done.15, ...), custom_call_target="tpu_custom_call" | custom-call | bytes 14000000 | tf_op jit(solution)/shard_map/pallas_call | solution.py:303
  139.5 4.5 %collective-permute-start.14 = (bf16[2,392,128]{2,1,0:T(8,128)(2,1)}, bf16[2,392,128]{2,1,0:T(8,128)(2,1)S(1)}, u32[]{:S(2)}, u32[]{:S(2)}) collective-permute-start(bf16[2,392,128]{2,1,0:T(8,128)(2,1)} %get-tuple-element.58), channel_id=1, source_target_pairs={{0,2},{2,4},{4,6},{6,8},{8,10},{10,12},{12,14},{14,16},{16,18},{18... | collective-permute-start | bytes 602120 | tf_op jit(solution)/shard_map/ppermute | solution.py:506
  144.9 2.2 shard_map.205
  147.1 1.4 collective-permute-start.26
  148.5 1.3 collective-permute-start.27
  149.8 1.9 collective-permute-start.15
  152.0 5.1 %collective-permute-done.15.high_ref = bf16[2,392,128]{2,1,0:T(8,128)(2,1)S(1)} collective-permute-done((bf16[2,392,128]{2,1,0:T(8,128)(2,1)S(1)}, bf16[2,392,128]{2,1,0:T(8,128)(2,1)S(1)}, u32[]{:S(2)}, u32[]{:S(2)}) %collective-permute-start.15) | collective-permute-done | bytes 200736 | tf_op jit(solution)/shard_map/ppermute | solution.py:507
  157.8 6.0 %shard_map.202.refs_8_.refs_0_ = bf16[12,384,128]{2,1,0:T(8,128)(2,1)} custom-call(s32[1]{0:T(128)} %bitcast.index_ref.place_ref, s32[12,12]{1,0:T(8,128)} %neighbour_ref.7, s32[12,12]{1,0:T(8,128)} %basis_ref.7, f32[12,12]{1,0:T(8,128)} %quad_ref.11, bf16[12,392,128]{2,1,0:T(8,128)(2,1)} %get-tuple-element.57.wave_ref, bf16[2,392,128]{2,1,0:T(8,128)(2,1)} %copy-done.29, ...), custom_call_target="tpu_custom_call" | custom-call | bytes 20000000 | tf_op jit(solution)/shard_map/pallas_call | solution.py:356
  163.7 4.1 %collective-permute-done.26.refs_5_ = bf16[4,12,24,128]{3,2,1,0:T(8,128)(2,1)S(1)} collective-permute-done((bf16[4,12,24,128]{3,2,1,0:T(8,128)(2,1)}, bf16[4,12,24,128]{3,2,1,0:T(8,128)(2,1)S(1)}, u32[]{:S(2)}, u32[]{:S(2)}) %collective-permute-start.26) | collective-permute-done | bytes 294944 | tf_op jit(solution)/shard_map/ppermute | solution.py:414
  167.9 8.3 %collective-permute-done.27.refs_6_ = bf16[4,12,24,128]{3,2,1,0:T(8,128)(2,1)S(1)} collective-permute-done((bf16[4,12,24,128]{3,2,1,0:T(8,128)(2,1)}, bf16[4,12,24,128]{3,2,1,0:T(8,128)(2,1)S(1)}, u32[]{:S(2)}, u32[]{:S(2)}) %collective-permute-start.27) | collective-permute-done | bytes 294944 | tf_op jit(solution)/shard_map/ppermute | solution.py:414
  176.9 4.2 %shard_map.206 = (bf16[12,392,128]{2,1,0:T(8,128)(2,1)}, bf16[12,392,128]{2,1,0:T(8,128)(2,1)}, bf16[2,392,128]{2,1,0:T(8,128)(2,1)}, bf16[2,392,128]{2,1,0:T(8,128)(2,1)}) custom-call(bf16[4,12,24,128]{3,2,1,0:T(8,128)(2,1)} %get-tuple-element.66.refs_0_, bf16[4,12,24,128]{3,2,1,0:T(8,128)(2,1)} %copy-done.8, bf16[4,12,24,128]{3,2,1,0:T(8,128)(2,1)} %copy-done.9, ...), custom_call_target="tpu_custom_call" | custom-call | bytes 14000000 | tf_op jit(solution)/shard_map/pallas_call | solution.py:303
  181.4 1.9 collective-permute-start.28
  183.3 10.2 %collective-permute-start.29 = (bf16[2,392,128]{2,1,0:T(8,128)(2,1)}, bf16[2,392,128]{2,1,0:T(8,128)(2,1)S(1)}, u32[]{:S(2)}, u32[]{:S(2)}) collective-permute-start(bf16[2,392,128]{2,1,0:T(8,128)(2,1)} %get-tuple-element.75), channel_id=1, source_target_pairs={{2,0},{4,2},{6,4},{8,6},{10,8},{12,10},{14,12},{16,14},{18,16},{20... | collective-permute-start | bytes 602120 | tf_op jit(solution)/shard_map/ppermute | solution.py:507
  193.5 1.0 copy-done.2
  194.5 1.8 shard_map.208
  196.3 1.9 collective-permute-start.31
  198.3 4.7 %collective-permute-start.32 = (bf16[2,392,128]{2,1,0:T(8,128)(2,1)}, bf16[2,392,128]{2,1,0:T(8,128)(2,1)S(1)}, u32[]{:S(2)}, u32[]{:S(2)}) collective-permute-start(bf16[2,392,128]{2,1,0:T(8,128)(2,1)} %get-tuple-element.78), channel_id=1, source_target_pairs={{2,0},{4,2},{6,4},{8,6},{10,8},{12,10},{14,12},{16,14},{18,16},{20... | collective-permute-start | bytes 602120 | tf_op jit(solution)/shard_map/ppermute | solution.py:507
  203.8 5.9 %shard_map.207.refs_1_ = bf16[12,384,128]{2,1,0:T(8,128)(2,1)} custom-call(s32[1]{0:T(128)} %bitcast.1.index_ref.place_ref, s32[12,12]{1,0:T(8,128)} %neighbour_ref.7, s32[12,12]{1,0:T(8,128)} %basis_ref.7, f32[12,12]{1,0:T(8,128)} %quad_ref.11, bf16[12,392,128]{2,1,0:T(8,128)(2,1)} %get-tuple-element.73.wave_ref, bf16[2,392,128]{2,1,0:T(8,128)(2,1)} %copy-done.30, ...), custom_call_target="tpu_custom_call" | custom-call | bytes 20000000 | tf_op jit(solution)/shard_map/pallas_call | solution.py:356
  211.1 6.0 %shard_map.209.refs_2_ = bf16[12,384,128]{2,1,0:T(8,128)(2,1)} custom-call(s32[1]{0:T(128)} %bitcast.2.index_ref.place_ref, s32[12,12]{1,0:T(8,128)} %neighbour_ref.7, s32[12,12]{1,0:T(8,128)} %basis_ref.7, f32[12,12]{1,0:T(8,128)} %quad_ref.11, bf16[12,392,128]{2,1,0:T(8,128)(2,1)} %copy-done.2, bf16[2,392,128]{2,1,0:T(8,128)(2,1)} %copy-done.32, ...), custom_call_target="tpu_custom_call" | custom-call | bytes 20000000 | tf_op jit(solution)/shard_map/pallas_call | solution.py:356
  217.1 1.0 copy-done.3
  218.1 1.8 shard_map.210
  219.8 1.9 collective-permute-start.34
  221.8 4.6 %collective-permute-start.35 = (bf16[2,392,128]{2,1,0:T(8,128)(2,1)}, bf16[2,392,128]{2,1,0:T(8,128)(2,1)S(1)}, u32[]{:S(2)}, u32[]{:S(2)}) collective-permute-start(bf16[2,392,128]{2,1,0:T(8,128)(2,1)} %get-tuple-element.81), channel_id=1, source_target_pairs={{2,0},{4,2},{6,4},{8,6},{10,8},{12,10},{14,12},{16,14},{18,16},{20... | collective-permute-start | bytes 602120 | tf_op jit(solution)/shard_map/ppermute | solution.py:507
  227.0 4.1 %collective-permute-done.35.high_ref = bf16[2,392,128]{2,1,0:T(8,128)(2,1)S(1)} collective-permute-done((bf16[2,392,128]{2,1,0:T(8,128)(2,1)}, bf16[2,392,128]{2,1,0:T(8,128)(2,1)S(1)}, u32[]{:S(2)}, u32[]{:S(2)}) %collective-permute-start.35) | collective-permute-done | bytes 200736 | tf_op jit(solution)/shard_map/ppermute | solution.py:507
  231.8 5.9 %shard_map.211.refs_3_ = bf16[12,384,128]{2,1,0:T(8,128)(2,1)} custom-call(s32[1]{0:T(128)} %bitcast.3.index_ref.place_ref, s32[12,12]{1,0:T(8,128)} %neighbour_ref.7, s32[12,12]{1,0:T(8,128)} %basis_ref.7, f32[12,12]{1,0:T(8,128)} %quad_ref.11, bf16[12,392,128]{2,1,0:T(8,128)(2,1)} %copy-done.3, bf16[2,392,128]{2,1,0:T(8,128)(2,1)} %copy-done.34, ...), custom_call_target="tpu_custom_call" | custom-call | bytes 20000000 | tf_op jit(solution)/shard_map/pallas_call | solution.py:356
  237.8 17.8 %shard_map.212 = (bf16[12,384,512]{2,1,0:T(8,128)(2,1)}, bf16[12,384,512]{2,1,0:T(8,128)(2,1)}) custom-call(s32[4]{0:T(128)} %pad_add_fusion.place_ref, bf16[12,384,128]{2,1,0:T(8,128)(2,1)} %shard_map.202.refs_8_.refs_0_, bf16[12,384,128]{2,1,0:T(8,128)(2,1)} %shard_map.207.refs_1_, bf16[12,384,128]{2,1,0:T(8,128)(2,1)} %shard_map.209.refs_2_, ...), custom_call_target="tpu_custom_call" | custom-call | flops 9663676416 | bytes 18874368 | tf_op jit(solution)/shard_map/pallas_call | solution.py:395
  (132 shorter events, 15.9 us)
Async XLA Ops:
  0.6 7.9 %copy-start = (bf16[12,192,192]{2,1,0:T(8,128)(2,1)S(1)}, bf16[12,192,192]{2,1,0:T(8,128)(2,1)}, u32[]{:S(2)}) copy-start(bf16[12,192,192]{2,1,0:T(8,128)(2,1)} %param.21) | copy-start | bytes 2654212
  0.7 2.5 copy-start.37
  0.7 2.7 %copy-start.43 = (bf16[2,384,384]{2,1,0:T(8,128)(2,1)S(1)}, bf16[2,384,384]{2,1,0:T(8,128)(2,1)}, u32[]{:S(2)}) copy-start(bf16[2,384,384]{2,1,0:T(8,128)(2,1)} %constant.47.clone) | copy-start | bytes 1769476
  2.9 27.0 %collective-permute-start = (bf16[12,384,128]{2,1,0:T(8,128)(2,1)}, bf16[12,384,128]{2,1,0:T(8,128)(2,1)S(1)}, u32[]{:S(2)}, u32[]{:S(2)}) collective-permute-start(bf16[12,384,128]{2,1,0:T(8,128)(2,1)} %shard_map.194), channel_id=1, source_target_pairs={{0,1},{1,0},{2,3},{3,2},{4,5},{5,4},{6,7},{7,6},{8,9},{9,8},{10,11... | collective-permute-start | bytes 3538952 | tf_op jit(solution)/shard_map/ppermute | solution.py:414
  7.2 48.2 %collective-permute-start.4 = (bf16[12,384,128]{2,1,0:T(8,128)(2,1)}, bf16[12,384,128]{2,1,0:T(8,128)(2,1)}, u32[]{:S(2)}, u32[]{:S(2)}) collective-permute-start(bf16[12,384,128]{2,1,0:T(8,128)(2,1)} %shard_map.196), channel_id=1, source_target_pairs={{0,1},{1,0},{2,3},{3,2},{4,5},{5,4},{6,7},{7,6},{8,9},{9,8},{10,11... | collective-permute-start | bytes 3538952 | tf_op jit(solution)/shard_map/ppermute | solution.py:414
  9.1 1.7 copy-start.1
  10.7 3.3 %copy-start.42 = (bf16[2,392,384]{2,1,0:T(8,128)(2,1)S(1)}, bf16[2,392,384]{2,1,0:T(8,128)(2,1)}, u32[]{:S(2)}) copy-start(bf16[2,392,384]{2,1,0:T(8,128)(2,1)} %constant.48.clone) | copy-start | bytes 1806340
  30.0 1.0 copy-start.13
  34.6 20.7 %collective-permute-start.1 = (bf16[4,12,24,128]{3,2,1,0:T(8,128)(2,1)}, bf16[4,12,24,128]{3,2,1,0:T(8,128)(2,1)S(1)}, u32[]{:S(2)}, u32[]{:S(2)}) collective-permute-start(bf16[4,12,24,128]{3,2,1,0:T(8,128)(2,1)} %get-tuple-element.43), channel_id=1, source_target_pairs={{0,8},{2,10},{4,12},{6,14},{8,0},{10,2},{12,4},{14,6},{16,24},{18,... | collective-permute-start | bytes 884744 | tf_op jit(solution)/shard_map/ppermute | solution.py:414
  35.9 23.8 %collective-permute-start.2 = (bf16[4,12,24,128]{3,2,1,0:T(8,128)(2,1)}, bf16[4,12,24,128]{3,2,1,0:T(8,128)(2,1)S(1)}, u32[]{:S(2)}, u32[]{:S(2)}) collective-permute-start(bf16[4,12,24,128]{3,2,1,0:T(8,128)(2,1)} %get-tuple-element.44), channel_id=1, source_target_pairs={{0,16},{2,18},{4,20},{6,22},{8,24},{10,26},{12,28},{14,30},{16,0},... | collective-permute-start | bytes 884744 | tf_op jit(solution)/shard_map/ppermute | solution.py:414
  36.0 25.4 %collective-permute-start.3 = (bf16[4,12,24,128]{3,2,1,0:T(8,128)(2,1)}, bf16[4,12,24,128]{3,2,1,0:T(8,128)(2,1)S(1)}, u32[]{:S(2)}, u32[]{:S(2)}) collective-permute-start(bf16[4,12,24,128]{3,2,1,0:T(8,128)(2,1)} %get-tuple-element.45), channel_id=1, source_target_pairs={{0,24},{2,26},{4,28},{6,30},{8,16},{10,18},{12,20},{14,22},{16,8},... | collective-permute-start | bytes 884744 | tf_op jit(solution)/shard_map/ppermute | solution.py:414
  59.7 9.2 %copy-start.40 = (bf16[4,12,24,128]{3,2,1,0:T(8,128)(2,1)S(1)}, bf16[4,12,24,128]{3,2,1,0:T(8,128)(2,1)}, u32[]{:S(2)}) copy-start(bf16[4,12,24,128]{3,2,1,0:T(8,128)(2,1)} %get-tuple-element.60) | copy-start | bytes 884740
  59.7 9.2 %copy-start.39 = (bf16[4,12,24,128]{3,2,1,0:T(8,128)(2,1)S(1)}, bf16[4,12,24,128]{3,2,1,0:T(8,128)(2,1)}, u32[]{:S(2)}) copy-start(bf16[4,12,24,128]{3,2,1,0:T(8,128)(2,1)} %get-tuple-element.61) | copy-start | bytes 884740
  59.7 10.6 %copy-start.38 = (bf16[4,12,24,128]{3,2,1,0:T(8,128)(2,1)S(1)}, bf16[4,12,24,128]{3,2,1,0:T(8,128)(2,1)}, u32[]{:S(2)}) copy-start(bf16[4,12,24,128]{3,2,1,0:T(8,128)(2,1)} %get-tuple-element.62) | copy-start | bytes 884740
  59.8 1.7 copy-start.11
  64.3 6.0 %collective-permute-start.5 = (bf16[4,12,24,128]{3,2,1,0:T(8,128)(2,1)}, bf16[4,12,24,128]{3,2,1,0:T(8,128)(2,1)S(1)}, u32[]{:S(2)}, u32[]{:S(2)}) collective-permute-start(bf16[4,12,24,128]{3,2,1,0:T(8,128)(2,1)} %get-tuple-element.47), channel_id=1, source_target_pairs={{0,2},{2,0},{4,6},{6,4},{8,10},{10,8},{12,14},{14,12},{16,18},{18,... | collective-permute-start | bytes 884744 | tf_op jit(solution)/shard_map/ppermute | solution.py:414
  67.3 8.8 %collective-permute-start.6 = (bf16[4,12,24,128]{3,2,1,0:T(8,128)(2,1)}, bf16[4,12,24,128]{3,2,1,0:T(8,128)(2,1)S(1)}, u32[]{:S(2)}, u32[]{:S(2)}) collective-permute-start(bf16[4,12,24,128]{3,2,1,0:T(8,128)(2,1)} %get-tuple-element.48), channel_id=1, source_target_pairs={{0,4},{2,6},{4,0},{6,2},{8,12},{10,14},{12,8},{14,10},{16,20},{18,... | collective-permute-start | bytes 884744 | tf_op jit(solution)/shard_map/ppermute | solution.py:414
  68.6 14.3 %collective-permute-start.7 = (bf16[4,12,24,128]{3,2,1,0:T(8,128)(2,1)}, bf16[4,12,24,128]{3,2,1,0:T(8,128)(2,1)S(1)}, u32[]{:S(2)}, u32[]{:S(2)}) collective-permute-start(bf16[4,12,24,128]{3,2,1,0:T(8,128)(2,1)} %get-tuple-element.49), channel_id=1, source_target_pairs={{0,6},{2,4},{4,2},{6,0},{8,14},{10,12},{12,10},{14,8},{16,22},{18,... | collective-permute-start | bytes 884744 | tf_op jit(solution)/shard_map/ppermute | solution.py:414
  69.0 20.2 %collective-permute-start.16 = (bf16[4,12,24,128]{3,2,1,0:T(8,128)(2,1)S(1)}, bf16[4,12,24,128]{3,2,1,0:T(8,128)(2,1)S(1)}, u32[]{:S(2)}, u32[]{:S(2)}) collective-permute-start(bf16[4,12,24,128]{3,2,1,0:T(8,128)(2,1)S(1)} %copy-done.40), channel_id=1, source_target_pairs={{0,8},{2,10},{4,12},{6,14},{8,0},{10,2},{12,4},{14,6},{16,24},{18,... | collective-permute-start | bytes 884744 | tf_op jit(solution)/shard_map/ppermute | solution.py:414
  69.0 21.0 %collective-permute-start.17 = (bf16[4,12,24,128]{3,2,1,0:T(8,128)(2,1)S(1)}, bf16[4,12,24,128]{3,2,1,0:T(8,128)(2,1)S(1)}, u32[]{:S(2)}, u32[]{:S(2)}) collective-permute-start(bf16[4,12,24,128]{3,2,1,0:T(8,128)(2,1)S(1)} %copy-done.39), channel_id=1, source_target_pairs={{0,16},{2,18},{4,20},{6,22},{8,24},{10,26},{12,28},{14,30},{16,0},... | collective-permute-start | bytes 884744 | tf_op jit(solution)/shard_map/ppermute | solution.py:414
  70.3 12.6 %copy-start.22 = (bf16[4,12,24,128]{3,2,1,0:T(8,128)(2,1)}, bf16[4,12,24,128]{3,2,1,0:T(8,128)(2,1)S(1)}, u32[]{:S(2)}) copy-start(bf16[4,12,24,128]{3,2,1,0:T(8,128)(2,1)S(1)} %collective-permute-done.5.refs_4_) | copy-start | bytes 884740
  70.3 26.9 %collective-permute-start.18 = (bf16[4,12,24,128]{3,2,1,0:T(8,128)(2,1)S(1)}, bf16[4,12,24,128]{3,2,1,0:T(8,128)(2,1)S(1)}, u32[]{:S(2)}, u32[]{:S(2)}) collective-permute-start(bf16[4,12,24,128]{3,2,1,0:T(8,128)(2,1)S(1)} %copy-done.38), channel_id=1, source_target_pairs={{0,24},{2,26},{4,28},{6,30},{8,16},{10,18},{12,20},{14,22},{16,8},... | collective-permute-start | bytes 884744 | tf_op jit(solution)/shard_map/ppermute | solution.py:414
  76.2 6.7 %copy-start.24 = (bf16[4,12,24,128]{3,2,1,0:T(8,128)(2,1)}, bf16[4,12,24,128]{3,2,1,0:T(8,128)(2,1)S(1)}, u32[]{:S(2)}) copy-start(bf16[4,12,24,128]{3,2,1,0:T(8,128)(2,1)S(1)} %collective-permute-done.6.refs_5_) | copy-start | bytes 884740
  87.9 14.9 %collective-permute-start.8 = (bf16[4,12,24,128]{3,2,1,0:T(8,128)(2,1)}, bf16[4,12,24,128]{3,2,1,0:T(8,128)(2,1)S(1)}, u32[]{:S(2)}, u32[]{:S(2)}) collective-permute-start(bf16[4,12,24,128]{3,2,1,0:T(8,128)(2,1)} %get-tuple-element.51), channel_id=1, source_target_pairs={{0,2},{2,0},{4,6},{6,4},{8,10},{10,8},{12,14},{14,12},{16,18},{18,... | collective-permute-start | bytes 884744 | tf_op jit(solution)/shard_map/ppermute | solution.py:414
  87.9 15.3 %collective-permute-start.9 = (bf16[4,12,24,128]{3,2,1,0:T(8,128)(2,1)}, bf16[4,12,24,128]{3,2,1,0:T(8,128)(2,1)S(1)}, u32[]{:S(2)}, u32[]{:S(2)}) collective-permute-start(bf16[4,12,24,128]{3,2,1,0:T(8,128)(2,1)} %get-tuple-element.52), channel_id=1, source_target_pairs={{0,4},{2,6},{4,0},{6,2},{8,12},{10,14},{12,8},{14,10},{16,20},{18,... | collective-permute-start | bytes 884744 | tf_op jit(solution)/shard_map/ppermute | solution.py:414
  89.1 8.1 %copy-start.5 = (bf16[4,12,24,128]{3,2,1,0:T(8,128)(2,1)}, bf16[4,12,24,128]{3,2,1,0:T(8,128)(2,1)S(1)}, u32[]{:S(2)}) copy-start(bf16[4,12,24,128]{3,2,1,0:T(8,128)(2,1)S(1)} %collective-permute-done.16.refs_1_) | copy-start | bytes 884740
  89.1 14.0 %collective-permute-start.10 = (bf16[4,12,24,128]{3,2,1,0:T(8,128)(2,1)}, bf16[4,12,24,128]{3,2,1,0:T(8,128)(2,1)S(1)}, u32[]{:S(2)}, u32[]{:S(2)}) collective-permute-start(bf16[4,12,24,128]{3,2,1,0:T(8,128)(2,1)} %get-tuple-element.53), channel_id=1, source_target_pairs={{0,6},{2,4},{4,2},{6,0},{8,14},{10,12},{12,10},{14,8},{16,22},{18,... | collective-permute-start | bytes 884744 | tf_op jit(solution)/shard_map/ppermute | solution.py:414
  90.0 7.2 %copy-start.6 = (bf16[4,12,24,128]{3,2,1,0:T(8,128)(2,1)}, bf16[4,12,24,128]{3,2,1,0:T(8,128)(2,1)S(1)}, u32[]{:S(2)}) copy-start(bf16[4,12,24,128]{3,2,1,0:T(8,128)(2,1)S(1)} %collective-permute-done.17.refs_2_) | copy-start | bytes 884740
  100.1 7.3 %collective-permute-start.19 = (bf16[4,12,24,128]{3,2,1,0:T(8,128)(2,1)}, bf16[4,12,24,128]{3,2,1,0:T(8,128)(2,1)S(1)}, u32[]{:S(2)}, u32[]{:S(2)}) collective-permute-start(bf16[4,12,24,128]{3,2,1,0:T(8,128)(2,1)} %get-tuple-element.63), channel_id=1, source_target_pairs={{0,2},{2,0},{4,6},{6,4},{8,10},{10,8},{12,14},{14,12},{16,18},{18,... | collective-permute-start | bytes 884744 | tf_op jit(solution)/shard_map/ppermute | solution.py:414
  101.5 8.8 %collective-permute-start.20 = (bf16[4,12,24,128]{3,2,1,0:T(8,128)(2,1)}, bf16[4,12,24,128]{3,2,1,0:T(8,128)(2,1)S(1)}, u32[]{:S(2)}, u32[]{:S(2)}) collective-permute-start(bf16[4,12,24,128]{3,2,1,0:T(8,128)(2,1)} %get-tuple-element.64), channel_id=1, source_target_pairs={{0,4},{2,6},{4,0},{6,2},{8,12},{10,14},{12,8},{14,10},{16,20},{18,... | collective-permute-start | bytes 884744 | tf_op jit(solution)/shard_map/ppermute | solution.py:414
  102.7 14.3 %collective-permute-start.21 = (bf16[4,12,24,128]{3,2,1,0:T(8,128)(2,1)}, bf16[4,12,24,128]{3,2,1,0:T(8,128)(2,1)S(1)}, u32[]{:S(2)}, u32[]{:S(2)}) collective-permute-start(bf16[4,12,24,128]{3,2,1,0:T(8,128)(2,1)} %get-tuple-element.65), channel_id=1, source_target_pairs={{0,6},{2,4},{4,2},{6,0},{8,14},{10,12},{12,10},{14,8},{16,22},{18,... | collective-permute-start | bytes 884744 | tf_op jit(solution)/shard_map/ppermute | solution.py:414
  103.2 0.8 copy-start.16
  106.1 17.1 %collective-permute-start.11 = (bf16[4,12,24,128]{3,2,1,0:T(8,128)(2,1)}, bf16[4,12,24,128]{3,2,1,0:T(8,128)(2,1)S(1)}, u32[]{:S(2)}, u32[]{:S(2)}) collective-permute-start(bf16[4,12,24,128]{3,2,1,0:T(8,128)(2,1)} %get-tuple-element.54), channel_id=1, source_target_pairs={{0,8},{2,10},{4,12},{6,14},{8,0},{10,2},{12,4},{14,6},{16,24},{18,... | collective-permute-start | bytes 884744 | tf_op jit(solution)/shard_map/ppermute | solution.py:414
  106.1 18.0 %collective-permute-start.12 = (bf16[4,12,24,128]{3,2,1,0:T(8,128)(2,1)}, bf16[4,12,24,128]{3,2,1,0:T(8,128)(2,1)S(1)}, u32[]{:S(2)}, u32[]{:S(2)}) collective-permute-start(bf16[4,12,24,128]{3,2,1,0:T(8,128)(2,1)} %get-tuple-element.55), channel_id=1, source_target_pairs={{0,16},{2,18},{4,20},{6,22},{8,24},{10,26},{12,28},{14,30},{16,0},... | collective-permute-start | bytes 884744 | tf_op jit(solution)/shard_map/ppermute | solution.py:414
  107.5 9.6 %copy-start.17 = (bf16[4,12,24,128]{3,2,1,0:T(8,128)(2,1)}, bf16[4,12,24,128]{3,2,1,0:T(8,128)(2,1)S(1)}, u32[]{:S(2)}) copy-start(bf16[4,12,24,128]{3,2,1,0:T(8,128)(2,1)S(1)} %collective-permute-done.19.refs_4_) | copy-start | bytes 884740
  107.5 27.1 %collective-permute-start.13 = (bf16[4,12,24,128]{3,2,1,0:T(8,128)(2,1)}, bf16[4,12,24,128]{3,2,1,0:T(8,128)(2,1)S(1)}, u32[]{:S(2)}, u32[]{:S(2)}) collective-permute-start(bf16[4,12,24,128]{3,2,1,0:T(8,128)(2,1)} %get-tuple-element.56), channel_id=1, source_target_pairs={{0,24},{2,26},{4,28},{6,30},{8,16},{10,18},{12,20},{14,22},{16,8},... | collective-permute-start | bytes 884744 | tf_op jit(solution)/shard_map/ppermute | solution.py:414
  110.3 6.7 %copy-start.18 = (bf16[4,12,24,128]{3,2,1,0:T(8,128)(2,1)}, bf16[4,12,24,128]{3,2,1,0:T(8,128)(2,1)S(1)}, u32[]{:S(2)}) copy-start(bf16[4,12,24,128]{3,2,1,0:T(8,128)(2,1)S(1)} %collective-permute-done.20.refs_5_) | copy-start | bytes 884740
  122.0 22.0 %collective-permute-start.22 = (bf16[4,12,24,128]{3,2,1,0:T(8,128)(2,1)}, bf16[4,12,24,128]{3,2,1,0:T(8,128)(2,1)S(1)}, u32[]{:S(2)}, u32[]{:S(2)}) collective-permute-start(bf16[4,12,24,128]{3,2,1,0:T(8,128)(2,1)} %get-tuple-element.67), channel_id=1, source_target_pairs={{0,2},{2,0},{4,6},{6,4},{8,10},{10,8},{12,14},{14,12},{16,18},{18,... | collective-permute-start | bytes 884744 | tf_op jit(solution)/shard_map/ppermute | solution.py:414
  122.0 22.0 %collective-permute-start.23 = (bf16[4,12,24,128]{3,2,1,0:T(8,128)(2,1)}, bf16[4,12,24,128]{3,2,1,0:T(8,128)(2,1)S(1)}, u32[]{:S(2)}, u32[]{:S(2)}) collective-permute-start(bf16[4,12,24,128]{3,2,1,0:T(8,128)(2,1)} %get-tuple-element.68), channel_id=1, source_target_pairs={{0,4},{2,6},{4,0},{6,2},{8,12},{10,14},{12,8},{14,10},{16,20},{18,... | collective-permute-start | bytes 884744 | tf_op jit(solution)/shard_map/ppermute | solution.py:414
  123.3 11.3 %copy-start.26 = (bf16[4,12,24,128]{3,2,1,0:T(8,128)(2,1)}, bf16[4,12,24,128]{3,2,1,0:T(8,128)(2,1)S(1)}, u32[]{:S(2)}) copy-start(bf16[4,12,24,128]{3,2,1,0:T(8,128)(2,1)S(1)} %collective-permute-done.11.refs_4_) | copy-start | bytes 884740
  123.3 20.8 %collective-permute-start.24 = (bf16[4,12,24,128]{3,2,1,0:T(8,128)(2,1)}, bf16[4,12,24,128]{3,2,1,0:T(8,128)(2,1)S(1)}, u32[]{:S(2)}, u32[]{:S(2)}) collective-permute-start(bf16[4,12,24,128]{3,2,1,0:T(8,128)(2,1)} %get-tuple-element.69), channel_id=1, source_target_pairs={{0,6},{2,4},{4,2},{6,0},{8,14},{10,12},{12,10},{14,8},{16,22},{18,... | collective-permute-start | bytes 884744 | tf_op jit(solution)/shard_map/ppermute | solution.py:414
  124.1 10.5 %copy-start.27 = (bf16[4,12,24,128]{3,2,1,0:T(8,128)(2,1)}, bf16[4,12,24,128]{3,2,1,0:T(8,128)(2,1)S(1)}, u32[]{:S(2)}) copy-start(bf16[4,12,24,128]{3,2,1,0:T(8,128)(2,1)S(1)} %collective-permute-done.12.refs_5_) | copy-start | bytes 884740
  139.5 10.3 %copy-start.41 = (bf16[2,392,128]{2,1,0:T(8,128)(2,1)S(1)}, bf16[2,392,128]{2,1,0:T(8,128)(2,1)}, u32[]{:S(2)}) copy-start(bf16[2,392,128]{2,1,0:T(8,128)(2,1)} %get-tuple-element.59) | copy-start | bytes 602116
  139.5 12.2 %collective-permute-start.14 = (bf16[2,392,128]{2,1,0:T(8,128)(2,1)}, bf16[2,392,128]{2,1,0:T(8,128)(2,1)S(1)}, u32[]{:S(2)}, u32[]{:S(2)}) collective-permute-start(bf16[2,392,128]{2,1,0:T(8,128)(2,1)} %get-tuple-element.58), channel_id=1, source_target_pairs={{0,2},{2,4},{4,6},{6,8},{8,10},{10,12},{12,14},{14,16},{16,18},{18... | collective-permute-start | bytes 602120 | tf_op jit(solution)/shard_map/ppermute | solution.py:506
  144.0 0.8 copy-start.9
  144.1 0.9 copy-start.10
  147.1 16.6 %collective-permute-start.25 = (bf16[4,12,24,128]{3,2,1,0:T(8,128)(2,1)}, bf16[4,12,24,128]{3,2,1,0:T(8,128)(2,1)S(1)}, u32[]{:S(2)}, u32[]{:S(2)}) collective-permute-start(bf16[4,12,24,128]{3,2,1,0:T(8,128)(2,1)} %get-tuple-element.70), channel_id=1, source_target_pairs={{0,8},{2,10},{4,12},{6,14},{8,0},{10,2},{12,4},{14,6},{16,24},{18,... | collective-permute-start | bytes 884744 | tf_op jit(solution)/shard_map/ppermute | solution.py:414
  147.1 20.7 %collective-permute-start.26 = (bf16[4,12,24,128]{3,2,1,0:T(8,128)(2,1)}, bf16[4,12,24,128]{3,2,1,0:T(8,128)(2,1)S(1)}, u32[]{:S(2)}, u32[]{:S(2)}) collective-permute-start(bf16[4,12,24,128]{3,2,1,0:T(8,128)(2,1)} %get-tuple-element.71), channel_id=1, source_target_pairs={{0,16},{2,18},{4,20},{6,22},{8,24},{10,26},{12,28},{14,30},{16,0},... | collective-permute-start | bytes 884744 | tf_op jit(solution)/shard_map/ppermute | solution.py:414
  148.5 27.7 %collective-permute-start.27 = (bf16[4,12,24,128]{3,2,1,0:T(8,128)(2,1)}, bf16[4,12,24,128]{3,2,1,0:T(8,128)(2,1)S(1)}, u32[]{:S(2)}, u32[]{:S(2)}) collective-permute-start(bf16[4,12,24,128]{3,2,1,0:T(8,128)(2,1)} %get-tuple-element.72), channel_id=1, source_target_pairs={{0,24},{2,26},{4,28},{6,30},{8,16},{10,18},{12,20},{14,22},{16,8},... | collective-permute-start | bytes 884744 | tf_op jit(solution)/shard_map/ppermute | solution.py:414
  149.8 7.3 %collective-permute-start.15 = (bf16[2,392,128]{2,1,0:T(8,128)(2,1)S(1)}, bf16[2,392,128]{2,1,0:T(8,128)(2,1)S(1)}, u32[]{:S(2)}, u32[]{:S(2)}) collective-permute-start(bf16[2,392,128]{2,1,0:T(8,128)(2,1)S(1)} %copy-done.41), channel_id=1, source_target_pairs={{2,0},{4,2},{6,4},{8,6},{10,8},{12,10},{14,12},{16,14},{18,16},{20... | collective-permute-start | bytes 602120 | tf_op jit(solution)/shard_map/ppermute | solution.py:507
  151.7 5.4 %copy-start.29 = (bf16[2,392,128]{2,1,0:T(8,128)(2,1)}, bf16[2,392,128]{2,1,0:T(8,128)(2,1)S(1)}, u32[]{:S(2)}) copy-start(bf16[2,392,128]{2,1,0:T(8,128)(2,1)S(1)} %collective-permute-done.14.low_ref) | copy-start | bytes 602116
  151.7 41.8 %collective-permute-start.30 = (bf16[12,392,128]{2,1,0:T(8,128)(2,1)}, bf16[12,392,128]{2,1,0:T(8,128)(2,1)S(1)}, u32[]{:S(2)}, u32[]{:S(2)}) collective-permute-start(bf16[12,392,128]{2,1,0:T(8,128)(2,1)} %get-tuple-element.76), channel_id=1, source_target_pairs={{0,1},{1,0},{2,3},{3,2},{4,5},{5,4},{6,7},{7,6},{8,9},{9,8},{10,11... | collective-permute-start | bytes 3612680 | tf_op jit(solution)/shard_map/ppermute | solution.py:414
  163.7 12.5 %copy-start.20 = (bf16[4,12,24,128]{3,2,1,0:T(8,128)(2,1)}, bf16[4,12,24,128]{3,2,1,0:T(8,128)(2,1)S(1)}, u32[]{:S(2)}) copy-start(bf16[4,12,24,128]{3,2,1,0:T(8,128)(2,1)S(1)} %collective-permute-done.25.refs_4_) | copy-start | bytes 884740
  167.9 8.3 %copy-start.21 = (bf16[4,12,24,128]{3,2,1,0:T(8,128)(2,1)}, bf16[4,12,24,128]{3,2,1,0:T(8,128)(2,1)S(1)}, u32[]{:S(2)}) copy-start(bf16[4,12,24,128]{3,2,1,0:T(8,128)(2,1)S(1)} %collective-permute-done.26.refs_5_) | copy-start | bytes 884740
  181.1 36.0 %collective-permute-start.33 = (bf16[12,392,128]{2,1,0:T(8,128)(2,1)}, bf16[12,392,128]{2,1,0:T(8,128)(2,1)S(1)}, u32[]{:S(2)}, u32[]{:S(2)}) collective-permute-start(bf16[12,392,128]{2,1,0:T(8,128)(2,1)} %get-tuple-element.79), channel_id=1, source_target_pairs={{0,1},{1,0},{2,3},{3,2},{4,5},{5,4},{6,7},{7,6},{8,9},{9,8},{10,11... | collective-permute-start | bytes 3612680 | tf_op jit(solution)/shard_map/ppermute | solution.py:414
  181.4 21.6 %collective-permute-start.28 = (bf16[2,392,128]{2,1,0:T(8,128)(2,1)}, bf16[2,392,128]{2,1,0:T(8,128)(2,1)S(1)}, u32[]{:S(2)}, u32[]{:S(2)}) collective-permute-start(bf16[2,392,128]{2,1,0:T(8,128)(2,1)} %get-tuple-element.74), channel_id=1, source_target_pairs={{0,2},{2,4},{4,6},{6,8},{8,10},{10,12},{12,14},{14,16},{16,18},{18... | collective-permute-start | bytes 602120 | tf_op jit(solution)/shard_map/ppermute | solution.py:506
  183.3 19.7 %collective-permute-start.29 = (bf16[2,392,128]{2,1,0:T(8,128)(2,1)}, bf16[2,392,128]{2,1,0:T(8,128)(2,1)S(1)}, u32[]{:S(2)}, u32[]{:S(2)}) collective-permute-start(bf16[2,392,128]{2,1,0:T(8,128)(2,1)} %get-tuple-element.75), channel_id=1, source_target_pairs={{2,0},{4,2},{6,4},{8,6},{10,8},{12,10},{14,12},{16,14},{18,16},{20... | collective-permute-start | bytes 602120 | tf_op jit(solution)/shard_map/ppermute | solution.py:507
  193.5 1.0 copy-start.2
  196.3 13.4 %collective-permute-start.31 = (bf16[2,392,128]{2,1,0:T(8,128)(2,1)}, bf16[2,392,128]{2,1,0:T(8,128)(2,1)S(1)}, u32[]{:S(2)}, u32[]{:S(2)}) collective-permute-start(bf16[2,392,128]{2,1,0:T(8,128)(2,1)} %get-tuple-element.77), channel_id=1, source_target_pairs={{0,2},{2,4},{4,6},{6,8},{8,10},{10,12},{12,14},{14,16},{16,18},{18... | collective-permute-start | bytes 602120 | tf_op jit(solution)/shard_map/ppermute | solution.py:506
  198.3 11.5 %collective-permute-start.32 = (bf16[2,392,128]{2,1,0:T(8,128)(2,1)}, bf16[2,392,128]{2,1,0:T(8,128)(2,1)S(1)}, u32[]{:S(2)}, u32[]{:S(2)}) collective-permute-start(bf16[2,392,128]{2,1,0:T(8,128)(2,1)} %get-tuple-element.78), channel_id=1, source_target_pairs={{2,0},{4,2},{6,4},{8,6},{10,8},{12,10},{14,12},{16,14},{18,16},{20... | collective-permute-start | bytes 602120 | tf_op jit(solution)/shard_map/ppermute | solution.py:507
  217.1 1.0 copy-start.3
  219.8 7.2 %collective-permute-start.34 = (bf16[2,392,128]{2,1,0:T(8,128)(2,1)}, bf16[2,392,128]{2,1,0:T(8,128)(2,1)S(1)}, u32[]{:S(2)}, u32[]{:S(2)}) collective-permute-start(bf16[2,392,128]{2,1,0:T(8,128)(2,1)} %get-tuple-element.80), channel_id=1, source_target_pairs={{0,2},{2,4},{4,6},{6,8},{8,10},{10,12},{12,14},{14,16},{16,18},{18... | collective-permute-start | bytes 602120 | tf_op jit(solution)/shard_map/ppermute | solution.py:506
  221.8 9.4 %collective-permute-start.35 = (bf16[2,392,128]{2,1,0:T(8,128)(2,1)}, bf16[2,392,128]{2,1,0:T(8,128)(2,1)S(1)}, u32[]{:S(2)}, u32[]{:S(2)}) collective-permute-start(bf16[2,392,128]{2,1,0:T(8,128)(2,1)} %get-tuple-element.81), channel_id=1, source_target_pairs={{2,0},{4,2},{6,4},{8,6},{10,8},{12,10},{14,12},{16,14},{18,16},{20... | collective-permute-start | bytes 602120 | tf_op jit(solution)/shard_map/ppermute | solution.py:507
  227.0 4.1 %copy-start.34 = (bf16[2,392,128]{2,1,0:T(8,128)(2,1)}, bf16[2,392,128]{2,1,0:T(8,128)(2,1)S(1)}, u32[]{:S(2)}) copy-start(bf16[2,392,128]{2,1,0:T(8,128)(2,1)S(1)} %collective-permute-done.34.low_ref) | copy-start | bytes 602116
  (16 other events, 11.4 us)

commit v6 on v5

--- a/solution.py
+++ b/solution.py
@@ -109,32 +109,6 @@
         compiler_params=params(),
         cost_estimate=cost(0, 4 * rows * cols * cw),
     )(index[None], array, *waits)
-
-
-def rows_kernel(first_in, last_in, *refs):
-    first_ref, last_ref = refs[-2:]
-    first_ref[...] = first_in[...]
-    last_ref[...] = last_in[...]
-
-
-def edge_rows(wave, waits):
-    rows, cols, cw = wave.shape
-    edge = jax.ShapeDtypeStruct((HALO, cols, cw), wave.dtype)
-    last = rows // HALO - 1
-    block = (HALO, cols, cw)
-    return pl.pallas_call(
-        rows_kernel,
-        grid=(1,),
-        in_specs=[
-            pl.BlockSpec(block, lambda t: (0, 0, 0)),
-            pl.BlockSpec(block, lambda t: (last, 0, 0)),
-        ]
-        + [any_spec()] * len(waits),
-        out_specs=[pl.BlockSpec(block, lambda t: (0, 0, 0))] * 2,
-        out_shape=[edge, edge],
-        compiler_params=params(),
-        cost_estimate=cost(0, 8 * edge.size),
-    )(wave, wave, *waits)
 
 
 def dft_kernel(lon_count, nz, waits, index_ref, quad_ref, *refs):
@@ -259,21 +233,44 @@
     )(*own, *others, leg, legt, gr, gi, *waits)
 
 
-def inverse_kernel(nz, lon_count, waits, *refs):
+def inverse_kernel(nz, lon_count, split, waits, *refs):
     near = refs[:NQ]
     far = refs[NQ : NQ + nz - 1]
     table_ref = refs[NQ + nz - 1]
-    outs = refs[NQ + nz + waits : NQ + nz + waits + lon_count]
-    first_ref, last_ref, wide = refs[-3:]
+    own_ref, first_ref, last_ref, *apart, wide = refs[NQ + nz + waits :]
+    step = pl.program_id(0)
     rows, _, cw = wide.shape
     wave_rows = near[0].shape[-2]
-    cols = outs[0].shape[1]
+    cols = own_ref.shape[1]
+    total = rows * pl.num_programs(0)
     for t in range(rows):
         for q in range(NQ):
             for d in range(nz):
                 at = (q * nz + d) * wave_rows
                 block = far[d - 1][q, t] if d else near[q][0, t]
                 wide[t, at : at + wave_rows, :] = block.astype(F32)
+    def put(s, i, value):
+        if s == 0:
+            own_ref[i] = value
+            return
+        if not split:
+            apart[s - 1][i] = value
+            return
+        edge_ref, inner_ref = apart[2 * s - 2 : 2 * s]
+        r = step * rows + i
+
+        @pl.when(r < HALO)
+        def _():
+            edge_ref[r] = value
+
+        @pl.when(r >= total - HALO)
+        def _():
+            edge_ref[r - total + 2 * HALO] = value
+
+        @pl.when((r >= HALO) & (r < total - HALO))
+        def _():
+            inner_ref[r - HALO] = value
+
     group = rows if cw % LANES == 0 else 1
     for first in range(0, rows, group):
         x = side_by_side([wide[first + i].astype(BF16) for i in range(group)])
@@ -281,42 +278,52 @@
         for i in range(group):
             for s in range(lon_count):
                 piece = acc[s * cols : (s + 1) * cols, i * cw : (i + 1) * cw]
-                outs[s][first + i] = piece.astype(BF16)
+                put(s, first + i, piece.astype(BF16))
     step = pl.program_id(0)
 
     @pl.when(step == 0)
     def _():
-        first_ref[...] = outs[0][:HALO]
+        first_ref[...] = own_ref[:HALO]
 
     @pl.when(step == pl.num_programs(0) - 1)
     def _():
-        last_ref[...] = outs[0][rows - HALO :]
-
-
-def inverse(near, far, table, lon_count, waits):
+        last_ref[...] = own_ref[rows - HALO :]
+
+
+def inverse(near, far, table, lon_count, split, waits):
     nz = len(far) + 1
     _, rows, wave_rows, cw = near[0].shape
     step = step_rows(rows, 6)
     cols = table.shape[0] // lon_count
+    extra = [HALO, HALO] + ([2 * HALO, rows - 2 * HALO] if split else [rows]) * (lon_count - 1)
+    extra = [jax.ShapeDtypeStruct((r, cols, cw), BF16) for r in extra]
+    moving = pl.BlockSpec((step, cols, cw), lambda t: (t, 0, 0))
     specs = [pl.BlockSpec((1, step, wave_rows, cw), lambda t: (0, t, 0, 0))] * NQ
     specs += [pl.BlockSpec((NQ, step, wave_rows, cw), lambda t: (0, t, 0, 0))] * (nz - 1)
     return pl.pallas_call(
-        functools.partial(inverse_kernel, nz, lon_count, len(waits)),
+        functools.partial(inverse_kernel, nz, lon_count, split, len(waits)),
         grid=(rows // step,),
         in_specs=specs + [whole_of(table)] + [any_spec()] * len(waits),
-        out_specs=[pl.BlockSpec((step, cols, cw), lambda t: (t, 0, 0))] * lon_count
-        + [pl.BlockSpec((HALO, cols, cw), lambda t: (0, 0, 0))] * 2,
-        out_shape=[jax.ShapeDtypeStruct((rows, cols, cw), BF16)] * lon_count
-        + [jax.ShapeDtypeStruct((HALO, cols, cw), BF16)] * 2,
+        out_specs=[moving]
+        + [
+            moving if a.shape[0] == rows else pl.BlockSpec(a.shape, lambda t: (0, 0, 0))
+            for a in extra
+        ],
+        out_shape=[jax.ShapeDtypeStruct((rows, cols, cw), BF16)] + extra,
         scratch_shapes=[pltpu.VMEM((step, nz * NQ * wave_rows, cw), F32)],
         compiler_params=params(),
         cost_estimate=cost(0, 14000000),
     )(*near, *far, table, *waits)
 
 
-def window_kernel(cols, place_ref, neighbour_ref, basis_ref, quad_ref, wave_ref, low_ref, high_ref, disco_ref, out_ref, ring):
+def window_kernel(cols, arrays, place_ref, neighbour_ref, basis_ref, quad_ref, low_ref, high_ref, disco_ref, *refs):
+    wave_ref = refs[arrays - 1]
+    edge_ref = refs[0]
+    out_ref, ring = refs[-2:]
     step = pl.program_id(0)
-    rows = wave_ref.shape[0]
+    rows = ring.shape[0] - 2 * HALO
+    inner = wave_ref.shape[0]
+    skipped = (rows - inner) // 2
     slots = neighbour_ref.shape[1]
     per_step = out_ref.shape[0]
     group = place_ref[0]
@@ -325,15 +332,17 @@
     def _():
         for r in range(HALO):
             ring[r] = low_ref[r].astype(F32)
-            ring[HALO + r] = wave_ref[r].astype(F32)
+            ring[HALO + r] = edge_ref[r].astype(F32)
             ring[rows + HALO + r] = high_ref[r].astype(F32)
+            if skipped:
+                ring[rows + r] = edge_ref[HALO + r].astype(F32)
 
     for i in range(per_step):
         t = step * per_step + i
 
-        @pl.when(t + HALO < rows)
+        @pl.when(t + HALO < rows - skipped)
         def _(t=t):
-            ring[t + 2 * HALO] = wave_ref[t + HALO].astype(F32)
+            ring[t + 2 * HALO] = wave_ref[t + HALO - skipped].astype(F32)
 
     tile = 48 if cols % 48 == 0 else 8
     for i in range(per_step):
@@ -350,19 +359,22 @@
             out_ref[i, pl.ds(at, tile), :] = acc.astype(BF16)
 
 
-def window(place, neighbour, basis, quad, wave, low, high, disco, cols):
-    rows, padded, cw = wave.shape
+def window(place, neighbour, basis, quad, low, high, disco, arrays, cols, waits):
+    rows = sum(a.shape[0] for a in arrays)
+    _, padded, cw = low.shape
     per_step = step_rows(rows, 2)
     return pl.pallas_call(
-        functools.partial(window_kernel, cols),
+        functools.partial(window_kernel, cols, len(arrays)),
         grid=(rows // per_step,),
-        in_specs=[smem_spec()] * 4 + [whole_of(a) for a in (wave, low, high, disco)],
+        in_specs=[smem_spec()] * 4
+        + [whole_of(a) for a in (low, high, disco, *arrays)]
+        + [any_spec()] * len(waits),
         out_specs=pl.BlockSpec((per_step, cols, cw), lambda t: (t, 0, 0)),
         out_shape=jax.ShapeDtypeStruct((rows, cols, cw), BF16),
         scratch_shapes=[pltpu.VMEM((rows + 2 * HALO, padded, cw), F32)],
         compiler_params=params(),
         cost_estimate=cost(0, 20000000),
-    )(place, neighbour, basis, quad, wave, low, high, disco)
+    )(place, neighbour, basis, quad, low, high, disco, *arrays, *waits)
 
 
 def mlp_kernel(place_ref, *refs):
@@ -501,13 +513,12 @@
     up = [(i, i + 1) for i in range(lat_count - 1)]
     down = [(i + 1, i) for i in range(lat_count - 1)]
 
-    def convolved(wave, edges, s, j):
-        first, last = edges
+    def convolved(arrays, first, last, s, j, waits):
         low = lax.ppermute(last, "lat", up)
         high = lax.ppermute(first, "lat", down)
         place = channel_index(s, j)
         done = window(
-            place[None], neighbour, basis, disco_quad, wave, low, high, disco, cols
+            place[None], neighbour, basis, disco_quad, low, high, disco, arrays, cols, waits
         )
         return place, done
 
@@ -541,18 +552,27 @@
         )
         near.append([full[0]] + across(full[1:]))
         waits = []
+    regroups = [regroup(blocks, []) for blocks in near]
     groups, sent, waits = [], [], []
     for j in range(nch):
-        *parts, first, last = inverse(
-            near[j], along(regroup(near[j], [])), inv, lon_count, waits
+        split = j == nch - 1
+        own, first, last, *apart = inverse(
+            near[j], along(regroups[j]), inv, lon_count, split, waits
         )
-        sent.append([swap(parts[s], "lon", s) for s in range(1, lon_count)])
-        groups.append(convolved(parts[0], (first, last), 0, j))
+        each = 2 if split else 1
+        sent.append(
+            [
+                [swap(part, "lon", s) for part in apart[each * (s - 1) : each * s]]
+                for s in range(1, lon_count)
+            ]
+        )
+        groups.append(convolved([own], first, last, 0, j, []))
         waits = [groups[-1][1]]
     for j in range(nch):
         waits = [done for _, done in groups] if j == nch - 1 else []
-        for s, wave in enumerate(sent[j], 1):
-            groups.append(convolved(wave, edge_rows(wave, waits), s, j))
+        for s, arrays in enumerate(sent[j], 1):
+            first, last = arrays[0][:HALO], arrays[0][-HALO:]
+            groups.append(convolved(arrays, first, last, s, j, waits))
     block_out, spatial = mlp(
         jnp.stack([place for place, _ in groups]),
         [done for _, done in groups],

time: 260 us -> 255 us (0.981)
  starting transfers between devices: 56.3 us -> 61.1 us
  waiting for transfers between devices: 93.1 us -> 88.7 us
    ppermute x4, waiting for transfers between devices: 9.2 us -> 5.23 us  [convolved(): high = lax.ppermute(first, 'lat', down)]
    ppermute x4, starting transfers between devices: 21.4 us -> 24.3 us  [convolved(): high = lax.ppermute(first, 'lat', down)]
    pallas_call x8 -> x6, Pallas kernels: 35.7 us -> 33.5 us  [the longest x4 24.5 us: window(): pl.pallas_call(functools.partial(window_kernel, cols, len(arrays)), grid=...]
    unnamed x88 -> x90, local copies, waits for them, and re-layouts: 13.3 us -> 11.5 us
    ppermute x28 -> x29, starting transfers between devices: 24.7 us -> 25.9 us  [swap(): return lax.ppermute(array, axis, [(i, i ^ mask) for i in range(count)])]
    ppermute x28 -> x29, waiting for transfers between devices: 83.9 us -> 83.4 us  [swap(): return lax.ppermute(array, axis, [(i, i ^ mask) for i in range(count)])]
  transfers between devices with their start and end apart: 36 -> 37, of which waited for: 13 -> 12; matrix products, arithmetic and copies ran while one was open for 4% -> 4% of each run, Pallas kernels for 20% -> 21%
where the time goes in v6:
time: 255 us; the launch traced here: 252 us
  waiting for transfers between devices  88.7 us (35%)
  Pallas kernels  80.2 us (31%)
  starting transfers between devices  61.1 us (24%)
  local copies, waits for them, and re-layouts  15.2 us (6%)
  matrix products  3.24 us (1%)
    ppermute x29, waiting for transfers between devices, swap(): return lax.ppermute(array, axis, [(i, i ^ mask) for i in range(count)])  83.4 us
    ppermute x29, starting transfers between devices, swap(): return lax.ppermute(array, axis, [(i, i ^ mask) for i in range(count)])  25.9 us
    pallas_call x4, Pallas kernels, window(): pl.pallas_call(functools.partial(window_kernel, cols, len(arrays)), grid=...  24.5 us
    ppermute x4, starting transfers between devices, convolved(): high = lax.ppermute(first, 'lat', down)  24.3 us
    pallas_call x1, Pallas kernels, mlp(): pl.pallas_call(mlp_kernel, grid=(rows // per_step,), in_specs=[smem_spec(...  17.8 us
    unnamed x90, local copies, waits for them, and re-layouts  11.5 us
    ppermute x4, starting transfers between devices, convolved(): low = lax.ppermute(last, 'lat', up)  10.9 us
    pallas_call x2, Pallas kernels, inverse(): pl.pallas_call(functools.partial(inverse_kernel, nz, lon_count, split, le...  9 us
  transfers between devices with their start and end apart: 37, of which 12 were waited for; matrix products, arithmetic and copies ran while one was open for 4% of the time, Pallas kernels for 21%

profile of v6, /device:TPU:19, one launch (start us, length us, event | category | flops | bytes accessed | tf_op | source)
XLA Modules:
  0.0 251.9 jit_solution(4622846679896319044)
XLA Ops:
  0.7 2.2 shard_map.194
  4.2 0.9 pad_maximum_fusion.1.refs_2_.refs_0_
  5.0 2.1 shard_map.196
  7.2 1.2 collective-permute-start.4
  9.2 1.5 copy.23.refs_3_.refs_7_
  10.7 1.9 constant_dynamic-slice_fusion
  12.6 1.5 convolution_convert_fusion.2
  14.5 0.9 pad_maximum_fusion.refs_5_.refs_7_
  15.4 14.5 %collective-permute-done.refs_1_ = bf16[12,384,128]{2,1,0:T(8,128)(2,1)S(1)} collective-permute-done((bf16[12,384,128]{2,1,0:T(8,128)(2,1)}, bf16[12,384,128]{2,1,0:T(8,128)(2,1)S(1)}, u32[]{:S(2)}, u32[]{:S(2)}) %collective-permute-start) | collective-permute-done | bytes 1179680 | tf_op jit(solution)/shard_map/ppermute | solution.py:426
  30.0 1.0 copy-done.13
  31.0 3.6 %shard_map.195 = (bf16[4,12,24,128]{3,2,1,0:T(8,128)(2,1)}, bf16[4,12,24,128]{3,2,1,0:T(8,128)(2,1)}, bf16[4,12,24,128]{3,2,1,0:T(8,128)(2,1)}, bf16[4,12,24,128]{3,2,1,0:T(8,128)(2,1)}) custom-call(s32[1]{0:T(128)} %bitcast.index_ref.place_ref, f32[12]{0:T(128)} %quad_ref.7, bf16[12,384,512]{2,1,0:T(8,128)(2,1)} %refs_9_.1, ...), custom_call_target="tpu_custom_call" | custom-call | flops 905969664 | bytes 4718592 | tf_op jit(solution)/shard_map/pallas_call | solution.py:142
  34.6 1.3 collective-permute-start.1
  36.0 1.3 collective-permute-start.3
  37.3 18.1 %collective-permute-done.4.refs_1_ = bf16[12,384,128]{2,1,0:T(8,128)(2,1)} collective-permute-done((bf16[12,384,128]{2,1,0:T(8,128)(2,1)}, bf16[12,384,128]{2,1,0:T(8,128)(2,1)}, u32[]{:S(2)}, u32[]{:S(2)}) %collective-permute-start.4) | collective-permute-done | bytes 1179680 | tf_op jit(solution)/shard_map/ppermute | solution.py:426
  56.1 3.6 %shard_map.197 = (bf16[4,12,24,128]{3,2,1,0:T(8,128)(2,1)}, bf16[4,12,24,128]{3,2,1,0:T(8,128)(2,1)}, bf16[4,12,24,128]{3,2,1,0:T(8,128)(2,1)}, bf16[4,12,24,128]{3,2,1,0:T(8,128)(2,1)}) custom-call(s32[1]{0:T(128)} %bitcast.1.index_ref.place_ref, f32[12]{0:T(128)} %quad_ref.7, bf16[12,384,512]{2,1,0:T(8,128)(2,1)} %refs_9_.1, ...), custom_call_target="tpu_custom_call" | custom-call | flops 905969664 | bytes 4718592 | tf_op jit(solution)/shard_map/pallas_call | solution.py:142
  59.8 1.7 collective-permute-done.3.refs_3_
  62.1 2.2 shard_map.198
  64.3 3.0 %collective-permute-start.5 = (bf16[4,12,24,128]{3,2,1,0:T(8,128)(2,1)}, bf16[4,12,24,128]{3,2,1,0:T(8,128)(2,1)S(1)}, u32[]{:S(2)}, u32[]{:S(2)}) collective-permute-start(bf16[4,12,24,128]{3,2,1,0:T(8,128)(2,1)} %get-tuple-element.44), channel_id=1, source_target_pairs={{0,2},{2,0},{4,6},{6,4},{8,10},{10,8},{12,14},{14,12},{16,18},{18,... | collective-permute-start | bytes 884744 | tf_op jit(solution)/shard_map/ppermute | solution.py:426
  67.4 1.2 collective-permute-start.6
  69.0 1.3 collective-permute-start.17
  70.4 1.4 collective-permute-start.18
  71.7 4.5 %collective-permute-done.6.refs_5_ = bf16[4,12,24,128]{3,2,1,0:T(8,128)(2,1)S(1)} collective-permute-done((bf16[4,12,24,128]{3,2,1,0:T(8,128)(2,1)}, bf16[4,12,24,128]{3,2,1,0:T(8,128)(2,1)S(1)}, u32[]{:S(2)}, u32[]{:S(2)}) %collective-permute-start.6) | collective-permute-done | bytes 294944 | tf_op jit(solution)/shard_map/ppermute | solution.py:426
  76.2 6.7 %collective-permute-done.7.refs_6_ = bf16[4,12,24,128]{3,2,1,0:T(8,128)(2,1)S(1)} collective-permute-done((bf16[4,12,24,128]{3,2,1,0:T(8,128)(2,1)}, bf16[4,12,24,128]{3,2,1,0:T(8,128)(2,1)S(1)}, u32[]{:S(2)}, u32[]{:S(2)}) %collective-permute-start.7) | collective-permute-done | bytes 294944 | tf_op jit(solution)/shard_map/ppermute | solution.py:426
  83.7 4.2 %shard_map.199 = (bf16[4,12,24,128]{3,2,1,0:T(8,128)(2,1)}, bf16[4,12,24,128]{3,2,1,0:T(8,128)(2,1)}, bf16[4,12,24,128]{3,2,1,0:T(8,128)(2,1)}, bf16[4,12,24,128]{3,2,1,0:T(8,128)(2,1)}) custom-call(bf16[4,12,24,128]{3,2,1,0:T(8,128)(2,1)} %get-tuple-element.39.refs_0_, bf16[4,12,24,128]{3,2,1,0:T(8,128)(2,1)} %copy-done.2, ...), custom_call_target="tpu_custom_call" | custom-call | bytes 14000000 | tf_op jit(solution)/shard_map/pallas_call | solution.py:222
  87.9 1.3 collective-permute-start.9
  89.2 0.9 collective-permute-start.10
  90.0 7.2 %collective-permute-done.18.refs_3_ = bf16[4,12,24,128]{3,2,1,0:T(8,128)(2,1)S(1)} collective-permute-done((bf16[4,12,24,128]{3,2,1,0:T(8,128)(2,1)S(1)}, bf16[4,12,24,128]{3,2,1,0:T(8,128)(2,1)S(1)}, u32[]{:S(2)}, u32[]{:S(2)}) %collective-permute-start.18) | collective-permute-done | bytes 294944 | tf_op jit(solution)/shard_map/ppermute | solution.py:426
  98.0 2.2 shard_map.203
  100.2 1.4 collective-permute-start.19
  101.5 1.2 collective-permute-start.20
  104.0 2.2 shard_map.200
  106.1 1.3 collective-permute-start.12
  107.5 1.3 collective-permute-start.13
  108.8 1.6 collective-permute-done.20.refs_5_
  110.4 6.7 %collective-permute-done.21.refs_6_ = bf16[4,12,24,128]{3,2,1,0:T(8,128)(2,1)S(1)} collective-permute-done((bf16[4,12,24,128]{3,2,1,0:T(8,128)(2,1)}, bf16[4,12,24,128]{3,2,1,0:T(8,128)(2,1)S(1)}, u32[]{:S(2)}, u32[]{:S(2)}) %collective-permute-start.21) | collective-permute-done | bytes 294944 | tf_op jit(solution)/shard_map/ppermute | solution.py:426
  117.1 0.7 copy-done.20
  117.8 4.2 %shard_map.204 = (bf16[4,12,24,128]{3,2,1,0:T(8,128)(2,1)}, bf16[4,12,24,128]{3,2,1,0:T(8,128)(2,1)}, bf16[4,12,24,128]{3,2,1,0:T(8,128)(2,1)}, bf16[4,12,24,128]{3,2,1,0:T(8,128)(2,1)}) custom-call(bf16[4,12,24,128]{3,2,1,0:T(8,128)(2,1)} %get-tuple-element.43.refs_4_.refs_0_, bf16[4,12,24,128]{3,2,1,0:T(8,128)(2,1)} %copy-done.5, ...), custom_call_target="tpu_custom_call" | custom-call | bytes 14000000 | tf_op jit(solution)/shard_map/pallas_call | solution.py:222
  122.1 1.3 collective-permute-start.23
  123.3 0.9 collective-permute-start.24
  124.2 10.4 %collective-permute-done.13.refs_6_ = bf16[4,12,24,128]{3,2,1,0:T(8,128)(2,1)S(1)} collective-permute-done((bf16[4,12,24,128]{3,2,1,0:T(8,128)(2,1)}, bf16[4,12,24,128]{3,2,1,0:T(8,128)(2,1)S(1)}, u32[]{:S(2)}, u32[]{:S(2)}) %collective-permute-start.13) | collective-permute-done | bytes 294944 | tf_op jit(solution)/shard_map/ppermute | solution.py:426
  135.3 4.2 %shard_map.201 = (bf16[12,392,128]{2,1,0:T(8,128)(2,1)}, bf16[2,392,128]{2,1,0:T(8,128)(2,1)}, bf16[2,392,128]{2,1,0:T(8,128)(2,1)}, bf16[12,392,128]{2,1,0:T(8,128)(2,1)}) custom-call(bf16[4,12,24,128]{3,2,1,0:T(8,128)(2,1)} %get-tuple-element.47.refs_0_, bf16[4,12,24,128]{3,2,1,0:T(8,128)(2,1)} %copy-done.14, bf16[4,12,24,128]{3,2,1,0:T(8,128)(2,1)} %copy-done.15, ...), custom_call_target="tpu_custom_call" | custom-call | bytes 14000000 | tf_op jit(solution)/shard_map/pallas_call | solution.py:303
  139.8 4.7 %collective-permute-start.14 = (bf16[2,392,128]{2,1,0:T(8,128)(2,1)}, bf16[2,392,128]{2,1,0:T(8,128)(2,1)S(1)}, u32[]{:S(2)}, u32[]{:S(2)}) collective-permute-start(bf16[2,392,128]{2,1,0:T(8,128)(2,1)} %get-tuple-element.54), channel_id=1, source_target_pairs={{0,2},{2,4},{4,6},{6,8},{8,10},{10,12},{12,14},{14,16},{16,18},{18... | collective-permute-start | bytes 602120 | tf_op jit(solution)/shard_map/ppermute | solution.py:517
  145.4 2.2 shard_map.205
  147.7 1.4 collective-permute-start.26
  149.0 1.3 collective-permute-start.27
  150.3 2.1 collective-permute-start.15
  152.4 5.2 %collective-permute-done.15.high_ref = bf16[2,392,128]{2,1,0:T(8,128)(2,1)S(1)} collective-permute-done((bf16[2,392,128]{2,1,0:T(8,128)(2,1)S(1)}, bf16[2,392,128]{2,1,0:T(8,128)(2,1)S(1)}, u32[]{:S(2)}, u32[]{:S(2)}) %collective-permute-start.15) | collective-permute-done | bytes 200736 | tf_op jit(solution)/shard_map/ppermute | solution.py:518
  158.3 6.1 %shard_map.202.refs_8_.refs_2_.refs_0_ = bf16[12,384,128]{2,1,0:T(8,128)(2,1)} custom-call(s32[1]{0:T(128)} %bitcast.index_ref.place_ref, s32[12,12]{1,0:T(8,128)} %neighbour_ref.7, s32[12,12]{1,0:T(8,128)} %basis_ref.7, f32[12,12]{1,0:T(8,128)} %quad_ref.11, bf16[2,392,128]{2,1,0:T(8,128)(2,1)} %copy-done.34, bf16[2,392,128]{2,1,0:T(8,128)(2,1)} %copy-done.37, ...), custom_call_target="tpu_custom_call" | custom-call | bytes 20000000 | tf_op jit(solution)/shard_map/pallas_call | solution.py:366
  164.4 3.9 %collective-permute-done.26.refs_5_ = bf16[4,12,24,128]{3,2,1,0:T(8,128)(2,1)S(1)} collective-permute-done((bf16[4,12,24,128]{3,2,1,0:T(8,128)(2,1)}, bf16[4,12,24,128]{3,2,1,0:T(8,128)(2,1)S(1)}, u32[]{:S(2)}, u32[]{:S(2)}) %collective-permute-start.26) | collective-permute-done | bytes 294944 | tf_op jit(solution)/shard_map/ppermute | solution.py:426
  168.4 8.0 %collective-permute-done.27.refs_6_ = bf16[4,12,24,128]{3,2,1,0:T(8,128)(2,1)S(1)} collective-permute-done((bf16[4,12,24,128]{3,2,1,0:T(8,128)(2,1)}, bf16[4,12,24,128]{3,2,1,0:T(8,128)(2,1)S(1)}, u32[]{:S(2)}, u32[]{:S(2)}) %collective-permute-start.27) | collective-permute-done | bytes 294944 | tf_op jit(solution)/shard_map/ppermute | solution.py:426
  176.4 0.7 copy-done.25
  177.2 4.8 %shard_map.206 = (bf16[12,392,128]{2,1,0:T(8,128)(2,1)}, bf16[2,392,128]{2,1,0:T(8,128)(2,1)}, bf16[2,392,128]{2,1,0:T(8,128)(2,1)}, bf16[4,392,128]{2,1,0:T(8,128)(2,1)}, bf16[8,392,128]{2,1,0:T(8,128)(2,1)}) custom-call(bf16[4,12,24,128]{3,2,1,0:T(8,128)(2,1)} %get-tuple-element.63.refs_0_, bf16[4,12,24,128]{3,2,1,0:T(8,128)(2,1)} %copy-done.8, ...), custom_call_target="tpu_custom_call" | custom-call | bytes 14000000 | tf_op jit(solution)/shard_map/pallas_call | solution.py:303
  182.0 1.3 collective-permute-start.33
  183.5 2.3 collective-permute-start.28
  185.9 10.4 %collective-permute-start.29 = (bf16[2,392,128]{2,1,0:T(8,128)(2,1)}, bf16[2,392,128]{2,1,0:T(8,128)(2,1)S(1)}, u32[]{:S(2)}, u32[]{:S(2)}) collective-permute-start(bf16[2,392,128]{2,1,0:T(8,128)(2,1)} %get-tuple-element.71), channel_id=1, source_target_pairs={{2,0},{4,2},{6,4},{8,6},{10,8},{12,10},{14,12},{16,14},{18,16},{20... | collective-permute-start | bytes 602120 | tf_op jit(solution)/shard_map/ppermute | solution.py:518
  196.4 8.2 %collective-permute-start.35 = (bf16[2,392,128]{2,1,0:T(8,128)(2,1)S(1)}, bf16[2,392,128]{2,1,0:T(8,128)(2,1)S(1)}, u32[]{:S(2)}, u32[]{:S(2)}) collective-permute-start(bf16[2,392,128]{2,1,0:T(8,128)(2,1)S(1)} %get-tuple-element.78), channel_id=1, source_target_pairs={{2,0},{4,2},{6,4},{8,6},{10,8},{12,10},{14,12},{16,14},{18,16},{20... | collective-permute-start | bytes 602120 | tf_op jit(solution)/shard_map/ppermute | solution.py:518
  204.6 3.6 %collective-permute-start.32 = (bf16[2,392,128]{2,1,0:T(8,128)(2,1)S(1)}, bf16[2,392,128]{2,1,0:T(8,128)(2,1)S(1)}, u32[]{:S(2)}, u32[]{:S(2)}) collective-permute-start(bf16[2,392,128]{2,1,0:T(8,128)(2,1)S(1)} %get-tuple-element.76), channel_id=1, source_target_pairs={{2,0},{4,2},{6,4},{8,6},{10,8},{12,10},{14,12},{16,14},{18,16},{20... | collective-permute-start | bytes 602120 | tf_op jit(solution)/shard_map/ppermute | solution.py:518
  208.2 2.0 collective-permute-start.31
  210.2 1.9 collective-permute-start.34
  212.7 6.2 %shard_map.207.refs_3_.refs_1_ = bf16[12,384,128]{2,1,0:T(8,128)(2,1)} custom-call(s32[1]{0:T(128)} %bitcast.1.index_ref.place_ref, s32[12,12]{1,0:T(8,128)} %neighbour_ref.7, s32[12,12]{1,0:T(8,128)} %basis_ref.7, f32[12,12]{1,0:T(8,128)} %quad_ref.11, bf16[2,392,128]{2,1,0:T(8,128)(2,1)} %copy-done.32, bf16[2,392,128]{2,1,0:T(8,128)(2,1)} %copy-done.33, ...), custom_call_target="tpu_custom_call" | custom-call | bytes 20000000 | tf_op jit(solution)/shard_map/pallas_call | solution.py:366
  220.3 6.1 %shard_map.208.refs_4_.refs_2_ = bf16[12,384,128]{2,1,0:T(8,128)(2,1)} custom-call(s32[1]{0:T(128)} %bitcast.2.index_ref.place_ref, s32[12,12]{1,0:T(8,128)} %neighbour_ref.7, s32[12,12]{1,0:T(8,128)} %basis_ref.7, f32[12,12]{1,0:T(8,128)} %quad_ref.11, bf16[2,392,128]{2,1,0:T(8,128)(2,1)} %copy-done.36, bf16[2,392,128]{2,1,0:T(8,128)(2,1)} %copy-done.35, ...), custom_call_target="tpu_custom_call" | custom-call | bytes 20000000 | tf_op jit(solution)/shard_map/pallas_call | solution.py:366
  227.1 0.9 copy-done.17
  228.0 6.1 %shard_map.209.refs_3_ = bf16[12,384,128]{2,1,0:T(8,128)(2,1)} custom-call(s32[1]{0:T(128)} %bitcast.3.index_ref.place_ref, s32[12,12]{1,0:T(8,128)} %neighbour_ref.7, s32[12,12]{1,0:T(8,128)} %basis_ref.7, f32[12,12]{1,0:T(8,128)} %quad_ref.11, bf16[2,392,128]{2,1,0:T(8,128)(2,1)} %copy-done.31, bf16[2,392,128]{2,1,0:T(8,128)(2,1)} %copy-done.30, ...), custom_call_target="tpu_custom_call" | custom-call | bytes 20000000 | tf_op jit(solution)/shard_map/pallas_call | solution.py:366
  234.1 17.8 %shard_map.210 = (bf16[12,384,512]{2,1,0:T(8,128)(2,1)}, bf16[12,384,512]{2,1,0:T(8,128)(2,1)}) custom-call(s32[4]{0:T(128)} %pad_add_fusion.place_ref, bf16[12,384,128]{2,1,0:T(8,128)(2,1)} %shard_map.202.refs_8_.refs_2_.refs_0_, bf16[12,384,128]{2,1,0:T(8,128)(2,1)} %shard_map.207.refs_3_.refs_1_, bf16[12,384,128]{2,1,0:T(8,128)(2,1)} %shard_map.208.refs_4_.refs_2_, ...), custom_call_target="tpu_custom_call" | custom-call | flops 9663676416 | bytes 18874368 | tf_op jit(solution)/shard_map/pallas_call | solution.py:407
  (136 shorter events, 12.8 us)
Async XLA Ops:
  0.6 7.9 %copy-start = (bf16[12,192,192]{2,1,0:T(8,128)(2,1)S(1)}, bf16[12,192,192]{2,1,0:T(8,128)(2,1)}, u32[]{:S(2)}) copy-start(bf16[12,192,192]{2,1,0:T(8,128)(2,1)} %param.21) | copy-start | bytes 2654212
  0.7 2.5 %copy-start.38 = (s32[16]{0:T(128)S(1)}, s32[16]{0:T(128)}, u32[]{:S(2)}) copy-start(s32[16]{0:T(128)} %constant.46.clone) | copy-start | bytes 196
  0.7 2.7 %copy-start.44 = (bf16[2,384,384]{2,1,0:T(8,128)(2,1)S(1)}, bf16[2,384,384]{2,1,0:T(8,128)(2,1)}, u32[]{:S(2)}) copy-start(bf16[2,384,384]{2,1,0:T(8,128)(2,1)} %constant.47.clone) | copy-start | bytes 1769476
  2.9 27.0 %collective-permute-start = (bf16[12,384,128]{2,1,0:T(8,128)(2,1)}, bf16[12,384,128]{2,1,0:T(8,128)(2,1)S(1)}, u32[]{:S(2)}, u32[]{:S(2)}) collective-permute-start(bf16[12,384,128]{2,1,0:T(8,128)(2,1)} %shard_map.194), channel_id=1, source_target_pairs={{0,1},{1,0},{2,3},{3,2},{4,5},{5,4},{6,7},{7,6},{8,9},{9,8},{10,11... | collective-permute-start | bytes 3538952 | tf_op jit(solution)/shard_map/ppermute | solution.py:426
  7.2 48.2 %collective-permute-start.4 = (bf16[12,384,128]{2,1,0:T(8,128)(2,1)}, bf16[12,384,128]{2,1,0:T(8,128)(2,1)}, u32[]{:S(2)}, u32[]{:S(2)}) collective-permute-start(bf16[12,384,128]{2,1,0:T(8,128)(2,1)} %shard_map.196), channel_id=1, source_target_pairs={{0,1},{1,0},{2,3},{3,2},{4,5},{5,4},{6,7},{7,6},{8,9},{9,8},{10,11... | collective-permute-start | bytes 3538952 | tf_op jit(solution)/shard_map/ppermute | solution.py:426
  9.1 1.7 copy-start.1
  10.7 3.3 %copy-start.43 = (bf16[2,392,384]{2,1,0:T(8,128)(2,1)S(1)}, bf16[2,392,384]{2,1,0:T(8,128)(2,1)}, u32[]{:S(2)}) copy-start(bf16[2,392,384]{2,1,0:T(8,128)(2,1)} %constant.48.clone) | copy-start | bytes 1806340
  30.0 1.0 copy-start.13
  34.6 20.7 %collective-permute-start.1 = (bf16[4,12,24,128]{3,2,1,0:T(8,128)(2,1)}, bf16[4,12,24,128]{3,2,1,0:T(8,128)(2,1)S(1)}, u32[]{:S(2)}, u32[]{:S(2)}) collective-permute-start(bf16[4,12,24,128]{3,2,1,0:T(8,128)(2,1)} %get-tuple-element.40), channel_id=1, source_target_pairs={{0,8},{2,10},{4,12},{6,14},{8,0},{10,2},{12,4},{14,6},{16,24},{18,... | collective-permute-start | bytes 884744 | tf_op jit(solution)/shard_map/ppermute | solution.py:426
  35.9 23.8 %collective-permute-start.2 = (bf16[4,12,24,128]{3,2,1,0:T(8,128)(2,1)}, bf16[4,12,24,128]{3,2,1,0:T(8,128)(2,1)S(1)}, u32[]{:S(2)}, u32[]{:S(2)}) collective-permute-start(bf16[4,12,24,128]{3,2,1,0:T(8,128)(2,1)} %get-tuple-element.41), channel_id=1, source_target_pairs={{0,16},{2,18},{4,20},{6,22},{8,24},{10,26},{12,28},{14,30},{16,0},... | collective-permute-start | bytes 884744 | tf_op jit(solution)/shard_map/ppermute | solution.py:426
  36.0 25.4 %collective-permute-start.3 = (bf16[4,12,24,128]{3,2,1,0:T(8,128)(2,1)}, bf16[4,12,24,128]{3,2,1,0:T(8,128)(2,1)S(1)}, u32[]{:S(2)}, u32[]{:S(2)}) collective-permute-start(bf16[4,12,24,128]{3,2,1,0:T(8,128)(2,1)} %get-tuple-element.42), channel_id=1, source_target_pairs={{0,24},{2,26},{4,28},{6,30},{8,16},{10,18},{12,20},{14,22},{16,8},... | collective-permute-start | bytes 884744 | tf_op jit(solution)/shard_map/ppermute | solution.py:426
  59.7 9.3 %copy-start.41 = (bf16[4,12,24,128]{3,2,1,0:T(8,128)(2,1)S(1)}, bf16[4,12,24,128]{3,2,1,0:T(8,128)(2,1)}, u32[]{:S(2)}) copy-start(bf16[4,12,24,128]{3,2,1,0:T(8,128)(2,1)} %get-tuple-element.57) | copy-start | bytes 884740
  59.7 9.3 %copy-start.40 = (bf16[4,12,24,128]{3,2,1,0:T(8,128)(2,1)S(1)}, bf16[4,12,24,128]{3,2,1,0:T(8,128)(2,1)}, u32[]{:S(2)}) copy-start(bf16[4,12,24,128]{3,2,1,0:T(8,128)(2,1)} %get-tuple-element.58) | copy-start | bytes 884740
  59.7 10.6 %copy-start.39 = (bf16[4,12,24,128]{3,2,1,0:T(8,128)(2,1)S(1)}, bf16[4,12,24,128]{3,2,1,0:T(8,128)(2,1)}, u32[]{:S(2)}) copy-start(bf16[4,12,24,128]{3,2,1,0:T(8,128)(2,1)} %get-tuple-element.59) | copy-start | bytes 884740
  59.7 1.7 copy-start.11
  64.3 6.0 %collective-permute-start.5 = (bf16[4,12,24,128]{3,2,1,0:T(8,128)(2,1)}, bf16[4,12,24,128]{3,2,1,0:T(8,128)(2,1)S(1)}, u32[]{:S(2)}, u32[]{:S(2)}) collective-permute-start(bf16[4,12,24,128]{3,2,1,0:T(8,128)(2,1)} %get-tuple-element.44), channel_id=1, source_target_pairs={{0,2},{2,0},{4,6},{6,4},{8,10},{10,8},{12,14},{14,12},{16,18},{18,... | collective-permute-start | bytes 884744 | tf_op jit(solution)/shard_map/ppermute | solution.py:426
  67.4 8.8 %collective-permute-start.6 = (bf16[4,12,24,128]{3,2,1,0:T(8,128)(2,1)}, bf16[4,12,24,128]{3,2,1,0:T(8,128)(2,1)S(1)}, u32[]{:S(2)}, u32[]{:S(2)}) collective-permute-start(bf16[4,12,24,128]{3,2,1,0:T(8,128)(2,1)} %get-tuple-element.45), channel_id=1, source_target_pairs={{0,4},{2,6},{4,0},{6,2},{8,12},{10,14},{12,8},{14,10},{16,20},{18,... | collective-permute-start | bytes 884744 | tf_op jit(solution)/shard_map/ppermute | solution.py:426
  68.6 14.3 %collective-permute-start.7 = (bf16[4,12,24,128]{3,2,1,0:T(8,128)(2,1)}, bf16[4,12,24,128]{3,2,1,0:T(8,128)(2,1)S(1)}, u32[]{:S(2)}, u32[]{:S(2)}) collective-permute-start(bf16[4,12,24,128]{3,2,1,0:T(8,128)(2,1)} %get-tuple-element.46), channel_id=1, source_target_pairs={{0,6},{2,4},{4,2},{6,0},{8,14},{10,12},{12,10},{14,8},{16,22},{18,... | collective-permute-start | bytes 884744 | tf_op jit(solution)/shard_map/ppermute | solution.py:426
  69.0 20.2 %collective-permute-start.16 = (bf16[4,12,24,128]{3,2,1,0:T(8,128)(2,1)S(1)}, bf16[4,12,24,128]{3,2,1,0:T(8,128)(2,1)S(1)}, u32[]{:S(2)}, u32[]{:S(2)}) collective-permute-start(bf16[4,12,24,128]{3,2,1,0:T(8,128)(2,1)S(1)} %copy-done.41), channel_id=1, source_target_pairs={{0,8},{2,10},{4,12},{6,14},{8,0},{10,2},{12,4},{14,6},{16,24},{18,... | collective-permute-start | bytes 884744 | tf_op jit(solution)/shard_map/ppermute | solution.py:426
  69.0 21.0 %collective-permute-start.17 = (bf16[4,12,24,128]{3,2,1,0:T(8,128)(2,1)S(1)}, bf16[4,12,24,128]{3,2,1,0:T(8,128)(2,1)S(1)}, u32[]{:S(2)}, u32[]{:S(2)}) collective-permute-start(bf16[4,12,24,128]{3,2,1,0:T(8,128)(2,1)S(1)} %copy-done.40), channel_id=1, source_target_pairs={{0,16},{2,18},{4,20},{6,22},{8,24},{10,26},{12,28},{14,30},{16,0},... | collective-permute-start | bytes 884744 | tf_op jit(solution)/shard_map/ppermute | solution.py:426
  70.4 12.6 %copy-start.23 = (bf16[4,12,24,128]{3,2,1,0:T(8,128)(2,1)}, bf16[4,12,24,128]{3,2,1,0:T(8,128)(2,1)S(1)}, u32[]{:S(2)}) copy-start(bf16[4,12,24,128]{3,2,1,0:T(8,128)(2,1)S(1)} %collective-permute-done.5.refs_4_) | copy-start | bytes 884740
  70.4 26.9 %collective-permute-start.18 = (bf16[4,12,24,128]{3,2,1,0:T(8,128)(2,1)S(1)}, bf16[4,12,24,128]{3,2,1,0:T(8,128)(2,1)S(1)}, u32[]{:S(2)}, u32[]{:S(2)}) collective-permute-start(bf16[4,12,24,128]{3,2,1,0:T(8,128)(2,1)S(1)} %copy-done.39), channel_id=1, source_target_pairs={{0,24},{2,26},{4,28},{6,30},{8,16},{10,18},{12,20},{14,22},{16,8},... | collective-permute-start | bytes 884744 | tf_op jit(solution)/shard_map/ppermute | solution.py:426
  76.2 6.7 %copy-start.24 = (bf16[4,12,24,128]{3,2,1,0:T(8,128)(2,1)}, bf16[4,12,24,128]{3,2,1,0:T(8,128)(2,1)S(1)}, u32[]{:S(2)}) copy-start(bf16[4,12,24,128]{3,2,1,0:T(8,128)(2,1)S(1)} %collective-permute-done.6.refs_5_) | copy-start | bytes 884740
  87.9 14.9 %collective-permute-start.8 = (bf16[4,12,24,128]{3,2,1,0:T(8,128)(2,1)}, bf16[4,12,24,128]{3,2,1,0:T(8,128)(2,1)S(1)}, u32[]{:S(2)}, u32[]{:S(2)}) collective-permute-start(bf16[4,12,24,128]{3,2,1,0:T(8,128)(2,1)} %get-tuple-element.48), channel_id=1, source_target_pairs={{0,2},{2,0},{4,6},{6,4},{8,10},{10,8},{12,14},{14,12},{16,18},{18,... | collective-permute-start | bytes 884744 | tf_op jit(solution)/shard_map/ppermute | solution.py:426
  87.9 15.3 %collective-permute-start.9 = (bf16[4,12,24,128]{3,2,1,0:T(8,128)(2,1)}, bf16[4,12,24,128]{3,2,1,0:T(8,128)(2,1)S(1)}, u32[]{:S(2)}, u32[]{:S(2)}) collective-permute-start(bf16[4,12,24,128]{3,2,1,0:T(8,128)(2,1)} %get-tuple-element.49), channel_id=1, source_target_pairs={{0,4},{2,6},{4,0},{6,2},{8,12},{10,14},{12,8},{14,10},{16,20},{18,... | collective-permute-start | bytes 884744 | tf_op jit(solution)/shard_map/ppermute | solution.py:426
  89.2 8.1 %copy-start.5 = (bf16[4,12,24,128]{3,2,1,0:T(8,128)(2,1)}, bf16[4,12,24,128]{3,2,1,0:T(8,128)(2,1)S(1)}, u32[]{:S(2)}) copy-start(bf16[4,12,24,128]{3,2,1,0:T(8,128)(2,1)S(1)} %collective-permute-done.16.refs_1_) | copy-start | bytes 884740
  89.2 14.0 %collective-permute-start.10 = (bf16[4,12,24,128]{3,2,1,0:T(8,128)(2,1)}, bf16[4,12,24,128]{3,2,1,0:T(8,128)(2,1)S(1)}, u32[]{:S(2)}, u32[]{:S(2)}) collective-permute-start(bf16[4,12,24,128]{3,2,1,0:T(8,128)(2,1)} %get-tuple-element.50), channel_id=1, source_target_pairs={{0,6},{2,4},{4,2},{6,0},{8,14},{10,12},{12,10},{14,8},{16,22},{18,... | collective-permute-start | bytes 884744 | tf_op jit(solution)/shard_map/ppermute | solution.py:426
  90.0 7.2 %copy-start.6 = (bf16[4,12,24,128]{3,2,1,0:T(8,128)(2,1)}, bf16[4,12,24,128]{3,2,1,0:T(8,128)(2,1)S(1)}, u32[]{:S(2)}) copy-start(bf16[4,12,24,128]{3,2,1,0:T(8,128)(2,1)S(1)} %collective-permute-done.17.refs_2_) | copy-start | bytes 884740
  100.2 7.3 %collective-permute-start.19 = (bf16[4,12,24,128]{3,2,1,0:T(8,128)(2,1)}, bf16[4,12,24,128]{3,2,1,0:T(8,128)(2,1)S(1)}, u32[]{:S(2)}, u32[]{:S(2)}) collective-permute-start(bf16[4,12,24,128]{3,2,1,0:T(8,128)(2,1)} %get-tuple-element.60), channel_id=1, source_target_pairs={{0,2},{2,0},{4,6},{6,4},{8,10},{10,8},{12,14},{14,12},{16,18},{18,... | collective-permute-start | bytes 884744 | tf_op jit(solution)/shard_map/ppermute | solution.py:426
  101.5 8.8 %collective-permute-start.20 = (bf16[4,12,24,128]{3,2,1,0:T(8,128)(2,1)}, bf16[4,12,24,128]{3,2,1,0:T(8,128)(2,1)S(1)}, u32[]{:S(2)}, u32[]{:S(2)}) collective-permute-start(bf16[4,12,24,128]{3,2,1,0:T(8,128)(2,1)} %get-tuple-element.61), channel_id=1, source_target_pairs={{0,4},{2,6},{4,0},{6,2},{8,12},{10,14},{12,8},{14,10},{16,20},{18,... | collective-permute-start | bytes 884744 | tf_op jit(solution)/shard_map/ppermute | solution.py:426
  102.8 14.3 %collective-permute-start.21 = (bf16[4,12,24,128]{3,2,1,0:T(8,128)(2,1)}, bf16[4,12,24,128]{3,2,1,0:T(8,128)(2,1)S(1)}, u32[]{:S(2)}, u32[]{:S(2)}) collective-permute-start(bf16[4,12,24,128]{3,2,1,0:T(8,128)(2,1)} %get-tuple-element.62), channel_id=1, source_target_pairs={{0,6},{2,4},{4,2},{6,0},{8,14},{10,12},{12,10},{14,8},{16,22},{18,... | collective-permute-start | bytes 884744 | tf_op jit(solution)/shard_map/ppermute | solution.py:426
  106.1 17.2 %collective-permute-start.11 = (bf16[4,12,24,128]{3,2,1,0:T(8,128)(2,1)}, bf16[4,12,24,128]{3,2,1,0:T(8,128)(2,1)S(1)}, u32[]{:S(2)}, u32[]{:S(2)}) collective-permute-start(bf16[4,12,24,128]{3,2,1,0:T(8,128)(2,1)} %get-tuple-element.51), channel_id=1, source_target_pairs={{0,8},{2,10},{4,12},{6,14},{8,0},{10,2},{12,4},{14,6},{16,24},{18,... | collective-permute-start | bytes 884744 | tf_op jit(solution)/shard_map/ppermute | solution.py:426
  106.1 18.1 %collective-permute-start.12 = (bf16[4,12,24,128]{3,2,1,0:T(8,128)(2,1)}, bf16[4,12,24,128]{3,2,1,0:T(8,128)(2,1)S(1)}, u32[]{:S(2)}, u32[]{:S(2)}) collective-permute-start(bf16[4,12,24,128]{3,2,1,0:T(8,128)(2,1)} %get-tuple-element.52), channel_id=1, source_target_pairs={{0,16},{2,18},{4,20},{6,22},{8,24},{10,26},{12,28},{14,30},{16,0},... | collective-permute-start | bytes 884744 | tf_op jit(solution)/shard_map/ppermute | solution.py:426
  107.5 9.6 %copy-start.18 = (bf16[4,12,24,128]{3,2,1,0:T(8,128)(2,1)}, bf16[4,12,24,128]{3,2,1,0:T(8,128)(2,1)S(1)}, u32[]{:S(2)}) copy-start(bf16[4,12,24,128]{3,2,1,0:T(8,128)(2,1)S(1)} %collective-permute-done.19.refs_4_) | copy-start | bytes 884740
  107.5 27.1 %collective-permute-start.13 = (bf16[4,12,24,128]{3,2,1,0:T(8,128)(2,1)}, bf16[4,12,24,128]{3,2,1,0:T(8,128)(2,1)S(1)}, u32[]{:S(2)}, u32[]{:S(2)}) collective-permute-start(bf16[4,12,24,128]{3,2,1,0:T(8,128)(2,1)} %get-tuple-element.53), channel_id=1, source_target_pairs={{0,24},{2,26},{4,28},{6,30},{8,16},{10,18},{12,20},{14,22},{16,8},... | collective-permute-start | bytes 884744 | tf_op jit(solution)/shard_map/ppermute | solution.py:426
  110.4 6.7 %copy-start.19 = (bf16[4,12,24,128]{3,2,1,0:T(8,128)(2,1)}, bf16[4,12,24,128]{3,2,1,0:T(8,128)(2,1)S(1)}, u32[]{:S(2)}) copy-start(bf16[4,12,24,128]{3,2,1,0:T(8,128)(2,1)S(1)} %collective-permute-done.20.refs_5_) | copy-start | bytes 884740
  122.1 22.4 %collective-permute-start.22 = (bf16[4,12,24,128]{3,2,1,0:T(8,128)(2,1)}, bf16[4,12,24,128]{3,2,1,0:T(8,128)(2,1)S(1)}, u32[]{:S(2)}, u32[]{:S(2)}) collective-permute-start(bf16[4,12,24,128]{3,2,1,0:T(8,128)(2,1)} %get-tuple-element.64), channel_id=1, source_target_pairs={{0,2},{2,0},{4,6},{6,4},{8,10},{10,8},{12,14},{14,12},{16,18},{18,... | collective-permute-start | bytes 884744 | tf_op jit(solution)/shard_map/ppermute | solution.py:426
  122.1 22.4 %collective-permute-start.23 = (bf16[4,12,24,128]{3,2,1,0:T(8,128)(2,1)}, bf16[4,12,24,128]{3,2,1,0:T(8,128)(2,1)S(1)}, u32[]{:S(2)}, u32[]{:S(2)}) collective-permute-start(bf16[4,12,24,128]{3,2,1,0:T(8,128)(2,1)} %get-tuple-element.65), channel_id=1, source_target_pairs={{0,4},{2,6},{4,0},{6,2},{8,12},{10,14},{12,8},{14,10},{16,20},{18,... | collective-permute-start | bytes 884744 | tf_op jit(solution)/shard_map/ppermute | solution.py:426
  123.3 11.3 %copy-start.27 = (bf16[4,12,24,128]{3,2,1,0:T(8,128)(2,1)}, bf16[4,12,24,128]{3,2,1,0:T(8,128)(2,1)S(1)}, u32[]{:S(2)}) copy-start(bf16[4,12,24,128]{3,2,1,0:T(8,128)(2,1)S(1)} %collective-permute-done.11.refs_4_) | copy-start | bytes 884740
  123.3 21.2 %collective-permute-start.24 = (bf16[4,12,24,128]{3,2,1,0:T(8,128)(2,1)}, bf16[4,12,24,128]{3,2,1,0:T(8,128)(2,1)S(1)}, u32[]{:S(2)}, u32[]{:S(2)}) collective-permute-start(bf16[4,12,24,128]{3,2,1,0:T(8,128)(2,1)} %get-tuple-element.66), channel_id=1, source_target_pairs={{0,6},{2,4},{4,2},{6,0},{8,14},{10,12},{12,10},{14,8},{16,22},{18,... | collective-permute-start | bytes 884744 | tf_op jit(solution)/shard_map/ppermute | solution.py:426
  124.2 10.4 %copy-start.28 = (bf16[4,12,24,128]{3,2,1,0:T(8,128)(2,1)}, bf16[4,12,24,128]{3,2,1,0:T(8,128)(2,1)S(1)}, u32[]{:S(2)}) copy-start(bf16[4,12,24,128]{3,2,1,0:T(8,128)(2,1)S(1)} %collective-permute-done.12.refs_5_) | copy-start | bytes 884740
  139.5 10.8 %copy-start.42 = (bf16[2,392,128]{2,1,0:T(8,128)(2,1)S(1)}, bf16[2,392,128]{2,1,0:T(8,128)(2,1)}, u32[]{:S(2)}) copy-start(bf16[2,392,128]{2,1,0:T(8,128)(2,1)} %get-tuple-element.55) | copy-start | bytes 602116
  139.5 65.0 %collective-permute-start.30 = (bf16[12,392,128]{2,1,0:T(8,128)(2,1)}, bf16[12,392,128]{2,1,0:T(8,128)(2,1)S(1)}, u32[]{:S(2)}, u32[]{:S(2)}) collective-permute-start(bf16[12,392,128]{2,1,0:T(8,128)(2,1)} %get-tuple-element.73), channel_id=1, source_target_pairs={{0,1},{1,0},{2,3},{3,2},{4,5},{5,4},{6,7},{7,6},{8,9},{9,8},{10,11... | collective-permute-start | bytes 3612680 | tf_op jit(solution)/shard_map/ppermute | solution.py:426
  139.8 10.5 %collective-permute-start.14 = (bf16[2,392,128]{2,1,0:T(8,128)(2,1)}, bf16[2,392,128]{2,1,0:T(8,128)(2,1)S(1)}, u32[]{:S(2)}, u32[]{:S(2)}) collective-permute-start(bf16[2,392,128]{2,1,0:T(8,128)(2,1)} %get-tuple-element.54), channel_id=1, source_target_pairs={{0,2},{2,4},{4,6},{6,8},{8,10},{10,12},{12,14},{14,16},{16,18},{18... | collective-permute-start | bytes 602120 | tf_op jit(solution)/shard_map/ppermute | solution.py:517
  144.5 0.9 copy-start.10
  147.6 16.8 %collective-permute-start.25 = (bf16[4,12,24,128]{3,2,1,0:T(8,128)(2,1)}, bf16[4,12,24,128]{3,2,1,0:T(8,128)(2,1)S(1)}, u32[]{:S(2)}, u32[]{:S(2)}) collective-permute-start(bf16[4,12,24,128]{3,2,1,0:T(8,128)(2,1)} %get-tuple-element.67), channel_id=1, source_target_pairs={{0,8},{2,10},{4,12},{6,14},{8,0},{10,2},{12,4},{14,6},{16,24},{18,... | collective-permute-start | bytes 884744 | tf_op jit(solution)/shard_map/ppermute | solution.py:426
  147.7 20.7 %collective-permute-start.26 = (bf16[4,12,24,128]{3,2,1,0:T(8,128)(2,1)}, bf16[4,12,24,128]{3,2,1,0:T(8,128)(2,1)S(1)}, u32[]{:S(2)}, u32[]{:S(2)}) collective-permute-start(bf16[4,12,24,128]{3,2,1,0:T(8,128)(2,1)} %get-tuple-element.68), channel_id=1, source_target_pairs={{0,16},{2,18},{4,20},{6,22},{8,24},{10,26},{12,28},{14,30},{16,0},... | collective-permute-start | bytes 884744 | tf_op jit(solution)/shard_map/ppermute | solution.py:426
  149.0 27.4 %collective-permute-start.27 = (bf16[4,12,24,128]{3,2,1,0:T(8,128)(2,1)}, bf16[4,12,24,128]{3,2,1,0:T(8,128)(2,1)S(1)}, u32[]{:S(2)}, u32[]{:S(2)}) collective-permute-start(bf16[4,12,24,128]{3,2,1,0:T(8,128)(2,1)} %get-tuple-element.69), channel_id=1, source_target_pairs={{0,24},{2,26},{4,28},{6,30},{8,16},{10,18},{12,20},{14,22},{16,8},... | collective-permute-start | bytes 884744 | tf_op jit(solution)/shard_map/ppermute | solution.py:426
  150.3 7.3 %copy-start.34 = (bf16[2,392,128]{2,1,0:T(8,128)(2,1)}, bf16[2,392,128]{2,1,0:T(8,128)(2,1)S(1)}, u32[]{:S(2)}) copy-start(bf16[2,392,128]{2,1,0:T(8,128)(2,1)S(1)} %collective-permute-done.14.low_ref) | copy-start | bytes 602116
  150.3 7.3 %collective-permute-start.15 = (bf16[2,392,128]{2,1,0:T(8,128)(2,1)S(1)}, bf16[2,392,128]{2,1,0:T(8,128)(2,1)S(1)}, u32[]{:S(2)}, u32[]{:S(2)}) collective-permute-start(bf16[2,392,128]{2,1,0:T(8,128)(2,1)S(1)} %copy-done.42), channel_id=1, source_target_pairs={{2,0},{4,2},{6,4},{8,6},{10,8},{12,10},{14,12},{16,14},{18,16},{20... | collective-permute-start | bytes 602120 | tf_op jit(solution)/shard_map/ppermute | solution.py:518
  164.4 12.0 %copy-start.21 = (bf16[4,12,24,128]{3,2,1,0:T(8,128)(2,1)}, bf16[4,12,24,128]{3,2,1,0:T(8,128)(2,1)S(1)}, u32[]{:S(2)}) copy-start(bf16[4,12,24,128]{3,2,1,0:T(8,128)(2,1)S(1)} %collective-permute-done.25.refs_4_) | copy-start | bytes 884740
  168.4 8.0 %copy-start.22 = (bf16[4,12,24,128]{3,2,1,0:T(8,128)(2,1)}, bf16[4,12,24,128]{3,2,1,0:T(8,128)(2,1)S(1)}, u32[]{:S(2)}) copy-start(bf16[4,12,24,128]{3,2,1,0:T(8,128)(2,1)S(1)} %collective-permute-done.26.refs_5_) | copy-start | bytes 884740
  182.0 14.3 %collective-permute-start.33 = (bf16[4,392,128]{2,1,0:T(8,128)(2,1)}, bf16[4,392,128]{2,1,0:T(8,128)(2,1)S(1)}, u32[]{:S(2)}, u32[]{:S(2)}) collective-permute-start(bf16[4,392,128]{2,1,0:T(8,128)(2,1)} %get-tuple-element.74), channel_id=1, source_target_pairs={{0,1},{1,0},{2,3},{3,2},{4,5},{5,4},{6,7},{7,6},{8,9},{9,8},{10,11... | collective-permute-start | bytes 1204232 | tf_op jit(solution)/shard_map/ppermute | solution.py:426
  183.3 43.1 %collective-permute-start.36 = (bf16[8,392,128]{2,1,0:T(8,128)(2,1)}, bf16[8,392,128]{2,1,0:T(8,128)(2,1)S(1)}, u32[]{:S(2)}, u32[]{:S(2)}) collective-permute-start(bf16[8,392,128]{2,1,0:T(8,128)(2,1)} %get-tuple-element.75), channel_id=1, source_target_pairs={{0,1},{1,0},{2,3},{3,2},{4,5},{5,4},{6,7},{7,6},{8,9},{9,8},{10,11... | collective-permute-start | bytes 2408456 | tf_op jit(solution)/shard_map/ppermute | solution.py:426
  183.5 24.7 %collective-permute-start.28 = (bf16[2,392,128]{2,1,0:T(8,128)(2,1)}, bf16[2,392,128]{2,1,0:T(8,128)(2,1)S(1)}, u32[]{:S(2)}, u32[]{:S(2)}) collective-permute-start(bf16[2,392,128]{2,1,0:T(8,128)(2,1)} %get-tuple-element.70), channel_id=1, source_target_pairs={{0,2},{2,4},{4,6},{6,8},{8,10},{10,12},{12,14},{14,16},{16,18},{18... | collective-permute-start | bytes 602120 | tf_op jit(solution)/shard_map/ppermute | solution.py:517
  185.9 24.3 %collective-permute-start.29 = (bf16[2,392,128]{2,1,0:T(8,128)(2,1)}, bf16[2,392,128]{2,1,0:T(8,128)(2,1)S(1)}, u32[]{:S(2)}, u32[]{:S(2)}) collective-permute-start(bf16[2,392,128]{2,1,0:T(8,128)(2,1)} %get-tuple-element.71), channel_id=1, source_target_pairs={{2,0},{4,2},{6,4},{8,6},{10,8},{12,10},{14,12},{16,14},{18,16},{20... | collective-permute-start | bytes 602120 | tf_op jit(solution)/shard_map/ppermute | solution.py:518
  196.3 22.6 %copy-start.4 = (bf16[4,392,128]{2,1,0:T(8,128)(2,1)}, bf16[4,392,128]{2,1,0:T(8,128)(2,1)S(1)}, u32[]{:S(2)}) copy-start(bf16[4,392,128]{2,1,0:T(8,128)(2,1)S(1)} %collective-permute-done.33.refs_0_) | copy-start | bytes 1204228
  196.4 30.0 %collective-permute-start.35 = (bf16[2,392,128]{2,1,0:T(8,128)(2,1)S(1)}, bf16[2,392,128]{2,1,0:T(8,128)(2,1)S(1)}, u32[]{:S(2)}, u32[]{:S(2)}) collective-permute-start(bf16[2,392,128]{2,1,0:T(8,128)(2,1)S(1)} %get-tuple-element.78), channel_id=1, source_target_pairs={{2,0},{4,2},{6,4},{8,6},{10,8},{12,10},{14,12},{16,14},{18,16},{20... | collective-permute-start | bytes 602120 | tf_op jit(solution)/shard_map/ppermute | solution.py:518
  204.5 14.3 %copy-start.3 = (bf16[12,392,128]{2,1,0:T(8,128)(2,1)}, bf16[12,392,128]{2,1,0:T(8,128)(2,1)S(1)}, u32[]{:S(2)}) copy-start(bf16[12,392,128]{2,1,0:T(8,128)(2,1)S(1)} %collective-permute-done.30.refs_0_) | copy-start | bytes 3612676
  204.6 14.3 %collective-permute-start.32 = (bf16[2,392,128]{2,1,0:T(8,128)(2,1)S(1)}, bf16[2,392,128]{2,1,0:T(8,128)(2,1)S(1)}, u32[]{:S(2)}, u32[]{:S(2)}) collective-permute-start(bf16[2,392,128]{2,1,0:T(8,128)(2,1)S(1)} %get-tuple-element.76), channel_id=1, source_target_pairs={{2,0},{4,2},{6,4},{8,6},{10,8},{12,10},{14,12},{16,14},{18,16},{20... | collective-permute-start | bytes 602120 | tf_op jit(solution)/shard_map/ppermute | solution.py:518
  208.2 4.5 %copy-start.32 = (bf16[2,392,128]{2,1,0:T(8,128)(2,1)}, bf16[2,392,128]{2,1,0:T(8,128)(2,1)S(1)}, u32[]{:S(2)}) copy-start(bf16[2,392,128]{2,1,0:T(8,128)(2,1)S(1)} %collective-permute-done.28.low_ref) | copy-start | bytes 602116
  208.2 10.7 %collective-permute-start.31 = (bf16[2,392,128]{2,1,0:T(8,128)(2,1)S(1)}, bf16[2,392,128]{2,1,0:T(8,128)(2,1)S(1)}, u32[]{:S(2)}, u32[]{:S(2)}) collective-permute-start(bf16[2,392,128]{2,1,0:T(8,128)(2,1)S(1)} %get-tuple-element.77), channel_id=1, source_target_pairs={{0,2},{2,4},{4,6},{6,8},{8,10},{10,12},{12,14},{14,16},{16,18},{18... | collective-permute-start | bytes 602120 | tf_op jit(solution)/shard_map/ppermute | solution.py:517
  210.2 2.5 copy-start.33
  210.2 16.2 %collective-permute-start.34 = (bf16[2,392,128]{2,1,0:T(8,128)(2,1)S(1)}, bf16[2,392,128]{2,1,0:T(8,128)(2,1)S(1)}, u32[]{:S(2)}, u32[]{:S(2)}) collective-permute-start(bf16[2,392,128]{2,1,0:T(8,128)(2,1)S(1)} %get-tuple-element.79), channel_id=1, source_target_pairs={{0,2},{2,4},{4,6},{6,8},{8,10},{10,12},{12,14},{14,16},{16,18},{18... | collective-permute-start | bytes 602120 | tf_op jit(solution)/shard_map/ppermute | solution.py:517
  (18 other events, 13.2 us)
